TPU v7x, 512 devices: a whole 4x4x16 slice. The times are simulated.
512 devices in a mesh: section: 16 (over z_lo, y), dp: 32 (over z_hi, x, core).
Axes of the slice: x: 4, y: 4, z: 16 (z_hi: 4, z_lo: 4; z = z_hi * 4 + z_lo), core: 2. Of those that a mesh axis runs over, the one named last changes fastest.
Arguments:
- acts: bfloat16 [2, 16, 2048, 4096], P(None, 'section', 'dp')
- norm_gain: float32 [16, 4096], P('section'), may hold values from 0.5 to 1.5
- value_grads: bfloat16 [2, 16, 2048, 512], P(None, 'section', 'dp')
- master: float32 [16, 4096, 512], P('section', 'dp'), may hold values from -0.09375 to 0.09375
- moment1: float32 [16, 4096, 512], P('section', 'dp'), may hold values from -6 to 6
- moment2: float32 [16, 4096, 512], P('section', 'dp'), may hold values from 0.25 to 4
- next_acts: bfloat16 [2, 16, 2048, 4096], P(None, 'section', 'dp')
- reward_table: bfloat16 [5, 4096], replicated, may hold values from -6 to 6
- reward_ids: int32 [2, 32], replicated, may hold values from 0 to 4
Outputs:
- input_grads: bfloat16 [2, 16, 2048, 4096], P(None, 'section', 'dp')
- moment1_new: float32 [16, 4096, 512], P('section', 'dp')
- moment2_new: float32 [16, 4096, 512], P('section', 'dp')
- fresh_values: bfloat16 [2, 16, 2048, 512], P(None, 'section', 'dp')
All inputs are finite; a program needn't handle non-finite values.
Results may differ from a plain program's by a relative error of at most 0.015.
Values may be sent and summed in bfloat16 or wider, within the bound.
No kernel may reach another device: no remote copies, remote signals or barrier semaphores. Data moves between devices by JAX's collectives and lax.ppermute only.
A program may use at most 64 MiB of HBM per device.

v0:
```python
import jax
import jax.numpy as jnp
from jax import lax
from jax.sharding import PartitionSpec as P

rms_epsilon = 1e-05
clip_level = 1.0
beta_first = 0.9
beta_second = 0.95
learn_rate = 0.001
decay_rate = 0.01
adam_epsilon = 1e-08
bias_first = 1.0 - 0.9**10
bias_second = 1.0 - 0.95**10


def from_behind(block, axis, distance):
    devices = range(lax.axis_size(axis))
    route = [(i - distance, i) for i in devices if i - distance in devices]
    return lax.ppermute(block, axis, route)


def normalize(floats):
    inverse = lax.rsqrt(jnp.mean(floats * floats, axis=-1, keepdims=True) + rms_epsilon)
    return (floats * inverse, inverse)


def per_device(
    acts, norm_gain, value_grads, master, moment1, moment2, next_acts, reward_table, reward_ids
):
    gain = norm_gain[0]
    values = value_grads[:, 0]
    scaled, inverse = normalize(acts[:, 0].astype(jnp.float32))
    normed = (scaled * gain).astype(jnp.bfloat16)
    weights_old = master[0].astype(jnp.bfloat16)
    tok_count = values.shape[1]
    value_width = values.shape[2]
    upstream = jnp.einsum(
        "mtk,dk->mtd",
        values,
        lax.all_gather(weights_old, "dp", axis=0, tiled=True),
        preferred_element_type=jnp.float32,
    )
    columns = normed
    grad = lax.psum_scatter(
        jnp.einsum("mtd,mtk->dk", columns, values, preferred_element_type=jnp.float32).astype(
            jnp.bfloat16
        ),
        "dp",
        scatter_dimension=0,
        tiled=True,
    ).astype(jnp.float32)
    mixed = gain * upstream
    branch = inverse * (mixed - scaled * jnp.mean(scaled * mixed, axis=-1, keepdims=True))
    suffix = branch
    distance = 1
    while distance < lax.axis_size("section"):
        suffix = suffix + from_behind(suffix.astype(jnp.bfloat16), "section", -distance).astype(
            suffix.dtype
        )
        distance = distance * 2
    input_grads = suffix.astype(jnp.bfloat16)[:, None]
    model_width = acts.shape[3]
    entries = lax.axis_size("section") * model_width * value_width
    squares = lax.psum(jnp.sum(grad * grad), ("section", "dp"))
    rms = jnp.sqrt(squares / entries + 1e-12)
    clipped = grad * jnp.minimum(1.0, clip_level / rms)
    moment1_new = beta_first * moment1[0] + (1.0 - beta_first) * clipped
    moment2_new = beta_second * moment2[0] + (1.0 - beta_second) * clipped * clipped
    update = (
        moment1_new / bias_first / (jnp.sqrt(moment2_new / bias_second) + adam_epsilon)
        + decay_rate * master[0]
    )
    weights_new = (master[0] - learn_rate * update).astype(jnp.bfloat16)
    local_pos = jnp.arange(tok_count, dtype=jnp.int32)
    first_rows = jnp.logical_and(local_pos == 0, lax.axis_index("section") == 0)
    seq_match = jnp.arange(reward_ids.shape[1], dtype=jnp.int32) == lax.axis_index("dp")
    seq_bins = jnp.sum(jnp.where(seq_match[None, :], reward_ids, 0), axis=-1)
    bin_match = (
        seq_bins[:, None] == jnp.arange(reward_table.shape[0], dtype=jnp.int32)[None, :]
    ).astype(jnp.bfloat16)
    embeds = jnp.dot(bin_match, reward_table, preferred_element_type=jnp.float32)
    fresh_inputs = jnp.where(
        first_rows[None, :, None], embeds[:, None, :], next_acts[:, 0].astype(jnp.float32)
    )
    fresh_scaled, unused = normalize(fresh_inputs)
    fresh_normed = (fresh_scaled * gain).astype(jnp.bfloat16)
    columns = fresh_normed
    fresh = jnp.einsum(
        "mtd,dk->mtk",
        columns,
        lax.all_gather(weights_new, "dp", axis=0, tiled=True),
        preferred_element_type=jnp.float32,
    )
    fresh_values = fresh.astype(jnp.bfloat16)[:, None]
    return (input_grads, moment1_new[None], moment2_new[None], fresh_values)


def solution(mesh):
    return jax.shard_map(
        per_device,
        mesh=mesh,
        in_specs=(
            P(None, "section", "dp", None),
            P("section", None),
            P(None, "section", "dp", None),
            P("section", "dp", None),
            P("section", "dp", None),
            P("section", "dp", None),
            P(None, "section", "dp", None),
            P(),
            P(),
        ),
        out_specs=(
            P(None, "section", "dp", None),
            P("section", "dp", None),
            P("section", "dp", None),
            P(None, "section", "dp", None),
        ),
        check_vma=False,
    )
```

profile of v0, /device:TPU:1, one launch (start us, length us, event | category | flops | bytes accessed | tf_op | source)
XLA Modules:
  0.0 459.3 jit_solution(1690286223195854917)
XLA Ops:
  7.2 0.0 copy-start
  7.2 0.0 reduce-scatter.2.cloned.1.call-start
  7.2 1.6 fusion.10
  8.8 0.0 copy-start.10
  8.8 0.0 copy-done
  8.8 4.6 bitcast_convert_fusion
  13.3 0.0 copy-done.10
  13.3 0.0 copy-start.4
  13.4 0.0 copy-start.1
  13.4 0.0 copy-start.6
  13.4 0.0 reduce-scatter.2.cloned.1.call-update
  13.4 0.0 all-gather.3.cloned.1.call-start
  13.4 0.9 copy-done.4
  14.3 0.7 bitcast_convert_fusion.1
  15.0 0.0 all-gather.3.cloned.1.call-update
  15.0 0.0 all-gather.5.cloned.1.call-start
  15.0 142.2 %reduce-scatter.2.cloned.1.call-done = bf16[128,512]{1,0:T(8,128)(2,1)} async-done(((bf16[4096,512]{1,0:T(8,128)(2,1)}), bf16[128,512]{1,0:T(8,128)(2,1)}) %reduce-scatter.2.cloned.1.call-update) | async-done | bytes 131088 | tf_op jit(solution)/shard_map/reduce_scatter | solution.py:45
  157.3 1.6 fusion.40
  158.8 114.2 %psum.7 = f32[]{:T(128)} all-reduce(f32[]{:T(128)} %fusion.40), channel_id=1, replica_groups=mesh['section'=16,'dp'=32] {'section','dp'}, use_global_device_ids=true, to_apply=%region_4.0 | all-reduce | flops 1 | bytes 8 | tf_op jit(solution)/shard_map/psum | solution.py:65
  273.7 0.0 all-gather.3.cloned.1.call-done
  273.7 0.0 copy-done.1
  273.7 0.0 copy-done.6
  273.8 0.0 copy-start.11
  273.8 3.8 fusion.7
  277.5 0.0 copy-start.13
  277.6 0.0 copy-done.11
  277.6 0.0 copy-start.5
  277.6 0.0 copy-start.7
  277.6 0.0 copy-start.8
  277.6 1.5 fusion.49
  279.1 0.0 copy-done.13
  279.1 1.3 collective-permute-start
  280.4 0.0 copy-done.5
  280.4 0.0 copy-done.7
  280.4 0.0 copy-done.8
  280.4 1.0 fusion.44
  281.4 0.0 all-gather.5.cloned.1.call-update
  281.4 0.0 copy-start.12
  281.4 0.0 copy-start.14
  281.4 24.0 %collective-permute-done = bf16[2,64,4096]{2,1,0:T(8,128)(2,1)} collective-permute-done((bf16[2,64,4096]{2,1,0:T(8,128)(2,1)}, bf16[2,64,4096]{2,1,0:T(8,128)(2,1)}, u32[]{:S(2)}, u32[]{:S(2)}) %collective-permute-start) | collective-permute-done | bytes 1048608 | tf_op jit(solution)/shard_map/ppermute | solution.py:20
  305.4 1.9 fusion.18
  307.2 1.3 collective-permute-start.1
  308.5 25.3 %collective-permute-done.1 = bf16[2,64,4096]{2,1,0:T(8,128)(2,1)S(1)} collective-permute-done((bf16[2,64,4096]{2,1,0:T(8,128)(2,1)S(1)}, bf16[2,64,4096]{2,1,0:T(8,128)(2,1)S(1)}, u32[]{:S(2)}, u32[]{:S(2)}) %collective-permute-start.1) | collective-permute-done | bytes 1048608 | tf_op jit(solution)/shard_map/ppermute | solution.py:20
  333.8 0.0 copy-done.12
  333.8 0.0 copy-done.14
  333.8 2.0 fusion.54
  335.8 0.0 copy-start.2
  335.8 1.3 collective-permute-start.2
  337.1 59.7 %collective-permute-done.2 = bf16[2,64,4096]{2,1,0:T(8,128)(2,1)S(1)} collective-permute-done((bf16[2,64,4096]{2,1,0:T(8,128)(2,1)S(1)}, bf16[2,64,4096]{2,1,0:T(8,128)(2,1)S(1)}, u32[]{:S(2)}, u32[]{:S(2)}) %collective-permute-start.2) | collective-permute-done | bytes 1048608 | tf_op jit(solution)/shard_map/ppermute | solution.py:20
  396.8 0.0 copy-start.15
  396.8 0.0 copy-start.9
  396.8 0.0 copy-start.3
  396.8 1.2 fusion.19
  398.0 0.0 copy-done.2
  398.0 1.3 collective-permute-start.3
  399.4 0.0 copy-done.15
  399.4 0.1 select_reduce_fusion
  399.5 0.0 copy-done.9
  399.5 0.2 fusion.50
  399.7 0.0 copy-done.3
  399.7 0.4 fusion.15
  400.1 46.1 %collective-permute-done.3 = bf16[2,64,4096]{2,1,0:T(8,128)(2,1)S(1)} collective-permute-done((bf16[2,64,4096]{2,1,0:T(8,128)(2,1)}, bf16[2,64,4096]{2,1,0:T(8,128)(2,1)S(1)}, u32[]{:S(2)}, u32[]{:S(2)}) %collective-permute-start.3) | collective-permute-done | bytes 1048608 | tf_op jit(solution)/shard_map/ppermute | solution.py:20
  446.2 2.9 fusion.26
  449.1 3.6 fusion.23
  (6 shorter events, 0.0 us)
Async XLA Ops:
  7.2 1.6 copy-start
  7.2 150.1 %reduce-scatter.2.cloned.1.call-start = ((), (), s32[]{:S(2)}) async-start(), calls=%async_computation.2 | async-start | bytes 4325376 | tf_op jit(solution)/shard_map/reduce_scatter | solution.py:45
  8.8 4.6 copy-start.10
  13.3 1.0 copy-start.4
  13.4 260.4 %copy-start.1 = (bf16[2,1,64,4096]{3,2,1,0:T(8,128)(2,1)S(1)}, bf16[2,1,64,4096]{3,2,1,0:T(8,128)(2,1)}, u32[]{:S(2)}) copy-start(bf16[2,1,64,4096]{3,2,1,0:T(8,128)(2,1)} %param.9) | copy-start | bytes 3145732
  13.4 260.4 %copy-start.6 = (f32[1,4096]{1,0:T(1,128)S(1)}, f32[1,4096]{1,0:T(1,128)}, u32[]{:S(2)}) copy-start(f32[1,4096]{1,0:T(1,128)} %param.10) | copy-start | bytes 49156
  13.4 260.3 %all-gather.3.cloned.1.call-start = ((), (), s32[]{:S(2)}) async-start(), calls=%async_computation.1 | async-start | bytes 4325376 | tf_op jit(solution)/shard_map/all_gather | solution.py:41
  15.0 434.1 %all-gather.5.cloned.1.call-start = ((), (), s32[]{:S(2)}) async-start(), calls=%async_computation.3 | async-start | bytes 4325376 | tf_op jit(solution)/shard_map/all_gather | solution.py:92
  273.8 3.8 copy-start.11
  277.5 1.5 copy-start.13
  277.6 2.8 copy-start.5
  277.6 2.8 copy-start.7
  277.6 2.8 copy-start.8
  279.1 26.3 %collective-permute-start = (bf16[2,64,4096]{2,1,0:T(8,128)(2,1)}, bf16[2,64,4096]{2,1,0:T(8,128)(2,1)}, u32[]{:S(2)}, u32[]{:S(2)}) collective-permute-start(bf16[2,64,4096]{2,1,0:T(8,128)(2,1)} %fusion.49), channel_id=1, source_target_pairs={{32,0},{64,32},{96,64},{128,96},{160,128},{192,160},{224,192},{256... | collective-permute-start | bytes 3145736 | tf_op jit(solution)/shard_map/ppermute | solution.py:20
  281.4 52.4 %copy-start.12 = (f32[2,64]{1,0:T(2,128)S(1)}, f32[2,64]{1,0:T(2,128)}, u32[]{:S(2)}) copy-start(f32[2,64]{1,0:T(2,128)} %copy-done.10) | copy-start | bytes 1540
  281.4 52.4 %copy-start.14 = (f32[2,64]{1,0:T(2,128)S(1)}, f32[2,64]{1,0:T(2,128)}, u32[]{:S(2)}) copy-start(f32[2,64]{1,0:T(2,128)} %copy-done.13) | copy-start | bytes 1540
  307.2 26.6 %collective-permute-start.1 = (bf16[2,64,4096]{2,1,0:T(8,128)(2,1)S(1)}, bf16[2,64,4096]{2,1,0:T(8,128)(2,1)S(1)}, u32[]{:S(2)}, u32[]{:S(2)}) collective-permute-start(bf16[2,64,4096]{2,1,0:T(8,128)(2,1)S(1)} %fusion.18), channel_id=1, source_target_pairs={{64,0},{96,32},{128,64},{160,96},{192,128},{224,160},{256,192},{28... | collective-permute-start | bytes 3145736 | tf_op jit(solution)/shard_map/ppermute | solution.py:20
  335.8 62.2 %copy-start.2 = (f32[2,64,4096]{2,1,0:T(8,128)}, f32[2,64,4096]{2,1,0:T(8,128)S(1)}, u32[]{:S(2)}) copy-start(f32[2,64,4096]{2,1,0:T(8,128)S(1)} %get-tuple-element.9) | copy-start | bytes 6291460
  335.8 61.0 %collective-permute-start.2 = (bf16[2,64,4096]{2,1,0:T(8,128)(2,1)S(1)}, bf16[2,64,4096]{2,1,0:T(8,128)(2,1)S(1)}, u32[]{:S(2)}, u32[]{:S(2)}) collective-permute-start(bf16[2,64,4096]{2,1,0:T(8,128)(2,1)S(1)} %get-tuple-element.8), channel_id=1, source_target_pairs={{128,0},{160,32},{192,64},{224,96},{256,128},{288,160},{320,192},{... | collective-permute-start | bytes 3145736 | tf_op jit(solution)/shard_map/ppermute | solution.py:20
  396.8 2.5 copy-start.15
  396.8 2.6 copy-start.9
  396.8 2.9 copy-start.3
  398.0 48.2 %collective-permute-start.3 = (bf16[2,64,4096]{2,1,0:T(8,128)(2,1)}, bf16[2,64,4096]{2,1,0:T(8,128)(2,1)S(1)}, u32[]{:S(2)}, u32[]{:S(2)}) collective-permute-start(bf16[2,64,4096]{2,1,0:T(8,128)(2,1)} %fusion.19), channel_id=1, source_target_pairs={{256,0},{288,32},{320,64},{352,96},{384,128},{416,160},{448,192},{... | collective-permute-start | bytes 3145736 | tf_op jit(solution)/shard_map/ppermute | solution.py:20
Sparse Core Ops, SparseCore 0:
  13.5 143.7 reduce-scatter.1
  161.4 92.7 all-gather.2
  281.5 91.8 all-gather.4
where the time goes:
time: 463 us; the launch traced here: 459 us
  waiting for transfers between devices  297 us (64%)
  blocking collectives  114 us (25%)
  other arithmetic  14.8 us (3%)
  between operations  14.7 us (3%)
  matrix products  12.1 us (3%)
  starting transfers between devices  5.27 us (1%)
    ppermute x4, waiting for transfers between devices, from_behind(): return lax.ppermute(block, axis, route)  155 us
    reduce_scatter x1, waiting for transfers between devices, per_device(): lax.psum_scatter(jnp.einsum('mtd,mtk->dk', columns, values, preferred_ele...  142 us
    psum x1, blocking collectives, per_device(): squares = lax.psum(jnp.sum(grad * grad), ('section', 'dp'))  114 us
  transfers between devices with their start and end apart: 7, of which 5 were waited for; matrix products, arithmetic and copies ran while one was open for 3% of the time, Pallas kernels for 0%

commit v1 on v0

v1 whole, which is shorter than its diff:
```python
import jax
import jax.numpy as jnp
from jax import lax
from jax.sharding import Mesh
from jax.sharding import PartitionSpec as P

rms_epsilon = 1e-05
clip_level = 1.0
beta_first = 0.9
beta_second = 0.95
learn_rate = 0.001
decay_rate = 0.01
adam_epsilon = 1e-08
bias_first = 1.0 - 0.9**10
bias_second = 1.0 - 0.95**10

factors = {"section": (4, 4), "dp": (4, 4, 2)}
axes = ("zlo", "y", "zhi", "x", "core")
section = ("zlo", "y")
dp = ("zhi", "x", "core")
near = ("x", "core")
f32 = jnp.float32
bf16 = jnp.bfloat16


def exchange(blocks, axis):
    return lax.all_to_all(blocks, axis, 0, 0)


def total(value, axis):
    size = lax.axis_size(axis)
    return jnp.sum(exchange(jnp.broadcast_to(value, (size,) + value.shape), axis), axis=0)


def from_behind(block, axis, distance):
    devices = range(lax.axis_size(axis))
    return lax.ppermute(block, axis, [(i + distance, i) for i in devices if i + distance in devices])


def inverse_rms(floats):
    return lax.rsqrt(jnp.mean(floats * floats, axis=-1, keepdims=True) + rms_epsilon)


def per_device(
    acts, norm_gain, value_grads, master, moment1, moment2, next_acts, reward_table, reward_ids
):
    micro, _, tok_dev, width = acts.shape
    kvw = value_grads.shape[3]
    toks = micro * tok_dev
    far = lax.axis_size("zhi")
    group = lax.axis_size("x") * lax.axis_size("core")
    layers_y = lax.axis_size("y")
    rows = width // (far * group)
    own_width = far * rows
    spot = lax.axis_index("x") * lax.axis_size("core") + lax.axis_index("core")
    gain = norm_gain[0]
    own_gain = lax.dynamic_index_in_dim(gain.reshape(far, group, rows), spot, 1, False)
    own_gain = own_gain.reshape(own_width)

    def by_features(block):
        parts = block.reshape(toks, far, group, rows)
        return jnp.transpose(parts, (2, 0, 1, 3)).reshape(group, toks, own_width)

    flat = acts[:, 0].reshape(toks, width)
    mine = exchange(by_features(flat), near).reshape(group * toks, own_width).astype(f32)
    inverse = inverse_rms(flat.astype(f32))
    values = value_grads[:, 0].reshape(toks, kvw).astype(f32)
    values = lax.all_gather((values * inverse).astype(bf16), near, axis=0, tiled=True)
    weights_old = lax.all_gather(master[0].astype(bf16), "zhi", axis=0, tiled=True)

    partial = jnp.einsum("td,tk->dk", mine.astype(bf16), values, preferred_element_type=f32)
    partial = (partial * own_gain[:, None]).astype(bf16)
    grad = jnp.sum(exchange(partial.reshape(far, rows, kvw), "zhi").astype(f32), axis=0)
    squares = jnp.broadcast_to(jnp.sum(grad * grad), (8, 128))
    squares = total(total(squares, ("zlo", "zhi")), ("y", "x", "core"))[0, 0]
    entries = lax.axis_size(section) * width * kvw
    rms = jnp.sqrt(squares / entries + 1e-12)
    clipped = grad * jnp.minimum(1.0, clip_level / rms)
    moment1_new = beta_first * moment1[0] + (1.0 - beta_first) * clipped
    moment2_new = beta_second * moment2[0] + (1.0 - beta_second) * clipped * clipped
    update = (
        moment1_new / bias_first / (jnp.sqrt(moment2_new / bias_second) + adam_epsilon)
        + decay_rate * master[0]
    )
    weights_new = (master[0] - learn_rate * update).astype(bf16)
    weights_new = lax.all_gather(weights_new, "zhi", axis=0, tiled=True)

    mixed = own_gain * jnp.einsum("tk,dk->td", values, weights_old, preferred_element_type=f32)
    sums = total(jnp.stack([jnp.sum(mine * mine, axis=1), jnp.sum(mine * mixed, axis=1)]), near)
    sums = sums / width
    inv = lax.rsqrt(sums[0] + rms_epsilon)[:, None]
    branch = mixed - mine * inv * (inv * sums[1][:, None])
    parts = jnp.transpose(branch.astype(bf16).reshape(group * toks, far, rows), (1, 0, 2))
    parts = exchange(parts, "y").astype(f32)
    suffix = [parts[layers_y - 1]]
    for layer in reversed(range(layers_y - 1)):
        suffix.insert(0, suffix[0] + parts[layer])
    top = suffix[0].astype(bf16)
    behind = from_behind(top, "zlo", 1).astype(f32)
    pair = (suffix[0] + behind).astype(bf16)
    behind = behind + from_behind(pair, "zlo", 2).astype(f32)
    suffix = jnp.stack([(s + behind).astype(bf16) for s in suffix])
    suffix = exchange(suffix, "y").reshape(far, group, toks, rows)
    suffix = exchange(jnp.transpose(suffix, (1, 2, 0, 3)), near)
    input_grads = jnp.transpose(suffix, (1, 2, 0, 3)).reshape(micro, 1, tok_dev, width)

    local_pos = jnp.arange(tok_dev, dtype=jnp.int32)
    first_rows = jnp.logical_and(local_pos == 0, lax.axis_index(section) == 0)
    seq_match = jnp.arange(reward_ids.shape[1], dtype=jnp.int32) == lax.axis_index(dp)
    seq_bins = jnp.sum(jnp.where(seq_match[None, :], reward_ids, 0), axis=-1)
    bin_match = (
        seq_bins[:, None] == jnp.arange(reward_table.shape[0], dtype=jnp.int32)[None, :]
    ).astype(bf16)
    embeds = jnp.dot(bin_match, reward_table, preferred_element_type=f32)
    fresh_inputs = jnp.where(
        first_rows[None, :, None], embeds[:, None, :], next_acts[:, 0].astype(f32)
    ).reshape(toks, width)
    fresh_normed = (fresh_inputs * inverse_rms(fresh_inputs) * gain).astype(bf16)
    fresh_normed = exchange(by_features(fresh_normed), near).reshape(group * toks, own_width)
    fresh = jnp.dot(fresh_normed, weights_new, preferred_element_type=f32)
    fresh = exchange(fresh.astype(bf16).reshape(group, toks, kvw), near)
    fresh = jnp.sum(fresh.astype(f32), axis=0).astype(bf16)
    fresh_values = fresh.reshape(micro, 1, tok_dev, kvw)
    return (input_grads, moment1_new[None], moment2_new[None], fresh_values)


def solution(mesh):
    fine = Mesh(mesh.devices.reshape(factors["section"] + factors["dp"]), axes)
    return jax.shard_map(
        per_device,
        mesh=fine,
        in_specs=(
            P(None, section, dp, None),
            P(section, None),
            P(None, section, dp, None),
            P(section, dp, None),
            P(section, dp, None),
            P(section, dp, None),
            P(None, section, dp, None),
            P(),
            P(),
        ),
        out_specs=(
            P(None, section, dp, None),
            P(section, dp, None),
            P(section, dp, None),
            P(None, section, dp, None),
        ),
        check_vma=False,
    )
```

time: 463 us -> 263 us (0.57)
  waiting for transfers between devices: 297 us -> 83.8 us
  starting transfers between devices: 5.27 us -> 56.9 us
  blocking collectives: 114 us -> 64.4 us
  local copies, waits for them, and re-layouts: 0.94 us -> 18.2 us
  matrix products: 12.1 us -> 6.82 us
    reduce_scatter x1 -> x0, waiting for transfers between devices: 142 us -> none  [per_device(): lax.psum_scatter(jnp.einsum('mtd,mtk->dk', columns, values, preferred_ele...]
    ppermute x4 -> x2, waiting for transfers between devices: 155 us -> 14.9 us  [from_behind(): lax.ppermute(block, axis, [(i + distance, i) for i in devices if i + dist...]
    psum x1 -> x0, blocking collectives: 114 us -> none  [per_device(): squares = lax.psum(jnp.sum(grad * grad), ('section', 'dp'))]
    all_to_all x0 -> x9, waiting for transfers between devices: none -> 68.8 us  [exchange(): return lax.all_to_all(blocks, axis, 0, 0)]
    all_to_all x0 -> x9, starting transfers between devices: none -> 54.3 us  [exchange(): return lax.all_to_all(blocks, axis, 0, 0)]
    all_gather x0 -> x2, blocking collectives: none -> 50.2 us  [the longest x1 26.1 us: per_device(): lax.all_gather(master[0].astype(bf16), 'zhi', axis=0, tiled=True)]
    all_to_all x0 -> x1, blocking collectives: none -> 14.2 us  [exchange(): return lax.all_to_all(blocks, axis, 0, 0)]
    dot_general x4, matrix products: 12.1 us -> 6.82 us  [the longest x1 2.82 us: per_device(): jnp.einsum('td,tk->dk', mine.astype(bf16), values, preferred_element_type...]
  transfers between devices with their start and end apart: 7 -> 12, of which waited for: 5 -> 7; matrix products, arithmetic and copies ran while one was open for 3% -> 12% of each run, Pallas kernels for 0% -> 0%
where the time goes in v1:
time: 263 us; the launch traced here: 262 us
  waiting for transfers between devices  83.8 us (32%)
  blocking collectives  64.4 us (24%)
  starting transfers between devices  56.9 us (22%)
  local copies, waits for them, and re-layouts  18.2 us (7%)
  other arithmetic  16.7 us (6%)
  between operations  15 us (6%)
  matrix products  6.82 us (3%)
    all_to_all x9, waiting for transfers between devices, exchange(): return lax.all_to_all(blocks, axis, 0, 0)  68.8 us
    all_to_all x9, starting transfers between devices, exchange(): return lax.all_to_all(blocks, axis, 0, 0)  54.3 us
    all_gather x1, blocking collectives, per_device(): lax.all_gather(master[0].astype(bf16), 'zhi', axis=0, tiled=True)  26.1 us
    all_gather x1, blocking collectives, per_device(): weights_new = lax.all_gather(weights_new, 'zhi', axis=0, tiled=True)  24.2 us
    ppermute x2, waiting for transfers between devices, from_behind(): lax.ppermute(block, axis, [(i + distance, i) for i in devices if i + dist...  14.9 us
    all_to_all x1, blocking collectives, exchange(): return lax.all_to_all(blocks, axis, 0, 0)  14.2 us
  transfers between devices with their start and end apart: 12, of which 7 were waited for; matrix products, arithmetic and copies ran while one was open for 12% of the time, Pallas kernels for 0%

profile of v1, /device:TPU:1, one launch (start us, length us, event | category | flops | bytes accessed | tf_op | source)
XLA Modules:
  0.0 261.9 jit_solution(5808538421705517018)
XLA Ops:
  7.2 0.0 copy-start
  7.2 0.0 all-gather.2.cloned.1.call-start
  7.2 1.6 multiply_reduce_fusion.1
  8.9 0.1 rsqrt.38
  8.9 1.6 fusion.25
  10.6 0.0 all-gather.2.cloned.1.call-update
  10.6 0.2 copy.51
  10.9 0.0 copy-start.9
  10.9 1.7 copy.41
  12.6 10.3 %all-to-all-start = ((bf16[8,128,512]{1,2,0:T(8,128)(2,1)}), bf16[8,128,512]{1,2,0:T(8,128)(2,1)S(1)}, u32[]{:S(2)}, u32[]{:S(2)}) async-start(bf16[8,128,512]{1,2,0:T(8,128)(2,1)} %bitcast.5), calls=%async_computation | async-start | bytes 2097152 | tf_op jit(solution)/shard_map/all_to_all | solution.py:27
  23.0 26.1 %all_gather.10 = bf16[512,512]{1,0:T(8,128)(2,1)} all-gather(bf16[128,512]{1,0:T(8,128)(2,1)S(1)} %bitcast_convert_fusion), channel_id=1, replica_groups=mesh['zlo'=4,'y'=4,'zhi'=4,'x'=4,'core'=2] {'zhi'}, dimensions={0}, use_global_device_ids=true | all-gather | bytes 655360 | tf_op jit(solution)/shard_map/all_gather | solution.py:69
  49.1 0.2 multiply_reduce_fusion
  49.3 0.0 all-gather.2.cloned.1.call-done
  49.3 2.1 fusion
  51.5 14.2 %all_to_all.50 = f32[8,2,1024]{2,1,0:T(2,128)S(1)} all-to-all(f32[8,2,1024]{2,1,0:T(2,128)S(1)} %broadcast_in_dim.52), channel_id=1, replica_groups=mesh['zlo'=4,'y'=4,'zhi'=4,'x'=4,'core'=2] {'x','core'}, dimensions={0} | all-to-all | bytes 131072 | tf_op jit(solution)/shard_map/all_to_all | solution.py:27
  65.7 1.4 fusion.3
  67.1 4.2 %all-to-all-start.2 = ((bf16[4,1024,128]{1,2,0:T(8,128)(2,1)}), bf16[4,1024,128]{1,2,0:T(8,128)(2,1)S(1)}, u32[]{:S(2)}, u32[]{:S(2)}) async-start(bf16[4,1024,128]{1,2,0:T(8,128)(2,1)} %bitcast.156), calls=%async_computation.2 | async-start | bytes 2097152 | tf_op jit(solution)/shard_map/all_to_all | solution.py:27
  71.3 2.8 %fusion.6 = bf16[512,512]{0,1:T(8,128)(2,1)} fusion(bf16[1024,512]{1,0:T(8,128)(2,1)} %all-gather.2.cloned.1.call-done, f32[512]{0:T(512)S(1)} %bitcast.168, bf16[8,128,512]{1,2,0:T(8,128)(2,1)S(1)} %all-to-all-done), kind=kOutput, calls=%fused_computation.14 | convolution fusion | flops 537395200 | bytes 2623488 | tf_op jit(solution)/shard_map/td,tk->dk/dot_general | solution.py:71
  74.1 11.2 %all-to-all-done.2 = bf16[4,1024,128]{1,2,0:T(8,128)(2,1)S(1)} async-done(((bf16[4,1024,128]{1,2,0:T(8,128)(2,1)}), bf16[4,1024,128]{1,2,0:T(8,128)(2,1)S(1)}, u32[]{:S(2)}, u32[]{:S(2)}) %all-to-all-start.2) | async-done | bytes 1048608 | tf_op jit(solution)/shard_map/all_to_all | solution.py:27
  85.3 6.4 %all-to-all-start.5 = ((bf16[4,128,512]{2,1,0:T(8,128)(2,1)}), bf16[4,128,512]{2,1,0:T(8,128)(2,1)}, u32[]{:S(2)}, u32[]{:S(2)}) async-start(bf16[4,128,512]{2,1,0:T(8,128)(2,1)} %bitcast.160), calls=%async_computation.5 | async-start | bytes 1048576 | tf_op jit(solution)/shard_map/all_to_all | solution.py:27
  91.7 0.1 select_reduce_fusion
  91.9 0.2 fusion.30
  92.1 0.4 fusion.5
  92.5 0.6 rsqrt.42
  93.1 0.2 broadcast_in_dim.59
  93.3 1.7 copy.52
  95.0 0.7 broadcast_in_dim.55
  95.7 1.6 copy.53
  97.3 0.2 convert_element_type.97
  97.6 0.2 fusion.34
  97.8 1.3 collective-permute-start
  99.1 19.7 %all-to-all-done.5 = bf16[4,128,512]{2,1,0:T(8,128)(2,1)} async-done(((bf16[4,128,512]{2,1,0:T(8,128)(2,1)}), bf16[4,128,512]{2,1,0:T(8,128)(2,1)}, u32[]{:S(2)}, u32[]{:S(2)}) %all-to-all-start.5) | async-done | bytes 524320 | tf_op jit(solution)/shard_map/all_to_all | solution.py:27
  118.8 1.1 convert_reduce_fusion
  119.9 0.7 multiply_reduce_fusion.2
  120.6 1.3 broadcast_in_dim_broadcast_in_dim.3
  121.9 6.4 %all-to-all-start.6 = ((f32[16,8,128]{2,1,0:T(8,128)}), f32[16,8,128]{2,1,0:T(8,128)S(1)}, u32[]{:S(2)}, u32[]{:S(2)}) async-start(f32[16,8,128]{2,1,0:T(8,128)} %broadcast_in_dim_broadcast_in_dim.3), calls=%async_computation.6 | async-start | bytes 131072 | tf_op jit(solution)/shard_map/all_to_all | solution.py:27
  128.3 3.6 %fusion.7 = bf16[8,128,4,128]{3,0,2,1:T(8,128)(2,1)} fusion(f32[128,4,8,128]{3,2,1,0:T(8,128)} %bitcast.147, f32[128,4,8,128]{3,2,1,0:T(8,128)} %bitcast.148, f32[4,8,128]{2,1,0:T(8,128)S(1)} %bitcast.165, f32[128]{0:T(128)} %rsqrt.42, pred[128]{0:T(512)(128)(4,1)} %broadcast_in_dim.55), kind=kLoop, calls=%fused_computation.15 | loop fusion | flops 2097152 | bytes 5259904 | tf_op jit(solution)/shard_map/transpose | solution.py:62
  131.8 2.7 %copy.46 = bf16[8,128,4,128]{1,3,2,0:T(8,128)(2,1)} copy(bf16[8,128,4,128]{3,0,2,1:T(8,128)(2,1)} %fusion.7) | data formatting | bytes 2097152 | tf_op jit(solution)/shard_map/transpose | solution.py:62
  134.6 5.3 %all-to-all-done.6 = f32[16,8,128]{2,1,0:T(8,128)S(1)} async-done(((f32[16,8,128]{2,1,0:T(8,128)}), f32[16,8,128]{2,1,0:T(8,128)S(1)}, u32[]{:S(2)}, u32[]{:S(2)}) %all-to-all-start.6) | async-done | bytes 65568 | tf_op jit(solution)/shard_map/all_to_all | solution.py:27
  139.9 8.8 %all-to-all-start.8 = ((bf16[8,128,512]{1,2,0:T(8,128)(2,1)}), bf16[8,128,512]{1,2,0:T(8,128)(2,1)}, u32[]{:S(2)}, u32[]{:S(2)}) async-start(bf16[8,128,512]{1,2,0:T(8,128)(2,1)} %bitcast.152), calls=%async_computation.8 | async-start | bytes 2097152 | tf_op jit(solution)/shard_map/all_to_all | solution.py:27
  148.7 0.1 fusion.10
  148.8 1.3 collective-permute-start.1
  150.1 14.9 %collective-permute-done.1 = bf16[1024,128]{0,1:T(8,128)(2,1)S(1)} collective-permute-done((bf16[1024,128]{0,1:T(8,128)(2,1)S(1)}, bf16[1024,128]{0,1:T(8,128)(2,1)S(1)}, u32[]{:S(2)}, u32[]{:S(2)}) %collective-permute-start.1) | collective-permute-done | bytes 262176 | tf_op jit(solution)/shard_map/ppermute | solution.py:37
  165.0 1.2 fusion.22
  166.2 0.7 broadcast_in_dim.53
  166.9 6.1 %all-to-all-start.7 = ((f32[32,8,128]{2,1,0:T(8,128)}), f32[32,8,128]{2,1,0:T(8,128)S(1)}, u32[]{:S(2)}, u32[]{:S(2)}) async-start(f32[32,8,128]{2,1,0:T(8,128)} %broadcast_in_dim.53), calls=%async_computation.7 | async-start | bytes 262144 | tf_op jit(solution)/shard_map/all_to_all | solution.py:27
  173.0 2.2 pad_maximum_fusion
  175.2 5.4 %all-to-all-done.7 = f32[32,8,128]{2,1,0:T(8,128)S(1)} async-done(((f32[32,8,128]{2,1,0:T(8,128)}), f32[32,8,128]{2,1,0:T(8,128)S(1)}, u32[]{:S(2)}, u32[]{:S(2)}) %all-to-all-start.7) | async-done | bytes 131104 | tf_op jit(solution)/shard_map/all_to_all | solution.py:27
  180.6 0.7 copy-done.7
  181.3 3.5 %all-to-all-start.3 = ((bf16[4,1024,128]{1,2,0:T(8,128)(2,1)}), bf16[4,1024,128]{1,2,0:T(8,128)(2,1)S(1)}, u32[]{:S(2)}, u32[]{:S(2)}) async-start(bf16[4,1024,128]{1,2,0:T(8,128)(2,1)} %pad_maximum_fusion), calls=%async_computation.3 | async-start | bytes 2097152 | tf_op jit(solution)/shard_map/all_to_all | solution.py:27
  184.8 1.5 copy.47
  186.4 0.5 slice.27
  187.6 0.2 fusion.28
  187.9 24.2 %all_gather.11 = bf16[512,512]{1,0:T(8,128)(2,1)S(1)} all-gather(bf16[128,512]{1,0:T(8,128)(2,1)S(1)} %fusion.28), channel_id=1, replica_groups=mesh['zlo'=4,'y'=4,'zhi'=4,'x'=4,'core'=2] {'zhi'}, dimensions={0}, use_global_device_ids=true | all-gather | bytes 655360 | tf_op jit(solution)/shard_map/all_gather | solution.py:86
  212.0 1.7 convolution_convert_fusion
  213.7 4.2 %all-to-all-start.9 = ((bf16[8,128,512]{2,1,0:T(8,128)(2,1)}), bf16[8,128,512]{2,1,0:T(8,128)(2,1)S(1)}, u32[]{:S(2)}, u32[]{:S(2)}) async-start(bf16[8,128,512]{2,1,0:T(8,128)(2,1)} %bitcast.159), calls=%async_computation.9 | async-start | bytes 2097152 | tf_op jit(solution)/shard_map/all_to_all | solution.py:27
  217.9 1.4 copy.44
  219.4 13.7 %all-to-all-done.9 = bf16[8,128,512]{2,1,0:T(8,128)(2,1)S(1)} async-done(((bf16[8,128,512]{2,1,0:T(8,128)(2,1)}), bf16[8,128,512]{2,1,0:T(8,128)(2,1)S(1)}, u32[]{:S(2)}, u32[]{:S(2)}) %all-to-all-start.9) | async-done | bytes 1048608 | tf_op jit(solution)/shard_map/all_to_all | solution.py:27
  233.1 4.3 %all-to-all-start.4 = ((bf16[8,128,4,128]{3,2,1,0:T(4,128)(2,1)}), bf16[8,128,4,128]{3,2,1,0:T(4,128)(2,1)S(1)}, u32[]{:S(2)}, u32[]{:S(2)}) async-start(bf16[8,128,4,128]{3,2,1,0:T(4,128)(2,1)} %bitcast.153), calls=%async_computation.4 | async-start | bytes 2097152 | tf_op jit(solution)/shard_map/all_to_all | solution.py:27
  237.4 0.9 fusion.14
  238.3 0.8 reduce_sum.112
  239.1 13.4 %all-to-all-done.4 = bf16[8,128,4,128]{3,2,1,0:T(4,128)(2,1)S(1)} async-done(((bf16[8,128,4,128]{3,2,1,0:T(4,128)(2,1)}), bf16[8,128,4,128]{3,2,1,0:T(4,128)(2,1)S(1)}, u32[]{:S(2)}, u32[]{:S(2)}) %all-to-all-start.4) | async-done | bytes 1048608 | tf_op jit(solution)/shard_map/all_to_all | solution.py:27
  252.5 1.2 copy.45
  253.7 1.3 reshape.181
  (38 shorter events, 0.3 us)
Async XLA Ops:
  7.2 84.7 %copy-start = (bf16[5,4096]{1,0:T(8,128)(2,1)S(1)}, bf16[5,4096]{1,0:T(8,128)(2,1)}, u32[]{:S(2)}) copy-start(bf16[5,4096]{1,0:T(8,128)(2,1)} %param.16) | copy-start | bytes 122884
  7.2 3.4 %copy-start.2 = (bf16[2,1,64,4096]{3,2,1,0:T(8,128)(2,1)S(1)}, bf16[2,1,64,4096]{3,2,1,0:T(8,128)(2,1)}, u32[]{:S(2)}) copy-start(bf16[2,1,64,4096]{3,2,1,0:T(8,128)(2,1)} %param.9) | copy-start | bytes 3145732
  7.2 42.1 %all-gather.2.cloned.1.call-start = ((), (), s32[]{:S(2)}) async-start(), calls=%async_computation.10 | async-start | bytes 1179648 | tf_op jit(solution)/shard_map/all_gather | solution.py:68
  10.9 12.1 %copy-start.9 = (f32[1,4096]{1,0:T(1,128)S(1)}, f32[1,4096]{1,0:T(1,128)}, u32[]{:S(2)}) copy-start(f32[1,4096]{1,0:T(1,128)} %param.10) | copy-start | bytes 49156
  10.9 12.1 %copy-start.5 = (f32[1,128,512]{2,1,0:T(8,128)S(1)}, f32[1,128,512]{2,1,0:T(8,128)}, u32[]{:S(2)}) copy-start(f32[1,128,512]{2,1,0:T(8,128)} %param.12) | copy-start | bytes 786436
  12.6 36.5 %all-to-all-start = ((bf16[8,128,512]{1,2,0:T(8,128)(2,1)}), bf16[8,128,512]{1,2,0:T(8,128)(2,1)S(1)}, u32[]{:S(2)}, u32[]{:S(2)}) async-start(bf16[8,128,512]{1,2,0:T(8,128)(2,1)} %bitcast.5), calls=%async_computation | async-start | bytes 2097152 | tf_op jit(solution)/shard_map/all_to_all | solution.py:27
  67.1 18.3 %all-to-all-start.2 = ((bf16[4,1024,128]{1,2,0:T(8,128)(2,1)}), bf16[4,1024,128]{1,2,0:T(8,128)(2,1)S(1)}, u32[]{:S(2)}, u32[]{:S(2)}) async-start(bf16[4,1024,128]{1,2,0:T(8,128)(2,1)} %bitcast.156), calls=%async_computation.2 | async-start | bytes 2097152 | tf_op jit(solution)/shard_map/all_to_all | solution.py:27
  71.3 20.5 %copy-start.10 = (s32[2,32]{1,0:T(2,128)S(1)}, s32[2,32]{1,0:T(2,128)}, u32[]{:S(2)}) copy-start(s32[2,32]{1,0:T(2,128)} %param.17) | copy-start | bytes 772
  71.3 20.8 %copy-start.1 = (bf16[2,1,64,4096]{3,2,1,0:T(8,128)(2,1)S(1)}, bf16[2,1,64,4096]{3,2,1,0:T(8,128)(2,1)}, u32[]{:S(2)}) copy-start(bf16[2,1,64,4096]{3,2,1,0:T(8,128)(2,1)} %param.15) | copy-start | bytes 3145732
  85.3 33.4 %all-to-all-start.5 = ((bf16[4,128,512]{2,1,0:T(8,128)(2,1)}), bf16[4,128,512]{2,1,0:T(8,128)(2,1)}, u32[]{:S(2)}, u32[]{:S(2)}) async-start(bf16[4,128,512]{2,1,0:T(8,128)(2,1)} %bitcast.160), calls=%async_computation.5 | async-start | bytes 1048576 | tf_op jit(solution)/shard_map/all_to_all | solution.py:27
  97.8 51.0 %collective-permute-start = (bf16[1024,128]{0,1:T(8,128)(2,1)S(1)}, bf16[1024,128]{0,1:T(8,128)(2,1)S(1)}, u32[]{:S(2)}, u32[]{:S(2)}) collective-permute-start(bf16[1024,128]{0,1:T(8,128)(2,1)S(1)} %get-tuple-element.16), channel_id=1, source_target_pairs={{128,0},{256,128},{384,256},{129,1},{257,129},{385,257},{130,2},{2... | collective-permute-start | bytes 786440 | tf_op jit(solution)/shard_map/ppermute | solution.py:37
  121.9 18.1 %all-to-all-start.6 = ((f32[16,8,128]{2,1,0:T(8,128)}), f32[16,8,128]{2,1,0:T(8,128)S(1)}, u32[]{:S(2)}, u32[]{:S(2)}) async-start(f32[16,8,128]{2,1,0:T(8,128)} %broadcast_in_dim_broadcast_in_dim.3), calls=%async_computation.6 | async-start | bytes 131072 | tf_op jit(solution)/shard_map/all_to_all | solution.py:27
  139.9 26.3 %all-to-all-start.8 = ((bf16[8,128,512]{1,2,0:T(8,128)(2,1)}), bf16[8,128,512]{1,2,0:T(8,128)(2,1)}, u32[]{:S(2)}, u32[]{:S(2)}) async-start(bf16[8,128,512]{1,2,0:T(8,128)(2,1)} %bitcast.152), calls=%async_computation.8 | async-start | bytes 2097152 | tf_op jit(solution)/shard_map/all_to_all | solution.py:27
  148.8 16.2 %collective-permute-start.1 = (bf16[1024,128]{0,1:T(8,128)(2,1)S(1)}, bf16[1024,128]{0,1:T(8,128)(2,1)S(1)}, u32[]{:S(2)}, u32[]{:S(2)}) collective-permute-start(bf16[1024,128]{0,1:T(8,128)(2,1)S(1)} %fusion.10), channel_id=1, source_target_pairs={{256,0},{384,128},{257,1},{385,129},{258,2},{386,130},{259,3},{387... | collective-permute-start | bytes 786440 | tf_op jit(solution)/shard_map/ppermute | solution.py:37
  166.9 13.8 %all-to-all-start.7 = ((f32[32,8,128]{2,1,0:T(8,128)}), f32[32,8,128]{2,1,0:T(8,128)S(1)}, u32[]{:S(2)}, u32[]{:S(2)}) async-start(f32[32,8,128]{2,1,0:T(8,128)} %broadcast_in_dim.53), calls=%async_computation.7 | async-start | bytes 262144 | tf_op jit(solution)/shard_map/all_to_all | solution.py:27
  175.2 12.4 %copy-start.3 = (f32[1,128,512]{2,1,0:T(8,128)S(1)}, f32[1,128,512]{2,1,0:T(8,128)}, u32[]{:S(2)}) copy-start(f32[1,128,512]{2,1,0:T(8,128)} %param.14) | copy-start | bytes 786436
  175.2 12.4 %copy-start.4 = (f32[1,128,512]{2,1,0:T(8,128)S(1)}, f32[1,128,512]{2,1,0:T(8,128)}, u32[]{:S(2)}) copy-start(f32[1,128,512]{2,1,0:T(8,128)} %param.13) | copy-start | bytes 786436
  175.2 12.4 %copy-start.6 = (f32[1,128,512]{2,1,0:T(8,128)S(1)}, f32[1,128,512]{2,1,0:T(8,128)}, u32[]{:S(2)}) copy-start(f32[1,128,512]{2,1,0:T(8,128)} %param.12) | copy-start | bytes 786436
  180.6 0.7 copy-start.7
  181.3 32.4 %all-to-all-start.3 = ((bf16[4,1024,128]{1,2,0:T(8,128)(2,1)}), bf16[4,1024,128]{1,2,0:T(8,128)(2,1)S(1)}, u32[]{:S(2)}, u32[]{:S(2)}) async-start(bf16[4,1024,128]{1,2,0:T(8,128)(2,1)} %pad_maximum_fusion), calls=%async_computation.3 | async-start | bytes 2097152 | tf_op jit(solution)/shard_map/all_to_all | solution.py:27
  184.8 1.5 copy-start.8
  213.7 19.3 %all-to-all-start.9 = ((bf16[8,128,512]{2,1,0:T(8,128)(2,1)}), bf16[8,128,512]{2,1,0:T(8,128)(2,1)S(1)}, u32[]{:S(2)}, u32[]{:S(2)}) async-start(bf16[8,128,512]{2,1,0:T(8,128)(2,1)} %bitcast.159), calls=%async_computation.9 | async-start | bytes 2097152 | tf_op jit(solution)/shard_map/all_to_all | solution.py:27
  233.1 19.5 %all-to-all-start.4 = ((bf16[8,128,4,128]{3,2,1,0:T(4,128)(2,1)}), bf16[8,128,4,128]{3,2,1,0:T(4,128)(2,1)S(1)}, u32[]{:S(2)}, u32[]{:S(2)}) async-start(bf16[8,128,4,128]{3,2,1,0:T(4,128)(2,1)} %bitcast.153), calls=%async_computation.4 | async-start | bytes 2097152 | tf_op jit(solution)/shard_map/all_to_all | solution.py:27
Sparse Core Ops, SparseCore 0:
  10.8 37.7 all-gather.1

commit v2 on v1

v2 whole, which is shorter than its diff:
```python
import jax
import jax.numpy as jnp
from jax import lax
from jax.sharding import Mesh
from jax.sharding import PartitionSpec as P

rms_epsilon = 1e-05
clip_level = 1.0
beta_first = 0.9
beta_second = 0.95
learn_rate = 0.001
decay_rate = 0.01
adam_epsilon = 1e-08
bias_first = 1.0 - 0.9**10
bias_second = 1.0 - 0.95**10

factors = {"section": (4, 4), "dp": (4, 4, 2)}
axes = ("zlo", "y", "zhi", "x", "core")
section = ("zlo", "y")
dp = ("zhi", "x", "core")
f32 = jnp.float32
bf16 = jnp.bfloat16


def exchange(blocks, axis):
    return lax.all_to_all(blocks, axis, 0, 0)


def total(value, axis):
    size = lax.axis_size(axis)
    return jnp.sum(exchange(jnp.broadcast_to(value, (size,) + value.shape), axis), axis=0)


def shifts(size):
    return sorted(range(1, size), key=lambda k: -min(k, size - k))


def by_shifts(blocks, axis):
    size = lax.axis_size(axis)
    spot = lax.axis_index(axis)
    return [
        lax.dynamic_index_in_dim(blocks, (spot + k) & (size - 1), 0, False) for k in range(size)
    ]


def shift(parts, axis):
    size = len(parts)
    came = [parts[0]] + [None] * (size - 1)
    for k in shifts(size):
        came[k] = lax.ppermute(parts[k], axis, [(i, (i + k) % size) for i in range(size)])
    return came


def swap_cores(block):
    return lax.ppermute(block, "core", [(0, 1), (1, 0)])


def sum_from_behind(block, axis):
    size = lax.axis_size(axis)
    moved = [
        lax.ppermute(block, axis, [(i + k, i) for i in range(size - k)])
        for k in range(size - 1, 0, -1)
    ]
    return sum(part.astype(f32) for part in moved)


def together(*values):
    return lax.optimization_barrier(values)


def inverse_rms(floats):
    return lax.rsqrt(jnp.mean(floats * floats, axis=-1, keepdims=True) + rms_epsilon)


def per_device(
    acts, norm_gain, value_grads, master, moment1, moment2, next_acts, reward_table, reward_ids
):
    micro, _, tok_dev, width = acts.shape
    kvw = value_grads.shape[3]
    toks = micro * tok_dev
    far = lax.axis_size("zhi")
    group = lax.axis_size("x")
    cores = lax.axis_size("core")
    layers_y = lax.axis_size("y")
    rows = width // (far * group * cores)
    strip = cores * rows
    own_width = far * strip
    core = lax.axis_index("core")
    gain = norm_gain[0]
    own_gain = lax.dynamic_index_in_dim(
        gain.reshape(far, group, strip), lax.axis_index("x"), 1, False
    ).reshape(own_width)

    def by_features(block):
        parts = block.reshape(toks, far, group, strip)
        return jnp.transpose(parts, (2, 0, 1, 3)).reshape(group, toks, own_width)

    def of_core(block, which, axis):
        shape = block.shape
        split = block.reshape(shape[:axis] + (far, cores, rows) + shape[axis + 1 :])
        split = lax.dynamic_index_in_dim(split, which, axis + 1, False)
        return split.reshape(shape[:axis] + (far * rows,) + shape[axis + 1 :])


    flat = acts[:, 0].reshape(toks, width)
    weights_old, flat = together(master[0].astype(bf16), flat)
    weights_old = lax.all_gather(weights_old, ("zhi", "core"), axis=0, tiled=True)
    mine = exchange(by_features(flat), "x").reshape(group * toks, own_width)
    inverse = inverse_rms(flat.astype(f32))
    values = value_grads[:, 0].reshape(toks, kvw).astype(f32)
    values = (values * inverse).astype(bf16)
    next_flat, values = together(next_acts[:, 0].reshape(toks, width), values)
    values = lax.all_gather(values, "x", axis=0, tiled=True)

    local_pos = jnp.arange(tok_dev, dtype=jnp.int32)
    first_rows = jnp.logical_and(local_pos == 0, lax.axis_index(section) == 0)
    seq_match = jnp.arange(reward_ids.shape[1], dtype=jnp.int32) == lax.axis_index(dp)
    seq_bins = jnp.sum(jnp.where(seq_match[None, :], reward_ids, 0), axis=-1)
    bin_match = (
        seq_bins[:, None] == jnp.arange(reward_table.shape[0], dtype=jnp.int32)[None, :]
    ).astype(bf16)
    embeds = jnp.dot(bin_match, reward_table, preferred_element_type=f32)
    fresh_inputs = jnp.where(
        first_rows[None, :, None], embeds[:, None, :], next_flat.reshape(micro, tok_dev, width).astype(f32)
    ).reshape(toks, width)
    fresh_normed = (fresh_inputs * inverse_rms(fresh_inputs) * gain).astype(bf16)
    fresh_normed, mine, values = together(by_features(fresh_normed), mine, values)
    fresh_normed = exchange(fresh_normed, "x")
    fresh_normed = fresh_normed.reshape(group * toks, own_width)

    def partial_of(which):
        part = jnp.einsum(
            "td,tk->dk", of_core(mine, which, 1), values, preferred_element_type=f32
        )
        return part * of_core(own_gain, which, 0)[:, None]

    other_part = swap_cores(partial_of(1 - core).astype(bf16))
    partial = (partial_of(core) + other_part.astype(f32)).astype(bf16).reshape(far, rows, kvw)
    partial = by_shifts(partial, "zhi")
    partial, late_values, weights_old = together(partial, values, weights_old)
    grad = sum(part.astype(f32) for part in shift(partial, "zhi"))
    squares = jnp.broadcast_to(jnp.sum(grad * grad), (8, 128))
    squares = total(squares, ("zlo", "zhi"))

    mixed = own_gain * jnp.einsum(
        "tk,dk->td", late_values, weights_old, preferred_element_type=f32
    )
    mine = mine.astype(f32)
    sums = jnp.stack([jnp.sum(mine * mine, axis=1), jnp.sum(mine * mixed, axis=1)])
    sums, fresh_normed = together(sums, fresh_normed)
    sums = total(sums, "x")
    sums = sums / width
    inv = lax.rsqrt(sums[0] + rms_epsilon)[:, None]
    branch = mixed - mine * inv * (inv * sums[1][:, None])
    parts = jnp.transpose(branch.astype(bf16).reshape(group * toks, far, strip), (1, 0, 2))
    came = [part.astype(f32) for part in shift(by_shifts(parts, "y"), "y")]
    whose = [(lax.axis_index("y") - k) & (layers_y - 1) for k in range(layers_y)]
    suffix = [
        sum(jnp.where(owner >= layer, part, 0.0) for owner, part in zip(whose, came))
        for layer in range(layers_y)
    ]
    top, squares = together(suffix[0].astype(bf16), squares)
    behind = sum_from_behind(top, "zlo")
    suffix = jnp.stack([(part + behind).astype(bf16) for part in suffix])

    squares = total(squares, ("y", "x", "core"))[0, 0]
    entries = lax.axis_size(section) * width * kvw
    rms = jnp.sqrt(squares / entries + 1e-12)
    clipped = grad * jnp.minimum(1.0, clip_level / rms)
    moment1_new = beta_first * moment1[0] + (1.0 - beta_first) * clipped
    moment2_new = beta_second * moment2[0] + (1.0 - beta_second) * clipped * clipped
    update = (
        moment1_new / bias_first / (jnp.sqrt(moment2_new / bias_second) + adam_epsilon)
        + decay_rate * master[0]
    )
    weights_new = (master[0] - learn_rate * update).astype(bf16)
    weights_new, suffix = together(weights_new, suffix)
    weights_new = lax.all_gather(weights_new, "zhi", axis=0, tiled=True)

    back = exchange(suffix.reshape(layers_y * group, toks, strip), ("y", "x"))

    weights_other = swap_cores(weights_new)
    fresh = jnp.dot(of_core(fresh_normed, core, 1), weights_new, preferred_element_type=f32)
    fresh = fresh + jnp.dot(
        of_core(fresh_normed, 1 - core, 1), weights_other, preferred_element_type=f32
    )
    fresh, back = together(fresh.astype(bf16).reshape(group, toks, kvw), back)
    fresh = exchange(fresh, "x")
    fresh = jnp.sum(fresh.astype(f32), axis=0).astype(bf16)
    fresh_values = fresh.reshape(micro, 1, tok_dev, kvw)
    input_grads = jnp.transpose(back, (1, 0, 2)).reshape(micro, 1, tok_dev, width)
    return (input_grads, moment1_new[None], moment2_new[None], fresh_values)


def solution(mesh):
    fine = Mesh(mesh.devices.reshape(factors["section"] + factors["dp"]), axes)
    return jax.shard_map(
        per_device,
        mesh=fine,
        in_specs=(
            P(None, section, dp, None),
            P(section, None),
            P(None, section, dp, None),
            P(section, dp, None),
            P(section, dp, None),
            P(section, dp, None),
            P(None, section, dp, None),
            P(),
            P(),
        ),
        out_specs=(
            P(None, section, dp, None),
            P(section, dp, None),
            P(section, dp, None),
            P(None, section, dp, None),
        ),
        check_vma=False,
    )
```

time: 263 us -> 247 us (0.939); the launches traced: 262 us -> 242 us
  starting transfers between devices: 56.9 us -> 96.6 us
  waiting for transfers between devices: 83.8 us -> 45.9 us
  blocking collectives: 64.4 us -> 31.9 us
  local copies, waits for them, and re-layouts: 18.2 us -> 26.8 us
  matrix products: 6.82 us -> 11.6 us
    ppermute x2 -> x11, starting transfers between devices: 2.58 us -> 53.8 us  [the longest x6 32.1 us: shift(): lax.ppermute(parts[k], axis, [(i, (i + k) % size) for i in range(size)])]
    all_to_all x9 -> x7, waiting for transfers between devices: 68.8 us -> 32.2 us  [exchange(): return lax.all_to_all(blocks, axis, 0, 0)]
    all_to_all x1 -> x0, blocking collectives: 14.2 us -> none  [exchange(): return lax.all_to_all(blocks, axis, 0, 0)]
    all_gather x1, blocking collectives: 26.1 us -> 14 us  [per_device(): values = lax.all_gather(values, 'x', axis=0, tiled=True)]
    all_to_all x9 -> x7, starting transfers between devices: 54.3 us -> 42.8 us  [exchange(): return lax.all_to_all(blocks, axis, 0, 0)]
    all_gather x1, blocking collectives: 24.2 us -> 17.9 us  [per_device(): weights_new = lax.all_gather(weights_new, 'zhi', axis=0, tiled=True)]
    reshape x1 -> x6, local copies, waits for them, and re-layouts: 1.27 us -> 6.65 us  [the longest x2 2.25 us: by_features(): parts = block.reshape(toks, far, group, strip)]
    dot_general x3 -> x5, matrix products: 6.61 us -> 11.4 us  [the longest x2 4.08 us: partial_of(): jnp.einsum('td,tk->dk', of_core(mine, which, 1), values, preferred_elemen...]
  transfers between devices with their start and end apart: 12 -> 19, of which waited for: 7 -> 7; matrix products, arithmetic and copies ran while one was open for 12% -> 16% of each run, Pallas kernels for 0% -> 0%
where the time goes in v2:
time: 247 us; the launch traced here: 242 us
  starting transfers between devices  96.6 us (39%)
  waiting for transfers between devices  45.9 us (19%)
  blocking collectives  31.9 us (13%)
  local copies, waits for them, and re-layouts  26.8 us (11%)
  between operations  15.3 us (6%)
  other arithmetic  14.2 us (6%)
  matrix products  11.6 us (5%)
    all_to_all x7, starting transfers between devices, exchange(): return lax.all_to_all(blocks, axis, 0, 0)  42.8 us
    all_to_all x7, waiting for transfers between devices, exchange(): return lax.all_to_all(blocks, axis, 0, 0)  32.2 us
    ppermute x6, starting transfers between devices, shift(): lax.ppermute(parts[k], axis, [(i, (i + k) % size) for i in range(size)])  32.1 us
    ppermute x2, starting transfers between devices, swap_cores(): return lax.ppermute(block, 'core', [(0, 1), (1, 0)])  17.9 us
    all_gather x1, blocking collectives, per_device(): weights_new = lax.all_gather(weights_new, 'zhi', axis=0, tiled=True)  17.9 us
    all_gather x1, blocking collectives, per_device(): values = lax.all_gather(values, 'x', axis=0, tiled=True)  14 us
    ppermute x3, waiting for transfers between devices, sum_from_behind(): lax.ppermute(block, axis, [(i + k, i) for i in range(size - k)])  11.6 us
    unnamed x28, local copies, waits for them, and re-layouts  7.36 us
  transfers between devices with their start and end apart: 19, of which 7 were waited for; matrix products, arithmetic and copies ran while one was open for 16% of the time, Pallas kernels for 0%

profile of v2, /device:TPU:1, one launch (start us, length us, event | category | flops | bytes accessed | tf_op | source)
XLA Modules:
  0.0 242.2 jit_solution(460056177001020131)
XLA Ops:
  7.2 1.7 bitcast_convert_fusion
  8.8 1.8 reshape.161
  11.1 1.5 reshape.162
  12.7 5.0 %all-to-all-start = ((bf16[4,128,1024]{2,1,0:T(8,128)(2,1)}), bf16[4,128,1024]{2,1,0:T(8,128)(2,1)S(1)}, u32[]{:S(2)}, u32[]{:S(2)}) async-start(bf16[4,128,1024]{2,1,0:T(8,128)(2,1)} %reshape.162), calls=%async_computation | async-start | bytes 2097152 | tf_op jit(solution)/shard_map/all_to_all | solution.py:26
  17.7 0.7 all-gather.2.cloned.1.call-update
  20.1 0.7 copy.64
  20.8 1.1 copy.65
  22.4 0.7 reduce.4
  23.1 14.0 %all_gather.9 = bf16[512,512]{1,0:T(8,128)(2,1)} all-gather(bf16[128,512]{1,0:T(8,128)(2,1)S(1)} %fusion.34), channel_id=1, replica_groups=mesh['zlo'=4,'y'=4,'zhi'=4,'x'=4,'core'=2] {'x'}, dimensions={0}, use_global_device_ids=true | all-gather | bytes 655360 | tf_op jit(solution)/shard_map/all_gather | solution.py:113
  37.1 0.7 reshape.164
  37.9 3.1 %constant_dynamic-slice_fusion.9 = (bf16[512,4,1,128]{3,2,1,0:T(2,128)(2,1)S(1)}, bf16[512,4,1,128]{3,2,1,0:T(2,128)(2,1)}) fusion(bf16[512,4,2,128]{3,2,1,0:T(2,128)(2,1)S(1)} %reshape.164, s32[]{:T(128)S(6)} %select_n.164, s32[]{:T(128)S(6)} %select_n.165), kind=kLoop, calls=%fused_computation.97 | loop fusion | bytes 2097160 | tf_op jit(solution)/shard_map/jit(dynamic_index_in_dim)/dynamic_slice | solution.py:101
  41.0 2.3 copy.79
  43.4 2.3 fusion.5
  45.7 9.1 %collective-permute-start = (bf16[512,512]{1,0:T(8,128)(2,1)}, bf16[512,512]{1,0:T(8,128)(2,1)}, u32[]{:S(2)}, u32[]{:S(2)}) collective-permute-start(bf16[512,512]{1,0:T(8,128)(2,1)} %fusion.5), channel_id=1, source_target_pairs={{0,1},{1,0},{2,3},{3,2},{4,5},{5,4},{6,7},{7,6},{8,9},{9,8},{10,11... | collective-permute-start | bytes 1572872 | tf_op jit(solution)/shard_map/ppermute | solution.py:55
  54.8 3.5 %all-to-all-start.1 = ((bf16[4,128,1024]{1,2,0:T(8,128)(2,1)}), bf16[4,128,1024]{1,2,0:T(8,128)(2,1)S(1)}, u32[]{:S(2)}, u32[]{:S(2)}) async-start(bf16[4,128,1024]{1,2,0:T(8,128)(2,1)} %bitcast.8), calls=%async_computation.1 | async-start | bytes 2097152 | tf_op jit(solution)/shard_map/all_to_all | solution.py:26
  58.3 2.3 copy.78
  60.6 1.8 add_convert_fusion
  62.4 0.8 dynamic-slice_bitcast_fusion
  63.2 10.3 %all-to-all-done.1 = bf16[4,128,1024]{1,2,0:T(8,128)(2,1)S(1)} async-done(((bf16[4,128,1024]{1,2,0:T(8,128)(2,1)}), bf16[4,128,1024]{1,2,0:T(8,128)(2,1)S(1)}, u32[]{:S(2)}, u32[]{:S(2)}) %all-to-all-start.1) | async-done | bytes 1048608 | tf_op jit(solution)/shard_map/all_to_all | solution.py:26
  73.5 0.5 copy.69
  74.2 3.5 %fusion = (f32[512]{0:T(512)S(1)}, f32[512]{0:T(512)S(1)}, f32[512,1024]{1,0:T(8,128)}) fusion(bf16[512,1024]{1,0:T(8,128)(2,1)S(1)} %bitcast.159, f32[1024]{0:T(1024)S(1)} %bitcast.179, bf16[512,512]{1,0:T(8,128)(2,1)} %all_gather.9, bf16[1024,512]{1,0:T(8,128)(2,1)} %all-gather.2.cloned.1.call-done), kind=kOutput, calls=%fused_computation.3 | convolution fusion | flops 540015616 | bytes 4726784 | tf_op jit(solution)/shard_map/tk,dk->td/dot_general | solution.py:145
  77.7 0.6 broadcast_in_dim.82
  78.3 4.3 %all-to-all-start.2 = ((f32[4,2,512]{2,1,0:T(2,128)}), f32[4,2,512]{2,1,0:T(2,128)S(1)}, u32[]{:S(2)}, u32[]{:S(2)}) async-start(f32[4,2,512]{2,1,0:T(2,128)} %broadcast_in_dim.82), calls=%async_computation.2 | async-start | bytes 32768 | tf_op jit(solution)/shard_map/all_to_all | solution.py:26
  82.6 5.6 %collective-permute-start.1 = (bf16[128,512]{1,0:T(8,128)(2,1)}, bf16[128,512]{1,0:T(8,128)(2,1)S(1)}, u32[]{:S(2)}, u32[]{:S(2)}) collective-permute-start(bf16[128,512]{1,0:T(8,128)(2,1)} %get-tuple-element.36), channel_id=1, source_target_pairs={{0,8},{8,16},{16,24},{24,0},{1,9},{9,17},{17,25},{25,1},{2,10},{10... | collective-permute-start | bytes 393224 | tf_op jit(solution)/shard_map/ppermute | solution.py:50
  88.2 10.6 %collective-permute-start.2 = (bf16[128,512]{1,0:T(8,128)(2,1)}, bf16[128,512]{1,0:T(8,128)(2,1)S(1)}, u32[]{:S(2)}, u32[]{:S(2)}) collective-permute-start(bf16[128,512]{1,0:T(8,128)(2,1)} %get-tuple-element.37), channel_id=1, source_target_pairs={{0,16},{8,24},{16,0},{24,8},{1,17},{9,25},{17,1},{25,9},{2,18},{10... | collective-permute-start | bytes 393224 | tf_op jit(solution)/shard_map/ppermute | solution.py:50
  98.8 5.2 %collective-permute-start.3 = (bf16[128,512]{1,0:T(8,128)(2,1)}, bf16[128,512]{1,0:T(8,128)(2,1)}, u32[]{:S(2)}, u32[]{:S(2)}) collective-permute-start(bf16[128,512]{1,0:T(8,128)(2,1)} %get-tuple-element.38), channel_id=1, source_target_pairs={{0,24},{8,0},{16,8},{24,16},{1,25},{9,1},{17,9},{25,17},{2,26},{10... | collective-permute-start | bytes 393224 | tf_op jit(solution)/shard_map/ppermute | solution.py:50
  104.1 2.0 fusion.4
  106.1 0.8 reshape.171
  106.9 2.2 constant_dynamic-slice_fusion.4
  109.2 3.2 %collective-permute-start.4 = (bf16[512,256]{1,0:T(8,128)(2,1)S(1)}, bf16[512,256]{1,0:T(8,128)(2,1)S(1)}, u32[]{:S(2)}, u32[]{:S(2)}) collective-permute-start(bf16[512,256]{1,0:T(8,128)(2,1)S(1)} %bitcast.175), channel_id=1, source_target_pairs={{0,32},{32,64},{64,96},{96,0},{1,33},{33,65},{65,97},{97,1},{2,34}... | collective-permute-start | bytes 786440 | tf_op jit(solution)/shard_map/ppermute | solution.py:50
  112.4 0.7 copy.91
  113.1 4.5 %collective-permute-start.5 = (bf16[512,256]{1,0:T(8,128)(2,1)}, bf16[512,256]{1,0:T(8,128)(2,1)S(1)}, u32[]{:S(2)}, u32[]{:S(2)}) collective-permute-start(bf16[512,256]{1,0:T(8,128)(2,1)} %bitcast.156), channel_id=1, source_target_pairs={{0,64},{32,96},{64,0},{96,32},{1,65},{33,97},{65,1},{97,33},{2,66}... | collective-permute-start | bytes 786440 | tf_op jit(solution)/shard_map/ppermute | solution.py:50
  117.7 0.7 copy.90
  118.4 3.0 %collective-permute-start.6 = (bf16[512,256]{1,0:T(8,128)(2,1)}, bf16[512,256]{1,0:T(8,128)(2,1)S(1)}, u32[]{:S(2)}, u32[]{:S(2)}) collective-permute-start(bf16[512,256]{1,0:T(8,128)(2,1)} %bitcast.155), channel_id=1, source_target_pairs={{0,96},{32,0},{64,32},{96,64},{1,97},{33,1},{65,33},{97,65},{2,98}... | collective-permute-start | bytes 786440 | tf_op jit(solution)/shard_map/ppermute | solution.py:50
  121.4 0.6 copy-done.8
  122.1 1.2 collective-permute-done.3
  123.3 1.7 multiply_reduce_fusion.2
  125.0 1.3 broadcast_in_dim_broadcast_in_dim.3
  126.3 9.5 %all-to-all-start.3 = ((f32[16,8,128]{2,1,0:T(8,128)}), f32[16,8,128]{2,1,0:T(8,128)S(1)}, u32[]{:S(2)}, u32[]{:S(2)}) async-start(f32[16,8,128]{2,1,0:T(8,128)} %broadcast_in_dim_broadcast_in_dim.3), calls=%async_computation.3 | async-start | bytes 131072 | tf_op jit(solution)/shard_map/all_to_all | solution.py:26
  135.8 0.9 fusion.40
  136.8 10.7 %all-to-all-done.3 = f32[16,8,128]{2,1,0:T(8,128)S(1)} async-done(((f32[16,8,128]{2,1,0:T(8,128)}), f32[16,8,128]{2,1,0:T(8,128)S(1)}, u32[]{:S(2)}, u32[]{:S(2)}) %all-to-all-start.3) | async-done | bytes 65568 | tf_op jit(solution)/shard_map/all_to_all | solution.py:26
  147.5 0.7 broadcast_in_dim.85
  148.2 9.4 %all-to-all-start.4 = ((f32[32,8,128]{2,1,0:T(8,128)}), f32[32,8,128]{2,1,0:T(8,128)}, u32[]{:S(2)}, u32[]{:S(2)}) async-start(f32[32,8,128]{2,1,0:T(8,128)} %broadcast_in_dim.85), calls=%async_computation.4 | async-start | bytes 262144 | tf_op jit(solution)/shard_map/all_to_all | solution.py:26
  157.6 1.3 collective-permute-start.7
  158.9 1.3 collective-permute-start.8
  160.2 1.3 collective-permute-start.9
  161.5 3.7 %all-to-all-done.4 = f32[32,8,128]{2,1,0:T(8,128)} async-done(((f32[32,8,128]{2,1,0:T(8,128)}), f32[32,8,128]{2,1,0:T(8,128)}, u32[]{:S(2)}, u32[]{:S(2)}) %all-to-all-start.4) | async-done | bytes 131104 | tf_op jit(solution)/shard_map/all_to_all | solution.py:26
  165.3 0.9 reduce_sum.101
  166.2 0.5 slice.11
  167.4 2.1 fusion.39
  169.5 11.6 %collective-permute-done.8 = bf16[512,256]{1,0:T(8,128)(2,1)S(1)} collective-permute-done((bf16[512,256]{1,0:T(8,128)(2,1)}, bf16[512,256]{1,0:T(8,128)(2,1)S(1)}, u32[]{:S(2)}, u32[]{:S(2)}) %collective-permute-start.8) | collective-permute-done | bytes 262176 | tf_op jit(solution)/shard_map/ppermute | solution.py:61
  181.4 0.6 fusion.30
  182.0 1.1 pad_maximum_fusion
  183.1 6.7 %all-to-all-start.5 = ((bf16[16,128,256]{2,1,0:T(8,128)(2,1)}), bf16[16,128,256]{2,1,0:T(8,128)(2,1)S(1)}, u32[]{:S(2)}, u32[]{:S(2)}) async-start(bf16[16,128,256]{2,1,0:T(8,128)(2,1)} %bitcast.45), calls=%async_computation.5 | async-start | bytes 2097152 | tf_op jit(solution)/shard_map/all_to_all | solution.py:26
  189.8 17.9 %all_gather.11 = bf16[512,512]{1,0:T(8,128)(2,1)} all-gather(bf16[128,512]{1,0:T(8,128)(2,1)S(1)} %copy-done.4), channel_id=1, replica_groups=mesh['zlo'=4,'y'=4,'zhi'=4,'x'=4,'core'=2] {'zhi'}, dimensions={0}, use_global_device_ids=true | all-gather | bytes 655360 | tf_op jit(solution)/shard_map/all_gather | solution.py:178
  207.7 8.8 %collective-permute-start.10 = (bf16[512,512]{1,0:T(8,128)(2,1)}, bf16[512,512]{1,0:T(8,128)(2,1)}, u32[]{:S(2)}, u32[]{:S(2)}) collective-permute-start(bf16[512,512]{1,0:T(8,128)(2,1)} %all_gather.11), channel_id=1, source_target_pairs={{0,1},{1,0},{2,3},{3,2},{4,5},{5,4},{6,7},{7,6},{8,9},{9,8},{10,11... | collective-permute-start | bytes 1572872 | tf_op jit(solution)/shard_map/ppermute | solution.py:55
  216.5 0.5 copy.70
  217.1 1.5 fusion.47
  218.6 2.3 fusion.6
  220.9 4.4 %all-to-all-start.6 = ((bf16[4,128,512]{2,1,0:T(8,128)(2,1)}), bf16[4,128,512]{2,1,0:T(8,128)(2,1)S(1)}, u32[]{:S(2)}, u32[]{:S(2)}) async-start(bf16[4,128,512]{2,1,0:T(8,128)(2,1)} %bitcast.44), calls=%async_computation.6 | async-start | bytes 1048576 | tf_op jit(solution)/shard_map/all_to_all | solution.py:26
  225.3 0.6 copy.76
  225.9 1.3 reshape.175
  227.2 7.4 %all-to-all-done.6 = bf16[4,128,512]{2,1,0:T(8,128)(2,1)S(1)} async-done(((bf16[4,128,512]{2,1,0:T(8,128)(2,1)}), bf16[4,128,512]{2,1,0:T(8,128)(2,1)S(1)}, u32[]{:S(2)}, u32[]{:S(2)}) %all-to-all-start.6) | async-done | bytes 524320 | tf_op jit(solution)/shard_map/all_to_all | solution.py:26
  234.6 0.7 reduce_sum.102
  (61 shorter events, 3.3 us)
Async XLA Ops:
  7.2 11.9 %copy-start = (bf16[5,4096]{1,0:T(8,128)(2,1)S(1)}, bf16[5,4096]{1,0:T(8,128)(2,1)}, u32[]{:S(2)}) copy-start(bf16[5,4096]{1,0:T(8,128)(2,1)} %param.16) | copy-start | bytes 122884
  11.1 7.3 %copy-start.1 = (bf16[2,1,64,4096]{3,2,1,0:T(8,128)(2,1)S(1)}, bf16[2,1,64,4096]{3,2,1,0:T(8,128)(2,1)}, u32[]{:S(2)}) copy-start(bf16[2,1,64,4096]{3,2,1,0:T(8,128)(2,1)} %param.9) | copy-start | bytes 3145732
  12.7 6.2 %copy-start.6 = (bf16[2,1,64,512]{3,2,1,0:T(8,128)(2,1)S(1)}, bf16[2,1,64,512]{3,2,1,0:T(8,128)(2,1)}, u32[]{:S(2)}) copy-start(bf16[2,1,64,512]{3,2,1,0:T(8,128)(2,1)} %param.11) | copy-start | bytes 393220
  12.7 6.3 %copy-start.10 = (s32[2,32]{1,0:T(2,128)S(1)}, s32[2,32]{1,0:T(2,128)}, u32[]{:S(2)}) copy-start(s32[2,32]{1,0:T(2,128)} %param.17) | copy-start | bytes 772
  12.7 6.6 %copy-start.2 = (bf16[2,1,64,4096]{3,2,1,0:T(8,128)(2,1)S(1)}, bf16[2,1,64,4096]{3,2,1,0:T(8,128)(2,1)}, u32[]{:S(2)}) copy-start(bf16[2,1,64,4096]{3,2,1,0:T(8,128)(2,1)} %param.15) | copy-start | bytes 3145732
  12.7 7.0 %copy-start.9 = (f32[1,4096]{1,0:T(1,128)S(1)}, f32[1,4096]{1,0:T(1,128)}, u32[]{:S(2)}) copy-start(f32[1,4096]{1,0:T(1,128)} %param.10) | copy-start | bytes 49156
  12.7 24.4 %all-to-all-start = ((bf16[4,128,1024]{2,1,0:T(8,128)(2,1)}), bf16[4,128,1024]{2,1,0:T(8,128)(2,1)S(1)}, u32[]{:S(2)}, u32[]{:S(2)}) async-start(bf16[4,128,1024]{2,1,0:T(8,128)(2,1)} %reshape.162), calls=%async_computation | async-start | bytes 2097152 | tf_op jit(solution)/shard_map/all_to_all | solution.py:26
  17.7 56.6 %all-gather.2.cloned.1.call-start = ((), (), s32[]{:S(2)}) async-start(), calls=%async_computation.7 | async-start | bytes 1179648 | tf_op jit(solution)/shard_map/all_gather | solution.py:107
  45.7 14.9 %collective-permute-start = (bf16[512,512]{1,0:T(8,128)(2,1)}, bf16[512,512]{1,0:T(8,128)(2,1)}, u32[]{:S(2)}, u32[]{:S(2)}) collective-permute-start(bf16[512,512]{1,0:T(8,128)(2,1)} %fusion.5), channel_id=1, source_target_pairs={{0,1},{1,0},{2,3},{3,2},{4,5},{5,4},{6,7},{7,6},{8,9},{9,8},{10,11... | collective-permute-start | bytes 1572872 | tf_op jit(solution)/shard_map/ppermute | solution.py:55
  54.8 18.8 %all-to-all-start.1 = ((bf16[4,128,1024]{1,2,0:T(8,128)(2,1)}), bf16[4,128,1024]{1,2,0:T(8,128)(2,1)S(1)}, u32[]{:S(2)}, u32[]{:S(2)}) async-start(bf16[4,128,1024]{1,2,0:T(8,128)(2,1)} %bitcast.8), calls=%async_computation.1 | async-start | bytes 2097152 | tf_op jit(solution)/shard_map/all_to_all | solution.py:26
  78.3 25.7 %all-to-all-start.2 = ((f32[4,2,512]{2,1,0:T(2,128)}), f32[4,2,512]{2,1,0:T(2,128)S(1)}, u32[]{:S(2)}, u32[]{:S(2)}) async-start(f32[4,2,512]{2,1,0:T(2,128)} %broadcast_in_dim.82), calls=%async_computation.2 | async-start | bytes 32768 | tf_op jit(solution)/shard_map/all_to_all | solution.py:26
  82.6 35.8 %collective-permute-start.1 = (bf16[128,512]{1,0:T(8,128)(2,1)}, bf16[128,512]{1,0:T(8,128)(2,1)S(1)}, u32[]{:S(2)}, u32[]{:S(2)}) collective-permute-start(bf16[128,512]{1,0:T(8,128)(2,1)} %get-tuple-element.36), channel_id=1, source_target_pairs={{0,8},{8,16},{16,24},{24,0},{1,9},{9,17},{17,25},{25,1},{2,10},{10... | collective-permute-start | bytes 393224 | tf_op jit(solution)/shard_map/ppermute | solution.py:50
  88.2 33.2 %collective-permute-start.2 = (bf16[128,512]{1,0:T(8,128)(2,1)}, bf16[128,512]{1,0:T(8,128)(2,1)S(1)}, u32[]{:S(2)}, u32[]{:S(2)}) collective-permute-start(bf16[128,512]{1,0:T(8,128)(2,1)} %get-tuple-element.37), channel_id=1, source_target_pairs={{0,16},{8,24},{16,0},{24,8},{1,17},{9,25},{17,1},{25,9},{2,18},{10... | collective-permute-start | bytes 393224 | tf_op jit(solution)/shard_map/ppermute | solution.py:50
  98.8 24.5 %collective-permute-start.3 = (bf16[128,512]{1,0:T(8,128)(2,1)}, bf16[128,512]{1,0:T(8,128)(2,1)}, u32[]{:S(2)}, u32[]{:S(2)}) collective-permute-start(bf16[128,512]{1,0:T(8,128)(2,1)} %get-tuple-element.38), channel_id=1, source_target_pairs={{0,24},{8,0},{16,8},{24,16},{1,25},{9,1},{17,9},{25,17},{2,26},{10... | collective-permute-start | bytes 393224 | tf_op jit(solution)/shard_map/ppermute | solution.py:50
  109.1 14.2 %copy-start.5 = (bf16[128,512]{1,0:T(8,128)(2,1)S(1)}, bf16[128,512]{1,0:T(8,128)(2,1)}, u32[]{:S(2)}) copy-start(bf16[128,512]{1,0:T(8,128)(2,1)} %get-tuple-element.35) | copy-start | bytes 393220
  109.2 26.6 %collective-permute-start.4 = (bf16[512,256]{1,0:T(8,128)(2,1)S(1)}, bf16[512,256]{1,0:T(8,128)(2,1)S(1)}, u32[]{:S(2)}, u32[]{:S(2)}) collective-permute-start(bf16[512,256]{1,0:T(8,128)(2,1)S(1)} %bitcast.175), channel_id=1, source_target_pairs={{0,32},{32,64},{64,96},{96,0},{1,33},{33,65},{65,97},{97,1},{2,34}... | collective-permute-start | bytes 786440 | tf_op jit(solution)/shard_map/ppermute | solution.py:50
  113.1 22.7 %collective-permute-start.5 = (bf16[512,256]{1,0:T(8,128)(2,1)}, bf16[512,256]{1,0:T(8,128)(2,1)S(1)}, u32[]{:S(2)}, u32[]{:S(2)}) collective-permute-start(bf16[512,256]{1,0:T(8,128)(2,1)} %bitcast.156), channel_id=1, source_target_pairs={{0,64},{32,96},{64,0},{96,32},{1,65},{33,97},{65,1},{97,33},{2,66}... | collective-permute-start | bytes 786440 | tf_op jit(solution)/shard_map/ppermute | solution.py:50
  117.7 49.8 %copy-start.3 = (f32[1,128,512]{2,1,0:T(8,128)S(1)}, f32[1,128,512]{2,1,0:T(8,128)}, u32[]{:S(2)}) copy-start(f32[1,128,512]{2,1,0:T(8,128)} %param.12) | copy-start | bytes 786436
  118.4 3.0 %copy-start.7 = (bf16[128,512]{1,0:T(8,128)(2,1)}, bf16[128,512]{1,0:T(8,128)(2,1)S(1)}, u32[]{:S(2)}) copy-start(bf16[128,512]{1,0:T(8,128)(2,1)S(1)} %collective-permute-done.1) | copy-start | bytes 393220
  118.4 17.4 %collective-permute-start.6 = (bf16[512,256]{1,0:T(8,128)(2,1)}, bf16[512,256]{1,0:T(8,128)(2,1)S(1)}, u32[]{:S(2)}, u32[]{:S(2)}) collective-permute-start(bf16[512,256]{1,0:T(8,128)(2,1)} %bitcast.155), channel_id=1, source_target_pairs={{0,96},{32,0},{64,32},{96,64},{1,97},{33,1},{65,33},{97,65},{2,98}... | collective-permute-start | bytes 786440 | tf_op jit(solution)/shard_map/ppermute | solution.py:50
  121.4 0.7 copy-start.8
  126.3 21.2 %all-to-all-start.3 = ((f32[16,8,128]{2,1,0:T(8,128)}), f32[16,8,128]{2,1,0:T(8,128)S(1)}, u32[]{:S(2)}, u32[]{:S(2)}) async-start(f32[16,8,128]{2,1,0:T(8,128)} %broadcast_in_dim_broadcast_in_dim.3), calls=%async_computation.3 | async-start | bytes 131072 | tf_op jit(solution)/shard_map/all_to_all | solution.py:26
  148.2 17.1 %all-to-all-start.4 = ((f32[32,8,128]{2,1,0:T(8,128)}), f32[32,8,128]{2,1,0:T(8,128)}, u32[]{:S(2)}, u32[]{:S(2)}) async-start(f32[32,8,128]{2,1,0:T(8,128)} %broadcast_in_dim.85), calls=%async_computation.4 | async-start | bytes 262144 | tf_op jit(solution)/shard_map/all_to_all | solution.py:26
  157.6 11.9 %collective-permute-start.7 = (bf16[512,256]{1,0:T(8,128)(2,1)}, bf16[512,256]{1,0:T(8,128)(2,1)S(1)}, u32[]{:S(2)}, u32[]{:S(2)}) collective-permute-start(bf16[512,256]{1,0:T(8,128)(2,1)} %get-tuple-element.41), channel_id=1, source_target_pairs={{384,0},{385,1},{386,2},{387,3},{388,4},{389,5},{390,6},{391,7},{3... | collective-permute-start | bytes 786440 | tf_op jit(solution)/shard_map/ppermute | solution.py:61
  158.9 22.1 %collective-permute-start.8 = (bf16[512,256]{1,0:T(8,128)(2,1)}, bf16[512,256]{1,0:T(8,128)(2,1)S(1)}, u32[]{:S(2)}, u32[]{:S(2)}) collective-permute-start(bf16[512,256]{1,0:T(8,128)(2,1)} %get-tuple-element.41), channel_id=1, source_target_pairs={{256,0},{384,128},{257,1},{385,129},{258,2},{386,130},{259,3},{387... | collective-permute-start | bytes 786440 | tf_op jit(solution)/shard_map/ppermute | solution.py:61
  160.2 20.8 %collective-permute-start.9 = (bf16[512,256]{1,0:T(8,128)(2,1)}, bf16[512,256]{1,0:T(8,128)(2,1)S(1)}, u32[]{:S(2)}, u32[]{:S(2)}) collective-permute-start(bf16[512,256]{1,0:T(8,128)(2,1)} %get-tuple-element.41), channel_id=1, source_target_pairs={{128,0},{256,128},{384,256},{129,1},{257,129},{385,257},{130,2},{2... | collective-permute-start | bytes 786440 | tf_op jit(solution)/shard_map/ppermute | solution.py:61
  182.0 7.8 %copy-start.4 = (bf16[128,512]{1,0:T(8,128)(2,1)S(1)}, bf16[128,512]{1,0:T(8,128)(2,1)}, u32[]{:S(2)}) copy-start(bf16[128,512]{1,0:T(8,128)(2,1)} %get-tuple-element.42) | copy-start | bytes 393220
  183.1 37.8 %all-to-all-start.5 = ((bf16[16,128,256]{2,1,0:T(8,128)(2,1)}), bf16[16,128,256]{2,1,0:T(8,128)(2,1)S(1)}, u32[]{:S(2)}, u32[]{:S(2)}) async-start(bf16[16,128,256]{2,1,0:T(8,128)(2,1)} %bitcast.45), calls=%async_computation.5 | async-start | bytes 2097152 | tf_op jit(solution)/shard_map/all_to_all | solution.py:26
  207.7 10.9 %collective-permute-start.10 = (bf16[512,512]{1,0:T(8,128)(2,1)}, bf16[512,512]{1,0:T(8,128)(2,1)}, u32[]{:S(2)}, u32[]{:S(2)}) collective-permute-start(bf16[512,512]{1,0:T(8,128)(2,1)} %all_gather.11), channel_id=1, source_target_pairs={{0,1},{1,0},{2,3},{3,2},{4,5},{5,4},{6,7},{7,6},{8,9},{9,8},{10,11... | collective-permute-start | bytes 1572872 | tf_op jit(solution)/shard_map/ppermute | solution.py:55
  220.9 13.6 %all-to-all-start.6 = ((bf16[4,128,512]{2,1,0:T(8,128)(2,1)}), bf16[4,128,512]{2,1,0:T(8,128)(2,1)S(1)}, u32[]{:S(2)}, u32[]{:S(2)}) async-start(bf16[4,128,512]{2,1,0:T(8,128)(2,1)} %bitcast.44), calls=%async_computation.6 | async-start | bytes 1048576 | tf_op jit(solution)/shard_map/all_to_all | solution.py:26
Sparse Core Ops, SparseCore 0:
  21.2 52.9 all-gather.1

commit v3 on v2

v3 whole, which is shorter than its diff:
```python
import functools

import jax
import jax.numpy as jnp
from jax import lax
from jax.experimental import pallas as pl
from jax.experimental.pallas import tpu as pltpu
from jax.sharding import Mesh
from jax.sharding import PartitionSpec as P

rms_epsilon = 1e-05
clip_level = 1.0
beta_first = 0.9
beta_second = 0.95
learn_rate = 0.001
decay_rate = 0.01
adam_epsilon = 1e-08
bias_first = 1.0 - 0.9**10
bias_second = 1.0 - 0.95**10

factors = {"section": (4, 4), "dp": (4, 4, 2)}
axes = ("zlo", "y", "zhi", "x", "core")
section = ("zlo", "y")
dp = ("zhi", "x", "core")
f32 = jnp.float32
bf16 = jnp.bfloat16


def exchange(blocks, axis):
    return lax.all_to_all(blocks, axis, 0, 0)


def total(value, axis):
    return jnp.sum(exchange(value, axis), axis=0)


def shifts(size):
    return sorted(range(1, size), key=lambda k: -min(k, size - k))


def shift(parts, axis):
    size = len(parts)
    came = [parts[0]] + [None] * (size - 1)
    for k in shifts(size):
        came[k] = lax.ppermute(parts[k], axis, [(i, (i + k) % size) for i in range(size)])
    return came


def swap_cores(block):
    return lax.ppermute(block, "core", [(0, 1), (1, 0)])


def sum_from_behind(block, axis):
    size = lax.axis_size(axis)
    moved = [
        lax.ppermute(block, axis, [(i + k, i) for i in range(size - k)])
        for k in range(size - 1, 0, -1)
    ]
    return sum(part.astype(f32) for part in moved)


def together(*values):
    return lax.optimization_barrier(values)


def inverse_rms(floats):
    return lax.rsqrt(jnp.mean(floats * floats, axis=-1, keepdims=True) + rms_epsilon)


def local(kernel, out_shapes, spots, *arrays, flops=0):
    moved = sum(a.size * a.dtype.itemsize for a in arrays)
    moved += sum(s.size * s.dtype.itemsize for s in out_shapes)
    return pl.pallas_call(
        kernel,
        out_shape=out_shapes,
        in_specs=[pl.BlockSpec(memory_space=pltpu.SMEM)]
        + [pl.BlockSpec(memory_space=pltpu.VMEM)] * len(arrays),
        out_specs=[pl.BlockSpec(memory_space=pltpu.VMEM)] * len(out_shapes),
        compiler_params=pltpu.CompilerParams(vmem_limit_bytes=48 * 1024 * 1024),
        cost_estimate=pl.CostEstimate(flops=0, bytes_accessed=0, transcendentals=0),
    )(spots, *arrays)


def strip_at(start, rows):
    return pl.ds(pl.multiple_of(start, rows), rows)


def split_kernel(sizes, spots, acts, values, out):
    far, group, cores, rows = sizes
    core = spots[0]
    half = far * rows
    floats = acts[...].astype(f32)
    scaled = (values[...].astype(f32) * inverse_rms(floats)).astype(bf16)
    for x in range(group):
        for z in range(far):
            for c in range(cores):
                start = ((z * group + x) * cores + ((core + c) & (cores - 1))) * rows
                out[x, :, c * half + z * rows : c * half + (z + 1) * rows] = acts[
                    :, strip_at(start, rows)
                ]
        out[x, :, cores * half :] = scaled


def other_kernel(half, spots, mine, gain, out):
    left = mine[:, half : 2 * half]
    part = lax.dot_general(
        left, mine[:, 2 * half :], (((0,), (0,)), ((), ())), preferred_element_type=f32
    )
    out[...] = (part * gain[...]).astype(bf16)


def own_kernel(half, spots, mine, gain, came, out):
    part = lax.dot_general(
        mine[:, :half], mine[:, 2 * half :], (((0,), (0,)), ((), ())), preferred_element_type=f32
    )
    out[...] = (part * gain[...] + came[...].astype(f32)).astype(bf16)


def upstream_kernel(half, spots, mine, own, other, gain, mixed, sums):
    values = mine[:, 2 * half :]
    squares, products = 0.0, 0.0
    for c, weights in enumerate((own, other)):
        cols = slice(c * half, (c + 1) * half)
        part = lax.dot_general(
            values, weights[...], (((1,), (1,)), ((), ())), preferred_element_type=f32
        )
        part = part * gain[:, cols]
        mixed[:, cols] = part
        floats = mine[:, cols].astype(f32)
        squares = squares + jnp.sum(floats * floats, axis=1, keepdims=True)
        products = products + jnp.sum(floats * part, axis=1, keepdims=True)
    lane = lax.broadcasted_iota(jnp.int32, (mine.shape[0], 128), 1)
    both = jnp.where(lane == 0, squares, jnp.where(lane == 1, products, 0.0))
    for x in range(sums.shape[0]):
        sums[x] = both.T[:8]


def branch_kernel(sizes, spots, mine, mixed, sums, *outs):
    far, rows, width = sizes
    half = far * rows
    both = jnp.concatenate([jnp.sum(sums[...], axis=0)] * 16, axis=0).T
    inv = lax.rsqrt(both[:, 0:1] / width + rms_epsilon)
    pull = inv * (inv * (both[:, 1:2] / width))
    for k, out in enumerate(outs):
        z = (spots[1] + k) & (far - 1)
        for c in range(2):
            cols = strip_at(c * half + z * rows, rows)
            block = mixed[:, cols] - mine[:, cols].astype(f32) * pull
            out[:, c * rows : (c + 1) * rows] = block.astype(bf16)


def fresh_kernel(sizes, ids_shape, spots, acts, gain, table, out):
    far, group, cores, rows = sizes
    micro, seqs = ids_shape
    core = spots[0]
    half = far * rows
    floats = acts[...].astype(f32)
    toks = floats.shape[0]
    row = lax.broadcasted_iota(jnp.int32, (toks, 1), 0)
    for m in range(micro):
        bin_id = spots[4 + m * seqs + spots[3]]
        embed = jnp.zeros((1, floats.shape[1]), f32)
        for b in range(table.shape[0]):
            embed = jnp.where(bin_id == b, table[b : b + 1, :].astype(f32), embed)
        first = jnp.logical_and(row == m * (toks // micro), spots[2] == 0)
        floats = jnp.where(first, embed, floats)
    inverse = inverse_rms(floats)
    normed = (floats * inverse * gain[...]).astype(bf16)
    for x in range(group):
        for z in range(far):
            start = (z * group + x) * cores * rows
            for c in range(cores):
                place = ((core + c) & (cores - 1)) * half + z * rows
                block = normed[:, start + c * rows : start + (c + 1) * rows]
                out[x, :, strip_at(place, rows)] = block


def join_kernel(rows, spots, back, out):
    cores = back.shape[2] // rows
    for j in range(back.shape[0]):
        for c in range(cores):
            start = (j * cores + ((spots[0] + c) & (cores - 1))) * rows
            out[:, strip_at(start, rows)] = back[j, :, c * rows : (c + 1) * rows]


def per_device(
    acts, norm_gain, value_grads, master, moment1, moment2, next_acts, reward_table, reward_ids
):
    micro, _, tok_dev, width = acts.shape
    kvw = value_grads.shape[3]
    toks = micro * tok_dev
    far = lax.axis_size("zhi")
    group = lax.axis_size("x")
    cores = lax.axis_size("core")
    layers_y = lax.axis_size("y")
    rows = width // (far * group * cores)
    half = far * rows
    all_toks = group * toks
    core, spot_y, spot_x = (lax.axis_index(name) for name in ("core", "y", "x"))
    spots = jnp.stack([core, spot_y, lax.axis_index(section), lax.axis_index(dp)])
    spots = jnp.concatenate([spots, reward_ids.reshape(-1)])
    shape = jax.ShapeDtypeStruct
    gain = norm_gain[0]

    def of_features(block):
        split = block.reshape(block.shape[:-1] + (far, group, cores, rows))
        split = lax.dynamic_index_in_dim(split, spot_x, split.ndim - 3, False)
        halves = [
            lax.dynamic_index_in_dim(split, core ^ c, split.ndim - 2, False) for c in range(cores)
        ]
        return jnp.concatenate([h.reshape(block.shape[:-1] + (half,)) for h in halves], axis=-1)

    own_gain = of_features(gain)

    flat = acts[:, 0].reshape(toks, width)
    blocks = local(
        functools.partial(split_kernel, (far, group, cores, rows)),
        [shape((group, toks, cores * half + kvw), bf16)],
        spots,
        flat,
        value_grads[:, 0].reshape(toks, kvw),
    )[0]
    weights_old, blocks = together(master[0].astype(bf16), blocks)
    mine = exchange(blocks, "x").reshape(all_toks, cores * half + kvw)
    weights_old = lax.all_gather(weights_old, "zhi", axis=0, tiled=True)
    mine, weights_old = together(mine, weights_old)
    weights_other = swap_cores(weights_old)

    flops = 2 * all_toks * half * kvw
    other = local(
        functools.partial(other_kernel, half),
        [shape((half, kvw), bf16)],
        spots,
        mine,
        own_gain[half:, None],
        flops=flops,
    )[0]
    partial = local(
        functools.partial(own_kernel, half),
        [shape((half, kvw), bf16)],
        spots,
        mine,
        own_gain[:half, None],
        swap_cores(other),
        flops=flops,
    )[0]
    partial, weights_other = together(partial, weights_other)
    grad = lax.psum_scatter(partial, "zhi", scatter_dimension=0, tiled=True).astype(f32)

    mixed, sums = local(
        functools.partial(upstream_kernel, half),
        [shape((all_toks, cores * half), f32), shape((group, 8, all_toks), f32)],
        spots,
        mine,
        weights_old,
        weights_other,
        own_gain[None],
        flops=2 * flops,
    )
    sums = exchange(sums, "x")
    parts = local(
        functools.partial(branch_kernel, (far, rows, width)),
        [shape((all_toks, cores * rows), bf16)] * layers_y,
        spots,
        mine,
        mixed,
        sums,
    )
    came = [part.astype(f32) for part in shift(parts, "y")]
    whose = [(spot_y - k) & (layers_y - 1) for k in range(layers_y)]
    suffix = [
        sum(jnp.where(owner >= layer, part, 0.0) for owner, part in zip(whose, came))
        for layer in range(layers_y)
    ]

    next_flat, parts = together(next_acts[:, 0].reshape(toks, width), parts)
    fresh_normed = local(
        functools.partial(fresh_kernel, (far, group, cores, rows), reward_ids.shape),
        [shape((group, toks, cores * half), bf16)],
        spots,
        next_flat,
        norm_gain,
        reward_table,
    )[0]
    fresh_normed = exchange(fresh_normed, "x").reshape(all_toks, cores * half)

    squares = jnp.broadcast_to(jnp.sum(grad * grad), (lax.axis_size(("zlo","zhi")), 8, 128))
    top, squares, fresh_normed = together(suffix[0].astype(bf16), squares, fresh_normed)
    squares = total(squares, ("zlo", "zhi"))
    behind = sum_from_behind(top, "zlo")
    suffix = jnp.stack([(part + behind).astype(bf16) for part in suffix])
    squares = total(jnp.broadcast_to(squares, (lax.axis_size(("y","x","core")), 8, 128)), ("y", "x", "core"))[0, 0]
    entries = lax.axis_size(section) * width * kvw
    rms = jnp.sqrt(squares / entries + 1e-12)
    clipped = grad * jnp.minimum(1.0, clip_level / rms)
    moment1_new = beta_first * moment1[0] + (1.0 - beta_first) * clipped
    moment2_new = beta_second * moment2[0] + (1.0 - beta_second) * clipped * clipped
    update = (
        moment1_new / bias_first / (jnp.sqrt(moment2_new / bias_second) + adam_epsilon)
        + decay_rate * master[0]
    )
    weights_new = (master[0] - learn_rate * update).astype(bf16)
    weights_new, suffix = together(weights_new, suffix)
    weights_new = lax.all_gather(weights_new, "zhi", axis=0, tiled=True)
    strip = cores * rows
    back = exchange(suffix.reshape(layers_y * group, toks, strip), ("y", "x"))

    fresh = jnp.dot(fresh_normed[:, :half], weights_new, preferred_element_type=f32)
    fresh = fresh + jnp.dot(
        fresh_normed[:, half:], swap_cores(weights_new), preferred_element_type=f32
    )
    fresh, back = together(fresh.astype(bf16).reshape(group, toks, kvw), back)
    fresh = jnp.sum(exchange(fresh, "x").astype(f32), axis=0).astype(bf16)
    fresh_values = fresh.reshape(micro, 1, tok_dev, kvw)

    input_grads = local(
        functools.partial(join_kernel, rows), [shape((toks, width), bf16)], spots, back
    )[0].reshape(micro, 1, tok_dev, width)
    return (input_grads, moment1_new[None], moment2_new[None], fresh_values)


def solution(mesh):
    fine = Mesh(mesh.devices.reshape(factors["section"] + factors["dp"]), axes)
    return jax.shard_map(
        per_device,
        mesh=fine,
        in_specs=(
            P(None, section, dp, None),
            P(section, None),
            P(None, section, dp, None),
            P(section, dp, None),
            P(section, dp, None),
            P(section, dp, None),
            P(None, section, dp, None),
            P(),
            P(),
        ),
        out_specs=(
            P(None, section, dp, None),
            P(section, dp, None),
            P(section, dp, None),
            P(None, section, dp, None),
        ),
        check_vma=False,
    )
```

time: 247 us -> 207 us (0.84); the launches traced: 242 us -> 205 us
  starting transfers between devices: 96.6 us -> 57.8 us
  blocking collectives: 31.9 us -> 63 us
  local copies, waits for them, and re-layouts: 26.8 us -> 5.83 us
  Pallas kernels: 0 us -> 12.3 us
  matrix products: 11.6 us -> 1.69 us
  other arithmetic: 14.2 us -> 6.58 us
  waiting for transfers between devices: 45.9 us -> 43 us
    ppermute x6 -> x3, starting transfers between devices: 32.1 us -> 9.5 us  [shift(): lax.ppermute(parts[k], axis, [(i, (i + k) % size) for i in range(size)])]
    all_gather x1, blocking collectives: 14 us -> 30.9 us  [per_device(): weights_old = lax.all_gather(weights_old, 'zhi', axis=0, tiled=True)]
    pallas_call x0 -> x7, Pallas kernels: none -> 12.3 us  [local(): pl.pallas_call(kernel, out_shape=out_shapes, in_specs=[pl.BlockSpec(memor...]
    ppermute x3, waiting for transfers between devices: 11.6 us -> 0.01 us  [sum_from_behind(): lax.ppermute(block, axis, [(i + k, i) for i in range(size - k)])]
    ppermute x6 -> x3, waiting for transfers between devices: 1.24 us -> 11.7 us  [shift(): lax.ppermute(parts[k], axis, [(i, (i + k) % size) for i in range(size)])]
    dot_general x6 -> x2, matrix products: 11.6 us -> 1.69 us  [the longest x1 1.25 us: per_device(): jnp.dot(fresh_normed[:, half:], swap_cores(weights_new), preferred_elemen...]
    all_to_all x7 -> x6, starting transfers between devices: 42.8 us -> 33.2 us  [exchange(): return lax.all_to_all(blocks, axis, 0, 0)]
    all_gather x1, blocking collectives: 17.9 us -> 25.3 us  [per_device(): weights_new = lax.all_gather(weights_new, 'zhi', axis=0, tiled=True)]
  transfers between devices with their start and end apart: 19 -> 16, of which waited for: 7 -> 7; matrix products, arithmetic and copies ran while one was open for 16% -> 3% of each run, Pallas kernels for 0% -> 4%
where the time goes in v3:
time: 207 us; the launch traced here: 205 us
  blocking collectives  63 us (30%)
  starting transfers between devices  57.8 us (28%)
  waiting for transfers between devices  43 us (21%)
  between operations  15.1 us (7%)
  Pallas kernels  12.3 us (6%)
  other arithmetic  6.58 us (3%)
  local copies, waits for them, and re-layouts  5.83 us (3%)
    all_to_all x6, starting transfers between devices, exchange(): return lax.all_to_all(blocks, axis, 0, 0)  33.2 us
    all_gather x1, blocking collectives, per_device(): weights_old = lax.all_gather(weights_old, 'zhi', axis=0, tiled=True)  30.9 us
    all_to_all x6, waiting for transfers between devices, exchange(): return lax.all_to_all(blocks, axis, 0, 0)  28.3 us
    all_gather x1, blocking collectives, per_device(): weights_new = lax.all_gather(weights_new, 'zhi', axis=0, tiled=True)  25.3 us
    pallas_call x7, Pallas kernels, local(): pl.pallas_call(kernel, out_shape=out_shapes, in_specs=[pl.BlockSpec(memor...  12.3 us
    ppermute x3, waiting for transfers between devices, shift(): lax.ppermute(parts[k], axis, [(i, (i + k) % size) for i in range(size)])  11.7 us
    ppermute x3, starting transfers between devices, swap_cores(): return lax.ppermute(block, 'core', [(0, 1), (1, 0)])  11.2 us
    ppermute x3, starting transfers between devices, shift(): lax.ppermute(parts[k], axis, [(i, (i + k) % size) for i in range(size)])  9.5 us
  transfers between devices with their start and end apart: 16, of which 7 were waited for; matrix products, arithmetic and copies ran while one was open for 3% of the time, Pallas kernels for 4%

profile of v3, /device:TPU:1, one launch (start us, length us, event | category | flops | bytes accessed | tf_op | source)
XLA Modules:
  0.0 205.3 jit_solution(972834335508664587)
XLA Ops:
  7.2 0.8 reshape.54
  7.9 1.0 bitcast_convert_fusion
  8.9 0.1 concatenate.6.spots
  9.0 1.2 copy-done.1
  10.2 0.9 copy-done.2
  11.1 2.2 %shard_map.120 = bf16[4,128,1536]{2,1,0:T(8,128)(2,1)} custom-call(s32[68]{0:T(128)S(1)} %concatenate.6.spots, bf16[128,4096]{1,0:T(8,128)(2,1)S(1)} %bitcast.71, bf16[128,512]{1,0:T(8,128)(2,1)S(1)} %bitcast.72), custom_call_target="tpu_custom_call" | custom-call | tf_op jit(solution)/shard_map/pallas_call | solution.py:73
  13.3 5.0 %all-to-all-start = ((bf16[4,128,1536]{2,1,0:T(8,128)(2,1)}), bf16[4,128,1536]{2,1,0:T(8,128)(2,1)S(1)}, u32[]{:S(2)}, u32[]{:S(2)}) async-start(bf16[4,128,1536]{2,1,0:T(8,128)(2,1)} %shard_map.120), calls=%async_computation | async-start | bytes 3145728 | tf_op jit(solution)/shard_map/all_to_all | solution.py:30
  18.3 0.1 copy.23.gain
  18.5 30.9 %all_gather.6.own = bf16[512,512]{1,0:T(8,128)(2,1)S(1)} all-gather(bf16[128,512]{1,0:T(8,128)(2,1)S(1)} %bitcast_convert_fusion), channel_id=1, replica_groups=mesh['zlo'=4,'y'=4,'zhi'=4,'x'=4,'core'=2] {'zhi'}, dimensions={0}, use_global_device_ids=true | all-gather | bytes 655360 | tf_op jit(solution)/shard_map/all_gather | solution.py:225
  49.3 0.0 all-to-all-done
  49.4 1.0 shard_map.121
  50.4 6.5 %collective-permute-start = (bf16[512,512]{1,0:T(8,128)(2,1)S(1)}, bf16[512,512]{1,0:T(8,128)(2,1)}, u32[]{:S(2)}, u32[]{:S(2)}) collective-permute-start(bf16[512,512]{1,0:T(8,128)(2,1)S(1)} %shard_map.121), channel_id=1, source_target_pairs={{0,1},{1,0},{2,3},{3,2},{4,5},{5,4},{6,7},{7,6},{8,9},{9,8},{10,11... | collective-permute-start | bytes 1572872 | tf_op jit(solution)/shard_map/ppermute | solution.py:50
  56.8 1.9 collective-permute-start.1
  58.8 0.1 copy.24.gain
  58.9 0.0 collective-permute-done.came
  58.9 2.3 %shard_map.122 = bf16[512,512]{1,0:T(8,128)(2,1)} custom-call(s32[68]{0:T(128)S(1)} %concatenate.6.spots, bf16[512,1536]{1,0:T(8,128)(2,1)S(1)} %bitcast.67, f32[512,1]{1,0:T(8,128)S(1)} %copy.24.gain, bf16[512,512]{1,0:T(8,128)(2,1)} %collective-permute-done.came), custom_call_target="tpu_custom_call" | custom-call | tf_op jit(solution)/shard_map/pallas_call | solution.py:73
  61.3 0.0 collective-permute-done.1.other
  61.3 0.0 reduce-scatter.2.cloned.1.call-update
  61.3 1.5 shard_map.123
  62.8 6.8 %all_to_all.35.sums = f32[4,8,512]{2,1,0:T(8,128)S(1)} all-to-all(f32[4,8,512]{2,1,0:T(8,128)S(1)} %get-tuple-element.30), channel_id=1, replica_groups=mesh['zlo'=4,'y'=4,'zhi'=4,'x'=4,'core'=2] {'x'}, dimensions={0} | all-to-all | bytes 131072 | tf_op jit(solution)/shard_map/all_to_all | solution.py:30
  69.7 1.2 shard_map.124
  70.8 0.1 copy-done
  70.9 2.3 %shard_map.125 = bf16[4,128,1024]{2,1,0:T(8,128)(2,1)} custom-call(s32[68]{0:T(128)S(1)} %concatenate.6.spots, bf16[128,4096]{1,0:T(8,128)(2,1)S(1)} %bitcast.70, f32[1,4096]{1,0:T(1,128)S(1)} %copy-done.4, bf16[5,4096]{1,0:T(8,128)(2,1)S(1)} %copy-done.3), custom_call_target="tpu_custom_call" | custom-call | tf_op jit(solution)/shard_map/pallas_call | solution.py:73
  73.2 3.5 %all-to-all-start.2 = ((bf16[4,128,1024]{2,1,0:T(8,128)(2,1)}), bf16[4,128,1024]{2,1,0:T(8,128)(2,1)S(1)}, u32[]{:S(2)}, u32[]{:S(2)}) async-start(bf16[4,128,1024]{2,1,0:T(8,128)(2,1)} %shard_map.125), calls=%async_computation.3 | async-start | bytes 2097152 | tf_op jit(solution)/shard_map/all_to_all | solution.py:30
  76.8 4.6 %collective-permute-start.4 = (bf16[512,256]{1,0:T(8,128)(2,1)S(1)}, bf16[512,256]{1,0:T(8,128)(2,1)S(1)}, u32[]{:S(2)}, u32[]{:S(2)}) collective-permute-start(bf16[512,256]{1,0:T(8,128)(2,1)S(1)} %get-tuple-element.34), channel_id=1, source_target_pairs={{0,96},{32,0},{64,32},{96,64},{1,97},{33,1},{65,33},{97,65},{2,98}... | collective-permute-start | bytes 786440 | tf_op jit(solution)/shard_map/ppermute | solution.py:45
  81.4 2.3 %collective-permute-start.3 = (bf16[512,256]{1,0:T(8,128)(2,1)S(1)}, bf16[512,256]{1,0:T(8,128)(2,1)S(1)}, u32[]{:S(2)}, u32[]{:S(2)}) collective-permute-start(bf16[512,256]{1,0:T(8,128)(2,1)S(1)} %get-tuple-element.33), channel_id=1, source_target_pairs={{0,64},{32,96},{64,0},{96,32},{1,65},{33,97},{65,1},{97,33},{2,66}... | collective-permute-start | bytes 786440 | tf_op jit(solution)/shard_map/ppermute | solution.py:45
  83.7 2.6 %collective-permute-start.2 = (bf16[512,256]{1,0:T(8,128)(2,1)S(1)}, bf16[512,256]{1,0:T(8,128)(2,1)S(1)}, u32[]{:S(2)}, u32[]{:S(2)}) collective-permute-start(bf16[512,256]{1,0:T(8,128)(2,1)S(1)} %get-tuple-element.32), channel_id=1, source_target_pairs={{0,32},{32,64},{64,96},{96,0},{1,33},{33,65},{65,97},{97,1},{2,34}... | collective-permute-start | bytes 786440 | tf_op jit(solution)/shard_map/ppermute | solution.py:45
  86.3 0.0 collective-permute-done.4
  86.3 4.5 %collective-permute-done.3 = bf16[512,256]{1,0:T(8,128)(2,1)S(1)} collective-permute-done((bf16[512,256]{1,0:T(8,128)(2,1)S(1)}, bf16[512,256]{1,0:T(8,128)(2,1)S(1)}, u32[]{:S(2)}, u32[]{:S(2)}) %collective-permute-start.3) | collective-permute-done | bytes 262176 | tf_op jit(solution)/shard_map/ppermute | solution.py:45
  90.8 7.3 %collective-permute-done.2 = bf16[512,256]{1,0:T(8,128)(2,1)S(1)} collective-permute-done((bf16[512,256]{1,0:T(8,128)(2,1)S(1)}, bf16[512,256]{1,0:T(8,128)(2,1)S(1)}, u32[]{:S(2)}, u32[]{:S(2)}) %collective-permute-start.2) | collective-permute-done | bytes 262176 | tf_op jit(solution)/shard_map/ppermute | solution.py:45
  98.0 0.2 fusion.35
  98.2 1.9 reduce-scatter.2.cloned.1.call-done
  100.1 1.6 fusion.24
  101.7 0.0 all-to-all-done.2
  101.7 1.3 broadcast_in_dim.36
  103.0 1.3 collective-permute-start.7
  104.3 1.3 collective-permute-start.6
  105.6 1.3 collective-permute-start.5
  106.9 8.4 %all-to-all-start.3 = ((f32[16,8,128]{2,1,0:T(8,128)}), f32[16,8,128]{2,1,0:T(8,128)S(1)}, u32[]{:S(2)}, u32[]{:S(2)}) async-start(f32[16,8,128]{2,1,0:T(8,128)} %broadcast_in_dim.36), calls=%async_computation.4 | async-start | bytes 131072 | tf_op jit(solution)/shard_map/all_to_all | solution.py:30
  115.3 15.6 %all-to-all-done.3 = f32[16,8,128]{2,1,0:T(8,128)S(1)} async-done(((f32[16,8,128]{2,1,0:T(8,128)}), f32[16,8,128]{2,1,0:T(8,128)S(1)}, u32[]{:S(2)}, u32[]{:S(2)}) %all-to-all-start.3) | async-done | bytes 65568 | tf_op jit(solution)/shard_map/all_to_all | solution.py:30
  131.0 0.7 broadcast_in_dim.37
  131.7 8.4 %all-to-all-start.4 = ((f32[32,8,128]{2,1,0:T(8,128)}), f32[32,8,128]{2,1,0:T(8,128)S(1)}, u32[]{:S(2)}, u32[]{:S(2)}) async-start(f32[32,8,128]{2,1,0:T(8,128)} %broadcast_in_dim.37), calls=%async_computation.5 | async-start | bytes 262144 | tf_op jit(solution)/shard_map/all_to_all | solution.py:30
  140.1 0.0 collective-permute-done.6
  140.1 0.0 collective-permute-done.5
  140.1 0.3 fusion.27
  140.4 0.6 fusion.26
  141.0 0.0 copy-start.7
  141.0 0.0 copy-start.9
  141.0 0.0 copy-start.10
  141.1 1.1 pad_maximum_fusion
  142.2 5.5 %all-to-all-done.4 = f32[32,8,128]{2,1,0:T(8,128)S(1)} async-done(((f32[32,8,128]{2,1,0:T(8,128)}), f32[32,8,128]{2,1,0:T(8,128)S(1)}, u32[]{:S(2)}, u32[]{:S(2)}) %all-to-all-start.4) | async-done | bytes 131104 | tf_op jit(solution)/shard_map/all_to_all | solution.py:30
  147.7 0.5 slice.10
  149.0 1.0 fusion.34
  150.0 3.8 %all-to-all-start.5 = ((bf16[16,128,256]{2,1,0:T(8,128)(2,1)}), bf16[16,128,256]{2,1,0:T(8,128)(2,1)S(1)}, u32[]{:S(2)}, u32[]{:S(2)}) async-start(bf16[16,128,256]{2,1,0:T(8,128)(2,1)} %bitcast.24), calls=%async_computation.6 | async-start | bytes 2097152 | tf_op jit(solution)/shard_map/all_to_all | solution.py:30
  153.7 25.3 %all_gather.7 = bf16[512,512]{1,0:T(8,128)(2,1)S(1)} all-gather(bf16[128,512]{1,0:T(8,128)(2,1)S(1)} %get-tuple-element.40), channel_id=1, replica_groups=mesh['zlo'=4,'y'=4,'zhi'=4,'x'=4,'core'=2] {'zhi'}, dimensions={0}, use_global_device_ids=true | all-gather | bytes 655360 | tf_op jit(solution)/shard_map/all_gather | solution.py:304
  179.0 2.8 %collective-permute-start.8 = (bf16[512,512]{1,0:T(8,128)(2,1)S(1)}, bf16[512,512]{1,0:T(8,128)(2,1)S(1)}, u32[]{:S(2)}, u32[]{:S(2)}) collective-permute-start(bf16[512,512]{1,0:T(8,128)(2,1)S(1)} %all_gather.7), channel_id=1, source_target_pairs={{0,1},{1,0},{2,3},{3,2},{4,5},{5,4},{6,7},{7,6},{8,9},{9,8},{10,11... | collective-permute-start | bytes 1572872 | tf_op jit(solution)/shard_map/ppermute | solution.py:50
  181.9 0.4 fusion.20
  182.3 1.1 collective-permute-done.8
  183.4 1.2 fusion
  184.6 0.0 all-to-all-done.5.back
  184.6 4.1 %all-to-all-start.6 = ((bf16[4,128,512]{2,1,0:T(8,128)(2,1)}), bf16[4,128,512]{2,1,0:T(8,128)(2,1)S(1)}, u32[]{:S(2)}, u32[]{:S(2)}) async-start(bf16[4,128,512]{2,1,0:T(8,128)(2,1)} %bitcast.23), calls=%async_computation.7 | async-start | bytes 1048576 | tf_op jit(solution)/shard_map/all_to_all | solution.py:30
  188.8 1.8 shard_map.126
  190.6 7.1 %all-to-all-done.6 = bf16[4,128,512]{2,1,0:T(8,128)(2,1)S(1)} async-done(((bf16[4,128,512]{2,1,0:T(8,128)(2,1)}), bf16[4,128,512]{2,1,0:T(8,128)(2,1)S(1)}, u32[]{:S(2)}, u32[]{:S(2)}) %all-to-all-start.6) | async-done | bytes 524320 | tf_op jit(solution)/shard_map/all_to_all | solution.py:30
  197.7 0.7 reduce_sum.42
  (22 shorter events, 0.1 us)
Async XLA Ops:
  9.0 1.2 copy-start.1
  10.2 0.9 copy-start.2
  13.3 5.0 %copy-start.4 = (f32[1,4096]{1,0:T(1,128)S(1)}, f32[1,4096]{1,0:T(1,128)}, u32[]{:S(2)}) copy-start(f32[1,4096]{1,0:T(1,128)} %gain.1) | copy-start | bytes 49156
  13.3 36.0 %all-to-all-start = ((bf16[4,128,1536]{2,1,0:T(8,128)(2,1)}), bf16[4,128,1536]{2,1,0:T(8,128)(2,1)S(1)}, u32[]{:S(2)}, u32[]{:S(2)}) async-start(bf16[4,128,1536]{2,1,0:T(8,128)(2,1)} %shard_map.120), calls=%async_computation | async-start | bytes 3145728 | tf_op jit(solution)/shard_map/all_to_all | solution.py:30
  18.3 81.8 %reduce-scatter.2.cloned.1.call-start = ((), (), s32[]{:S(2)}) async-start(), calls=%async_computation.8 | async-start | bytes 655360 | tf_op jit(solution)/shard_map/reduce_scatter | solution.py:248
  50.4 8.6 %collective-permute-start = (bf16[512,512]{1,0:T(8,128)(2,1)S(1)}, bf16[512,512]{1,0:T(8,128)(2,1)}, u32[]{:S(2)}, u32[]{:S(2)}) collective-permute-start(bf16[512,512]{1,0:T(8,128)(2,1)S(1)} %shard_map.121), channel_id=1, source_target_pairs={{0,1},{1,0},{2,3},{3,2},{4,5},{5,4},{6,7},{7,6},{8,9},{9,8},{10,11... | collective-permute-start | bytes 1572872 | tf_op jit(solution)/shard_map/ppermute | solution.py:50
  56.8 4.4 %collective-permute-start.1 = (bf16[512,512]{1,0:T(8,128)(2,1)S(1)}, bf16[512,512]{1,0:T(8,128)(2,1)S(1)}, u32[]{:S(2)}, u32[]{:S(2)}) collective-permute-start(bf16[512,512]{1,0:T(8,128)(2,1)S(1)} %all_gather.6.own), channel_id=1, source_target_pairs={{0,1},{1,0},{2,3},{3,2},{4,5},{5,4},{6,7},{7,6},{8,9},{9,8},{10,11... | collective-permute-start | bytes 1572872 | tf_op jit(solution)/shard_map/ppermute | solution.py:50
  69.7 1.2 copy-start
  69.7 1.2 copy-start.3
  73.2 28.5 %all-to-all-start.2 = ((bf16[4,128,1024]{2,1,0:T(8,128)(2,1)}), bf16[4,128,1024]{2,1,0:T(8,128)(2,1)S(1)}, u32[]{:S(2)}, u32[]{:S(2)}) async-start(bf16[4,128,1024]{2,1,0:T(8,128)(2,1)} %shard_map.125), calls=%async_computation.3 | async-start | bytes 2097152 | tf_op jit(solution)/shard_map/all_to_all | solution.py:30
  76.8 9.5 %collective-permute-start.4 = (bf16[512,256]{1,0:T(8,128)(2,1)S(1)}, bf16[512,256]{1,0:T(8,128)(2,1)S(1)}, u32[]{:S(2)}, u32[]{:S(2)}) collective-permute-start(bf16[512,256]{1,0:T(8,128)(2,1)S(1)} %get-tuple-element.34), channel_id=1, source_target_pairs={{0,96},{32,0},{64,32},{96,64},{1,97},{33,1},{65,33},{97,65},{2,98}... | collective-permute-start | bytes 786440 | tf_op jit(solution)/shard_map/ppermute | solution.py:45
  81.4 9.3 %collective-permute-start.3 = (bf16[512,256]{1,0:T(8,128)(2,1)S(1)}, bf16[512,256]{1,0:T(8,128)(2,1)S(1)}, u32[]{:S(2)}, u32[]{:S(2)}) collective-permute-start(bf16[512,256]{1,0:T(8,128)(2,1)S(1)} %get-tuple-element.33), channel_id=1, source_target_pairs={{0,64},{32,96},{64,0},{96,32},{1,65},{33,97},{65,1},{97,33},{2,66}... | collective-permute-start | bytes 786440 | tf_op jit(solution)/shard_map/ppermute | solution.py:45
  83.7 14.4 %collective-permute-start.2 = (bf16[512,256]{1,0:T(8,128)(2,1)S(1)}, bf16[512,256]{1,0:T(8,128)(2,1)S(1)}, u32[]{:S(2)}, u32[]{:S(2)}) collective-permute-start(bf16[512,256]{1,0:T(8,128)(2,1)S(1)} %get-tuple-element.32), channel_id=1, source_target_pairs={{0,32},{32,64},{64,96},{96,0},{1,33},{33,65},{65,97},{97,1},{2,34}... | collective-permute-start | bytes 786440 | tf_op jit(solution)/shard_map/ppermute | solution.py:45
  101.7 39.3 %copy-start.5 = (bf16[4,128,1024]{2,1,0:T(8,128)(2,1)}, bf16[4,128,1024]{2,1,0:T(8,128)(2,1)S(1)}, u32[]{:S(2)}) copy-start(bf16[4,128,1024]{2,1,0:T(8,128)(2,1)S(1)} %all-to-all-done.2) | copy-start | bytes 3145732
  103.0 37.1 %collective-permute-start.7 = (bf16[512,256]{1,0:T(8,128)(2,1)S(1)}, bf16[512,256]{1,0:T(8,128)(2,1)S(1)}, u32[]{:S(2)}, u32[]{:S(2)}) collective-permute-start(bf16[512,256]{1,0:T(8,128)(2,1)S(1)} %fusion.35), channel_id=1, source_target_pairs={{128,0},{256,128},{384,256},{129,1},{257,129},{385,257},{130,2},{2... | collective-permute-start | bytes 786440 | tf_op jit(solution)/shard_map/ppermute | solution.py:56
  104.3 35.8 %collective-permute-start.6 = (bf16[512,256]{1,0:T(8,128)(2,1)S(1)}, bf16[512,256]{1,0:T(8,128)(2,1)S(1)}, u32[]{:S(2)}, u32[]{:S(2)}) collective-permute-start(bf16[512,256]{1,0:T(8,128)(2,1)S(1)} %fusion.35), channel_id=1, source_target_pairs={{256,0},{384,128},{257,1},{385,129},{258,2},{386,130},{259,3},{387... | collective-permute-start | bytes 786440 | tf_op jit(solution)/shard_map/ppermute | solution.py:56
  105.6 34.5 %collective-permute-start.5 = (bf16[512,256]{1,0:T(8,128)(2,1)S(1)}, bf16[512,256]{1,0:T(8,128)(2,1)S(1)}, u32[]{:S(2)}, u32[]{:S(2)}) collective-permute-start(bf16[512,256]{1,0:T(8,128)(2,1)S(1)} %fusion.35), channel_id=1, source_target_pairs={{384,0},{385,1},{386,2},{387,3},{388,4},{389,5},{390,6},{391,7},{3... | collective-permute-start | bytes 786440 | tf_op jit(solution)/shard_map/ppermute | solution.py:56
  106.9 24.1 %all-to-all-start.3 = ((f32[16,8,128]{2,1,0:T(8,128)}), f32[16,8,128]{2,1,0:T(8,128)S(1)}, u32[]{:S(2)}, u32[]{:S(2)}) async-start(f32[16,8,128]{2,1,0:T(8,128)} %broadcast_in_dim.36), calls=%async_computation.4 | async-start | bytes 131072 | tf_op jit(solution)/shard_map/all_to_all | solution.py:30
  131.7 16.0 %all-to-all-start.4 = ((f32[32,8,128]{2,1,0:T(8,128)}), f32[32,8,128]{2,1,0:T(8,128)S(1)}, u32[]{:S(2)}, u32[]{:S(2)}) async-start(f32[32,8,128]{2,1,0:T(8,128)} %broadcast_in_dim.37), calls=%async_computation.5 | async-start | bytes 262144 | tf_op jit(solution)/shard_map/all_to_all | solution.py:30
  141.0 7.9 %copy-start.7 = (f32[1,128,512]{2,1,0:T(8,128)S(1)}, f32[1,128,512]{2,1,0:T(8,128)}, u32[]{:S(2)}) copy-start(f32[1,128,512]{2,1,0:T(8,128)} %param.12) | copy-start | bytes 786436
  141.0 7.9 %copy-start.8 = (bf16[128,512]{1,0:T(8,128)(2,1)S(1)}, bf16[128,512]{1,0:T(8,128)(2,1)}, u32[]{:S(2)}) copy-start(bf16[128,512]{1,0:T(8,128)(2,1)} %reduce-scatter.2.cloned.1.call-done) | copy-start | bytes 393220
  141.0 7.9 %copy-start.9 = (f32[1,128,512]{2,1,0:T(8,128)S(1)}, f32[1,128,512]{2,1,0:T(8,128)}, u32[]{:S(2)}) copy-start(f32[1,128,512]{2,1,0:T(8,128)} %param.14) | copy-start | bytes 786436
  141.0 7.9 %copy-start.10 = (f32[1,128,512]{2,1,0:T(8,128)S(1)}, f32[1,128,512]{2,1,0:T(8,128)}, u32[]{:S(2)}) copy-start(f32[1,128,512]{2,1,0:T(8,128)} %param.13) | copy-start | bytes 786436
  150.0 31.9 %copy-start.6 = (bf16[4,128,1024]{2,1,0:T(8,128)(2,1)S(1)}, bf16[4,128,1024]{2,1,0:T(8,128)(2,1)}, u32[]{:S(2)}) copy-start(bf16[4,128,1024]{2,1,0:T(8,128)(2,1)} %copy-done.5) | copy-start | bytes 3145732
  150.0 34.7 %all-to-all-start.5 = ((bf16[16,128,256]{2,1,0:T(8,128)(2,1)}), bf16[16,128,256]{2,1,0:T(8,128)(2,1)S(1)}, u32[]{:S(2)}, u32[]{:S(2)}) async-start(bf16[16,128,256]{2,1,0:T(8,128)(2,1)} %bitcast.24), calls=%async_computation.6 | async-start | bytes 2097152 | tf_op jit(solution)/shard_map/all_to_all | solution.py:30
  179.0 4.4 %collective-permute-start.8 = (bf16[512,512]{1,0:T(8,128)(2,1)S(1)}, bf16[512,512]{1,0:T(8,128)(2,1)S(1)}, u32[]{:S(2)}, u32[]{:S(2)}) collective-permute-start(bf16[512,512]{1,0:T(8,128)(2,1)S(1)} %all_gather.7), channel_id=1, source_target_pairs={{0,1},{1,0},{2,3},{3,2},{4,5},{5,4},{6,7},{7,6},{8,9},{9,8},{10,11... | collective-permute-start | bytes 1572872 | tf_op jit(solution)/shard_map/ppermute | solution.py:50
  184.6 13.0 %all-to-all-start.6 = ((bf16[4,128,512]{2,1,0:T(8,128)(2,1)}), bf16[4,128,512]{2,1,0:T(8,128)(2,1)S(1)}, u32[]{:S(2)}, u32[]{:S(2)}) async-start(bf16[4,128,512]{2,1,0:T(8,128)(2,1)} %bitcast.23), calls=%async_computation.7 | async-start | bytes 1048576 | tf_op jit(solution)/shard_map/all_to_all | solution.py:30
Sparse Core Ops, SparseCore 0:
  61.4 38.6 reduce-scatter.1

commit v4 on v3

--- a/solution.py
+++ b/solution.py
@@ -22,16 +22,13 @@
 axes = ("zlo", "y", "zhi", "x", "core")
 section = ("zlo", "y")
 dp = ("zhi", "x", "core")
+heavy = 2 * 10**10
 f32 = jnp.float32
 bf16 = jnp.bfloat16
 
 
 def exchange(blocks, axis):
     return lax.all_to_all(blocks, axis, 0, 0)
-
-
-def total(value, axis):
-    return jnp.sum(exchange(value, axis), axis=0)
 
 
 def shifts(size):
@@ -50,13 +47,12 @@
     return lax.ppermute(block, "core", [(0, 1), (1, 0)])
 
 
-def sum_from_behind(block, axis):
+def from_behind(block, axis):
     size = lax.axis_size(axis)
-    moved = [
+    return [
         lax.ppermute(block, axis, [(i + k, i) for i in range(size - k)])
         for k in range(size - 1, 0, -1)
     ]
-    return sum(part.astype(f32) for part in moved)
 
 
 def together(*values):
@@ -67,9 +63,7 @@
     return lax.rsqrt(jnp.mean(floats * floats, axis=-1, keepdims=True) + rms_epsilon)
 
 
-def local(kernel, out_shapes, spots, *arrays, flops=0):
-    moved = sum(a.size * a.dtype.itemsize for a in arrays)
-    moved += sum(s.size * s.dtype.itemsize for s in out_shapes)
+def local(kernel, out_shapes, spots, *arrays, weight=0):
     return pl.pallas_call(
         kernel,
         out_shape=out_shapes,
@@ -77,7 +71,7 @@
         + [pl.BlockSpec(memory_space=pltpu.VMEM)] * len(arrays),
         out_specs=[pl.BlockSpec(memory_space=pltpu.VMEM)] * len(out_shapes),
         compiler_params=pltpu.CompilerParams(vmem_limit_bytes=48 * 1024 * 1024),
-        cost_estimate=pl.CostEstimate(flops=0, bytes_accessed=0, transcendentals=0),
+        cost_estimate=pl.CostEstimate(flops=weight, bytes_accessed=0, transcendentals=0),
     )(spots, *arrays)
 
 
@@ -175,6 +169,49 @@
                 out[x, :, strip_at(place, rows)] = block
 
 
+def top_kernel(spots, *refs):
+    *came, out = refs
+    out[...] = sum(part[...].astype(f32) for part in came).astype(bf16)
+
+
+def suffix_kernel(layers, group, spots, *refs):
+    *parts, out = refs
+    came = [part[...].astype(f32) for part in parts[:layers]]
+    behind = sum(part[...].astype(f32) for part in parts[layers:])
+    toks = out.shape[1]
+    for layer in range(layers):
+        block = behind
+        for k in range(layers):
+            here = ((spots[1] - k) & (layers - 1)) >= layer
+            block = block + jnp.where(here, came[k], 0.0)
+        for x in range(group):
+            out[layer * group + x] = block[x * toks : (x + 1) * toks].astype(bf16)
+
+
+def squares_kernel(spots, grad, out):
+    floats = grad[...].astype(f32)
+    out[...] = jnp.broadcast_to(jnp.sum(floats * floats), out.shape)
+
+
+def relay_kernel(spots, sums, out):
+    out[...] = jnp.broadcast_to(jnp.sum(sums[...], axis=0, keepdims=True), out.shape)
+
+
+def adam_kernel(entries, spots, sums, grad, master, first, second, first_new, second_new, weights):
+    squares = jnp.sum(sums[...], axis=0)
+    clip = jnp.minimum(1.0, clip_level / jnp.sqrt(squares / entries + 1e-12))[0:1, 0:1]
+    clipped = grad[...].astype(f32) * clip
+    moment1 = beta_first * first[...] + (1.0 - beta_first) * clipped
+    moment2 = beta_second * second[...] + (1.0 - beta_second) * clipped * clipped
+    first_new[...] = moment1
+    second_new[...] = moment2
+    update = (
+        moment1 / bias_first / (jnp.sqrt(moment2 / bias_second) + adam_epsilon)
+        + decay_rate * master[...]
+    )
+    weights[...] = (master[...] - learn_rate * update).astype(bf16)
+
+
 def join_kernel(rows, spots, back, out):
     cores = back.shape[2] // rows
     for j in range(back.shape[0]):
@@ -224,16 +261,13 @@
     mine = exchange(blocks, "x").reshape(all_toks, cores * half + kvw)
     weights_old = lax.all_gather(weights_old, "zhi", axis=0, tiled=True)
     mine, weights_old = together(mine, weights_old)
-    weights_other = swap_cores(weights_old)
-
-    flops = 2 * all_toks * half * kvw
+
     other = local(
         functools.partial(other_kernel, half),
         [shape((half, kvw), bf16)],
         spots,
         mine,
         own_gain[half:, None],
-        flops=flops,
     )[0]
     partial = local(
         functools.partial(own_kernel, half),
@@ -242,10 +276,10 @@
         mine,
         own_gain[:half, None],
         swap_cores(other),
-        flops=flops,
-    )[0]
-    partial, weights_other = together(partial, weights_other)
-    grad = lax.psum_scatter(partial, "zhi", scatter_dimension=0, tiled=True).astype(f32)
+    )[0]
+    partial, weights_old = together(partial, weights_old)
+    grad = lax.psum_scatter(partial, "zhi", scatter_dimension=0, tiled=True)
+    weights_other = swap_cores(weights_old)
 
     mixed, sums = local(
         functools.partial(upstream_kernel, half),
@@ -255,7 +289,6 @@
         weights_old,
         weights_other,
         own_gain[None],
-        flops=2 * flops,
     )
     sums = exchange(sums, "x")
     parts = local(
@@ -266,12 +299,9 @@
         mixed,
         sums,
     )
-    came = [part.astype(f32) for part in shift(parts, "y")]
-    whose = [(spot_y - k) & (layers_y - 1) for k in range(layers_y)]
-    suffix = [
-        sum(jnp.where(owner >= layer, part, 0.0) for owner, part in zip(whose, came))
-        for layer in range(layers_y)
-    ]
+    came = shift(parts, "y")
+    top_shape = shape((all_toks, cores * rows), bf16)
+    top = local(top_kernel, [top_shape], spots, *came)[0]
 
     next_flat, parts = together(next_acts[:, 0].reshape(toks, width), parts)
     fresh_normed = local(
@@ -284,26 +314,38 @@
     )[0]
     fresh_normed = exchange(fresh_normed, "x").reshape(all_toks, cores * half)
 
-    squares = jnp.broadcast_to(jnp.sum(grad * grad), (lax.axis_size(("zlo","zhi")), 8, 128))
-    top, squares, fresh_normed = together(suffix[0].astype(bf16), squares, fresh_normed)
-    squares = total(squares, ("zlo", "zhi"))
-    behind = sum_from_behind(top, "zlo")
-    suffix = jnp.stack([(part + behind).astype(bf16) for part in suffix])
-    squares = total(jnp.broadcast_to(squares, (lax.axis_size(("y","x","core")), 8, 128)), ("y", "x", "core"))[0, 0]
-    entries = lax.axis_size(section) * width * kvw
-    rms = jnp.sqrt(squares / entries + 1e-12)
-    clipped = grad * jnp.minimum(1.0, clip_level / rms)
-    moment1_new = beta_first * moment1[0] + (1.0 - beta_first) * clipped
-    moment2_new = beta_second * moment2[0] + (1.0 - beta_second) * clipped * clipped
-    update = (
-        moment1_new / bias_first / (jnp.sqrt(moment2_new / bias_second) + adam_epsilon)
-        + decay_rate * master[0]
-    )
-    weights_new = (master[0] - learn_rate * update).astype(bf16)
+    near = ("y", "x", "core")
+    along = ("zlo", "zhi")
+    tile = (8, 128)
+    squares = local(
+        squares_kernel, [shape((lax.axis_size(near),) + tile, f32)], spots, grad, weight=heavy
+    )[0]
+    top, squares, fresh_normed = together(top, squares, fresh_normed)
+    behind = from_behind(top, "zlo")
+    squares = exchange(squares, near)
+    squares = local(relay_kernel, [shape((lax.axis_size(along),) + tile, f32)], spots, squares)[0]
+    squares = exchange(squares, along)
+    shard = shape((rows, kvw), f32)
+    moment1_new, moment2_new, weights_new = local(
+        functools.partial(adam_kernel, lax.axis_size(section) * width * kvw),
+        [shard, shard, shape((rows, kvw), bf16)],
+        spots,
+        squares,
+        grad,
+        master[0],
+        moment1[0],
+        moment2[0],
+    )
+    suffix = local(
+        functools.partial(suffix_kernel, layers_y, group),
+        [shape((layers_y * group, toks, cores * rows), bf16)],
+        spots,
+        *came,
+        *behind,
+    )[0]
     weights_new, suffix = together(weights_new, suffix)
     weights_new = lax.all_gather(weights_new, "zhi", axis=0, tiled=True)
-    strip = cores * rows
-    back = exchange(suffix.reshape(layers_y * group, toks, strip), ("y", "x"))
+    back = exchange(suffix, ("y", "x"))
 
     fresh = jnp.dot(fresh_normed[:, :half], weights_new, preferred_element_type=f32)
     fresh = fresh + jnp.dot(

time: 207 us -> 206 us (level); the launches traced: 205 us -> 202 us
  Pallas kernels: 12.3 us -> 18.7 us
  waiting for transfers between devices: 43 us -> 37.1 us
  other arithmetic: 6.58 us -> 1.72 us
  starting transfers between devices: 57.8 us -> 61.1 us
  matrix products: 1.69 us -> 3.76 us
    all_to_all x6, waiting for transfers between devices: 28.3 us -> 12.9 us  [exchange(): return lax.all_to_all(blocks, axis, 0, 0)]
    ppermute x3, waiting for transfers between devices: 0.01 us -> 13.9 us  [from_behind(): lax.ppermute(block, axis, [(i + k, i) for i in range(size - k)])]
    ppermute x3, waiting for transfers between devices: 11.7 us -> 0.78 us  [shift(): lax.ppermute(parts[k], axis, [(i, (i + k) % size) for i in range(size)])]
    pallas_call x7 -> x12, Pallas kernels: 12.3 us -> 18.7 us  [local(): pl.pallas_call(kernel, out_shape=out_shapes, in_specs=[pl.BlockSpec(memor...]
    reduce_scatter x1, waiting for transfers between devices: 1.89 us -> 6.59 us  [per_device(): grad = lax.psum_scatter(partial, 'zhi', scatter_dimension=0, tiled=True)]
  transfers between devices with their start and end apart: 16 -> 16, of which waited for: 7 -> 8; matrix products, arithmetic and copies ran while one was open for 3% -> 2% of each run, Pallas kernels for 4% -> 6%
where the time goes in v4:
time: 206 us; the launch traced here: 202 us
  blocking collectives  61.2 us (30%)
  starting transfers between devices  61.1 us (30%)
  waiting for transfers between devices  37.1 us (18%)
  Pallas kernels  18.7 us (9%)
  between operations  14.3 us (7%)
  local copies, waits for them, and re-layouts  4.21 us (2%)
  matrix products  3.76 us (2%)
    all_to_all x6, starting transfers between devices, exchange(): return lax.all_to_all(blocks, axis, 0, 0)  33.8 us
    all_gather x1, blocking collectives, per_device(): weights_old = lax.all_gather(weights_old, 'zhi', axis=0, tiled=True)  30.9 us
    all_gather x1, blocking collectives, per_device(): weights_new = lax.all_gather(weights_new, 'zhi', axis=0, tiled=True)  23.5 us
    pallas_call x12, Pallas kernels, local(): pl.pallas_call(kernel, out_shape=out_shapes, in_specs=[pl.BlockSpec(memor...  18.7 us
    ppermute x3, waiting for transfers between devices, from_behind(): lax.ppermute(block, axis, [(i + k, i) for i in range(size - k)])  13.9 us
    all_to_all x6, waiting for transfers between devices, exchange(): return lax.all_to_all(blocks, axis, 0, 0)  12.9 us
    ppermute x3, starting transfers between devices, swap_cores(): return lax.ppermute(block, 'core', [(0, 1), (1, 0)])  12.6 us
    ppermute x3, starting transfers between devices, shift(): lax.ppermute(parts[k], axis, [(i, (i + k) % size) for i in range(size)])  10.7 us
  transfers between devices with their start and end apart: 16, of which 8 were waited for; matrix products, arithmetic and copies ran while one was open for 2% of the time, Pallas kernels for 6%

profile of v4, /device:TPU:1, one launch (start us, length us, event | category | flops | bytes accessed | tf_op | source)
XLA Modules:
  0.0 202.1 jit_solution(14508802638076172147)
XLA Ops:
  7.2 0.8 reshape.40
  7.9 1.0 bitcast_convert_fusion
  8.9 0.1 concatenate.6.spots
  9.0 1.2 copy-done.2
  10.2 0.9 copy-done.5
  11.1 2.2 %shard_map.120 = bf16[4,128,1536]{2,1,0:T(8,128)(2,1)} custom-call(s32[68]{0:T(128)S(1)} %concatenate.6.spots, bf16[128,4096]{1,0:T(8,128)(2,1)S(1)} %bitcast.40, bf16[128,512]{1,0:T(8,128)(2,1)S(1)} %bitcast.43), custom_call_target="tpu_custom_call" | custom-call | tf_op jit(solution)/shard_map/pallas_call | solution.py:67
  13.4 5.0 %all-to-all-start = ((bf16[4,128,1536]{2,1,0:T(8,128)(2,1)}), bf16[4,128,1536]{2,1,0:T(8,128)(2,1)S(1)}, u32[]{:S(2)}, u32[]{:S(2)}) async-start(bf16[4,128,1536]{2,1,0:T(8,128)(2,1)} %shard_map.120), calls=%async_computation | async-start | bytes 3145728 | tf_op jit(solution)/shard_map/all_to_all | solution.py:31
  18.3 0.0 reduce-scatter.2.cloned.1.call-start
  18.3 0.0 copy-done.9
  18.4 0.1 copy.18.gain
  18.5 30.9 %all_gather.6.own = bf16[512,512]{1,0:T(8,128)(2,1)S(1)} all-gather(bf16[128,512]{1,0:T(8,128)(2,1)S(1)} %bitcast_convert_fusion), channel_id=1, replica_groups=mesh['zlo'=4,'y'=4,'zhi'=4,'x'=4,'core'=2] {'zhi'}, dimensions={0}, use_global_device_ids=true | all-gather | bytes 655360 | tf_op jit(solution)/shard_map/all_gather | solution.py:262
  49.4 0.0 all-to-all-done
  49.4 1.0 shard_map.121
  50.4 6.4 %collective-permute-start = (bf16[512,512]{1,0:T(8,128)(2,1)S(1)}, bf16[512,512]{1,0:T(8,128)(2,1)S(1)}, u32[]{:S(2)}, u32[]{:S(2)}) collective-permute-start(bf16[512,512]{1,0:T(8,128)(2,1)S(1)} %shard_map.121), channel_id=1, source_target_pairs={{0,1},{1,0},{2,3},{3,2},{4,5},{5,4},{6,7},{7,6},{8,9},{9,8},{10,11... | collective-permute-start | bytes 1572872 | tf_op jit(solution)/shard_map/ppermute | solution.py:47
  56.8 0.1 copy.19.gain
  57.0 1.4 collective-permute-done.came
  58.3 1.8 shard_map.122
  60.2 0.0 reduce-scatter.2.cloned.1.call-update
  60.2 2.3 %collective-permute-start.1 = (bf16[512,512]{1,0:T(8,128)(2,1)S(1)}, bf16[512,512]{1,0:T(8,128)(2,1)S(1)}, u32[]{:S(2)}, u32[]{:S(2)}) collective-permute-start(bf16[512,512]{1,0:T(8,128)(2,1)S(1)} %all_gather.6.own), channel_id=1, source_target_pairs={{0,1},{1,0},{2,3},{3,2},{4,5},{5,4},{6,7},{7,6},{8,9},{9,8},{10,11... | collective-permute-start | bytes 1572872 | tf_op jit(solution)/shard_map/ppermute | solution.py:47
  62.5 1.5 collective-permute-done.1.other
  64.0 1.5 shard_map.123
  65.5 6.8 %all_to_all.35.sums = f32[4,8,512]{2,1,0:T(8,128)S(1)} all-to-all(f32[4,8,512]{2,1,0:T(8,128)S(1)} %get-tuple-element.33), channel_id=1, replica_groups=mesh['zlo'=4,'y'=4,'zhi'=4,'x'=4,'core'=2] {'x'}, dimensions={0} | all-to-all | bytes 131072 | tf_op jit(solution)/shard_map/all_to_all | solution.py:31
  72.3 1.2 shard_map.124
  73.5 3.2 %collective-permute-start.2 = (bf16[512,256]{1,0:T(8,128)(2,1)S(1)}, bf16[512,256]{1,0:T(8,128)(2,1)S(1)}, u32[]{:S(2)}, u32[]{:S(2)}) collective-permute-start(bf16[512,256]{1,0:T(8,128)(2,1)S(1)} %get-tuple-element.35), channel_id=1, source_target_pairs={{0,32},{32,64},{64,96},{96,0},{1,33},{33,65},{65,97},{97,1},{2,34}... | collective-permute-start | bytes 786440 | tf_op jit(solution)/shard_map/ppermute | solution.py:42
  76.7 4.5 %collective-permute-start.3 = (bf16[512,256]{1,0:T(8,128)(2,1)S(1)}, bf16[512,256]{1,0:T(8,128)(2,1)S(1)}, u32[]{:S(2)}, u32[]{:S(2)}) collective-permute-start(bf16[512,256]{1,0:T(8,128)(2,1)S(1)} %get-tuple-element.36), channel_id=1, source_target_pairs={{0,64},{32,96},{64,0},{96,32},{1,65},{33,97},{65,1},{97,33},{2,66}... | collective-permute-start | bytes 786440 | tf_op jit(solution)/shard_map/ppermute | solution.py:42
  81.2 3.0 %collective-permute-start.4 = (bf16[512,256]{1,0:T(8,128)(2,1)S(1)}, bf16[512,256]{1,0:T(8,128)(2,1)S(1)}, u32[]{:S(2)}, u32[]{:S(2)}) collective-permute-start(bf16[512,256]{1,0:T(8,128)(2,1)S(1)} %get-tuple-element.37), channel_id=1, source_target_pairs={{0,96},{32,0},{64,32},{96,64},{1,97},{33,1},{65,33},{97,65},{2,98}... | collective-permute-start | bytes 786440 | tf_op jit(solution)/shard_map/ppermute | solution.py:42
  84.2 2.3 %shard_map.127 = bf16[4,128,1024]{2,1,0:T(8,128)(2,1)} custom-call(s32[68]{0:T(128)S(1)} %concatenate.6.spots, bf16[128,4096]{1,0:T(8,128)(2,1)S(1)} %bitcast.38, f32[1,4096]{1,0:T(1,128)S(1)} %copy-done.9, bf16[5,4096]{1,0:T(8,128)(2,1)S(1)} %copy-done.8), custom_call_target="tpu_custom_call" | custom-call | tf_op jit(solution)/shard_map/pallas_call | solution.py:67
  86.6 4.2 %all-to-all-start.2 = ((bf16[4,128,1024]{2,1,0:T(8,128)(2,1)}), bf16[4,128,1024]{2,1,0:T(8,128)(2,1)}, u32[]{:S(2)}, u32[]{:S(2)}) async-start(bf16[4,128,1024]{2,1,0:T(8,128)(2,1)} %shard_map.127), calls=%async_computation.3 | async-start | bytes 2097152 | tf_op jit(solution)/shard_map/all_to_all | solution.py:31
  90.8 0.0 collective-permute-done.2.refs_1_
  90.8 0.0 collective-permute-done.3.refs_2_
  90.8 0.8 collective-permute-done.4.refs_3_
  91.6 0.7 shard_map.125
  92.3 6.6 %reduce-scatter.2.cloned.1.call-done.grad = bf16[128,512]{1,0:T(8,128)(2,1)} async-done(((bf16[512,512]{1,0:T(8,128)(2,1)}), bf16[128,512]{1,0:T(8,128)(2,1)}) %reduce-scatter.2.cloned.1.call-update) | async-done | bytes 131088 | tf_op jit(solution)/shard_map/reduce_scatter | solution.py:281
  98.9 0.9 copy-done.6
  99.8 1.4 shard_map.126
  101.2 2.1 %all-to-all-done.2 = bf16[4,128,1024]{2,1,0:T(8,128)(2,1)} async-done(((bf16[4,128,1024]{2,1,0:T(8,128)(2,1)}), bf16[4,128,1024]{2,1,0:T(8,128)(2,1)}, u32[]{:S(2)}, u32[]{:S(2)}) %all-to-all-start.2) | async-done | bytes 1048608 | tf_op jit(solution)/shard_map/all_to_all | solution.py:31
  103.3 7.1 %all-to-all-start.3 = ((f32[32,8,128]{2,1,0:T(8,128)}), f32[32,8,128]{2,1,0:T(8,128)S(1)}, u32[]{:S(2)}, u32[]{:S(2)}) async-start(f32[32,8,128]{2,1,0:T(8,128)} %shard_map.126), calls=%async_computation.4 | async-start | bytes 262144 | tf_op jit(solution)/shard_map/all_to_all | solution.py:31
  110.5 0.0 copy-start.1
  110.5 0.0 copy-start.3
  110.5 0.0 copy-start.4
  110.5 1.4 collective-permute-start.7
  111.9 1.3 collective-permute-start.6
  113.2 1.3 collective-permute-start.5
  114.5 3.7 %all-to-all-done.3.sums = f32[32,8,128]{2,1,0:T(8,128)S(1)} async-done(((f32[32,8,128]{2,1,0:T(8,128)}), f32[32,8,128]{2,1,0:T(8,128)S(1)}, u32[]{:S(2)}, u32[]{:S(2)}) %all-to-all-start.3) | async-done | bytes 131104 | tf_op jit(solution)/shard_map/all_to_all | solution.py:31
  118.2 1.2 shard_map.128
  119.4 6.6 %all-to-all-start.4 = ((f32[16,8,128]{2,1,0:T(8,128)}), f32[16,8,128]{2,1,0:T(8,128)S(1)}, u32[]{:S(2)}, u32[]{:S(2)}) async-start(f32[16,8,128]{2,1,0:T(8,128)} %shard_map.128), calls=%async_computation.5 | async-start | bytes 131072 | tf_op jit(solution)/shard_map/all_to_all | solution.py:31
  126.0 0.0 collective-permute-done.7.refs_6_
  126.0 13.9 %collective-permute-done.6.refs_5_ = bf16[512,256]{1,0:T(8,128)(2,1)S(1)} collective-permute-done((bf16[512,256]{1,0:T(8,128)(2,1)S(1)}, bf16[512,256]{1,0:T(8,128)(2,1)S(1)}, u32[]{:S(2)}, u32[]{:S(2)}) %collective-permute-start.6) | collective-permute-done | bytes 262176 | tf_op jit(solution)/shard_map/ppermute | solution.py:53
  139.9 0.0 collective-permute-done.5.refs_4_
  139.9 2.2 %shard_map.130 = bf16[16,128,256]{2,1,0:T(8,128)(2,1)} custom-call(s32[68]{0:T(128)S(1)} %concatenate.6.spots, bf16[512,256]{1,0:T(8,128)(2,1)S(1)} %get-tuple-element.34.refs_0_, bf16[512,256]{1,0:T(8,128)(2,1)S(1)} %collective-permute-done.2.refs_1_, bf16[512,256]{1,0:T(8,128)(2,1)S(1)} %collective-permute-done.3.refs_2_, ...), custom_call_target="tpu_custom_call" | custom-call | tf_op jit(solution)/shard_map/pallas_call | solution.py:67
  142.1 0.0 all-to-all-done.4.sums
  142.1 0.0 copy-done.1
  142.1 1.5 shard_map.129
  143.6 6.8 %all-to-all-start.5 = ((bf16[16,128,256]{2,1,0:T(8,128)(2,1)}), bf16[16,128,256]{2,1,0:T(8,128)(2,1)S(1)}, u32[]{:S(2)}, u32[]{:S(2)}) async-start(bf16[16,128,256]{2,1,0:T(8,128)(2,1)} %shard_map.130), calls=%async_computation.6 | async-start | bytes 2097152 | tf_op jit(solution)/shard_map/all_to_all | solution.py:31
  150.4 23.5 %all_gather.7 = bf16[512,512]{1,0:T(8,128)(2,1)S(1)} all-gather(bf16[128,512]{1,0:T(8,128)(2,1)S(1)} %get-tuple-element.44), channel_id=1, replica_groups=mesh['zlo'=4,'y'=4,'zhi'=4,'x'=4,'core'=2] {'zhi'}, dimensions={0}, use_global_device_ids=true | all-gather | bytes 655360 | tf_op jit(solution)/shard_map/all_gather | solution.py:347
  173.8 3.9 %collective-permute-start.8 = (bf16[512,512]{1,0:T(8,128)(2,1)S(1)}, bf16[512,512]{1,0:T(8,128)(2,1)S(1)}, u32[]{:S(2)}, u32[]{:S(2)}) collective-permute-start(bf16[512,512]{1,0:T(8,128)(2,1)S(1)} %all_gather.7), channel_id=1, source_target_pairs={{0,1},{1,0},{2,3},{3,2},{4,5},{5,4},{6,7},{7,6},{8,9},{9,8},{10,11... | collective-permute-start | bytes 1572872 | tf_op jit(solution)/shard_map/ppermute | solution.py:47
  177.8 1.5 fusion.2
  179.2 0.0 collective-permute-done.8
  179.3 2.3 %fusion = bf16[512,512]{1,0:T(8,128)(2,1)} fusion(f32[512,512]{1,0:T(8,128)S(1)} %fusion.2, bf16[512,512]{1,0:T(8,128)(2,1)S(1)} %collective-permute-done.8, bf16[512,1024]{1,0:T(8,128)(2,1)} %bitcast.15), kind=kOutput, calls=%fused_computation.1 | convolution fusion | flops 268959744 | bytes 2621440 | tf_op jit(solution)/shard_map/dot_general | solution.py:351
  181.6 0.0 all-to-all-done.5.back
  181.6 4.0 %all-to-all-start.6 = ((bf16[4,128,512]{2,1,0:T(8,128)(2,1)}), bf16[4,128,512]{2,1,0:T(8,128)(2,1)S(1)}, u32[]{:S(2)}, u32[]{:S(2)}) async-start(bf16[4,128,512]{2,1,0:T(8,128)(2,1)} %bitcast.18), calls=%async_computation.7 | async-start | bytes 1048576 | tf_op jit(solution)/shard_map/all_to_all | solution.py:31
  185.6 1.8 shard_map.131
  187.4 7.1 %all-to-all-done.6 = bf16[4,128,512]{2,1,0:T(8,128)(2,1)S(1)} async-done(((bf16[4,128,512]{2,1,0:T(8,128)(2,1)}), bf16[4,128,512]{2,1,0:T(8,128)(2,1)S(1)}, u32[]{:S(2)}, u32[]{:S(2)}) %all-to-all-start.6) | async-done | bytes 524320 | tf_op jit(solution)/shard_map/all_to_all | solution.py:31
  194.5 0.7 reduce_sum.12
  (14 shorter events, 0.0 us)
Async XLA Ops:
  9.0 1.2 copy-start.2
  10.2 0.9 copy-start.5
  13.4 5.0 %copy-start.9 = (f32[1,4096]{1,0:T(1,128)S(1)}, f32[1,4096]{1,0:T(1,128)}, u32[]{:S(2)}) copy-start(f32[1,4096]{1,0:T(1,128)} %gain.1) | copy-start | bytes 49156
  13.4 36.0 %all-to-all-start = ((bf16[4,128,1536]{2,1,0:T(8,128)(2,1)}), bf16[4,128,1536]{2,1,0:T(8,128)(2,1)S(1)}, u32[]{:S(2)}, u32[]{:S(2)}) async-start(bf16[4,128,1536]{2,1,0:T(8,128)(2,1)} %shard_map.120), calls=%async_computation | async-start | bytes 3145728 | tf_op jit(solution)/shard_map/all_to_all | solution.py:31
  18.3 80.6 %reduce-scatter.2.cloned.1.call-start = ((), (), s32[]{:S(2)}) async-start(), calls=%async_computation.8 | async-start | bytes 655360 | tf_op jit(solution)/shard_map/reduce_scatter | solution.py:281
  50.4 8.0 %collective-permute-start = (bf16[512,512]{1,0:T(8,128)(2,1)S(1)}, bf16[512,512]{1,0:T(8,128)(2,1)S(1)}, u32[]{:S(2)}, u32[]{:S(2)}) collective-permute-start(bf16[512,512]{1,0:T(8,128)(2,1)S(1)} %shard_map.121), channel_id=1, source_target_pairs={{0,1},{1,0},{2,3},{3,2},{4,5},{5,4},{6,7},{7,6},{8,9},{9,8},{10,11... | collective-permute-start | bytes 1572872 | tf_op jit(solution)/shard_map/ppermute | solution.py:47
  60.2 3.8 %collective-permute-start.1 = (bf16[512,512]{1,0:T(8,128)(2,1)S(1)}, bf16[512,512]{1,0:T(8,128)(2,1)S(1)}, u32[]{:S(2)}, u32[]{:S(2)}) collective-permute-start(bf16[512,512]{1,0:T(8,128)(2,1)S(1)} %all_gather.6.own), channel_id=1, source_target_pairs={{0,1},{1,0},{2,3},{3,2},{4,5},{5,4},{6,7},{7,6},{8,9},{9,8},{10,11... | collective-permute-start | bytes 1572872 | tf_op jit(solution)/shard_map/ppermute | solution.py:47
  72.3 11.9 %copy-start = (bf16[2,1,64,4096]{3,2,1,0:T(8,128)(2,1)S(1)}, bf16[2,1,64,4096]{3,2,1,0:T(8,128)(2,1)}, u32[]{:S(2)}) copy-start(bf16[2,1,64,4096]{3,2,1,0:T(8,128)(2,1)} %param.15) | copy-start | bytes 3145732
  72.3 11.9 %copy-start.8 = (bf16[5,4096]{1,0:T(8,128)(2,1)S(1)}, bf16[5,4096]{1,0:T(8,128)(2,1)}, u32[]{:S(2)}) copy-start(bf16[5,4096]{1,0:T(8,128)(2,1)} %table.1) | copy-start | bytes 122884
  73.5 17.3 %collective-permute-start.2 = (bf16[512,256]{1,0:T(8,128)(2,1)S(1)}, bf16[512,256]{1,0:T(8,128)(2,1)S(1)}, u32[]{:S(2)}, u32[]{:S(2)}) collective-permute-start(bf16[512,256]{1,0:T(8,128)(2,1)S(1)} %get-tuple-element.35), channel_id=1, source_target_pairs={{0,32},{32,64},{64,96},{96,0},{1,33},{33,65},{65,97},{97,1},{2,34}... | collective-permute-start | bytes 786440 | tf_op jit(solution)/shard_map/ppermute | solution.py:42
  76.7 14.1 %collective-permute-start.3 = (bf16[512,256]{1,0:T(8,128)(2,1)S(1)}, bf16[512,256]{1,0:T(8,128)(2,1)S(1)}, u32[]{:S(2)}, u32[]{:S(2)}) collective-permute-start(bf16[512,256]{1,0:T(8,128)(2,1)S(1)} %get-tuple-element.36), channel_id=1, source_target_pairs={{0,64},{32,96},{64,0},{96,32},{1,65},{33,97},{65,1},{97,33},{2,66}... | collective-permute-start | bytes 786440 | tf_op jit(solution)/shard_map/ppermute | solution.py:42
  81.2 10.4 %collective-permute-start.4 = (bf16[512,256]{1,0:T(8,128)(2,1)S(1)}, bf16[512,256]{1,0:T(8,128)(2,1)S(1)}, u32[]{:S(2)}, u32[]{:S(2)}) collective-permute-start(bf16[512,256]{1,0:T(8,128)(2,1)S(1)} %get-tuple-element.37), channel_id=1, source_target_pairs={{0,96},{32,0},{64,32},{96,64},{1,97},{33,1},{65,33},{97,65},{2,98}... | collective-permute-start | bytes 786440 | tf_op jit(solution)/shard_map/ppermute | solution.py:42
  86.6 16.7 %all-to-all-start.2 = ((bf16[4,128,1024]{2,1,0:T(8,128)(2,1)}), bf16[4,128,1024]{2,1,0:T(8,128)(2,1)}, u32[]{:S(2)}, u32[]{:S(2)}) async-start(bf16[4,128,1024]{2,1,0:T(8,128)(2,1)} %shard_map.127), calls=%async_computation.3 | async-start | bytes 2097152 | tf_op jit(solution)/shard_map/all_to_all | solution.py:31
  98.9 0.9 copy-start.6
  103.3 14.9 %all-to-all-start.3 = ((f32[32,8,128]{2,1,0:T(8,128)}), f32[32,8,128]{2,1,0:T(8,128)S(1)}, u32[]{:S(2)}, u32[]{:S(2)}) async-start(f32[32,8,128]{2,1,0:T(8,128)} %shard_map.126), calls=%async_computation.4 | async-start | bytes 262144 | tf_op jit(solution)/shard_map/all_to_all | solution.py:31
  110.5 31.6 %copy-start.1 = (f32[1,128,512]{2,1,0:T(8,128)S(1)}, f32[1,128,512]{2,1,0:T(8,128)}, u32[]{:S(2)}) copy-start(f32[1,128,512]{2,1,0:T(8,128)} %param.12) | copy-start | bytes 786436
  110.5 31.6 %copy-start.3 = (f32[1,128,512]{2,1,0:T(8,128)S(1)}, f32[1,128,512]{2,1,0:T(8,128)}, u32[]{:S(2)}) copy-start(f32[1,128,512]{2,1,0:T(8,128)} %param.13) | copy-start | bytes 786436
  110.5 31.6 %copy-start.4 = (f32[1,128,512]{2,1,0:T(8,128)S(1)}, f32[1,128,512]{2,1,0:T(8,128)}, u32[]{:S(2)}) copy-start(f32[1,128,512]{2,1,0:T(8,128)} %param.14) | copy-start | bytes 786436
  110.5 31.6 %copy-start.7 = (bf16[128,512]{1,0:T(8,128)(2,1)S(1)}, bf16[128,512]{1,0:T(8,128)(2,1)}, u32[]{:S(2)}) copy-start(bf16[128,512]{1,0:T(8,128)(2,1)} %reduce-scatter.2.cloned.1.call-done.grad) | copy-start | bytes 393220
  110.5 15.5 %collective-permute-start.7 = (bf16[512,256]{1,0:T(8,128)(2,1)S(1)}, bf16[512,256]{1,0:T(8,128)(2,1)S(1)}, u32[]{:S(2)}, u32[]{:S(2)}) collective-permute-start(bf16[512,256]{1,0:T(8,128)(2,1)S(1)} %shard_map.125), channel_id=1, source_target_pairs={{128,0},{256,128},{384,256},{129,1},{257,129},{385,257},{130,2},{2... | collective-permute-start | bytes 786440 | tf_op jit(solution)/shard_map/ppermute | solution.py:53
  111.9 27.9 %collective-permute-start.6 = (bf16[512,256]{1,0:T(8,128)(2,1)S(1)}, bf16[512,256]{1,0:T(8,128)(2,1)S(1)}, u32[]{:S(2)}, u32[]{:S(2)}) collective-permute-start(bf16[512,256]{1,0:T(8,128)(2,1)S(1)} %shard_map.125), channel_id=1, source_target_pairs={{256,0},{384,128},{257,1},{385,129},{258,2},{386,130},{259,3},{387... | collective-permute-start | bytes 786440 | tf_op jit(solution)/shard_map/ppermute | solution.py:53
  113.2 26.6 %collective-permute-start.5 = (bf16[512,256]{1,0:T(8,128)(2,1)S(1)}, bf16[512,256]{1,0:T(8,128)(2,1)S(1)}, u32[]{:S(2)}, u32[]{:S(2)}) collective-permute-start(bf16[512,256]{1,0:T(8,128)(2,1)S(1)} %shard_map.125), channel_id=1, source_target_pairs={{384,0},{385,1},{386,2},{387,3},{388,4},{389,5},{390,6},{391,7},{3... | collective-permute-start | bytes 786440 | tf_op jit(solution)/shard_map/ppermute | solution.py:53
  119.4 22.7 %all-to-all-start.4 = ((f32[16,8,128]{2,1,0:T(8,128)}), f32[16,8,128]{2,1,0:T(8,128)S(1)}, u32[]{:S(2)}, u32[]{:S(2)}) async-start(f32[16,8,128]{2,1,0:T(8,128)} %shard_map.128), calls=%async_computation.5 | async-start | bytes 131072 | tf_op jit(solution)/shard_map/all_to_all | solution.py:31
  143.6 38.0 %all-to-all-start.5 = ((bf16[16,128,256]{2,1,0:T(8,128)(2,1)}), bf16[16,128,256]{2,1,0:T(8,128)(2,1)S(1)}, u32[]{:S(2)}, u32[]{:S(2)}) async-start(bf16[16,128,256]{2,1,0:T(8,128)(2,1)} %shard_map.130), calls=%async_computation.6 | async-start | bytes 2097152 | tf_op jit(solution)/shard_map/all_to_all | solution.py:31
  173.8 5.4 %collective-permute-start.8 = (bf16[512,512]{1,0:T(8,128)(2,1)S(1)}, bf16[512,512]{1,0:T(8,128)(2,1)S(1)}, u32[]{:S(2)}, u32[]{:S(2)}) collective-permute-start(bf16[512,512]{1,0:T(8,128)(2,1)S(1)} %all_gather.7), channel_id=1, source_target_pairs={{0,1},{1,0},{2,3},{3,2},{4,5},{5,4},{6,7},{7,6},{8,9},{9,8},{10,11... | collective-permute-start | bytes 1572872 | tf_op jit(solution)/shard_map/ppermute | solution.py:47
  181.6 12.9 %all-to-all-start.6 = ((bf16[4,128,512]{2,1,0:T(8,128)(2,1)}), bf16[4,128,512]{2,1,0:T(8,128)(2,1)S(1)}, u32[]{:S(2)}, u32[]{:S(2)}) async-start(bf16[4,128,512]{2,1,0:T(8,128)(2,1)} %bitcast.18), calls=%async_computation.7 | async-start | bytes 1048576 | tf_op jit(solution)/shard_map/all_to_all | solution.py:31
Sparse Core Ops, SparseCore 0:
  60.3 38.5 reduce-scatter.1

commit v5 on v4

--- a/solution.py
+++ b/solution.py
@@ -47,12 +47,9 @@
     return lax.ppermute(block, "core", [(0, 1), (1, 0)])
 
 
-def from_behind(block, axis):
+def from_behind(block, axis, distance):
     size = lax.axis_size(axis)
-    return [
-        lax.ppermute(block, axis, [(i + k, i) for i in range(size - k)])
-        for k in range(size - 1, 0, -1)
-    ]
+    return lax.ppermute(block, axis, [(i + distance, i) for i in range(size - distance)])
 
 
 def together(*values):
@@ -63,16 +60,21 @@
     return lax.rsqrt(jnp.mean(floats * floats, axis=-1, keepdims=True) + rms_epsilon)
 
 
-def local(kernel, out_shapes, spots, *arrays, weight=0):
+def local(kernel, out_shapes, spots, *arrays, weight=0, scratch=(), after=()):
+    def body(spots, *refs):
+        kernel(spots, *refs[: len(arrays)], *refs[len(arrays) + len(after) :])
+
     return pl.pallas_call(
-        kernel,
+        body,
         out_shape=out_shapes,
         in_specs=[pl.BlockSpec(memory_space=pltpu.SMEM)]
-        + [pl.BlockSpec(memory_space=pltpu.VMEM)] * len(arrays),
+        + [pl.BlockSpec(memory_space=pltpu.VMEM)] * len(arrays)
+        + [pl.BlockSpec(memory_space=pl.ANY)] * len(after),
         out_specs=[pl.BlockSpec(memory_space=pltpu.VMEM)] * len(out_shapes),
+        scratch_shapes=scratch,
         compiler_params=pltpu.CompilerParams(vmem_limit_bytes=48 * 1024 * 1024),
         cost_estimate=pl.CostEstimate(flops=weight, bytes_accessed=0, transcendentals=0),
-    )(spots, *arrays)
+    )(spots, *arrays, *after)
 
 
 def strip_at(start, rows):
@@ -129,61 +131,68 @@
         sums[x] = both.T[:8]
 
 
-def branch_kernel(sizes, spots, mine, mixed, sums, *outs):
+def branch_kernel(sizes, spots, mine, mixed, sums, out):
     far, rows, width = sizes
     half = far * rows
     both = jnp.concatenate([jnp.sum(sums[...], axis=0)] * 16, axis=0).T
     inv = lax.rsqrt(both[:, 0:1] / width + rms_epsilon)
     pull = inv * (inv * (both[:, 1:2] / width))
-    for k, out in enumerate(outs):
-        z = (spots[1] + k) & (far - 1)
-        for c in range(2):
-            cols = strip_at(c * half + z * rows, rows)
+    for z in range(far):
+        for c in range(mixed.shape[1] // half):
+            cols = slice(c * half + z * rows, c * half + (z + 1) * rows)
             block = mixed[:, cols] - mine[:, cols].astype(f32) * pull
-            out[:, c * rows : (c + 1) * rows] = block.astype(bf16)
-
-
-def fresh_kernel(sizes, ids_shape, spots, acts, gain, table, out):
+            out[z, :, c * rows : (c + 1) * rows] = block.astype(bf16)
+
+
+def fresh_kernel(sizes, ids_shape, spots, acts, gain, table, *refs):
+    *outs, normed = refs
     far, group, cores, rows = sizes
     micro, seqs = ids_shape
-    core = spots[0]
     half = far * rows
     floats = acts[...].astype(f32)
     toks = floats.shape[0]
     row = lax.broadcasted_iota(jnp.int32, (toks, 1), 0)
     for m in range(micro):
-        bin_id = spots[4 + m * seqs + spots[3]]
+        bin_id = spots[5 + m * seqs + spots[3]]
         embed = jnp.zeros((1, floats.shape[1]), f32)
         for b in range(table.shape[0]):
             embed = jnp.where(bin_id == b, table[b : b + 1, :].astype(f32), embed)
         first = jnp.logical_and(row == m * (toks // micro), spots[2] == 0)
         floats = jnp.where(first, embed, floats)
-    inverse = inverse_rms(floats)
-    normed = (floats * inverse * gain[...]).astype(bf16)
-    for x in range(group):
+    normed[...] = (floats * inverse_rms(floats) * gain[...]).astype(bf16)
+    for k, out in enumerate(outs):
+        x = (spots[4] + k) & (group - 1)
         for z in range(far):
-            start = (z * group + x) * cores * rows
             for c in range(cores):
-                place = ((core + c) & (cores - 1)) * half + z * rows
-                block = normed[:, start + c * rows : start + (c + 1) * rows]
-                out[x, :, strip_at(place, rows)] = block
-
-
-def top_kernel(spots, *refs):
-    *came, out = refs
-    out[...] = sum(part[...].astype(f32) for part in came).astype(bf16)
-
-
-def suffix_kernel(layers, group, spots, *refs):
+                start = ((z * group + x) * cores + ((spots[0] + c) & (cores - 1))) * rows
+                out[:, c * half + z * rows : c * half + (z + 1) * rows] = normed[
+                    :, strip_at(start, rows)
+                ]
+
+
+def values_kernel(half, spots, *refs):
+    *blocks, own, other, out = refs
+    group = len(blocks)
+    for k, block in enumerate(blocks):
+        part = jnp.dot(block[:, :half], own[...], preferred_element_type=f32)
+        part = part + jnp.dot(block[:, half:], other[...], preferred_element_type=f32)
+        out[(spots[4] - k) & (group - 1)] = part.astype(bf16)
+
+
+def top_kernel(spots, came, out):
+    out[...] = jnp.sum(came[...].astype(f32), axis=0).astype(bf16)
+
+
+def pair_kernel(spots, top, behind, out):
+    out[...] = (top[...].astype(f32) + behind[...].astype(f32)).astype(bf16)
+
+
+def suffix_kernel(group, spots, came, *refs):
     *parts, out = refs
-    came = [part[...].astype(f32) for part in parts[:layers]]
-    behind = sum(part[...].astype(f32) for part in parts[layers:])
+    block = sum(part[...].astype(f32) for part in parts)
     toks = out.shape[1]
-    for layer in range(layers):
-        block = behind
-        for k in range(layers):
-            here = ((spots[1] - k) & (layers - 1)) >= layer
-            block = block + jnp.where(here, came[k], 0.0)
+    for layer in reversed(range(came.shape[0])):
+        block = block + came[layer].astype(f32)
         for x in range(group):
             out[layer * group + x] = block[x * toks : (x + 1) * toks].astype(bf16)
 
@@ -234,7 +243,7 @@
     half = far * rows
     all_toks = group * toks
     core, spot_y, spot_x = (lax.axis_index(name) for name in ("core", "y", "x"))
-    spots = jnp.stack([core, spot_y, lax.axis_index(section), lax.axis_index(dp)])
+    spots = jnp.stack([core, spot_y, lax.axis_index(section), lax.axis_index(dp), spot_x])
     spots = jnp.concatenate([spots, reward_ids.reshape(-1)])
     shape = jax.ShapeDtypeStruct
     gain = norm_gain[0]
@@ -277,7 +286,6 @@
         own_gain[:half, None],
         swap_cores(other),
     )[0]
-    partial, weights_old = together(partial, weights_old)
     grad = lax.psum_scatter(partial, "zhi", scatter_dimension=0, tiled=True)
     weights_other = swap_cores(weights_old)
 
@@ -289,41 +297,45 @@
         weights_old,
         weights_other,
         own_gain[None],
+        after=[partial],
     )
     sums = exchange(sums, "x")
     parts = local(
         functools.partial(branch_kernel, (far, rows, width)),
-        [shape((all_toks, cores * rows), bf16)] * layers_y,
+        [shape((layers_y, all_toks, cores * rows), bf16)],
         spots,
         mine,
         mixed,
         sums,
-    )
-    came = shift(parts, "y")
-    top_shape = shape((all_toks, cores * rows), bf16)
-    top = local(top_kernel, [top_shape], spots, *came)[0]
-
+    )[0]
     next_flat, parts = together(next_acts[:, 0].reshape(toks, width), parts)
-    fresh_normed = local(
+    came = exchange(parts, "y")
+
+    fresh_blocks = local(
         functools.partial(fresh_kernel, (far, group, cores, rows), reward_ids.shape),
-        [shape((group, toks, cores * half), bf16)],
+        [shape((toks, cores * half), bf16)] * group,
         spots,
         next_flat,
         norm_gain,
         reward_table,
-    )[0]
-    fresh_normed = exchange(fresh_normed, "x").reshape(all_toks, cores * half)
+        scratch=[pltpu.VMEM((toks, width), bf16)],
+    )
+    fresh_normed = shift(fresh_blocks, "x")
+
+    top_shape = shape((all_toks, cores * rows), bf16)
+    top = local(top_kernel, [top_shape], spots, came, after=fresh_normed[1:3])[0]
+    behind = [from_behind(top, "zlo", 1)]
+    pair = local(pair_kernel, [top_shape], spots, top, behind[0])[0]
+    behind.append(from_behind(pair, "zlo", 2))
 
     near = ("y", "x", "core")
     along = ("zlo", "zhi")
     tile = (8, 128)
     squares = local(
-        squares_kernel, [shape((lax.axis_size(near),) + tile, f32)], spots, grad, weight=heavy
-    )[0]
-    top, squares, fresh_normed = together(top, squares, fresh_normed)
-    behind = from_behind(top, "zlo")
+        squares_kernel, [shape((lax.axis_size(near),) + tile, f32)], spots, grad, after=[top]
+    )[0]
     squares = exchange(squares, near)
-    squares = local(relay_kernel, [shape((lax.axis_size(along),) + tile, f32)], spots, squares)[0]
+    squares = local(relay_kernel, [shape((lax.axis_size(along),) + tile, f32)], spots, squares, after=fresh_normed)[0]
     squares = exchange(squares, along)
     shard = shape((rows, kvw), f32)
     moment1_new, moment2_new, weights_new = local(
@@ -337,21 +349,25 @@
         moment2[0],
     )
     suffix = local(
-        functools.partial(suffix_kernel, layers_y, group),
+        functools.partial(suffix_kernel, group),
         [shape((layers_y * group, toks, cores * rows), bf16)],
         spots,
-        *came,
+        came,
         *behind,
     )[0]
     weights_new, suffix = together(weights_new, suffix)
     weights_new = lax.all_gather(weights_new, "zhi", axis=0, tiled=True)
     back = exchange(suffix, ("y", "x"))
 
-    fresh = jnp.dot(fresh_normed[:, :half], weights_new, preferred_element_type=f32)
-    fresh = fresh + jnp.dot(
-        fresh_normed[:, half:], swap_cores(weights_new), preferred_element_type=f32
-    )
-    fresh, back = together(fresh.astype(bf16).reshape(group, toks, kvw), back)
+    fresh = local(
+        functools.partial(values_kernel, half),
+        [shape((group, toks, kvw), bf16)],
+        spots,
+        *fresh_normed,
+        weights_new,
+        swap_cores(weights_new),
+    )[0]
+    fresh, back = together(fresh, back)
     fresh = jnp.sum(exchange(fresh, "x").astype(f32), axis=0).astype(bf16)
     fresh_values = fresh.reshape(micro, 1, tok_dev, kvw)
 

time: 206 us -> 197 us (0.956)
  starting transfers between devices: 61.1 us -> 56.3 us
  Pallas kernels: 18.7 us -> 22.7 us
  matrix products: 3.76 us -> 0 us
    ppermute x3 -> x2, waiting for transfers between devices: 13.9 us -> 2.29 us  [from_behind(): lax.ppermute(block, axis, [(i + distance, i) for i in range(size - distan...]
    ppermute x3, waiting for transfers between devices: 0.78 us -> 8.13 us  [shift(): lax.ppermute(parts[k], axis, [(i, (i + k) % size) for i in range(size)])]
    all_to_all x6, waiting for transfers between devices: 12.9 us -> 19.5 us  [exchange(): return lax.all_to_all(blocks, axis, 0, 0)]
    pallas_call x12 -> x14, Pallas kernels: 18.7 us -> 22.7 us  [local(): pl.pallas_call(body, out_shape=out_shapes, in_specs=[pl.BlockSpec(memory_...]
    dot_general x2 -> x0, matrix products: 3.76 us -> none  [the longest x1 2.29 us: per_device(): jnp.dot(fresh_normed[:, half:], swap_cores(weights_new), preferred_elemen...]
    ppermute x3, starting transfers between devices: 10.7 us -> 7.8 us  [shift(): lax.ppermute(parts[k], axis, [(i, (i + k) % size) for i in range(size)])]
  transfers between devices with their start and end apart: 16 -> 15, of which waited for: 8 -> 8; matrix products, arithmetic and copies ran while one was open for 2% -> 0% of each run, Pallas kernels for 6% -> 9%
where the time goes in v5:
time: 197 us; the launch traced here: 195 us
  blocking collectives  59.5 us (30%)
  starting transfers between devices  56.3 us (29%)
  waiting for transfers between devices  36.1 us (18%)
  Pallas kernels  22.7 us (12%)
  between operations  14.3 us (7%)
  local copies, waits for them, and re-layouts  4.2 us (2%)
    all_to_all x6, starting transfers between devices, exchange(): return lax.all_to_all(blocks, axis, 0, 0)  34.7 us
    all_gather x1, blocking collectives, per_device(): weights_old = lax.all_gather(weights_old, 'zhi', axis=0, tiled=True)  30.9 us
    pallas_call x14, Pallas kernels, local(): pl.pallas_call(body, out_shape=out_shapes, in_specs=[pl.BlockSpec(memory_...  22.7 us
    all_gather x1, blocking collectives, per_device(): weights_new = lax.all_gather(weights_new, 'zhi', axis=0, tiled=True)  21.8 us
    all_to_all x6, waiting for transfers between devices, exchange(): return lax.all_to_all(blocks, axis, 0, 0)  19.5 us
    ppermute x3, starting transfers between devices, swap_cores(): return lax.ppermute(block, 'core', [(0, 1), (1, 0)])  11.2 us
    ppermute x3, waiting for transfers between devices, shift(): lax.ppermute(parts[k], axis, [(i, (i + k) % size) for i in range(size)])  8.13 us
    ppermute x3, starting transfers between devices, shift(): lax.ppermute(parts[k], axis, [(i, (i + k) % size) for i in range(size)])  7.8 us
  transfers between devices with their start and end apart: 15, of which 8 were waited for; matrix products, arithmetic and copies ran while one was open for 0% of the time, Pallas kernels for 9%

profile of v5, /device:TPU:1, one launch (start us, length us, event | category | flops | bytes accessed | tf_op | source)
XLA Modules:
  0.0 194.8 jit_solution(1830942815835027500)
XLA Ops:
  7.2 0.8 reshape.34
  7.9 1.0 bitcast_convert_fusion
  8.9 0.1 concatenate.6.spots
  9.0 1.2 copy-done.1
  10.2 0.9 copy-done.7
  11.1 2.2 %shard_map.120 = bf16[4,128,1536]{2,1,0:T(8,128)(2,1)} custom-call(s32[69]{0:T(128)S(1)} %concatenate.6.spots, bf16[128,4096]{1,0:T(8,128)(2,1)S(1)} %bitcast.36, bf16[128,512]{1,0:T(8,128)(2,1)S(1)} %bitcast.40), custom_call_target="tpu_custom_call" | custom-call | tf_op jit(solution)/shard_map/pallas_call | solution.py:67
  13.4 5.0 %all-to-all-start = ((bf16[4,128,1536]{2,1,0:T(8,128)(2,1)}), bf16[4,128,1536]{2,1,0:T(8,128)(2,1)S(1)}, u32[]{:S(2)}, u32[]{:S(2)}) async-start(bf16[4,128,1536]{2,1,0:T(8,128)(2,1)} %shard_map.120), calls=%async_computation | async-start | bytes 3145728 | tf_op jit(solution)/shard_map/all_to_all | solution.py:31
  18.3 0.0 reduce-scatter.2.cloned.1.call-start
  18.3 0.0 copy-done.9
  18.4 0.1 copy.18.refs_1_
  18.5 30.9 %all_gather.6.refs_1_ = bf16[512,512]{1,0:T(8,128)(2,1)S(1)} all-gather(bf16[128,512]{1,0:T(8,128)(2,1)S(1)} %bitcast_convert_fusion), channel_id=1, replica_groups=mesh['zlo'=4,'y'=4,'zhi'=4,'x'=4,'core'=2] {'zhi'}, dimensions={0}, use_global_device_ids=true | all-gather | bytes 655360 | tf_op jit(solution)/shard_map/all_gather | solution.py:271
  49.4 0.0 all-to-all-done
  49.4 1.0 shard_map.121
  50.4 6.4 %collective-permute-start.1 = (bf16[512,512]{1,0:T(8,128)(2,1)S(1)}, bf16[512,512]{1,0:T(8,128)(2,1)}, u32[]{:S(2)}, u32[]{:S(2)}) collective-permute-start(bf16[512,512]{1,0:T(8,128)(2,1)S(1)} %shard_map.121), channel_id=1, source_target_pairs={{0,1},{1,0},{2,3},{3,2},{4,5},{5,4},{6,7},{7,6},{8,9},{9,8},{10,11... | collective-permute-start | bytes 1572872 | tf_op jit(solution)/shard_map/ppermute | solution.py:47
  56.8 1.9 collective-permute-start
  58.8 0.1 copy.19.refs_1_
  58.9 0.0 collective-permute-done.1.refs_2_
  58.9 2.3 %shard_map.122.refs_4_ = bf16[512,512]{1,0:T(8,128)(2,1)} custom-call(s32[69]{0:T(128)S(1)} %concatenate.6.spots, bf16[512,1536]{1,0:T(8,128)(2,1)S(1)} %bitcast.32, f32[512,1]{1,0:T(8,128)S(1)} %copy.19.refs_1_, bf16[512,512]{1,0:T(8,128)(2,1)} %collective-permute-done.1.refs_2_), custom_call_target="tpu_custom_call" | custom-call | tf_op jit(solution)/shard_map/pallas_call | solution.py:67
  61.3 0.0 reduce-scatter.2.cloned.1.call-update
  61.3 0.0 collective-permute-done.refs_2_
  61.3 1.5 shard_map.123
  62.8 6.8 %all_to_all.35.refs_2_ = f32[4,8,512]{2,1,0:T(8,128)S(1)} all-to-all(f32[4,8,512]{2,1,0:T(8,128)S(1)} %get-tuple-element.28), channel_id=1, replica_groups=mesh['zlo'=4,'y'=4,'zhi'=4,'x'=4,'core'=2] {'x'}, dimensions={0} | all-to-all | bytes 131072 | tf_op jit(solution)/shard_map/all_to_all | solution.py:31
  69.6 2.0 %shard_map.124 = bf16[4,512,256]{2,1,0:T(8,128)(2,1)} custom-call(s32[69]{0:T(128)S(1)} %concatenate.6.spots, bf16[512,1536]{1,0:T(8,128)(2,1)S(1)} %bitcast.34, f32[512,1024]{1,0:T(8,128)S(1)} %get-tuple-element.27.refs_1_, f32[4,8,512]{2,1,0:T(8,128)S(1)} %all_to_all.35.refs_2_), custom_call_target="tpu_custom_call" | custom-call | tf_op jit(solution)/shard_map/pallas_call | solution.py:67
  71.6 4.3 %all-to-all-start.2 = ((bf16[4,512,256]{2,1,0:T(8,128)(2,1)}), bf16[4,512,256]{2,1,0:T(8,128)(2,1)S(1)}, u32[]{:S(2)}, u32[]{:S(2)}) async-start(bf16[4,512,256]{2,1,0:T(8,128)(2,1)} %shard_map.124), calls=%async_computation.3 | async-start | bytes 2097152 | tf_op jit(solution)/shard_map/all_to_all | solution.py:31
  76.0 0.0 copy-done.2
  76.0 0.0 copy-done.8
  76.0 1.6 shard_map.125
  77.5 2.2 %collective-permute-start.2 = (bf16[128,1024]{1,0:T(8,128)(2,1)S(1)}, bf16[128,1024]{1,0:T(8,128)(2,1)S(1)}, u32[]{:S(2)}, u32[]{:S(2)}) collective-permute-start(bf16[128,1024]{1,0:T(8,128)(2,1)S(1)} %get-tuple-element.31), channel_id=1, source_target_pairs={{0,2},{2,4},{4,6},{6,0},{1,3},{3,5},{5,7},{7,1},{8,10},{10,12},{12... | collective-permute-start | bytes 786440 | tf_op jit(solution)/shard_map/ppermute | solution.py:42
  79.7 3.7 %collective-permute-start.3 = (bf16[128,1024]{1,0:T(8,128)(2,1)S(1)}, bf16[128,1024]{1,0:T(8,128)(2,1)S(1)}, u32[]{:S(2)}, u32[]{:S(2)}) collective-permute-start(bf16[128,1024]{1,0:T(8,128)(2,1)S(1)} %get-tuple-element.32), channel_id=1, source_target_pairs={{0,4},{2,6},{4,0},{6,2},{1,5},{3,7},{5,1},{7,3},{8,12},{10,14},{12... | collective-permute-start | bytes 786440 | tf_op jit(solution)/shard_map/ppermute | solution.py:42
  83.4 3.7 %collective-permute-done.2.refs_1_.refs_2_ = bf16[128,1024]{1,0:T(8,128)(2,1)S(1)} collective-permute-done((bf16[128,1024]{1,0:T(8,128)(2,1)S(1)}, bf16[128,1024]{1,0:T(8,128)(2,1)S(1)}, u32[]{:S(2)}, u32[]{:S(2)}) %collective-permute-start.2) | collective-permute-done | bytes 262176 | tf_op jit(solution)/shard_map/ppermute | solution.py:42
  87.2 4.4 %collective-permute-done.3.refs_2_.refs_3_ = bf16[128,1024]{1,0:T(8,128)(2,1)S(1)} collective-permute-done((bf16[128,1024]{1,0:T(8,128)(2,1)S(1)}, bf16[128,1024]{1,0:T(8,128)(2,1)S(1)}, u32[]{:S(2)}, u32[]{:S(2)}) %collective-permute-start.3) | collective-permute-done | bytes 262176 | tf_op jit(solution)/shard_map/ppermute | solution.py:42
  91.6 0.0 all-to-all-done.2.refs_0_
  91.6 0.7 shard_map.126.refs_1_.refs_0_
  92.3 1.3 collective-permute-start.5
  93.6 1.9 collective-permute-start.4
  95.5 4.6 %reduce-scatter.2.cloned.1.call-done.refs_0_.refs_1_ = bf16[128,512]{1,0:T(8,128)(2,1)} async-done(((bf16[512,512]{1,0:T(8,128)(2,1)}), bf16[128,512]{1,0:T(8,128)(2,1)}) %reduce-scatter.2.cloned.1.call-update) | async-done | bytes 131088 | tf_op jit(solution)/shard_map/reduce_scatter | solution.py:289
  100.1 0.9 copy-done.3
  101.0 1.4 shard_map.127
  102.4 8.2 %all-to-all-start.3 = ((f32[32,8,128]{2,1,0:T(8,128)}), f32[32,8,128]{2,1,0:T(8,128)S(1)}, u32[]{:S(2)}, u32[]{:S(2)}) async-start(f32[32,8,128]{2,1,0:T(8,128)} %shard_map.127), calls=%async_computation.4 | async-start | bytes 262144 | tf_op jit(solution)/shard_map/all_to_all | solution.py:31
  110.6 0.0 collective-permute-done.5.refs_1_
  110.6 1.3 shard_map.130
  111.9 1.3 collective-permute-start.6
  113.2 0.0 collective-permute-done.4.refs_4_.refs_3_
  113.2 5.0 %all-to-all-done.3.refs_0_ = f32[32,8,128]{2,1,0:T(8,128)S(1)} async-done(((f32[32,8,128]{2,1,0:T(8,128)}), f32[32,8,128]{2,1,0:T(8,128)S(1)}, u32[]{:S(2)}, u32[]{:S(2)}) %all-to-all-start.3) | async-done | bytes 131104 | tf_op jit(solution)/shard_map/all_to_all | solution.py:31
  118.2 1.2 shard_map.128
  119.4 7.1 %all-to-all-start.4 = ((f32[16,8,128]{2,1,0:T(8,128)}), f32[16,8,128]{2,1,0:T(8,128)S(1)}, u32[]{:S(2)}, u32[]{:S(2)}) async-start(f32[16,8,128]{2,1,0:T(8,128)} %shard_map.128), calls=%async_computation.5 | async-start | bytes 131072 | tf_op jit(solution)/shard_map/all_to_all | solution.py:31
  126.5 2.3 %collective-permute-done.6.refs_2_ = bf16[512,256]{1,0:T(8,128)(2,1)} collective-permute-done((bf16[512,256]{1,0:T(8,128)(2,1)}, bf16[512,256]{1,0:T(8,128)(2,1)}, u32[]{:S(2)}, u32[]{:S(2)}) %collective-permute-start.6) | collective-permute-done | bytes 262176 | tf_op jit(solution)/shard_map/ppermute | solution.py:52
  128.8 2.2 %shard_map.131 = bf16[16,128,256]{2,1,0:T(8,128)(2,1)} custom-call(s32[69]{0:T(128)S(1)} %concatenate.6.spots, bf16[4,512,256]{2,1,0:T(8,128)(2,1)S(1)} %all-to-all-done.2.refs_0_, bf16[512,256]{1,0:T(8,128)(2,1)S(1)} %collective-permute-done.5.refs_1_, bf16[512,256]{1,0:T(8,128)(2,1)} %collective-permute-done.6.refs_2_), custom_call_target="tpu_custom_call" | custom-call | tf_op jit(solution)/shard_map/pallas_call | solution.py:67
  130.9 7.3 %all-to-all-done.4.refs_0_ = f32[16,8,128]{2,1,0:T(8,128)S(1)} async-done(((f32[16,8,128]{2,1,0:T(8,128)}), f32[16,8,128]{2,1,0:T(8,128)S(1)}, u32[]{:S(2)}, u32[]{:S(2)}) %all-to-all-start.4) | async-done | bytes 65568 | tf_op jit(solution)/shard_map/all_to_all | solution.py:31
  138.3 0.0 copy-done
  138.3 0.0 copy-done.4
  138.3 0.0 copy-done.5
  138.3 0.0 copy-done.6
  138.3 1.5 shard_map.129
  139.7 3.7 %all-to-all-start.5 = ((bf16[16,128,256]{2,1,0:T(8,128)(2,1)}), bf16[16,128,256]{2,1,0:T(8,128)(2,1)S(1)}, u32[]{:S(2)}, u32[]{:S(2)}) async-start(bf16[16,128,256]{2,1,0:T(8,128)(2,1)} %shard_map.131), calls=%async_computation.6 | async-start | bytes 2097152 | tf_op jit(solution)/shard_map/all_to_all | solution.py:31
  143.4 21.8 %all_gather.7.refs_4_ = bf16[512,512]{1,0:T(8,128)(2,1)S(1)} all-gather(bf16[128,512]{1,0:T(8,128)(2,1)S(1)} %get-tuple-element.36), channel_id=1, replica_groups=mesh['zlo'=4,'y'=4,'zhi'=4,'x'=4,'core'=2] {'zhi'}, dimensions={0}, use_global_device_ids=true | all-gather | bytes 655360 | tf_op jit(solution)/shard_map/all_gather | solution.py:359
  165.2 2.8 %collective-permute-start.7 = (bf16[512,512]{1,0:T(8,128)(2,1)S(1)}, bf16[512,512]{1,0:T(8,128)(2,1)S(1)}, u32[]{:S(2)}, u32[]{:S(2)}) collective-permute-start(bf16[512,512]{1,0:T(8,128)(2,1)S(1)} %all_gather.7.refs_4_), channel_id=1, source_target_pairs={{0,1},{1,0},{2,3},{3,2},{4,5},{5,4},{6,7},{7,6},{8,9},{9,8},{10,11... | collective-permute-start | bytes 1572872 | tf_op jit(solution)/shard_map/ppermute | solution.py:47
  168.1 1.5 collective-permute-done.7.refs_5_
  169.6 2.1 %shard_map.132 = bf16[4,128,512]{2,1,0:T(8,128)(2,1)} custom-call(s32[69]{0:T(128)S(1)} %concatenate.6.spots, bf16[128,1024]{1,0:T(8,128)(2,1)S(1)} %get-tuple-element.30.refs_1_.refs_0_, bf16[128,1024]{1,0:T(8,128)(2,1)S(1)} %collective-permute-done.2.refs_1_.refs_2_, bf16[128,1024]{1,0:T(8,128)(2,1)S(1)} %collective-permute-done.3.refs_2_.refs_3_, ...), custom_call_target="tpu_custom_call" | custom-call | tf_op jit(solution)/shard_map/pallas_call | solution.py:67
  171.7 0.0 all-to-all-done.5.refs_0_
  171.7 6.5 %all-to-all-start.6 = ((bf16[4,128,512]{2,1,0:T(8,128)(2,1)}), bf16[4,128,512]{2,1,0:T(8,128)(2,1)S(1)}, u32[]{:S(2)}, u32[]{:S(2)}) async-start(bf16[4,128,512]{2,1,0:T(8,128)(2,1)} %shard_map.132), calls=%async_computation.7 | async-start | bytes 1048576 | tf_op jit(solution)/shard_map/all_to_all | solution.py:31
  178.3 1.8 shard_map.133
  180.1 7.1 %all-to-all-done.6 = bf16[4,128,512]{2,1,0:T(8,128)(2,1)S(1)} async-done(((bf16[4,128,512]{2,1,0:T(8,128)(2,1)}), bf16[4,128,512]{2,1,0:T(8,128)(2,1)S(1)}, u32[]{:S(2)}, u32[]{:S(2)}) %all-to-all-start.6) | async-done | bytes 524320 | tf_op jit(solution)/shard_map/all_to_all | solution.py:31
  187.2 0.7 reduce_sum.12
  (12 shorter events, 0.0 us)
Async XLA Ops:
  9.0 1.2 copy-start.1
  10.2 0.9 copy-start.7
  13.4 5.0 %copy-start.9 = (f32[1,4096]{1,0:T(1,128)S(1)}, f32[1,4096]{1,0:T(1,128)}, u32[]{:S(2)}) copy-start(f32[1,4096]{1,0:T(1,128)} %refs_1_.1) | copy-start | bytes 49156
  13.4 36.0 %all-to-all-start = ((bf16[4,128,1536]{2,1,0:T(8,128)(2,1)}), bf16[4,128,1536]{2,1,0:T(8,128)(2,1)S(1)}, u32[]{:S(2)}, u32[]{:S(2)}) async-start(bf16[4,128,1536]{2,1,0:T(8,128)(2,1)} %shard_map.120), calls=%async_computation | async-start | bytes 3145728 | tf_op jit(solution)/shard_map/all_to_all | solution.py:31
  18.3 81.8 %reduce-scatter.2.cloned.1.call-start = ((), (), s32[]{:S(2)}) async-start(), calls=%async_computation.8 | async-start | bytes 655360 | tf_op jit(solution)/shard_map/reduce_scatter | solution.py:289
  50.4 8.5 %collective-permute-start.1 = (bf16[512,512]{1,0:T(8,128)(2,1)S(1)}, bf16[512,512]{1,0:T(8,128)(2,1)}, u32[]{:S(2)}, u32[]{:S(2)}) collective-permute-start(bf16[512,512]{1,0:T(8,128)(2,1)S(1)} %shard_map.121), channel_id=1, source_target_pairs={{0,1},{1,0},{2,3},{3,2},{4,5},{5,4},{6,7},{7,6},{8,9},{9,8},{10,11... | collective-permute-start | bytes 1572872 | tf_op jit(solution)/shard_map/ppermute | solution.py:47
  56.8 4.5 %collective-permute-start = (bf16[512,512]{1,0:T(8,128)(2,1)S(1)}, bf16[512,512]{1,0:T(8,128)(2,1)S(1)}, u32[]{:S(2)}, u32[]{:S(2)}) collective-permute-start(bf16[512,512]{1,0:T(8,128)(2,1)S(1)} %all_gather.6.refs_1_), channel_id=1, source_target_pairs={{0,1},{1,0},{2,3},{3,2},{4,5},{5,4},{6,7},{7,6},{8,9},{9,8},{10,11... | collective-permute-start | bytes 1572872 | tf_op jit(solution)/shard_map/ppermute | solution.py:47
  71.6 4.3 %copy-start.2 = (bf16[2,1,64,4096]{3,2,1,0:T(8,128)(2,1)S(1)}, bf16[2,1,64,4096]{3,2,1,0:T(8,128)(2,1)}, u32[]{:S(2)}) copy-start(bf16[2,1,64,4096]{3,2,1,0:T(8,128)(2,1)} %param.15) | copy-start | bytes 3145732
  71.6 4.3 %copy-start.8 = (bf16[5,4096]{1,0:T(8,128)(2,1)S(1)}, bf16[5,4096]{1,0:T(8,128)(2,1)}, u32[]{:S(2)}) copy-start(bf16[5,4096]{1,0:T(8,128)(2,1)} %refs_2_.1) | copy-start | bytes 122884
  71.6 19.9 %all-to-all-start.2 = ((bf16[4,512,256]{2,1,0:T(8,128)(2,1)}), bf16[4,512,256]{2,1,0:T(8,128)(2,1)S(1)}, u32[]{:S(2)}, u32[]{:S(2)}) async-start(bf16[4,512,256]{2,1,0:T(8,128)(2,1)} %shard_map.124), calls=%async_computation.3 | async-start | bytes 2097152 | tf_op jit(solution)/shard_map/all_to_all | solution.py:31
  77.5 9.6 %collective-permute-start.2 = (bf16[128,1024]{1,0:T(8,128)(2,1)S(1)}, bf16[128,1024]{1,0:T(8,128)(2,1)S(1)}, u32[]{:S(2)}, u32[]{:S(2)}) collective-permute-start(bf16[128,1024]{1,0:T(8,128)(2,1)S(1)} %get-tuple-element.31), channel_id=1, source_target_pairs={{0,2},{2,4},{4,6},{6,0},{1,3},{3,5},{5,7},{7,1},{8,10},{10,12},{12... | collective-permute-start | bytes 786440 | tf_op jit(solution)/shard_map/ppermute | solution.py:42
  79.7 11.8 %collective-permute-start.3 = (bf16[128,1024]{1,0:T(8,128)(2,1)S(1)}, bf16[128,1024]{1,0:T(8,128)(2,1)S(1)}, u32[]{:S(2)}, u32[]{:S(2)}) collective-permute-start(bf16[128,1024]{1,0:T(8,128)(2,1)S(1)} %get-tuple-element.32), channel_id=1, source_target_pairs={{0,4},{2,6},{4,0},{6,2},{1,5},{3,7},{5,1},{7,3},{8,12},{10,14},{12... | collective-permute-start | bytes 786440 | tf_op jit(solution)/shard_map/ppermute | solution.py:42
  92.3 18.3 %collective-permute-start.5 = (bf16[512,256]{1,0:T(8,128)(2,1)S(1)}, bf16[512,256]{1,0:T(8,128)(2,1)S(1)}, u32[]{:S(2)}, u32[]{:S(2)}) collective-permute-start(bf16[512,256]{1,0:T(8,128)(2,1)S(1)} %shard_map.126.refs_1_.refs_0_), channel_id=1, source_target_pairs={{128,0},{256,128},{384,256},{129,1},{257,129},{385,257},{130,2},{2... | collective-permute-start | bytes 786440 | tf_op jit(solution)/shard_map/ppermute | solution.py:52
  93.6 19.6 %collective-permute-start.4 = (bf16[128,1024]{1,0:T(8,128)(2,1)S(1)}, bf16[128,1024]{1,0:T(8,128)(2,1)S(1)}, u32[]{:S(2)}, u32[]{:S(2)}) collective-permute-start(bf16[128,1024]{1,0:T(8,128)(2,1)S(1)} %get-tuple-element.33), channel_id=1, source_target_pairs={{0,6},{2,0},{4,2},{6,4},{1,7},{3,1},{5,3},{7,5},{8,14},{10,8},{12,... | collective-permute-start | bytes 786440 | tf_op jit(solution)/shard_map/ppermute | solution.py:42
  100.1 0.9 copy-start.3
  102.4 15.8 %all-to-all-start.3 = ((f32[32,8,128]{2,1,0:T(8,128)}), f32[32,8,128]{2,1,0:T(8,128)S(1)}, u32[]{:S(2)}, u32[]{:S(2)}) async-start(f32[32,8,128]{2,1,0:T(8,128)} %shard_map.127), calls=%async_computation.4 | async-start | bytes 262144 | tf_op jit(solution)/shard_map/all_to_all | solution.py:31
  111.9 16.9 %collective-permute-start.6 = (bf16[512,256]{1,0:T(8,128)(2,1)}, bf16[512,256]{1,0:T(8,128)(2,1)}, u32[]{:S(2)}, u32[]{:S(2)}) collective-permute-start(bf16[512,256]{1,0:T(8,128)(2,1)} %shard_map.130), channel_id=1, source_target_pairs={{256,0},{384,128},{257,1},{385,129},{258,2},{386,130},{259,3},{387... | collective-permute-start | bytes 786440 | tf_op jit(solution)/shard_map/ppermute | solution.py:52
  119.4 18.8 %copy-start = (f32[1,128,512]{2,1,0:T(8,128)S(1)}, f32[1,128,512]{2,1,0:T(8,128)}, u32[]{:S(2)}) copy-start(f32[1,128,512]{2,1,0:T(8,128)} %param.12) | copy-start | bytes 786436
  119.4 18.8 %copy-start.4 = (bf16[128,512]{1,0:T(8,128)(2,1)S(1)}, bf16[128,512]{1,0:T(8,128)(2,1)}, u32[]{:S(2)}) copy-start(bf16[128,512]{1,0:T(8,128)(2,1)} %reduce-scatter.2.cloned.1.call-done.refs_0_.refs_1_) | copy-start | bytes 393220
  119.4 18.8 %copy-start.5 = (f32[1,128,512]{2,1,0:T(8,128)S(1)}, f32[1,128,512]{2,1,0:T(8,128)}, u32[]{:S(2)}) copy-start(f32[1,128,512]{2,1,0:T(8,128)} %param.13) | copy-start | bytes 786436
  119.4 18.9 %copy-start.6 = (f32[1,128,512]{2,1,0:T(8,128)S(1)}, f32[1,128,512]{2,1,0:T(8,128)}, u32[]{:S(2)}) copy-start(f32[1,128,512]{2,1,0:T(8,128)} %param.14) | copy-start | bytes 786436
  119.4 18.8 %all-to-all-start.4 = ((f32[16,8,128]{2,1,0:T(8,128)}), f32[16,8,128]{2,1,0:T(8,128)S(1)}, u32[]{:S(2)}, u32[]{:S(2)}) async-start(f32[16,8,128]{2,1,0:T(8,128)} %shard_map.128), calls=%async_computation.5 | async-start | bytes 131072 | tf_op jit(solution)/shard_map/all_to_all | solution.py:31
  139.7 32.0 %all-to-all-start.5 = ((bf16[16,128,256]{2,1,0:T(8,128)(2,1)}), bf16[16,128,256]{2,1,0:T(8,128)(2,1)S(1)}, u32[]{:S(2)}, u32[]{:S(2)}) async-start(bf16[16,128,256]{2,1,0:T(8,128)(2,1)} %shard_map.131), calls=%async_computation.6 | async-start | bytes 2097152 | tf_op jit(solution)/shard_map/all_to_all | solution.py:31
  165.2 4.3 %collective-permute-start.7 = (bf16[512,512]{1,0:T(8,128)(2,1)S(1)}, bf16[512,512]{1,0:T(8,128)(2,1)S(1)}, u32[]{:S(2)}, u32[]{:S(2)}) collective-permute-start(bf16[512,512]{1,0:T(8,128)(2,1)S(1)} %all_gather.7.refs_4_), channel_id=1, source_target_pairs={{0,1},{1,0},{2,3},{3,2},{4,5},{5,4},{6,7},{7,6},{8,9},{9,8},{10,11... | collective-permute-start | bytes 1572872 | tf_op jit(solution)/shard_map/ppermute | solution.py:47
  171.7 15.5 %all-to-all-start.6 = ((bf16[4,128,512]{2,1,0:T(8,128)(2,1)}), bf16[4,128,512]{2,1,0:T(8,128)(2,1)S(1)}, u32[]{:S(2)}, u32[]{:S(2)}) async-start(bf16[4,128,512]{2,1,0:T(8,128)(2,1)} %shard_map.132), calls=%async_computation.7 | async-start | bytes 1048576 | tf_op jit(solution)/shard_map/all_to_all | solution.py:31
Sparse Core Ops, SparseCore 0:
  61.4 38.6 reduce-scatter.1

commit v6 on v5

--- a/solution.py
+++ b/solution.py
@@ -68,7 +68,10 @@
         body,
         out_shape=out_shapes,
         in_specs=[pl.BlockSpec(memory_space=pltpu.SMEM)]
-        + [pl.BlockSpec(memory_space=pltpu.VMEM)] * len(arrays)
+        + [
+            pl.BlockSpec(memory_space=pltpu.SMEM if a.dtype == jnp.int32 else pltpu.VMEM)
+            for a in arrays
+        ]
         + [pl.BlockSpec(memory_space=pl.ANY)] * len(after),
         out_specs=[pl.BlockSpec(memory_space=pltpu.VMEM)] * len(out_shapes),
         scratch_shapes=scratch,
@@ -81,10 +84,11 @@
     return pl.ds(pl.multiple_of(start, rows), rows)
 
 
-def split_kernel(sizes, spots, acts, values, out):
+def split_kernel(sizes, spots, acts, values, master, out, weights):
     far, group, cores, rows = sizes
     core = spots[0]
     half = far * rows
+    weights[...] = master[...].astype(bf16)
     floats = acts[...].astype(f32)
     scaled = (values[...].astype(f32) * inverse_rms(floats)).astype(bf16)
     for x in range(group):
@@ -97,6 +101,35 @@
         out[x, :, cores * half :] = scaled
 
 
+def split(sizes, spots, acts, values, master):
+    far, group, cores, rows = sizes
+    toks, width = acts.shape
+    kvw = values.shape[1]
+    steps = 4
+    cut = toks // steps
+    lanes = cores * far * rows + kvw
+    return pl.pallas_call(
+        functools.partial(split_kernel, sizes),
+        grid=(steps,),
+        out_shape=[
+            jax.ShapeDtypeStruct((group, toks, lanes), bf16),
+            jax.ShapeDtypeStruct((rows, kvw), bf16),
+        ],
+        in_specs=[
+            pl.BlockSpec(memory_space=pltpu.SMEM),
+            pl.BlockSpec((cut, width), lambda i: (i, 0)),
+            pl.BlockSpec((cut, kvw), lambda i: (i, 0)),
+            pl.BlockSpec((rows // steps, kvw), lambda i: (i, 0)),
+        ],
+        out_specs=[
+            pl.BlockSpec((group, cut, lanes), lambda i: (0, i, 0)),
+            pl.BlockSpec((rows // steps, kvw), lambda i: (i, 0)),
+        ],
+        compiler_params=pltpu.CompilerParams(vmem_limit_bytes=63 * 1024 * 1024),
+        cost_estimate=pl.CostEstimate(flops=0, bytes_accessed=0, transcendentals=0),
+    )(spots, acts, values, master)
+
+
 def other_kernel(half, spots, mine, gain, out):
     left = mine[:, half : 2 * half]
     part = lax.dot_general(
@@ -105,11 +138,15 @@
     out[...] = (part * gain[...]).astype(bf16)
 
 
-def own_kernel(half, spots, mine, gain, came, out):
+def own_kernel(half, spots, mine, gain, out):
     part = lax.dot_general(
         mine[:, :half], mine[:, 2 * half :], (((0,), (0,)), ((), ())), preferred_element_type=f32
     )
-    out[...] = (part * gain[...] + came[...].astype(f32)).astype(bf16)
+    out[...] = part * gain[...]
+
+
+def add_kernel(spots, own, came, out):
+    out[...] = (own[...] + came[...].astype(f32)).astype(bf16)
 
 
 def upstream_kernel(half, spots, mine, own, other, gain, mixed, sums):
@@ -144,16 +181,16 @@
             out[z, :, c * rows : (c + 1) * rows] = block.astype(bf16)
 
 
-def fresh_kernel(sizes, ids_shape, spots, acts, gain, table, *refs):
+def fresh_kernel(sizes, spots, ids, acts, gain, table, *refs):
     *outs, normed = refs
     far, group, cores, rows = sizes
-    micro, seqs = ids_shape
+    micro = ids.shape[0]
     half = far * rows
     floats = acts[...].astype(f32)
     toks = floats.shape[0]
     row = lax.broadcasted_iota(jnp.int32, (toks, 1), 0)
     for m in range(micro):
-        bin_id = spots[5 + m * seqs + spots[3]]
+        bin_id = ids[m, spots[3]]
         embed = jnp.zeros((1, floats.shape[1]), f32)
         for b in range(table.shape[0]):
             embed = jnp.where(bin_id == b, table[b : b + 1, :].astype(f32), embed)
@@ -170,21 +207,23 @@
                 ]
 
 
-def values_kernel(half, spots, *refs):
-    *blocks, own, other, out = refs
-    group = len(blocks)
+def first_kernel(half, spots, *refs):
+    *blocks, weights, out = refs
     for k, block in enumerate(blocks):
-        part = jnp.dot(block[:, :half], own[...], preferred_element_type=f32)
-        part = part + jnp.dot(block[:, half:], other[...], preferred_element_type=f32)
-        out[(spots[4] - k) & (group - 1)] = part.astype(bf16)
+        part = jnp.dot(block[:, :half], weights[...], preferred_element_type=f32)
+        out[(spots[4] - k) & (len(blocks) - 1)] = part
+
+
+def second_kernel(half, spots, *refs):
+    *blocks, weights, first, out = refs
+    for k, block in enumerate(blocks):
+        x = (spots[4] - k) & (len(blocks) - 1)
+        part = jnp.dot(block[:, half:], weights[...], preferred_element_type=f32)
+        out[x] = (first[x] + part).astype(bf16)
 
 
 def top_kernel(spots, came, out):
     out[...] = jnp.sum(came[...].astype(f32), axis=0).astype(bf16)
-
-
-def pair_kernel(spots, top, behind, out):
-    out[...] = (top[...].astype(f32) + behind[...].astype(f32)).astype(bf16)
 
 
 def suffix_kernel(group, spots, came, *refs):
@@ -244,7 +283,6 @@
     all_toks = group * toks
     core, spot_y, spot_x = (lax.axis_index(name) for name in ("core", "y", "x"))
     spots = jnp.stack([core, spot_y, lax.axis_index(section), lax.axis_index(dp), spot_x])
-    spots = jnp.concatenate([spots, reward_ids.reshape(-1)])
     shape = jax.ShapeDtypeStruct
     gain = norm_gain[0]
 
@@ -259,14 +297,9 @@
     own_gain = of_features(gain)
 
     flat = acts[:, 0].reshape(toks, width)
-    blocks = local(
-        functools.partial(split_kernel, (far, group, cores, rows)),
-        [shape((group, toks, cores * half + kvw), bf16)],
-        spots,
-        flat,
-        value_grads[:, 0].reshape(toks, kvw),
-    )[0]
-    weights_old, blocks = together(master[0].astype(bf16), blocks)
+    blocks, weights_old = split(
+        (far, group, cores, rows), spots, flat, value_grads[:, 0].reshape(toks, kvw), master[0]
+    )
     mine = exchange(blocks, "x").reshape(all_toks, cores * half + kvw)
     weights_old = lax.all_gather(weights_old, "zhi", axis=0, tiled=True)
     mine, weights_old = together(mine, weights_old)
@@ -278,14 +311,17 @@
         mine,
         own_gain[half:, None],
     )[0]
-    partial = local(
+    came = swap_cores(other)
+    own = local(
         functools.partial(own_kernel, half),
-        [shape((half, kvw), bf16)],
+        [shape((half, kvw), f32)],
         spots,
         mine,
         own_gain[:half, None],
-        swap_cores(other),
-    )[0]
+        after=[other],
+    )[0]
+    partial = local(add_kernel, [shape((half, kvw), bf16)], spots, own, came)[0]
+    partial, weights_old = together(partial, weights_old)
     grad = lax.psum_scatter(partial, "zhi", scatter_dimension=0, tiled=True)
     weights_other = swap_cores(weights_old)
 
@@ -312,9 +348,10 @@
     came = exchange(parts, "y")
 
     fresh_blocks = local(
-        functools.partial(fresh_kernel, (far, group, cores, rows), reward_ids.shape),
+        functools.partial(fresh_kernel, (far, group, cores, rows)),
         [shape((toks, cores * half), bf16)] * group,
         spots,
+        reward_ids,
         next_flat,
         norm_gain,
         reward_table,
@@ -324,9 +361,8 @@
 
     top_shape = shape((all_toks, cores * rows), bf16)
     top = local(top_kernel, [top_shape], spots, came, after=fresh_normed[1:3])[0]
-    behind = [from_behind(top, "zlo", 1)]
-    pair = local(pair_kernel, [top_shape], spots, top, behind[0])[0]
-    behind.append(from_behind(pair, "zlo", 2))
+    sections = lax.axis_size("zlo")
+    behind = [from_behind(top, "zlo", k) for k in range(sections - 1, 0, -1)]
 
     near = ("y", "x", "core")
     along = ("zlo", "zhi")
@@ -335,7 +371,7 @@
         squares_kernel, [shape((lax.axis_size(near),) + tile, f32)], spots, grad, after=[top]
     )[0]
     squares = exchange(squares, near)
-    squares = local(relay_kernel, [shape((lax.axis_size(along),) + tile, f32)], spots, squares, after=fresh_normed)[0]
+    squares = local(relay_kernel, [shape((lax.axis_size(along),) + tile, f32)], spots, squares, after=fresh_normed + behind)[0]
     squares = exchange(squares, along)
     shard = shape((rows, kvw), f32)
     moment1_new, moment2_new, weights_new = local(
@@ -359,13 +395,21 @@
     weights_new = lax.all_gather(weights_new, "zhi", axis=0, tiled=True)
     back = exchange(suffix, ("y", "x"))
 
-    fresh = local(
-        functools.partial(values_kernel, half),
-        [shape((group, toks, kvw), bf16)],
+    weights_other = swap_cores(weights_new)
+    first = local(
+        functools.partial(first_kernel, half),
+        [shape((group, toks, kvw), f32)],
         spots,
         *fresh_normed,
         weights_new,
-        swap_cores(weights_new),
+    )[0]
+    fresh = local(
+        functools.partial(second_kernel, half),
+        [shape((group, toks, kvw), bf16)],
+        spots,
+        *fresh_normed,
+        weights_other,
+        first,
     )[0]
     fresh, back = together(fresh, back)
     fresh = jnp.sum(exchange(fresh, "x").astype(f32), axis=0).astype(bf16)

time: 197 us -> 205 us (1.041)
  starting transfers between devices: 56.3 us -> 68.2 us
  waiting for transfers between devices: 36.1 us -> 33.9 us
    ppermute x3, starting transfers between devices: 11.2 us -> 16.5 us  [swap_cores(): return lax.ppermute(block, 'core', [(0, 1), (1, 0)])]
    all_to_all x6, waiting for transfers between devices: 19.5 us -> 24.7 us  [exchange(): return lax.all_to_all(blocks, axis, 0, 0)]
    all_to_all x6, starting transfers between devices: 34.7 us -> 39.1 us  [exchange(): return lax.all_to_all(blocks, axis, 0, 0)]
    pallas_call x0 -> x1, Pallas kernels: none -> 3.82 us  [split(): pl.pallas_call(functools.partial(split_kernel, sizes), grid=(steps,), out...]
    reduce_scatter x1, waiting for transfers between devices: 4.62 us -> 1.32 us  [per_device(): grad = lax.psum_scatter(partial, 'zhi', scatter_dimension=0, tiled=True)]
    pallas_call x14, Pallas kernels: 22.7 us -> 19.9 us  [local(): pl.pallas_call(body, out_shape=out_shapes, in_specs=[pl.BlockSpec(memory_...]
    ppermute x3, waiting for transfers between devices: 8.13 us -> 5.5 us  [shift(): lax.ppermute(parts[k], axis, [(i, (i + k) % size) for i in range(size)])]
    ppermute x2 -> x3, waiting for transfers between devices: 2.29 us -> 0.01 us  [from_behind(): lax.ppermute(block, axis, [(i + distance, i) for i in range(size - distan...]
  transfers between devices with their start and end apart: 15 -> 16, of which waited for: 8 -> 9; matrix products, arithmetic and copies ran while one was open for 0% -> 0% of each run, Pallas kernels for 9% -> 7%
where the time goes in v6:
time: 205 us; the launch traced here: 204 us
  starting transfers between devices  68.2 us (33%)
  blocking collectives  59.3 us (29%)
  waiting for transfers between devices  33.9 us (17%)
  Pallas kernels  23.8 us (12%)
  between operations  14.3 us (7%)
  local copies, waits for them, and re-layouts  3.46 us (2%)
    all_to_all x6, starting transfers between devices, exchange(): return lax.all_to_all(blocks, axis, 0, 0)  39.1 us
    all_gather x1, blocking collectives, per_device(): weights_old = lax.all_gather(weights_old, 'zhi', axis=0, tiled=True)  30.9 us
    all_to_all x6, waiting for transfers between devices, exchange(): return lax.all_to_all(blocks, axis, 0, 0)  24.7 us
    all_gather x1, blocking collectives, per_device(): weights_new = lax.all_gather(weights_new, 'zhi', axis=0, tiled=True)  21.6 us
    pallas_call x14, Pallas kernels, local(): pl.pallas_call(body, out_shape=out_shapes, in_specs=[pl.BlockSpec(memory_...  19.9 us
    ppermute x3, starting transfers between devices, swap_cores(): return lax.ppermute(block, 'core', [(0, 1), (1, 0)])  16.5 us
    ppermute x3, starting transfers between devices, shift(): lax.ppermute(parts[k], axis, [(i, (i + k) % size) for i in range(size)])  8.65 us
    all_to_all x1, blocking collectives, exchange(): return lax.all_to_all(blocks, axis, 0, 0)  6.84 us
  transfers between devices with their start and end apart: 16, of which 9 were waited for; matrix products, arithmetic and copies ran while one was open for 0% of the time, Pallas kernels for 7%

profile of v6, /device:TPU:1, one launch (start us, length us, event | category | flops | bytes accessed | tf_op | source)
XLA Modules:
  0.0 203.6 jit_solution(6877057412106260895)
XLA Ops:
  7.2 0.7 stack.23.spots
  7.8 3.8 %shard_map.120 = (bf16[4,128,1536]{2,1,0:T(8,128)(2,1)}, bf16[128,512]{1,0:T(8,128)(2,1)}) custom-call(s32[5]{0:T(128)} %stack.23.spots, bf16[128,4096]{1,0:T(8,128)(2,1)} %bitcast.42, bf16[128,512]{1,0:T(8,128)(2,1)} %bitcast.44, f32[128,512]{1,0:T(8,128)} %bitcast.35), custom_call_target="tpu_custom_call" | custom-call | tf_op jit(solution)/shard_map/pallas_call | solution.py:111
  11.7 0.0 copy-start.7
  11.7 5.0 %all-to-all-start = ((bf16[4,128,1536]{2,1,0:T(8,128)(2,1)}), bf16[4,128,1536]{2,1,0:T(8,128)(2,1)S(1)}, u32[]{:S(2)}, u32[]{:S(2)}) async-start(bf16[4,128,1536]{2,1,0:T(8,128)(2,1)} %get-tuple-element.25), calls=%async_computation | async-start | bytes 3145728 | tf_op jit(solution)/shard_map/all_to_all | solution.py:31
  16.7 0.0 reduce-scatter.2.cloned.1.call-start
  16.7 0.0 copy-done.9
  16.7 0.1 copy.18.refs_1_
  16.8 30.9 %all_gather.6.refs_1_ = bf16[512,512]{1,0:T(8,128)(2,1)S(1)} all-gather(bf16[128,512]{1,0:T(8,128)(2,1)S(1)} %copy-done.11), channel_id=1, replica_groups=mesh['zlo'=4,'y'=4,'zhi'=4,'x'=4,'core'=2] {'zhi'}, dimensions={0}, use_global_device_ids=true | all-gather | bytes 655360 | tf_op jit(solution)/shard_map/all_gather | solution.py:304
  47.7 0.0 all-to-all-done
  47.7 1.0 shard_map.121.refs_2_
  48.7 6.5 %collective-permute-start = (bf16[512,512]{1,0:T(8,128)(2,1)S(1)}, bf16[512,512]{1,0:T(8,128)(2,1)S(1)}, u32[]{:S(2)}, u32[]{:S(2)}) collective-permute-start(bf16[512,512]{1,0:T(8,128)(2,1)S(1)} %shard_map.121.refs_2_), channel_id=1, source_target_pairs={{0,1},{1,0},{2,3},{3,2},{4,5},{5,4},{6,7},{7,6},{8,9},{9,8},{10,11... | collective-permute-start | bytes 1572872 | tf_op jit(solution)/shard_map/ppermute | solution.py:47
  55.2 0.1 copy.19.refs_1_
  55.4 1.0 shard_map.122.refs_0_
  56.4 0.4 collective-permute-done.refs_1_
  56.7 1.4 shard_map.123.refs_4_
  58.1 2.3 %collective-permute-start.1 = (bf16[512,512]{1,0:T(8,128)(2,1)S(1)}, bf16[512,512]{1,0:T(8,128)(2,1)S(1)}, u32[]{:S(2)}, u32[]{:S(2)}) collective-permute-start(bf16[512,512]{1,0:T(8,128)(2,1)S(1)} %all_gather.6.refs_1_), channel_id=1, source_target_pairs={{0,1},{1,0},{2,3},{3,2},{4,5},{5,4},{6,7},{7,6},{8,9},{9,8},{10,11... | collective-permute-start | bytes 1572872 | tf_op jit(solution)/shard_map/ppermute | solution.py:47
  60.4 0.0 reduce-scatter.2.cloned.1.call-update
  60.4 1.5 collective-permute-done.1.refs_2_
  61.9 1.5 shard_map.124
  63.4 6.8 %all_to_all.35.refs_2_ = f32[4,8,512]{2,1,0:T(8,128)S(1)} all-to-all(f32[4,8,512]{2,1,0:T(8,128)S(1)} %get-tuple-element.32), channel_id=1, replica_groups=mesh['zlo'=4,'y'=4,'zhi'=4,'x'=4,'core'=2] {'x'}, dimensions={0} | all-to-all | bytes 131072 | tf_op jit(solution)/shard_map/all_to_all | solution.py:31
  70.2 2.0 shard_map.125
  72.3 4.3 %all-to-all-start.2 = ((bf16[4,512,256]{2,1,0:T(8,128)(2,1)}), bf16[4,512,256]{2,1,0:T(8,128)(2,1)S(1)}, u32[]{:S(2)}, u32[]{:S(2)}) async-start(bf16[4,512,256]{2,1,0:T(8,128)(2,1)} %shard_map.125), calls=%async_computation.3 | async-start | bytes 2097152 | tf_op jit(solution)/shard_map/all_to_all | solution.py:31
  76.6 0.0 copy-done.10
  76.6 2.3 %shard_map.126 = (bf16[128,1024]{1,0:T(8,128)(2,1)S(1)}, bf16[128,1024]{1,0:T(8,128)(2,1)S(1)}, bf16[128,1024]{1,0:T(8,128)(2,1)S(1)}, bf16[128,1024]{1,0:T(8,128)(2,1)}) custom-call(s32[5]{0:T(128)S(1)} %copy-done.7, s32[2,32]{1,0:T(2,128)S(1)} %copy-done.10, bf16[128,4096]{1,0:T(8,128)(2,1)S(1)} %bitcast.34, f32[1,4096]{1,0:T(1,128)S(1)} %copy-done.9, ...), custom_call_target="tpu_custom_call" | custom-call | tf_op jit(solution)/shard_map/pallas_call | solution.py:67
  78.9 2.2 %collective-permute-start.2 = (bf16[128,1024]{1,0:T(8,128)(2,1)S(1)}, bf16[128,1024]{1,0:T(8,128)(2,1)S(1)}, u32[]{:S(2)}, u32[]{:S(2)}) collective-permute-start(bf16[128,1024]{1,0:T(8,128)(2,1)S(1)} %get-tuple-element.35), channel_id=1, source_target_pairs={{0,2},{2,4},{4,6},{6,0},{1,3},{3,5},{5,7},{7,1},{8,10},{10,12},{12... | collective-permute-start | bytes 786440 | tf_op jit(solution)/shard_map/ppermute | solution.py:42
  81.1 3.7 %collective-permute-start.3 = (bf16[128,1024]{1,0:T(8,128)(2,1)S(1)}, bf16[128,1024]{1,0:T(8,128)(2,1)S(1)}, u32[]{:S(2)}, u32[]{:S(2)}) collective-permute-start(bf16[128,1024]{1,0:T(8,128)(2,1)S(1)} %get-tuple-element.36), channel_id=1, source_target_pairs={{0,4},{2,6},{4,0},{6,2},{1,5},{3,7},{5,1},{7,3},{8,12},{10,14},{12... | collective-permute-start | bytes 786440 | tf_op jit(solution)/shard_map/ppermute | solution.py:42
  84.8 2.8 %collective-permute-start.4 = (bf16[128,1024]{1,0:T(8,128)(2,1)}, bf16[128,1024]{1,0:T(8,128)(2,1)S(1)}, u32[]{:S(2)}, u32[]{:S(2)}) collective-permute-start(bf16[128,1024]{1,0:T(8,128)(2,1)} %get-tuple-element.37), channel_id=1, source_target_pairs={{0,6},{2,0},{4,2},{6,4},{1,7},{3,1},{5,3},{7,5},{8,14},{10,8},{12,... | collective-permute-start | bytes 786440 | tf_op jit(solution)/shard_map/ppermute | solution.py:42
  87.5 1.1 collective-permute-done.2.refs_1_.refs_2_
  88.7 4.4 %collective-permute-done.3.refs_2_.refs_3_ = bf16[128,1024]{1,0:T(8,128)(2,1)S(1)} collective-permute-done((bf16[128,1024]{1,0:T(8,128)(2,1)S(1)}, bf16[128,1024]{1,0:T(8,128)(2,1)S(1)}, u32[]{:S(2)}, u32[]{:S(2)}) %collective-permute-start.3) | collective-permute-done | bytes 262176 | tf_op jit(solution)/shard_map/ppermute | solution.py:42
  93.0 0.0 all-to-all-done.2.refs_0_
  93.1 0.7 shard_map.127.refs_1_
  93.7 1.3 collective-permute-start.5
  95.0 1.3 collective-permute-start.6
  96.3 1.3 collective-permute-start.7
  97.6 1.3 reduce-scatter.2.cloned.1.call-done.refs_0_.refs_1_
  99.0 0.9 copy-done.2
  99.9 1.4 shard_map.128
  101.2 8.4 %all-to-all-start.3 = ((f32[32,8,128]{2,1,0:T(8,128)}), f32[32,8,128]{2,1,0:T(8,128)S(1)}, u32[]{:S(2)}, u32[]{:S(2)}) async-start(f32[32,8,128]{2,1,0:T(8,128)} %shard_map.128), calls=%async_computation.4 | async-start | bytes 262144 | tf_op jit(solution)/shard_map/all_to_all | solution.py:31
  109.7 0.0 collective-permute-done.4.refs_4_.refs_3_
  109.7 7.6 %all-to-all-done.3.refs_0_ = f32[32,8,128]{2,1,0:T(8,128)S(1)} async-done(((f32[32,8,128]{2,1,0:T(8,128)}), f32[32,8,128]{2,1,0:T(8,128)S(1)}, u32[]{:S(2)}, u32[]{:S(2)}) %all-to-all-start.3) | async-done | bytes 131104 | tf_op jit(solution)/shard_map/all_to_all | solution.py:31
  117.3 0.0 collective-permute-done.5.refs_5_.refs_1_
  117.3 0.0 collective-permute-done.6.refs_6_.refs_2_
  117.3 0.0 collective-permute-done.7.refs_7_.refs_3_
  117.3 0.6 shard_map.129
  117.9 0.0 copy-start.6
  117.9 0.6 copy-done.6
  118.5 11.2 %all-to-all-start.4 = ((f32[16,8,128]{2,1,0:T(8,128)}), f32[16,8,128]{2,1,0:T(8,128)}, u32[]{:S(2)}, u32[]{:S(2)}) async-start(f32[16,8,128]{2,1,0:T(8,128)} %copy-done.6), calls=%async_computation.5 | async-start | bytes 131072 | tf_op jit(solution)/shard_map/all_to_all | solution.py:31
  129.8 1.8 shard_map.131
  131.5 10.0 %all-to-all-done.4.refs_0_ = f32[16,8,128]{2,1,0:T(8,128)} async-done(((f32[16,8,128]{2,1,0:T(8,128)}), f32[16,8,128]{2,1,0:T(8,128)}, u32[]{:S(2)}, u32[]{:S(2)}) %all-to-all-start.4) | async-done | bytes 65568 | tf_op jit(solution)/shard_map/all_to_all | solution.py:31
  141.5 0.0 copy-done.3
  141.5 0.0 copy-start.5
  141.5 0.9 copy-done.5
  142.5 1.8 shard_map.130
  144.2 5.7 %all-to-all-start.5 = ((bf16[16,128,256]{2,1,0:T(8,128)(2,1)}), bf16[16,128,256]{2,1,0:T(8,128)(2,1)S(1)}, u32[]{:S(2)}, u32[]{:S(2)}) async-start(bf16[16,128,256]{2,1,0:T(8,128)(2,1)} %shard_map.131), calls=%async_computation.6 | async-start | bytes 2097152 | tf_op jit(solution)/shard_map/all_to_all | solution.py:31
  149.9 21.6 %all_gather.7.refs_4_ = bf16[512,512]{1,0:T(8,128)(2,1)S(1)} all-gather(bf16[128,512]{1,0:T(8,128)(2,1)S(1)} %get-tuple-element.40), channel_id=1, replica_groups=mesh['zlo'=4,'y'=4,'zhi'=4,'x'=4,'core'=2] {'zhi'}, dimensions={0}, use_global_device_ids=true | all-gather | bytes 655360 | tf_op jit(solution)/shard_map/all_gather | solution.py:395
  171.6 7.8 %collective-permute-start.8 = (bf16[512,512]{1,0:T(8,128)(2,1)S(1)}, bf16[512,512]{1,0:T(8,128)(2,1)S(1)}, u32[]{:S(2)}, u32[]{:S(2)}) collective-permute-start(bf16[512,512]{1,0:T(8,128)(2,1)S(1)} %all_gather.7.refs_4_), channel_id=1, source_target_pairs={{0,1},{1,0},{2,3},{3,2},{4,5},{5,4},{6,7},{7,6},{8,9},{9,8},{10,11... | collective-permute-start | bytes 1572872 | tf_op jit(solution)/shard_map/ppermute | solution.py:47
  179.4 1.0 shard_map.132.refs_5_
  180.3 0.5 collective-permute-done.8.refs_4_
  180.9 1.8 shard_map.133
  182.6 0.0 all-to-all-done.5.refs_0_
  182.6 4.5 %all-to-all-start.6 = ((bf16[4,128,512]{2,1,0:T(8,128)(2,1)}), bf16[4,128,512]{2,1,0:T(8,128)(2,1)S(1)}, u32[]{:S(2)}, u32[]{:S(2)}) async-start(bf16[4,128,512]{2,1,0:T(8,128)(2,1)} %shard_map.133), calls=%async_computation.7 | async-start | bytes 1048576 | tf_op jit(solution)/shard_map/all_to_all | solution.py:31
  187.1 1.8 shard_map.134
  188.9 7.1 %all-to-all-done.6 = bf16[4,128,512]{2,1,0:T(8,128)(2,1)S(1)} async-done(((bf16[4,128,512]{2,1,0:T(8,128)(2,1)}), bf16[4,128,512]{2,1,0:T(8,128)(2,1)S(1)}, u32[]{:S(2)}, u32[]{:S(2)}) %all-to-all-start.6) | async-done | bytes 524320 | tf_op jit(solution)/shard_map/all_to_all | solution.py:31
  196.1 0.7 reduce_sum.12
  (17 shorter events, 0.0 us)
Async XLA Ops:
  11.7 5.0 %copy-start.9 = (f32[1,4096]{1,0:T(1,128)S(1)}, f32[1,4096]{1,0:T(1,128)}, u32[]{:S(2)}) copy-start(f32[1,4096]{1,0:T(1,128)} %refs_2_.1) | copy-start | bytes 49156
  11.7 5.2 %copy-start.11 = (bf16[128,512]{1,0:T(8,128)(2,1)S(1)}, bf16[128,512]{1,0:T(8,128)(2,1)}, u32[]{:S(2)}) copy-start(bf16[128,512]{1,0:T(8,128)(2,1)} %get-tuple-element.26) | copy-start | bytes 393220
  11.7 36.0 %copy-start.7 = (s32[5]{0:T(128)S(1)}, s32[5]{0:T(128)}, u32[]{:S(2)}) copy-start(s32[5]{0:T(128)} %stack.23.spots) | copy-start | bytes 64
  11.7 36.0 %all-to-all-start = ((bf16[4,128,1536]{2,1,0:T(8,128)(2,1)}), bf16[4,128,1536]{2,1,0:T(8,128)(2,1)S(1)}, u32[]{:S(2)}, u32[]{:S(2)}) async-start(bf16[4,128,1536]{2,1,0:T(8,128)(2,1)} %get-tuple-element.25), calls=%async_computation | async-start | bytes 3145728 | tf_op jit(solution)/shard_map/all_to_all | solution.py:31
  16.7 82.3 %reduce-scatter.2.cloned.1.call-start = ((), (), s32[]{:S(2)}) async-start(), calls=%async_computation.8 | async-start | bytes 655360 | tf_op jit(solution)/shard_map/reduce_scatter | solution.py:325
  48.7 8.0 %collective-permute-start = (bf16[512,512]{1,0:T(8,128)(2,1)S(1)}, bf16[512,512]{1,0:T(8,128)(2,1)S(1)}, u32[]{:S(2)}, u32[]{:S(2)}) collective-permute-start(bf16[512,512]{1,0:T(8,128)(2,1)S(1)} %shard_map.121.refs_2_), channel_id=1, source_target_pairs={{0,1},{1,0},{2,3},{3,2},{4,5},{5,4},{6,7},{7,6},{8,9},{9,8},{10,11... | collective-permute-start | bytes 1572872 | tf_op jit(solution)/shard_map/ppermute | solution.py:47
  58.1 3.8 %collective-permute-start.1 = (bf16[512,512]{1,0:T(8,128)(2,1)S(1)}, bf16[512,512]{1,0:T(8,128)(2,1)S(1)}, u32[]{:S(2)}, u32[]{:S(2)}) collective-permute-start(bf16[512,512]{1,0:T(8,128)(2,1)S(1)} %all_gather.6.refs_1_), channel_id=1, source_target_pairs={{0,1},{1,0},{2,3},{3,2},{4,5},{5,4},{6,7},{7,6},{8,9},{9,8},{10,11... | collective-permute-start | bytes 1572872 | tf_op jit(solution)/shard_map/ppermute | solution.py:47
  72.2 4.3 %copy-start = (bf16[2,1,64,4096]{3,2,1,0:T(8,128)(2,1)S(1)}, bf16[2,1,64,4096]{3,2,1,0:T(8,128)(2,1)}, u32[]{:S(2)}) copy-start(bf16[2,1,64,4096]{3,2,1,0:T(8,128)(2,1)} %param.15) | copy-start | bytes 3145732
  72.3 4.3 %copy-start.8 = (bf16[5,4096]{1,0:T(8,128)(2,1)S(1)}, bf16[5,4096]{1,0:T(8,128)(2,1)}, u32[]{:S(2)}) copy-start(bf16[5,4096]{1,0:T(8,128)(2,1)} %refs_3_.1) | copy-start | bytes 122884
  72.3 4.3 %copy-start.10 = (s32[2,32]{1,0:T(2,128)S(1)}, s32[2,32]{1,0:T(2,128)}, u32[]{:S(2)}) copy-start(s32[2,32]{1,0:T(2,128)} %refs_0_.1) | copy-start | bytes 772
  72.3 20.8 %all-to-all-start.2 = ((bf16[4,512,256]{2,1,0:T(8,128)(2,1)}), bf16[4,512,256]{2,1,0:T(8,128)(2,1)S(1)}, u32[]{:S(2)}, u32[]{:S(2)}) async-start(bf16[4,512,256]{2,1,0:T(8,128)(2,1)} %shard_map.125), calls=%async_computation.3 | async-start | bytes 2097152 | tf_op jit(solution)/shard_map/all_to_all | solution.py:31
  78.9 9.8 %collective-permute-start.2 = (bf16[128,1024]{1,0:T(8,128)(2,1)S(1)}, bf16[128,1024]{1,0:T(8,128)(2,1)S(1)}, u32[]{:S(2)}, u32[]{:S(2)}) collective-permute-start(bf16[128,1024]{1,0:T(8,128)(2,1)S(1)} %get-tuple-element.35), channel_id=1, source_target_pairs={{0,2},{2,4},{4,6},{6,0},{1,3},{3,5},{5,7},{7,1},{8,10},{10,12},{12... | collective-permute-start | bytes 786440 | tf_op jit(solution)/shard_map/ppermute | solution.py:42
  81.1 12.0 %collective-permute-start.3 = (bf16[128,1024]{1,0:T(8,128)(2,1)S(1)}, bf16[128,1024]{1,0:T(8,128)(2,1)S(1)}, u32[]{:S(2)}, u32[]{:S(2)}) collective-permute-start(bf16[128,1024]{1,0:T(8,128)(2,1)S(1)} %get-tuple-element.36), channel_id=1, source_target_pairs={{0,4},{2,6},{4,0},{6,2},{1,5},{3,7},{5,1},{7,3},{8,12},{10,14},{12... | collective-permute-start | bytes 786440 | tf_op jit(solution)/shard_map/ppermute | solution.py:42
  84.8 24.9 %collective-permute-start.4 = (bf16[128,1024]{1,0:T(8,128)(2,1)}, bf16[128,1024]{1,0:T(8,128)(2,1)S(1)}, u32[]{:S(2)}, u32[]{:S(2)}) collective-permute-start(bf16[128,1024]{1,0:T(8,128)(2,1)} %get-tuple-element.37), channel_id=1, source_target_pairs={{0,6},{2,0},{4,2},{6,4},{1,7},{3,1},{5,3},{7,5},{8,14},{10,8},{12,... | collective-permute-start | bytes 786440 | tf_op jit(solution)/shard_map/ppermute | solution.py:42
  93.7 23.6 %collective-permute-start.5 = (bf16[512,256]{1,0:T(8,128)(2,1)S(1)}, bf16[512,256]{1,0:T(8,128)(2,1)S(1)}, u32[]{:S(2)}, u32[]{:S(2)}) collective-permute-start(bf16[512,256]{1,0:T(8,128)(2,1)S(1)} %shard_map.127.refs_1_), channel_id=1, source_target_pairs={{384,0},{385,1},{386,2},{387,3},{388,4},{389,5},{390,6},{391,7},{3... | collective-permute-start | bytes 786440 | tf_op jit(solution)/shard_map/ppermute | solution.py:52
  95.0 22.3 %collective-permute-start.6 = (bf16[512,256]{1,0:T(8,128)(2,1)S(1)}, bf16[512,256]{1,0:T(8,128)(2,1)S(1)}, u32[]{:S(2)}, u32[]{:S(2)}) collective-permute-start(bf16[512,256]{1,0:T(8,128)(2,1)S(1)} %shard_map.127.refs_1_), channel_id=1, source_target_pairs={{256,0},{384,128},{257,1},{385,129},{258,2},{386,130},{259,3},{387... | collective-permute-start | bytes 786440 | tf_op jit(solution)/shard_map/ppermute | solution.py:52
  96.3 21.0 %collective-permute-start.7 = (bf16[512,256]{1,0:T(8,128)(2,1)S(1)}, bf16[512,256]{1,0:T(8,128)(2,1)S(1)}, u32[]{:S(2)}, u32[]{:S(2)}) collective-permute-start(bf16[512,256]{1,0:T(8,128)(2,1)S(1)} %shard_map.127.refs_1_), channel_id=1, source_target_pairs={{128,0},{256,128},{384,256},{129,1},{257,129},{385,257},{130,2},{2... | collective-permute-start | bytes 786440 | tf_op jit(solution)/shard_map/ppermute | solution.py:52
  99.0 0.9 copy-start.2
  101.2 16.1 %all-to-all-start.3 = ((f32[32,8,128]{2,1,0:T(8,128)}), f32[32,8,128]{2,1,0:T(8,128)S(1)}, u32[]{:S(2)}, u32[]{:S(2)}) async-start(f32[32,8,128]{2,1,0:T(8,128)} %shard_map.128), calls=%async_computation.4 | async-start | bytes 262144 | tf_op jit(solution)/shard_map/all_to_all | solution.py:31
  117.9 0.6 copy-start.6
  118.5 23.0 %copy-start.1 = (f32[1,128,512]{2,1,0:T(8,128)S(1)}, f32[1,128,512]{2,1,0:T(8,128)}, u32[]{:S(2)}) copy-start(f32[1,128,512]{2,1,0:T(8,128)} %param.12) | copy-start | bytes 786436
  118.5 23.0 %copy-start.3 = (bf16[128,512]{1,0:T(8,128)(2,1)S(1)}, bf16[128,512]{1,0:T(8,128)(2,1)}, u32[]{:S(2)}) copy-start(bf16[128,512]{1,0:T(8,128)(2,1)} %reduce-scatter.2.cloned.1.call-done.refs_0_.refs_1_) | copy-start | bytes 393220
  118.5 23.0 %copy-start.4 = (f32[1,128,512]{2,1,0:T(8,128)S(1)}, f32[1,128,512]{2,1,0:T(8,128)}, u32[]{:S(2)}) copy-start(f32[1,128,512]{2,1,0:T(8,128)} %param.13) | copy-start | bytes 786436
  118.5 22.9 %all-to-all-start.4 = ((f32[16,8,128]{2,1,0:T(8,128)}), f32[16,8,128]{2,1,0:T(8,128)}, u32[]{:S(2)}, u32[]{:S(2)}) async-start(f32[16,8,128]{2,1,0:T(8,128)} %copy-done.6), calls=%async_computation.5 | async-start | bytes 131072 | tf_op jit(solution)/shard_map/all_to_all | solution.py:31
  141.5 1.0 copy-start.5
  144.2 38.4 %all-to-all-start.5 = ((bf16[16,128,256]{2,1,0:T(8,128)(2,1)}), bf16[16,128,256]{2,1,0:T(8,128)(2,1)S(1)}, u32[]{:S(2)}, u32[]{:S(2)}) async-start(bf16[16,128,256]{2,1,0:T(8,128)(2,1)} %shard_map.131), calls=%async_computation.6 | async-start | bytes 2097152 | tf_op jit(solution)/shard_map/all_to_all | solution.py:31
  171.6 9.3 %collective-permute-start.8 = (bf16[512,512]{1,0:T(8,128)(2,1)S(1)}, bf16[512,512]{1,0:T(8,128)(2,1)S(1)}, u32[]{:S(2)}, u32[]{:S(2)}) collective-permute-start(bf16[512,512]{1,0:T(8,128)(2,1)S(1)} %all_gather.7.refs_4_), channel_id=1, source_target_pairs={{0,1},{1,0},{2,3},{3,2},{4,5},{5,4},{6,7},{7,6},{8,9},{9,8},{10,11... | collective-permute-start | bytes 1572872 | tf_op jit(solution)/shard_map/ppermute | solution.py:47
  182.6 13.4 %all-to-all-start.6 = ((bf16[4,128,512]{2,1,0:T(8,128)(2,1)}), bf16[4,128,512]{2,1,0:T(8,128)(2,1)S(1)}, u32[]{:S(2)}, u32[]{:S(2)}) async-start(bf16[4,128,512]{2,1,0:T(8,128)(2,1)} %shard_map.133), calls=%async_computation.7 | async-start | bytes 1048576 | tf_op jit(solution)/shard_map/all_to_all | solution.py:31
Sparse Core Ops, SparseCore 0:
  60.6 38.3 reduce-scatter.1

commit v7 on v6

--- a/solution.py
+++ b/solution.py
@@ -226,6 +226,10 @@
     out[...] = jnp.sum(came[...].astype(f32), axis=0).astype(bf16)
 
 
+def pair_kernel(spots, top, behind, out):
+    out[...] = (top[...].astype(f32) + behind[...].astype(f32)).astype(bf16)
+
+
 def suffix_kernel(group, spots, came, *refs):
     *parts, out = refs
     block = sum(part[...].astype(f32) for part in parts)
@@ -361,8 +365,9 @@
 
     top_shape = shape((all_toks, cores * rows), bf16)
     top = local(top_kernel, [top_shape], spots, came, after=fresh_normed[1:3])[0]
-    sections = lax.axis_size("zlo")
-    behind = [from_behind(top, "zlo", k) for k in range(sections - 1, 0, -1)]
+    behind = [from_behind(top, "zlo", 1)]
+    pair = local(pair_kernel, [top_shape], spots, top, behind[0])[0]
+    behind.append(from_behind(pair, "zlo", 2))
 
     near = ("y", "x", "core")
     along = ("zlo", "zhi")
@@ -371,8 +376,15 @@
         squares_kernel, [shape((lax.axis_size(near),) + tile, f32)], spots, grad, after=[top]
     )[0]
     squares = exchange(squares, near)
-    squares = local(relay_kernel, [shape((lax.axis_size(along),) + tile, f32)], spots, squares, after=fresh_normed + behind)[0]
+    squares = local(relay_kernel, [shape((lax.axis_size(along),) + tile, f32)], spots, squares, after=fresh_normed)[0]
     squares = exchange(squares, along)
+    suffix = local(
+        functools.partial(suffix_kernel, group),
+        [shape((layers_y * group, toks, cores * rows), bf16)],
+        spots,
+        came,
+        *behind,
+    )[0]
     shard = shape((rows, kvw), f32)
     moment1_new, moment2_new, weights_new = local(
         functools.partial(adam_kernel, lax.axis_size(section) * width * kvw),
@@ -383,14 +395,8 @@
         master[0],
         moment1[0],
         moment2[0],
-    )
-    suffix = local(
-        functools.partial(suffix_kernel, group),
-        [shape((layers_y * group, toks, cores * rows), bf16)],
-        spots,
-        came,
-        *behind,
-    )[0]
+        after=[suffix],
+    )
     weights_new, suffix = together(weights_new, suffix)
     weights_new = lax.all_gather(weights_new, "zhi", axis=0, tiled=True)
     back = exchange(suffix, ("y", "x"))

time: 205 us -> 199 us (0.971); the launches traced: 204 us -> 195 us
  starting transfers between devices: 68.2 us -> 58.2 us
    all_to_all x6, starting transfers between devices: 39.1 us -> 32.6 us  [exchange(): return lax.all_to_all(blocks, axis, 0, 0)]
    all_to_all x6, waiting for transfers between devices: 24.7 us -> 20.4 us  [exchange(): return lax.all_to_all(blocks, axis, 0, 0)]
    ppermute x3, waiting for transfers between devices: 5.5 us -> 8.3 us  [shift(): lax.ppermute(parts[k], axis, [(i, (i + k) % size) for i in range(size)])]
    pallas_call x14 -> x15, Pallas kernels: 19.9 us -> 21.3 us  [local(): pl.pallas_call(body, out_shape=out_shapes, in_specs=[pl.BlockSpec(memory_...]
  transfers between devices with their start and end apart: 16 -> 15, of which waited for: 9 -> 10; matrix products, arithmetic and copies ran while one was open for 0% -> 0% of each run, Pallas kernels for 7% -> 9%
where the time goes in v7:
time: 199 us; the launch traced here: 195 us
  blocking collectives  59.9 us (30%)
  starting transfers between devices  58.2 us (29%)
  waiting for transfers between devices  34.2 us (17%)
  Pallas kernels  25.2 us (13%)
  between operations  14.3 us (7%)
  local copies, waits for them, and re-layouts  2.59 us (1%)
    all_to_all x6, starting transfers between devices, exchange(): return lax.all_to_all(blocks, axis, 0, 0)  32.6 us
    all_gather x1, blocking collectives, per_device(): weights_old = lax.all_gather(weights_old, 'zhi', axis=0, tiled=True)  30.9 us
    all_gather x1, blocking collectives, per_device(): weights_new = lax.all_gather(weights_new, 'zhi', axis=0, tiled=True)  22.2 us
    pallas_call x15, Pallas kernels, local(): pl.pallas_call(body, out_shape=out_shapes, in_specs=[pl.BlockSpec(memory_...  21.3 us
    all_to_all x6, waiting for transfers between devices, exchange(): return lax.all_to_all(blocks, axis, 0, 0)  20.4 us
    ppermute x3, starting transfers between devices, swap_cores(): return lax.ppermute(block, 'core', [(0, 1), (1, 0)])  15.1 us
    ppermute x3, waiting for transfers between devices, shift(): lax.ppermute(parts[k], axis, [(i, (i + k) % size) for i in range(size)])  8.3 us
    ppermute x3, starting transfers between devices, shift(): lax.ppermute(parts[k], axis, [(i, (i + k) % size) for i in range(size)])  7.92 us
  transfers between devices with their start and end apart: 15, of which 10 were waited for; matrix products, arithmetic and copies ran while one was open for 0% of the time, Pallas kernels for 9%

profile of v7, /device:TPU:1, one launch (start us, length us, event | category | flops | bytes accessed | tf_op | source)
XLA Modules:
  0.0 195.0 jit_solution(16647383738158690772)
XLA Ops:
  7.2 0.7 stack.23.spots
  7.8 3.8 %shard_map.120 = (bf16[4,128,1536]{2,1,0:T(8,128)(2,1)}, bf16[128,512]{1,0:T(8,128)(2,1)}) custom-call(s32[5]{0:T(128)} %stack.23.spots, bf16[128,4096]{1,0:T(8,128)(2,1)} %bitcast.42, bf16[128,512]{1,0:T(8,128)(2,1)} %bitcast.44, f32[128,512]{1,0:T(8,128)} %bitcast.35), custom_call_target="tpu_custom_call" | custom-call | tf_op jit(solution)/shard_map/pallas_call | solution.py:111
  11.7 0.0 copy-start.6
  11.7 5.0 %all-to-all-start = ((bf16[4,128,1536]{2,1,0:T(8,128)(2,1)}), bf16[4,128,1536]{2,1,0:T(8,128)(2,1)S(1)}, u32[]{:S(2)}, u32[]{:S(2)}) async-start(bf16[4,128,1536]{2,1,0:T(8,128)(2,1)} %get-tuple-element.25), calls=%async_computation | async-start | bytes 3145728 | tf_op jit(solution)/shard_map/all_to_all | solution.py:31
  16.7 0.0 reduce-scatter.2.cloned.1.call-start
  16.7 0.0 copy-done.8
  16.7 0.1 copy.18.refs_1_
  16.8 0.0 copy-done.12
  16.8 30.9 %all_gather.6.refs_1_ = bf16[512,512]{1,0:T(8,128)(2,1)S(1)} all-gather(bf16[128,512]{1,0:T(8,128)(2,1)S(1)} %copy-done.12), channel_id=1, replica_groups=mesh['zlo'=4,'y'=4,'zhi'=4,'x'=4,'core'=2] {'zhi'}, dimensions={0}, use_global_device_ids=true | all-gather | bytes 655360 | tf_op jit(solution)/shard_map/all_gather | solution.py:308
  47.7 0.0 all-to-all-done
  47.7 0.0 copy-done.6
  47.7 1.0 shard_map.121.refs_2_
  48.7 6.5 %collective-permute-start = (bf16[512,512]{1,0:T(8,128)(2,1)S(1)}, bf16[512,512]{1,0:T(8,128)(2,1)S(1)}, u32[]{:S(2)}, u32[]{:S(2)}) collective-permute-start(bf16[512,512]{1,0:T(8,128)(2,1)S(1)} %shard_map.121.refs_2_), channel_id=1, source_target_pairs={{0,1},{1,0},{2,3},{3,2},{4,5},{5,4},{6,7},{7,6},{8,9},{9,8},{10,11... | collective-permute-start | bytes 1572872 | tf_op jit(solution)/shard_map/ppermute | solution.py:47
  55.2 0.1 copy.19.refs_1_
  55.4 1.0 shard_map.122.refs_0_
  56.4 0.4 collective-permute-done.refs_1_
  56.7 1.4 shard_map.123.refs_4_
  58.1 2.3 %collective-permute-start.1 = (bf16[512,512]{1,0:T(8,128)(2,1)S(1)}, bf16[512,512]{1,0:T(8,128)(2,1)S(1)}, u32[]{:S(2)}, u32[]{:S(2)}) collective-permute-start(bf16[512,512]{1,0:T(8,128)(2,1)S(1)} %all_gather.6.refs_1_), channel_id=1, source_target_pairs={{0,1},{1,0},{2,3},{3,2},{4,5},{5,4},{6,7},{7,6},{8,9},{9,8},{10,11... | collective-permute-start | bytes 1572872 | tf_op jit(solution)/shard_map/ppermute | solution.py:47
  60.4 0.0 reduce-scatter.2.cloned.1.call-update
  60.4 1.5 collective-permute-done.1.refs_2_
  61.9 1.5 shard_map.124
  63.4 6.8 %all_to_all.35.refs_2_ = f32[4,8,512]{2,1,0:T(8,128)S(1)} all-to-all(f32[4,8,512]{2,1,0:T(8,128)S(1)} %get-tuple-element.32), channel_id=1, replica_groups=mesh['zlo'=4,'y'=4,'zhi'=4,'x'=4,'core'=2] {'x'}, dimensions={0} | all-to-all | bytes 131072 | tf_op jit(solution)/shard_map/all_to_all | solution.py:31
  70.3 2.0 %shard_map.125 = bf16[4,512,256]{2,1,0:T(8,128)(2,1)} custom-call(s32[5]{0:T(128)S(1)} %copy-done.6, bf16[512,1536]{1,0:T(8,128)(2,1)S(1)} %bitcast.33, f32[512,1024]{1,0:T(8,128)S(1)} %get-tuple-element.31.refs_1_, f32[4,8,512]{2,1,0:T(8,128)S(1)} %all_to_all.35.refs_2_), custom_call_target="tpu_custom_call" | custom-call | tf_op jit(solution)/shard_map/pallas_call | solution.py:67
  72.3 4.3 %all-to-all-start.2 = ((bf16[4,512,256]{2,1,0:T(8,128)(2,1)}), bf16[4,512,256]{2,1,0:T(8,128)(2,1)S(1)}, u32[]{:S(2)}, u32[]{:S(2)}) async-start(bf16[4,512,256]{2,1,0:T(8,128)(2,1)} %shard_map.125), calls=%async_computation.3 | async-start | bytes 2097152 | tf_op jit(solution)/shard_map/all_to_all | solution.py:31
  76.6 0.0 copy-done
  76.6 0.0 copy-done.7
  76.6 0.0 copy-done.9
  76.6 1.6 shard_map.126
  78.2 0.0 copy-start.10
  78.2 0.7 copy-done.10
  78.9 2.3 %collective-permute-start.2 = (bf16[128,1024]{1,0:T(8,128)(2,1)S(1)}, bf16[128,1024]{1,0:T(8,128)(2,1)S(1)}, u32[]{:S(2)}, u32[]{:S(2)}) collective-permute-start(bf16[128,1024]{1,0:T(8,128)(2,1)S(1)} %get-tuple-element.35), channel_id=1, source_target_pairs={{0,2},{2,4},{4,6},{6,0},{1,3},{3,5},{5,7},{7,1},{8,10},{10,12},{12... | collective-permute-start | bytes 786440 | tf_op jit(solution)/shard_map/ppermute | solution.py:42
  81.3 3.7 %collective-permute-start.3 = (bf16[128,1024]{1,0:T(8,128)(2,1)S(1)}, bf16[128,1024]{1,0:T(8,128)(2,1)S(1)}, u32[]{:S(2)}, u32[]{:S(2)}) collective-permute-start(bf16[128,1024]{1,0:T(8,128)(2,1)S(1)} %get-tuple-element.36), channel_id=1, source_target_pairs={{0,4},{2,6},{4,0},{6,2},{1,5},{3,7},{5,1},{7,3},{8,12},{10,14},{12... | collective-permute-start | bytes 786440 | tf_op jit(solution)/shard_map/ppermute | solution.py:42
  84.9 3.9 %collective-permute-done.2.refs_1_.refs_2_ = bf16[128,1024]{1,0:T(8,128)(2,1)S(1)} collective-permute-done((bf16[128,1024]{1,0:T(8,128)(2,1)S(1)}, bf16[128,1024]{1,0:T(8,128)(2,1)S(1)}, u32[]{:S(2)}, u32[]{:S(2)}) %collective-permute-start.2) | collective-permute-done | bytes 262176 | tf_op jit(solution)/shard_map/ppermute | solution.py:42
  88.9 4.4 %collective-permute-done.3.refs_2_.refs_3_ = bf16[128,1024]{1,0:T(8,128)(2,1)S(1)} collective-permute-done((bf16[128,1024]{1,0:T(8,128)(2,1)S(1)}, bf16[128,1024]{1,0:T(8,128)(2,1)S(1)}, u32[]{:S(2)}, u32[]{:S(2)}) %collective-permute-start.3) | collective-permute-done | bytes 262176 | tf_op jit(solution)/shard_map/ppermute | solution.py:42
  93.2 0.0 all-to-all-done.2.refs_0_
  93.2 0.7 shard_map.127.refs_1_.refs_0_
  93.9 1.3 collective-permute-start.5
  95.2 1.9 collective-permute-start.4
  97.2 1.8 reduce-scatter.2.cloned.1.call-done.refs_0_.refs_1_
  99.0 0.9 copy-done.2
  99.9 1.4 shard_map.128
  101.2 8.1 %all-to-all-start.3 = ((f32[32,8,128]{2,1,0:T(8,128)}), f32[32,8,128]{2,1,0:T(8,128)S(1)}, u32[]{:S(2)}, u32[]{:S(2)}) async-start(f32[32,8,128]{2,1,0:T(8,128)} %shard_map.128), calls=%async_computation.4 | async-start | bytes 262144 | tf_op jit(solution)/shard_map/all_to_all | solution.py:31
  109.4 0.0 collective-permute-done.5.refs_1_
  109.4 1.3 shard_map.130
  110.7 1.3 collective-permute-start.6
  112.0 0.0 collective-permute-done.4.refs_4_.refs_3_
  112.0 5.0 %all-to-all-done.3.refs_0_ = f32[32,8,128]{2,1,0:T(8,128)S(1)} async-done(((f32[32,8,128]{2,1,0:T(8,128)}), f32[32,8,128]{2,1,0:T(8,128)S(1)}, u32[]{:S(2)}, u32[]{:S(2)}) %all-to-all-start.3) | async-done | bytes 131104 | tf_op jit(solution)/shard_map/all_to_all | solution.py:31
  117.0 1.2 shard_map.129
  118.2 7.5 %all-to-all-start.4 = ((f32[16,8,128]{2,1,0:T(8,128)}), f32[16,8,128]{2,1,0:T(8,128)S(1)}, u32[]{:S(2)}, u32[]{:S(2)}) async-start(f32[16,8,128]{2,1,0:T(8,128)} %shard_map.129), calls=%async_computation.5 | async-start | bytes 131072 | tf_op jit(solution)/shard_map/all_to_all | solution.py:31
  125.8 1.3 collective-permute-done.6.refs_2_
  127.1 2.2 %shard_map.131.refs_5_ = bf16[16,128,256]{2,1,0:T(8,128)(2,1)} custom-call(s32[5]{0:T(128)S(1)} %copy-done.6, bf16[4,512,256]{2,1,0:T(8,128)(2,1)S(1)} %all-to-all-done.2.refs_0_, bf16[512,256]{1,0:T(8,128)(2,1)S(1)} %collective-permute-done.5.refs_1_, bf16[512,256]{1,0:T(8,128)(2,1)} %collective-permute-done.6.refs_2_), custom_call_target="tpu_custom_call" | custom-call | tf_op jit(solution)/shard_map/pallas_call | solution.py:67
  129.3 8.2 %all-to-all-done.4.refs_0_ = f32[16,8,128]{2,1,0:T(8,128)S(1)} async-done(((f32[16,8,128]{2,1,0:T(8,128)}), f32[16,8,128]{2,1,0:T(8,128)S(1)}, u32[]{:S(2)}, u32[]{:S(2)}) %all-to-all-start.4) | async-done | bytes 65568 | tf_op jit(solution)/shard_map/all_to_all | solution.py:31
  137.5 1.5 shard_map.132
  139.0 4.0 %all-to-all-start.5 = ((bf16[16,128,256]{2,1,0:T(8,128)(2,1)}), bf16[16,128,256]{2,1,0:T(8,128)(2,1)S(1)}, u32[]{:S(2)}, u32[]{:S(2)}) async-start(bf16[16,128,256]{2,1,0:T(8,128)(2,1)} %shard_map.131.refs_5_), calls=%async_computation.6 | async-start | bytes 2097152 | tf_op jit(solution)/shard_map/all_to_all | solution.py:31
  143.1 22.2 %all_gather.7.refs_4_ = bf16[512,512]{1,0:T(8,128)(2,1)S(1)} all-gather(bf16[128,512]{1,0:T(8,128)(2,1)S(1)} %get-tuple-element.40), channel_id=1, replica_groups=mesh['zlo'=4,'y'=4,'zhi'=4,'x'=4,'core'=2] {'zhi'}, dimensions={0}, use_global_device_ids=true | all-gather | bytes 655360 | tf_op jit(solution)/shard_map/all_gather | solution.py:401
  165.2 6.4 %collective-permute-start.7 = (bf16[512,512]{1,0:T(8,128)(2,1)S(1)}, bf16[512,512]{1,0:T(8,128)(2,1)S(1)}, u32[]{:S(2)}, u32[]{:S(2)}) collective-permute-start(bf16[512,512]{1,0:T(8,128)(2,1)S(1)} %all_gather.7.refs_4_), channel_id=1, source_target_pairs={{0,1},{1,0},{2,3},{3,2},{4,5},{5,4},{6,7},{7,6},{8,9},{9,8},{10,11... | collective-permute-start | bytes 1572872 | tf_op jit(solution)/shard_map/ppermute | solution.py:47
  171.6 1.0 shard_map.133.refs_5_
  172.6 0.5 collective-permute-done.7.refs_4_
  173.1 1.8 shard_map.134
  174.9 0.0 all-to-all-done.5.refs_0_
  174.9 3.6 %all-to-all-start.6 = ((bf16[4,128,512]{2,1,0:T(8,128)(2,1)}), bf16[4,128,512]{2,1,0:T(8,128)(2,1)S(1)}, u32[]{:S(2)}, u32[]{:S(2)}) async-start(bf16[4,128,512]{2,1,0:T(8,128)(2,1)} %shard_map.134), calls=%async_computation.7 | async-start | bytes 1048576 | tf_op jit(solution)/shard_map/all_to_all | solution.py:31
  178.5 1.8 shard_map.135
  180.3 7.1 %all-to-all-done.6 = bf16[4,128,512]{2,1,0:T(8,128)(2,1)S(1)} async-done(((bf16[4,128,512]{2,1,0:T(8,128)(2,1)}), bf16[4,128,512]{2,1,0:T(8,128)(2,1)S(1)}, u32[]{:S(2)}, u32[]{:S(2)}) %all-to-all-start.6) | async-done | bytes 524320 | tf_op jit(solution)/shard_map/all_to_all | solution.py:31
  187.4 0.7 reduce_sum.12
  (18 shorter events, 0.0 us)
Async XLA Ops:
  11.7 5.0 %copy-start.8 = (f32[1,4096]{1,0:T(1,128)S(1)}, f32[1,4096]{1,0:T(1,128)}, u32[]{:S(2)}) copy-start(f32[1,4096]{1,0:T(1,128)} %refs_2_.1) | copy-start | bytes 49156
  11.7 5.2 %copy-start.12 = (bf16[128,512]{1,0:T(8,128)(2,1)S(1)}, bf16[128,512]{1,0:T(8,128)(2,1)}, u32[]{:S(2)}) copy-start(bf16[128,512]{1,0:T(8,128)(2,1)} %get-tuple-element.26) | copy-start | bytes 393220
  11.7 36.0 %copy-start.6 = (s32[5]{0:T(128)S(1)}, s32[5]{0:T(128)}, u32[]{:S(2)}) copy-start(s32[5]{0:T(128)} %stack.23.spots) | copy-start | bytes 64
  11.7 36.0 %all-to-all-start = ((bf16[4,128,1536]{2,1,0:T(8,128)(2,1)}), bf16[4,128,1536]{2,1,0:T(8,128)(2,1)S(1)}, u32[]{:S(2)}, u32[]{:S(2)}) async-start(bf16[4,128,1536]{2,1,0:T(8,128)(2,1)} %get-tuple-element.25), calls=%async_computation | async-start | bytes 3145728 | tf_op jit(solution)/shard_map/all_to_all | solution.py:31
  16.7 82.3 %reduce-scatter.2.cloned.1.call-start = ((), (), s32[]{:S(2)}) async-start(), calls=%async_computation.8 | async-start | bytes 655360 | tf_op jit(solution)/shard_map/reduce_scatter | solution.py:329
  48.7 8.0 %collective-permute-start = (bf16[512,512]{1,0:T(8,128)(2,1)S(1)}, bf16[512,512]{1,0:T(8,128)(2,1)S(1)}, u32[]{:S(2)}, u32[]{:S(2)}) collective-permute-start(bf16[512,512]{1,0:T(8,128)(2,1)S(1)} %shard_map.121.refs_2_), channel_id=1, source_target_pairs={{0,1},{1,0},{2,3},{3,2},{4,5},{5,4},{6,7},{7,6},{8,9},{9,8},{10,11... | collective-permute-start | bytes 1572872 | tf_op jit(solution)/shard_map/ppermute | solution.py:47
  58.1 3.8 %collective-permute-start.1 = (bf16[512,512]{1,0:T(8,128)(2,1)S(1)}, bf16[512,512]{1,0:T(8,128)(2,1)S(1)}, u32[]{:S(2)}, u32[]{:S(2)}) collective-permute-start(bf16[512,512]{1,0:T(8,128)(2,1)S(1)} %all_gather.6.refs_1_), channel_id=1, source_target_pairs={{0,1},{1,0},{2,3},{3,2},{4,5},{5,4},{6,7},{7,6},{8,9},{9,8},{10,11... | collective-permute-start | bytes 1572872 | tf_op jit(solution)/shard_map/ppermute | solution.py:47
  72.3 4.3 %copy-start = (bf16[2,1,64,4096]{3,2,1,0:T(8,128)(2,1)S(1)}, bf16[2,1,64,4096]{3,2,1,0:T(8,128)(2,1)}, u32[]{:S(2)}) copy-start(bf16[2,1,64,4096]{3,2,1,0:T(8,128)(2,1)} %param.15) | copy-start | bytes 3145732
  72.3 4.3 %copy-start.7 = (bf16[5,4096]{1,0:T(8,128)(2,1)S(1)}, bf16[5,4096]{1,0:T(8,128)(2,1)}, u32[]{:S(2)}) copy-start(bf16[5,4096]{1,0:T(8,128)(2,1)} %refs_3_.1) | copy-start | bytes 122884
  72.3 4.3 %copy-start.9 = (s32[2,32]{1,0:T(2,128)S(1)}, s32[2,32]{1,0:T(2,128)}, u32[]{:S(2)}) copy-start(s32[2,32]{1,0:T(2,128)} %refs_0_.1) | copy-start | bytes 772
  72.3 20.9 %all-to-all-start.2 = ((bf16[4,512,256]{2,1,0:T(8,128)(2,1)}), bf16[4,512,256]{2,1,0:T(8,128)(2,1)S(1)}, u32[]{:S(2)}, u32[]{:S(2)}) async-start(bf16[4,512,256]{2,1,0:T(8,128)(2,1)} %shard_map.125), calls=%async_computation.3 | async-start | bytes 2097152 | tf_op jit(solution)/shard_map/all_to_all | solution.py:31
  78.2 0.7 copy-start.10
  78.9 16.3 %copy-start.11 = (bf16[128,1024]{1,0:T(8,128)(2,1)S(1)}, bf16[128,1024]{1,0:T(8,128)(2,1)}, u32[]{:S(2)}) copy-start(bf16[128,1024]{1,0:T(8,128)(2,1)} %copy-done.10) | copy-start | bytes 786436
  78.9 9.9 %collective-permute-start.2 = (bf16[128,1024]{1,0:T(8,128)(2,1)S(1)}, bf16[128,1024]{1,0:T(8,128)(2,1)S(1)}, u32[]{:S(2)}, u32[]{:S(2)}) collective-permute-start(bf16[128,1024]{1,0:T(8,128)(2,1)S(1)} %get-tuple-element.35), channel_id=1, source_target_pairs={{0,2},{2,4},{4,6},{6,0},{1,3},{3,5},{5,7},{7,1},{8,10},{10,12},{12... | collective-permute-start | bytes 786440 | tf_op jit(solution)/shard_map/ppermute | solution.py:42
  81.3 12.0 %collective-permute-start.3 = (bf16[128,1024]{1,0:T(8,128)(2,1)S(1)}, bf16[128,1024]{1,0:T(8,128)(2,1)S(1)}, u32[]{:S(2)}, u32[]{:S(2)}) collective-permute-start(bf16[128,1024]{1,0:T(8,128)(2,1)S(1)} %get-tuple-element.36), channel_id=1, source_target_pairs={{0,4},{2,6},{4,0},{6,2},{1,5},{3,7},{5,1},{7,3},{8,12},{10,14},{12... | collective-permute-start | bytes 786440 | tf_op jit(solution)/shard_map/ppermute | solution.py:42
  93.9 15.5 %collective-permute-start.5 = (bf16[512,256]{1,0:T(8,128)(2,1)S(1)}, bf16[512,256]{1,0:T(8,128)(2,1)S(1)}, u32[]{:S(2)}, u32[]{:S(2)}) collective-permute-start(bf16[512,256]{1,0:T(8,128)(2,1)S(1)} %shard_map.127.refs_1_.refs_0_), channel_id=1, source_target_pairs={{128,0},{256,128},{384,256},{129,1},{257,129},{385,257},{130,2},{2... | collective-permute-start | bytes 786440 | tf_op jit(solution)/shard_map/ppermute | solution.py:52
  95.2 16.8 %collective-permute-start.4 = (bf16[128,1024]{1,0:T(8,128)(2,1)S(1)}, bf16[128,1024]{1,0:T(8,128)(2,1)S(1)}, u32[]{:S(2)}, u32[]{:S(2)}) collective-permute-start(bf16[128,1024]{1,0:T(8,128)(2,1)S(1)} %copy-done.11), channel_id=1, source_target_pairs={{0,6},{2,0},{4,2},{6,4},{1,7},{3,1},{5,3},{7,5},{8,14},{10,8},{12,... | collective-permute-start | bytes 786440 | tf_op jit(solution)/shard_map/ppermute | solution.py:42
  99.0 0.9 copy-start.2
  101.2 15.8 %all-to-all-start.3 = ((f32[32,8,128]{2,1,0:T(8,128)}), f32[32,8,128]{2,1,0:T(8,128)S(1)}, u32[]{:S(2)}, u32[]{:S(2)}) async-start(f32[32,8,128]{2,1,0:T(8,128)} %shard_map.128), calls=%async_computation.4 | async-start | bytes 262144 | tf_op jit(solution)/shard_map/all_to_all | solution.py:31
  110.7 16.4 %collective-permute-start.6 = (bf16[512,256]{1,0:T(8,128)(2,1)}, bf16[512,256]{1,0:T(8,128)(2,1)}, u32[]{:S(2)}, u32[]{:S(2)}) collective-permute-start(bf16[512,256]{1,0:T(8,128)(2,1)} %shard_map.130), channel_id=1, source_target_pairs={{256,0},{384,128},{257,1},{385,129},{258,2},{386,130},{259,3},{387... | collective-permute-start | bytes 786440 | tf_op jit(solution)/shard_map/ppermute | solution.py:52
  118.2 19.3 %copy-start.1 = (f32[1,128,512]{2,1,0:T(8,128)S(1)}, f32[1,128,512]{2,1,0:T(8,128)}, u32[]{:S(2)}) copy-start(f32[1,128,512]{2,1,0:T(8,128)} %param.12) | copy-start | bytes 786436
  118.2 19.3 %copy-start.3 = (bf16[128,512]{1,0:T(8,128)(2,1)S(1)}, bf16[128,512]{1,0:T(8,128)(2,1)}, u32[]{:S(2)}) copy-start(bf16[128,512]{1,0:T(8,128)(2,1)} %reduce-scatter.2.cloned.1.call-done.refs_0_.refs_1_) | copy-start | bytes 393220
  118.2 19.3 %copy-start.4 = (f32[1,128,512]{2,1,0:T(8,128)S(1)}, f32[1,128,512]{2,1,0:T(8,128)}, u32[]{:S(2)}) copy-start(f32[1,128,512]{2,1,0:T(8,128)} %param.13) | copy-start | bytes 786436
  118.2 19.3 %copy-start.5 = (f32[1,128,512]{2,1,0:T(8,128)S(1)}, f32[1,128,512]{2,1,0:T(8,128)}, u32[]{:S(2)}) copy-start(f32[1,128,512]{2,1,0:T(8,128)} %param.14) | copy-start | bytes 786436
  118.2 19.3 %all-to-all-start.4 = ((f32[16,8,128]{2,1,0:T(8,128)}), f32[16,8,128]{2,1,0:T(8,128)S(1)}, u32[]{:S(2)}, u32[]{:S(2)}) async-start(f32[16,8,128]{2,1,0:T(8,128)} %shard_map.129), calls=%async_computation.5 | async-start | bytes 131072 | tf_op jit(solution)/shard_map/all_to_all | solution.py:31
  139.0 35.9 %all-to-all-start.5 = ((bf16[16,128,256]{2,1,0:T(8,128)(2,1)}), bf16[16,128,256]{2,1,0:T(8,128)(2,1)S(1)}, u32[]{:S(2)}, u32[]{:S(2)}) async-start(bf16[16,128,256]{2,1,0:T(8,128)(2,1)} %shard_map.131.refs_5_), calls=%async_computation.6 | async-start | bytes 2097152 | tf_op jit(solution)/shard_map/all_to_all | solution.py:31
  165.2 7.9 %collective-permute-start.7 = (bf16[512,512]{1,0:T(8,128)(2,1)S(1)}, bf16[512,512]{1,0:T(8,128)(2,1)S(1)}, u32[]{:S(2)}, u32[]{:S(2)}) collective-permute-start(bf16[512,512]{1,0:T(8,128)(2,1)S(1)} %all_gather.7.refs_4_), channel_id=1, source_target_pairs={{0,1},{1,0},{2,3},{3,2},{4,5},{5,4},{6,7},{7,6},{8,9},{9,8},{10,11... | collective-permute-start | bytes 1572872 | tf_op jit(solution)/shard_map/ppermute | solution.py:47
  174.9 12.5 %all-to-all-start.6 = ((bf16[4,128,512]{2,1,0:T(8,128)(2,1)}), bf16[4,128,512]{2,1,0:T(8,128)(2,1)S(1)}, u32[]{:S(2)}, u32[]{:S(2)}) async-start(bf16[4,128,512]{2,1,0:T(8,128)(2,1)} %shard_map.134), calls=%async_computation.7 | async-start | bytes 1048576 | tf_op jit(solution)/shard_map/all_to_all | solution.py:31
Sparse Core Ops, SparseCore 0:
  60.6 38.3 reduce-scatter.1

commit v8 on v7

--- a/solution.py
+++ b/solution.py
@@ -364,7 +364,7 @@
     fresh_normed = shift(fresh_blocks, "x")
 
     top_shape = shape((all_toks, cores * rows), bf16)
-    top = local(top_kernel, [top_shape], spots, came, after=fresh_normed[1:3])[0]
+    top = local(top_kernel, [top_shape], spots, came, after=fresh_blocks[:1])[0]
     behind = [from_behind(top, "zlo", 1)]
     pair = local(pair_kernel, [top_shape], spots, top, behind[0])[0]
     behind.append(from_behind(pair, "zlo", 2))
@@ -373,10 +373,10 @@
     along = ("zlo", "zhi")
     tile = (8, 128)
     squares = local(
-        squares_kernel, [shape((lax.axis_size(near),) + tile, f32)], spots, grad, after=[top]
+        squares_kernel, [shape((lax.axis_size(near),) + tile, f32)], spots, grad, after=[top] + fresh_normed[1:]
     )[0]
     squares = exchange(squares, near)
-    squares = local(relay_kernel, [shape((lax.axis_size(along),) + tile, f32)], spots, squares, after=fresh_normed)[0]
+    squares = local(relay_kernel, [shape((lax.axis_size(along),) + tile, f32)], spots, squares)[0]
     squares = exchange(squares, along)
     suffix = local(
         functools.partial(suffix_kernel, group),

time: 199 us -> 198 us (level)
  the two profiles are of different devices: /device:TPU:1 before, /device:TPU:56 now
where the time goes in v8:
time: 198 us; the launch traced here: 197 us
  blocking collectives  66.8 us (34%)
  starting transfers between devices  58.4 us (29%)
  waiting for transfers between devices  29.4 us (15%)
  Pallas kernels  25.2 us (13%)
  between operations  14.2 us (7%)
    all_to_all x6, starting transfers between devices, exchange(): return lax.all_to_all(blocks, axis, 0, 0)  39.2 us
    all_gather x1, blocking collectives, per_device(): weights_old = lax.all_gather(weights_old, 'zhi', axis=0, tiled=True)  32.8 us
    all_gather x1, blocking collectives, per_device(): weights_new = lax.all_gather(weights_new, 'zhi', axis=0, tiled=True)  24.6 us
    all_to_all x6, waiting for transfers between devices, exchange(): return lax.all_to_all(blocks, axis, 0, 0)  22.1 us
    pallas_call x15, Pallas kernels, local(): pl.pallas_call(body, out_shape=out_shapes, in_specs=[pl.BlockSpec(memory_...  21.3 us
    all_to_all x1, blocking collectives, exchange(): return lax.all_to_all(blocks, axis, 0, 0)  9.44 us
    ppermute x3, starting transfers between devices, shift(): lax.ppermute(parts[k], axis, [(i, (i + k) % size) for i in range(size)])  9.35 us
    ppermute x3, starting transfers between devices, swap_cores(): return lax.ppermute(block, 'core', [(0, 1), (1, 0)])  5.86 us
  transfers between devices with their start and end apart: 15, of which 9 were waited for; matrix products, arithmetic and copies ran while one was open for 0% of the time, Pallas kernels for 9%

profile of v8, /device:TPU:56, one launch (start us, length us, event | category | flops | bytes accessed | tf_op | source)
XLA Modules:
  0.0 196.7 jit_solution(14585560349258867606)
XLA Ops:
  7.2 0.6 stack.23.spots
  7.8 3.8 %shard_map.120 = (bf16[4,128,1536]{2,1,0:T(8,128)(2,1)}, bf16[128,512]{1,0:T(8,128)(2,1)}) custom-call(s32[5]{0:T(128)} %stack.23.spots, bf16[128,4096]{1,0:T(8,128)(2,1)} %bitcast.42, bf16[128,512]{1,0:T(8,128)(2,1)} %bitcast.44, f32[128,512]{1,0:T(8,128)} %bitcast.35), custom_call_target="tpu_custom_call" | custom-call | tf_op jit(solution)/shard_map/pallas_call | solution.py:111
  11.6 0.0 copy-start.6
  11.6 4.4 %all-to-all-start = ((bf16[4,128,1536]{2,1,0:T(8,128)(2,1)}), bf16[4,128,1536]{2,1,0:T(8,128)(2,1)S(1)}, u32[]{:S(2)}, u32[]{:S(2)}) async-start(bf16[4,128,1536]{2,1,0:T(8,128)(2,1)} %get-tuple-element.25), calls=%async_computation | async-start | bytes 3145728 | tf_op jit(solution)/shard_map/all_to_all | solution.py:31
  16.1 0.0 reduce-scatter.2.cloned.1.call-start
  16.1 0.0 copy-done.8
  16.1 0.1 copy.18.refs_1_
  16.3 0.0 copy-done.10
  16.3 32.8 %all_gather.6.refs_1_ = bf16[512,512]{1,0:T(8,128)(2,1)S(1)} all-gather(bf16[128,512]{1,0:T(8,128)(2,1)S(1)} %copy-done.10), channel_id=1, replica_groups=mesh['zlo'=4,'y'=4,'zhi'=4,'x'=4,'core'=2] {'zhi'}, dimensions={0}, use_global_device_ids=true | all-gather | bytes 655360 | tf_op jit(solution)/shard_map/all_gather | solution.py:308
  49.0 0.0 all-to-all-done
  49.0 0.0 copy-done.6
  49.0 1.0 shard_map.121.refs_2_
  50.1 1.9 collective-permute-start
  52.0 0.1 copy.19.refs_1_
  52.1 1.0 shard_map.122.refs_0_
  53.1 0.7 collective-permute-done.refs_1_
  53.9 1.4 shard_map.123.refs_4_
  55.3 2.0 %collective-permute-start.1 = (bf16[512,512]{1,0:T(8,128)(2,1)S(1)}, bf16[512,512]{1,0:T(8,128)(2,1)S(1)}, u32[]{:S(2)}, u32[]{:S(2)}) collective-permute-start(bf16[512,512]{1,0:T(8,128)(2,1)S(1)} %all_gather.6.refs_1_), channel_id=1, source_target_pairs={{0,1},{1,0},{2,3},{3,2},{4,5},{5,4},{6,7},{7,6},{8,9},{9,8},{10,11... | collective-permute-start | bytes 1572872 | tf_op jit(solution)/shard_map/ppermute | solution.py:47
  57.3 0.0 reduce-scatter.2.cloned.1.call-update
  57.4 1.7 collective-permute-done.1.refs_2_
  59.1 1.5 shard_map.124
  60.6 9.4 %all_to_all.35.refs_2_ = f32[4,8,512]{2,1,0:T(8,128)S(1)} all-to-all(f32[4,8,512]{2,1,0:T(8,128)S(1)} %get-tuple-element.32), channel_id=1, replica_groups=mesh['zlo'=4,'y'=4,'zhi'=4,'x'=4,'core'=2] {'x'}, dimensions={0} | all-to-all | bytes 131072 | tf_op jit(solution)/shard_map/all_to_all | solution.py:31
  70.0 2.0 %shard_map.125 = bf16[4,512,256]{2,1,0:T(8,128)(2,1)} custom-call(s32[5]{0:T(128)S(1)} %copy-done.6, bf16[512,1536]{1,0:T(8,128)(2,1)S(1)} %bitcast.33, f32[512,1024]{1,0:T(8,128)S(1)} %get-tuple-element.31.refs_1_, f32[4,8,512]{2,1,0:T(8,128)S(1)} %all_to_all.35.refs_2_), custom_call_target="tpu_custom_call" | custom-call | tf_op jit(solution)/shard_map/pallas_call | solution.py:67
  72.0 4.8 %all-to-all-start.2 = ((bf16[4,512,256]{2,1,0:T(8,128)(2,1)}), bf16[4,512,256]{2,1,0:T(8,128)(2,1)S(1)}, u32[]{:S(2)}, u32[]{:S(2)}) async-start(bf16[4,512,256]{2,1,0:T(8,128)(2,1)} %shard_map.125), calls=%async_computation.3 | async-start | bytes 2097152 | tf_op jit(solution)/shard_map/all_to_all | solution.py:31
  76.8 0.0 copy-done
  76.8 0.0 copy-done.7
  76.9 0.0 copy-done.9
  76.9 1.6 shard_map.126
  78.5 2.5 %collective-permute-start.2 = (bf16[128,1024]{1,0:T(8,128)(2,1)S(1)}, bf16[128,1024]{1,0:T(8,128)(2,1)S(1)}, u32[]{:S(2)}, u32[]{:S(2)}) collective-permute-start(bf16[128,1024]{1,0:T(8,128)(2,1)S(1)} %get-tuple-element.35), channel_id=1, source_target_pairs={{0,2},{2,4},{4,6},{6,0},{1,3},{3,5},{5,7},{7,1},{8,10},{10,12},{12... | collective-permute-start | bytes 786440 | tf_op jit(solution)/shard_map/ppermute | solution.py:42
  80.9 4.0 %collective-permute-start.3 = (bf16[128,1024]{1,0:T(8,128)(2,1)S(1)}, bf16[128,1024]{1,0:T(8,128)(2,1)S(1)}, u32[]{:S(2)}, u32[]{:S(2)}) collective-permute-start(bf16[128,1024]{1,0:T(8,128)(2,1)S(1)} %get-tuple-element.36), channel_id=1, source_target_pairs={{0,4},{2,6},{4,0},{6,2},{1,5},{3,7},{5,1},{7,3},{8,12},{10,14},{12... | collective-permute-start | bytes 786440 | tf_op jit(solution)/shard_map/ppermute | solution.py:42
  84.9 2.9 %collective-permute-start.4 = (bf16[128,1024]{1,0:T(8,128)(2,1)S(1)}, bf16[128,1024]{1,0:T(8,128)(2,1)S(1)}, u32[]{:S(2)}, u32[]{:S(2)}) collective-permute-start(bf16[128,1024]{1,0:T(8,128)(2,1)S(1)} %get-tuple-element.37), channel_id=1, source_target_pairs={{0,6},{2,0},{4,2},{6,4},{1,7},{3,1},{5,3},{7,5},{8,14},{10,8},{12,... | collective-permute-start | bytes 786440 | tf_op jit(solution)/shard_map/ppermute | solution.py:42
  87.8 0.9 all-to-all-done.2.refs_0_
  88.8 0.7 shard_map.127.refs_1_.refs_0_
  89.4 2.5 %collective-permute-start.5 = (bf16[512,256]{1,0:T(8,128)(2,1)S(1)}, bf16[512,256]{1,0:T(8,128)(2,1)S(1)}, u32[]{:S(2)}, u32[]{:S(2)}) collective-permute-start(bf16[512,256]{1,0:T(8,128)(2,1)S(1)} %shard_map.127.refs_1_.refs_0_), channel_id=1, source_target_pairs={{128,0},{256,128},{384,256},{129,1},{257,129},{385,257},{130,2},{2... | collective-permute-start | bytes 786440 | tf_op jit(solution)/shard_map/ppermute | solution.py:52
  92.0 1.6 collective-permute-done.2.refs_2_.refs_1_
  93.5 0.0 collective-permute-done.3.refs_3_.refs_2_
  93.5 2.5 %collective-permute-done.4.refs_4_.refs_3_ = bf16[128,1024]{1,0:T(8,128)(2,1)S(1)} collective-permute-done((bf16[128,1024]{1,0:T(8,128)(2,1)S(1)}, bf16[128,1024]{1,0:T(8,128)(2,1)S(1)}, u32[]{:S(2)}, u32[]{:S(2)}) %collective-permute-start.4) | collective-permute-done | bytes 262176 | tf_op jit(solution)/shard_map/ppermute | solution.py:42
  96.0 0.9 copy-done.2
  96.9 1.4 shard_map.128
  98.3 7.1 %all-to-all-start.3 = ((f32[32,8,128]{2,1,0:T(8,128)}), f32[32,8,128]{2,1,0:T(8,128)S(1)}, u32[]{:S(2)}, u32[]{:S(2)}) async-start(f32[32,8,128]{2,1,0:T(8,128)} %shard_map.128), calls=%async_computation.4 | async-start | bytes 262144 | tf_op jit(solution)/shard_map/all_to_all | solution.py:31
  105.5 0.0 collective-permute-done.5.refs_1_
  105.5 1.3 shard_map.130
  106.8 1.4 collective-permute-start.6
  108.2 3.1 %all-to-all-done.3.refs_0_ = f32[32,8,128]{2,1,0:T(8,128)S(1)} async-done(((f32[32,8,128]{2,1,0:T(8,128)}), f32[32,8,128]{2,1,0:T(8,128)S(1)}, u32[]{:S(2)}, u32[]{:S(2)}) %all-to-all-start.3) | async-done | bytes 131104 | tf_op jit(solution)/shard_map/all_to_all | solution.py:31
  111.3 1.2 shard_map.129
  112.5 9.8 %all-to-all-start.4 = ((f32[16,8,128]{2,1,0:T(8,128)}), f32[16,8,128]{2,1,0:T(8,128)S(1)}, u32[]{:S(2)}, u32[]{:S(2)}) async-start(f32[16,8,128]{2,1,0:T(8,128)} %shard_map.129), calls=%async_computation.5 | async-start | bytes 131072 | tf_op jit(solution)/shard_map/all_to_all | solution.py:31
  122.3 0.0 collective-permute-done.6.refs_2_
  122.3 2.2 %shard_map.131.refs_5_ = bf16[16,128,256]{2,1,0:T(8,128)(2,1)} custom-call(s32[5]{0:T(128)S(1)} %copy-done.6, bf16[4,512,256]{2,1,0:T(8,128)(2,1)S(1)} %all-to-all-done.2.refs_0_, bf16[512,256]{1,0:T(8,128)(2,1)S(1)} %collective-permute-done.5.refs_1_, bf16[512,256]{1,0:T(8,128)(2,1)} %collective-permute-done.6.refs_2_), custom_call_target="tpu_custom_call" | custom-call | tf_op jit(solution)/shard_map/pallas_call | solution.py:67
  124.5 10.0 %all-to-all-done.4.refs_0_ = f32[16,8,128]{2,1,0:T(8,128)S(1)} async-done(((f32[16,8,128]{2,1,0:T(8,128)}), f32[16,8,128]{2,1,0:T(8,128)S(1)}, u32[]{:S(2)}, u32[]{:S(2)}) %all-to-all-start.4) | async-done | bytes 65568 | tf_op jit(solution)/shard_map/all_to_all | solution.py:31
  134.5 0.0 copy-done.1
  134.5 0.0 copy-done.3
  134.5 0.0 copy-done.4
  134.5 1.5 shard_map.132
  136.0 5.8 %all-to-all-start.5 = ((bf16[16,128,256]{2,1,0:T(8,128)(2,1)}), bf16[16,128,256]{2,1,0:T(8,128)(2,1)S(1)}, u32[]{:S(2)}, u32[]{:S(2)}) async-start(bf16[16,128,256]{2,1,0:T(8,128)(2,1)} %shard_map.131.refs_5_), calls=%async_computation.6 | async-start | bytes 2097152 | tf_op jit(solution)/shard_map/all_to_all | solution.py:31
  141.8 24.6 %all_gather.7.refs_4_ = bf16[512,512]{1,0:T(8,128)(2,1)S(1)} all-gather(bf16[128,512]{1,0:T(8,128)(2,1)S(1)} %get-tuple-element.40), channel_id=1, replica_groups=mesh['zlo'=4,'y'=4,'zhi'=4,'x'=4,'core'=2] {'zhi'}, dimensions={0}, use_global_device_ids=true | all-gather | bytes 655360 | tf_op jit(solution)/shard_map/all_gather | solution.py:401
  166.5 1.9 collective-permute-start.7
  168.4 1.0 shard_map.133.refs_5_
  169.4 0.9 collective-permute-done.7.refs_4_
  170.3 1.8 shard_map.134
  172.1 0.0 all-to-all-done.5.refs_0_
  172.1 7.2 %all-to-all-start.6 = ((bf16[4,128,512]{2,1,0:T(8,128)(2,1)}), bf16[4,128,512]{2,1,0:T(8,128)(2,1)S(1)}, u32[]{:S(2)}, u32[]{:S(2)}) async-start(bf16[4,128,512]{2,1,0:T(8,128)(2,1)} %shard_map.134), calls=%async_computation.7 | async-start | bytes 1048576 | tf_op jit(solution)/shard_map/all_to_all | solution.py:31
  179.3 1.8 shard_map.135
  181.1 8.0 %all-to-all-done.6 = bf16[4,128,512]{2,1,0:T(8,128)(2,1)S(1)} async-done(((bf16[4,128,512]{2,1,0:T(8,128)(2,1)}), bf16[4,128,512]{2,1,0:T(8,128)(2,1)S(1)}, u32[]{:S(2)}, u32[]{:S(2)}) %all-to-all-start.6) | async-done | bytes 524320 | tf_op jit(solution)/shard_map/all_to_all | solution.py:31
  189.1 0.7 reduce_sum.12
  (14 shorter events, 0.0 us)
Async XLA Ops:
  11.6 4.5 %copy-start.8 = (f32[1,4096]{1,0:T(1,128)S(1)}, f32[1,4096]{1,0:T(1,128)}, u32[]{:S(2)}) copy-start(f32[1,4096]{1,0:T(1,128)} %refs_2_.1) | copy-start | bytes 49156
  11.6 4.6 %copy-start.10 = (bf16[128,512]{1,0:T(8,128)(2,1)S(1)}, bf16[128,512]{1,0:T(8,128)(2,1)}, u32[]{:S(2)}) copy-start(bf16[128,512]{1,0:T(8,128)(2,1)} %get-tuple-element.26) | copy-start | bytes 393220
  11.6 37.4 %copy-start.6 = (s32[5]{0:T(128)S(1)}, s32[5]{0:T(128)}, u32[]{:S(2)}) copy-start(s32[5]{0:T(128)} %stack.23.spots) | copy-start | bytes 64
  11.6 37.4 %all-to-all-start = ((bf16[4,128,1536]{2,1,0:T(8,128)(2,1)}), bf16[4,128,1536]{2,1,0:T(8,128)(2,1)S(1)}, u32[]{:S(2)}, u32[]{:S(2)}) async-start(bf16[4,128,1536]{2,1,0:T(8,128)(2,1)} %get-tuple-element.25), calls=%async_computation | async-start | bytes 3145728 | tf_op jit(solution)/shard_map/all_to_all | solution.py:31
  16.1 80.0 %reduce-scatter.2.cloned.1.call-start = ((), (), s32[]{:S(2)}) async-start(), calls=%async_computation.8 | async-start | bytes 655360 | tf_op jit(solution)/shard_map/reduce_scatter | solution.py:329
  50.1 3.8 %collective-permute-start = (bf16[512,512]{1,0:T(8,128)(2,1)S(1)}, bf16[512,512]{1,0:T(8,128)(2,1)S(1)}, u32[]{:S(2)}, u32[]{:S(2)}) collective-permute-start(bf16[512,512]{1,0:T(8,128)(2,1)S(1)} %shard_map.121.refs_2_), channel_id=1, source_target_pairs={{0,1},{1,0},{2,3},{3,2},{4,5},{5,4},{6,7},{7,6},{8,9},{9,8},{10,11... | collective-permute-start | bytes 1572872 | tf_op jit(solution)/shard_map/ppermute | solution.py:47
  55.3 3.8 %collective-permute-start.1 = (bf16[512,512]{1,0:T(8,128)(2,1)S(1)}, bf16[512,512]{1,0:T(8,128)(2,1)S(1)}, u32[]{:S(2)}, u32[]{:S(2)}) collective-permute-start(bf16[512,512]{1,0:T(8,128)(2,1)S(1)} %all_gather.6.refs_1_), channel_id=1, source_target_pairs={{0,1},{1,0},{2,3},{3,2},{4,5},{5,4},{6,7},{7,6},{8,9},{9,8},{10,11... | collective-permute-start | bytes 1572872 | tf_op jit(solution)/shard_map/ppermute | solution.py:47
  72.0 4.8 %copy-start = (bf16[2,1,64,4096]{3,2,1,0:T(8,128)(2,1)S(1)}, bf16[2,1,64,4096]{3,2,1,0:T(8,128)(2,1)}, u32[]{:S(2)}) copy-start(bf16[2,1,64,4096]{3,2,1,0:T(8,128)(2,1)} %param.15) | copy-start | bytes 3145732
  72.0 4.8 %copy-start.7 = (bf16[5,4096]{1,0:T(8,128)(2,1)S(1)}, bf16[5,4096]{1,0:T(8,128)(2,1)}, u32[]{:S(2)}) copy-start(bf16[5,4096]{1,0:T(8,128)(2,1)} %refs_3_.1) | copy-start | bytes 122884
  72.0 4.8 %copy-start.9 = (s32[2,32]{1,0:T(2,128)S(1)}, s32[2,32]{1,0:T(2,128)}, u32[]{:S(2)}) copy-start(s32[2,32]{1,0:T(2,128)} %refs_0_.1) | copy-start | bytes 772
  72.0 16.7 %all-to-all-start.2 = ((bf16[4,512,256]{2,1,0:T(8,128)(2,1)}), bf16[4,512,256]{2,1,0:T(8,128)(2,1)S(1)}, u32[]{:S(2)}, u32[]{:S(2)}) async-start(bf16[4,512,256]{2,1,0:T(8,128)(2,1)} %shard_map.125), calls=%async_computation.3 | async-start | bytes 2097152 | tf_op jit(solution)/shard_map/all_to_all | solution.py:31
  78.5 15.1 %collective-permute-start.2 = (bf16[128,1024]{1,0:T(8,128)(2,1)S(1)}, bf16[128,1024]{1,0:T(8,128)(2,1)S(1)}, u32[]{:S(2)}, u32[]{:S(2)}) collective-permute-start(bf16[128,1024]{1,0:T(8,128)(2,1)S(1)} %get-tuple-element.35), channel_id=1, source_target_pairs={{0,2},{2,4},{4,6},{6,0},{1,3},{3,5},{5,7},{7,1},{8,10},{10,12},{12... | collective-permute-start | bytes 786440 | tf_op jit(solution)/shard_map/ppermute | solution.py:42
  80.9 12.6 %collective-permute-start.3 = (bf16[128,1024]{1,0:T(8,128)(2,1)S(1)}, bf16[128,1024]{1,0:T(8,128)(2,1)S(1)}, u32[]{:S(2)}, u32[]{:S(2)}) collective-permute-start(bf16[128,1024]{1,0:T(8,128)(2,1)S(1)} %get-tuple-element.36), channel_id=1, source_target_pairs={{0,4},{2,6},{4,0},{6,2},{1,5},{3,7},{5,1},{7,3},{8,12},{10,14},{12... | collective-permute-start | bytes 786440 | tf_op jit(solution)/shard_map/ppermute | solution.py:42
  84.9 11.1 %collective-permute-start.4 = (bf16[128,1024]{1,0:T(8,128)(2,1)S(1)}, bf16[128,1024]{1,0:T(8,128)(2,1)S(1)}, u32[]{:S(2)}, u32[]{:S(2)}) collective-permute-start(bf16[128,1024]{1,0:T(8,128)(2,1)S(1)} %get-tuple-element.37), channel_id=1, source_target_pairs={{0,6},{2,0},{4,2},{6,4},{1,7},{3,1},{5,3},{7,5},{8,14},{10,8},{12,... | collective-permute-start | bytes 786440 | tf_op jit(solution)/shard_map/ppermute | solution.py:42
  89.4 16.0 %collective-permute-start.5 = (bf16[512,256]{1,0:T(8,128)(2,1)S(1)}, bf16[512,256]{1,0:T(8,128)(2,1)S(1)}, u32[]{:S(2)}, u32[]{:S(2)}) collective-permute-start(bf16[512,256]{1,0:T(8,128)(2,1)S(1)} %shard_map.127.refs_1_.refs_0_), channel_id=1, source_target_pairs={{128,0},{256,128},{384,256},{129,1},{257,129},{385,257},{130,2},{2... | collective-permute-start | bytes 786440 | tf_op jit(solution)/shard_map/ppermute | solution.py:52
  96.0 0.9 copy-start.2
  98.3 13.0 %all-to-all-start.3 = ((f32[32,8,128]{2,1,0:T(8,128)}), f32[32,8,128]{2,1,0:T(8,128)S(1)}, u32[]{:S(2)}, u32[]{:S(2)}) async-start(f32[32,8,128]{2,1,0:T(8,128)} %shard_map.128), calls=%async_computation.4 | async-start | bytes 262144 | tf_op jit(solution)/shard_map/all_to_all | solution.py:31
  106.8 27.8 %copy-start.1 = (f32[1,128,512]{2,1,0:T(8,128)S(1)}, f32[1,128,512]{2,1,0:T(8,128)}, u32[]{:S(2)}) copy-start(f32[1,128,512]{2,1,0:T(8,128)} %param.12) | copy-start | bytes 786436
  106.8 27.8 %copy-start.3 = (bf16[128,512]{1,0:T(8,128)(2,1)S(1)}, bf16[128,512]{1,0:T(8,128)(2,1)}, u32[]{:S(2)}) copy-start(bf16[128,512]{1,0:T(8,128)(2,1)} %reduce-scatter.2.cloned.1.call-done.refs_0_.refs_1_) | copy-start | bytes 393220
  106.8 27.8 %copy-start.4 = (f32[1,128,512]{2,1,0:T(8,128)S(1)}, f32[1,128,512]{2,1,0:T(8,128)}, u32[]{:S(2)}) copy-start(f32[1,128,512]{2,1,0:T(8,128)} %param.13) | copy-start | bytes 786436
  106.8 27.8 %copy-start.5 = (f32[1,128,512]{2,1,0:T(8,128)S(1)}, f32[1,128,512]{2,1,0:T(8,128)}, u32[]{:S(2)}) copy-start(f32[1,128,512]{2,1,0:T(8,128)} %param.14) | copy-start | bytes 786436
  106.8 15.6 %collective-permute-start.6 = (bf16[512,256]{1,0:T(8,128)(2,1)}, bf16[512,256]{1,0:T(8,128)(2,1)}, u32[]{:S(2)}, u32[]{:S(2)}) collective-permute-start(bf16[512,256]{1,0:T(8,128)(2,1)} %shard_map.130), channel_id=1, source_target_pairs={{256,0},{384,128},{257,1},{385,129},{258,2},{386,130},{259,3},{387... | collective-permute-start | bytes 786440 | tf_op jit(solution)/shard_map/ppermute | solution.py:52
  112.5 22.0 %all-to-all-start.4 = ((f32[16,8,128]{2,1,0:T(8,128)}), f32[16,8,128]{2,1,0:T(8,128)S(1)}, u32[]{:S(2)}, u32[]{:S(2)}) async-start(f32[16,8,128]{2,1,0:T(8,128)} %shard_map.129), calls=%async_computation.5 | async-start | bytes 131072 | tf_op jit(solution)/shard_map/all_to_all | solution.py:31
  136.0 36.1 %all-to-all-start.5 = ((bf16[16,128,256]{2,1,0:T(8,128)(2,1)}), bf16[16,128,256]{2,1,0:T(8,128)(2,1)S(1)}, u32[]{:S(2)}, u32[]{:S(2)}) async-start(bf16[16,128,256]{2,1,0:T(8,128)(2,1)} %shard_map.131.refs_5_), calls=%async_computation.6 | async-start | bytes 2097152 | tf_op jit(solution)/shard_map/all_to_all | solution.py:31
  166.5 3.8 %collective-permute-start.7 = (bf16[512,512]{1,0:T(8,128)(2,1)S(1)}, bf16[512,512]{1,0:T(8,128)(2,1)S(1)}, u32[]{:S(2)}, u32[]{:S(2)}) collective-permute-start(bf16[512,512]{1,0:T(8,128)(2,1)S(1)} %all_gather.7.refs_4_), channel_id=1, source_target_pairs={{0,1},{1,0},{2,3},{3,2},{4,5},{5,4},{6,7},{7,6},{8,9},{9,8},{10,11... | collective-permute-start | bytes 1572872 | tf_op jit(solution)/shard_map/ppermute | solution.py:47
  172.1 17.0 %all-to-all-start.6 = ((bf16[4,128,512]{2,1,0:T(8,128)(2,1)}), bf16[4,128,512]{2,1,0:T(8,128)(2,1)S(1)}, u32[]{:S(2)}, u32[]{:S(2)}) async-start(bf16[4,128,512]{2,1,0:T(8,128)(2,1)} %shard_map.134), calls=%async_computation.7 | async-start | bytes 1048576 | tf_op jit(solution)/shard_map/all_to_all | solution.py:31
Sparse Core Ops, SparseCore 0:
  57.5 37.5 reduce-scatter.1

commit v9 on v8

--- a/solution.py
+++ b/solution.py
@@ -22,6 +22,7 @@
 axes = ("zlo", "y", "zhi", "x", "core")
 section = ("zlo", "y")
 dp = ("zhi", "x", "core")
+near = ("x", "core")
 heavy = 2 * 10**10
 f32 = jnp.float32
 bf16 = jnp.bfloat16
@@ -325,7 +326,6 @@
         after=[other],
     )[0]
     partial = local(add_kernel, [shape((half, kvw), bf16)], spots, own, came)[0]
-    partial, weights_old = together(partial, weights_old)
     grad = lax.psum_scatter(partial, "zhi", scatter_dimension=0, tiled=True)
     weights_other = swap_cores(weights_old)
 
@@ -369,15 +369,15 @@
     pair = local(pair_kernel, [top_shape], spots, top, behind[0])[0]
     behind.append(from_behind(pair, "zlo", 2))
 
-    near = ("y", "x", "core")
-    along = ("zlo", "zhi")
+    first_axes = ("zlo", "zhi")
+    last_axes = ("y", "x", "core")
     tile = (8, 128)
     squares = local(
-        squares_kernel, [shape((lax.axis_size(near),) + tile, f32)], spots, grad, after=[top] + fresh_normed[1:]
-    )[0]
-    squares = exchange(squares, near)
-    squares = local(relay_kernel, [shape((lax.axis_size(along),) + tile, f32)], spots, squares)[0]
-    squares = exchange(squares, along)
+        squares_kernel, [shape((lax.axis_size(first_axes),) + tile, f32)], spots, grad, after=[top] + fresh_normed[1:]
+    )[0]
+    squares = exchange(squares, first_axes)
+    squares = local(relay_kernel, [shape((lax.axis_size(last_axes),) + tile, f32)], spots, squares)[0]
+    squares = exchange(squares, last_axes)
     suffix = local(
         functools.partial(suffix_kernel, group),
         [shape((layers_y * group, toks, cores * rows), bf16)],

time: 198 us -> 195 us (0.985)
  the two profiles are of different devices: /device:TPU:56 before, /device:TPU:1 now
where the time goes in v9:
time: 195 us; the launch traced here: 192 us
  blocking collectives  58.4 us (30%)
  starting transfers between devices  57.5 us (29%)
  waiting for transfers between devices  33.3 us (17%)
  Pallas kernels  25.7 us (13%)
  between operations  14.3 us (7%)
    all_to_all x6, starting transfers between devices, exchange(): return lax.all_to_all(blocks, axis, 0, 0)  34.5 us
    all_gather x1, blocking collectives, per_device(): weights_old = lax.all_gather(weights_old, 'zhi', axis=0, tiled=True)  30.9 us
    all_to_all x6, waiting for transfers between devices, exchange(): return lax.all_to_all(blocks, axis, 0, 0)  24.3 us
    pallas_call x15, Pallas kernels, local(): pl.pallas_call(body, out_shape=out_shapes, in_specs=[pl.BlockSpec(memory_...  21.9 us
    all_gather x1, blocking collectives, per_device(): weights_new = lax.all_gather(weights_new, 'zhi', axis=0, tiled=True)  20.7 us
    ppermute x3, starting transfers between devices, swap_cores(): return lax.ppermute(block, 'core', [(0, 1), (1, 0)])  11.5 us
    ppermute x3, starting transfers between devices, shift(): lax.ppermute(parts[k], axis, [(i, (i + k) % size) for i in range(size)])  8.77 us
    all_to_all x1, blocking collectives, exchange(): return lax.all_to_all(blocks, axis, 0, 0)  6.84 us
  transfers between devices with their start and end apart: 15, of which 8 were waited for; matrix products, arithmetic and copies ran while one was open for 0% of the time, Pallas kernels for 10%

profile of v9, /device:TPU:1, one launch (start us, length us, event | category | flops | bytes accessed | tf_op | source)
XLA Modules:
  0.0 191.7 jit_solution(13658585861039651352)
XLA Ops:
  7.2 0.6 stack.23.spots
  7.8 3.8 %shard_map.120 = (bf16[4,128,1536]{2,1,0:T(8,128)(2,1)}, bf16[128,512]{1,0:T(8,128)(2,1)}) custom-call(s32[5]{0:T(128)} %stack.23.spots, bf16[128,4096]{1,0:T(8,128)(2,1)} %bitcast.42, bf16[128,512]{1,0:T(8,128)(2,1)} %bitcast.44, f32[128,512]{1,0:T(8,128)} %bitcast.35), custom_call_target="tpu_custom_call" | custom-call | tf_op jit(solution)/shard_map/pallas_call | solution.py:112
  11.6 0.0 copy-start.6
  11.6 5.0 %all-to-all-start = ((bf16[4,128,1536]{2,1,0:T(8,128)(2,1)}), bf16[4,128,1536]{2,1,0:T(8,128)(2,1)S(1)}, u32[]{:S(2)}, u32[]{:S(2)}) async-start(bf16[4,128,1536]{2,1,0:T(8,128)(2,1)} %get-tuple-element.23), calls=%async_computation | async-start | bytes 3145728 | tf_op jit(solution)/shard_map/all_to_all | solution.py:32
  16.6 0.0 reduce-scatter.2.cloned.1.call-start
  16.6 0.0 copy-done.8
  16.7 0.1 copy.18.refs_1_
  16.8 0.0 copy-done.10
  16.8 30.9 %all_gather.6.refs_1_ = bf16[512,512]{1,0:T(8,128)(2,1)S(1)} all-gather(bf16[128,512]{1,0:T(8,128)(2,1)S(1)} %copy-done.10), channel_id=1, replica_groups=mesh['zlo'=4,'y'=4,'zhi'=4,'x'=4,'core'=2] {'zhi'}, dimensions={0}, use_global_device_ids=true | all-gather | bytes 655360 | tf_op jit(solution)/shard_map/all_gather | solution.py:309
  47.7 0.0 all-to-all-done
  47.7 0.0 copy-done.6
  47.7 1.0 shard_map.121.refs_2_
  48.7 6.5 %collective-permute-start.1 = (bf16[512,512]{1,0:T(8,128)(2,1)S(1)}, bf16[512,512]{1,0:T(8,128)(2,1)S(1)}, u32[]{:S(2)}, u32[]{:S(2)}) collective-permute-start(bf16[512,512]{1,0:T(8,128)(2,1)S(1)} %shard_map.121.refs_2_), channel_id=1, source_target_pairs={{0,1},{1,0},{2,3},{3,2},{4,5},{5,4},{6,7},{7,6},{8,9},{9,8},{10,11... | collective-permute-start | bytes 1572872 | tf_op jit(solution)/shard_map/ppermute | solution.py:48
  55.2 1.9 %collective-permute-start = (bf16[512,512]{1,0:T(8,128)(2,1)S(1)}, bf16[512,512]{1,0:T(8,128)(2,1)}, u32[]{:S(2)}, u32[]{:S(2)}) collective-permute-start(bf16[512,512]{1,0:T(8,128)(2,1)S(1)} %all_gather.6.refs_1_), channel_id=1, source_target_pairs={{0,1},{1,0},{2,3},{3,2},{4,5},{5,4},{6,7},{7,6},{8,9},{9,8},{10,11... | collective-permute-start | bytes 1572872 | tf_op jit(solution)/shard_map/ppermute | solution.py:48
  57.1 0.1 copy.19.refs_1_
  57.3 1.0 shard_map.122.refs_0_
  58.3 0.0 collective-permute-done.1.refs_1_
  58.3 1.5 shard_map.123.refs_4_
  59.7 0.0 reduce-scatter.2.cloned.1.call-update
  59.8 0.0 collective-permute-done.refs_2_
  59.8 2.0 %shard_map.124 = (f32[512,1024]{1,0:T(8,128)S(1)}, f32[4,8,512]{2,1,0:T(8,128)S(1)}) custom-call(s32[5]{0:T(128)S(1)} %copy-done.6, bf16[512,1536]{1,0:T(8,128)(2,1)S(1)} %bitcast.32, bf16[512,512]{1,0:T(8,128)(2,1)S(1)} %all_gather.6.refs_1_, bf16[512,512]{1,0:T(8,128)(2,1)} %collective-permute-done.refs_2_, f32[1,1024]{1,0:T(1,128)S(1)} %bitcast.40, ...), custom_call_target="tpu_custom_call" | custom-call | tf_op jit(solution)/shard_map/pallas_call | solution.py:68
  61.8 6.8 %all_to_all.35.refs_2_ = f32[4,8,512]{2,1,0:T(8,128)S(1)} all-to-all(f32[4,8,512]{2,1,0:T(8,128)S(1)} %get-tuple-element.28), channel_id=1, replica_groups=mesh['zlo'=4,'y'=4,'zhi'=4,'x'=4,'core'=2] {'x'}, dimensions={0} | all-to-all | bytes 131072 | tf_op jit(solution)/shard_map/all_to_all | solution.py:32
  68.6 2.0 %shard_map.125 = bf16[4,512,256]{2,1,0:T(8,128)(2,1)} custom-call(s32[5]{0:T(128)S(1)} %copy-done.6, bf16[512,1536]{1,0:T(8,128)(2,1)S(1)} %bitcast.33, f32[512,1024]{1,0:T(8,128)S(1)} %get-tuple-element.27.refs_1_, f32[4,8,512]{2,1,0:T(8,128)S(1)} %all_to_all.35.refs_2_), custom_call_target="tpu_custom_call" | custom-call | tf_op jit(solution)/shard_map/pallas_call | solution.py:68
  70.6 4.3 %all-to-all-start.2 = ((bf16[4,512,256]{2,1,0:T(8,128)(2,1)}), bf16[4,512,256]{2,1,0:T(8,128)(2,1)S(1)}, u32[]{:S(2)}, u32[]{:S(2)}) async-start(bf16[4,512,256]{2,1,0:T(8,128)(2,1)} %shard_map.125), calls=%async_computation.3 | async-start | bytes 2097152 | tf_op jit(solution)/shard_map/all_to_all | solution.py:32
  75.0 0.0 copy-done
  75.0 0.0 copy-done.7
  75.0 0.0 copy-done.9
  75.0 1.6 shard_map.126
  76.6 2.2 %collective-permute-start.2 = (bf16[128,1024]{1,0:T(8,128)(2,1)S(1)}, bf16[128,1024]{1,0:T(8,128)(2,1)S(1)}, u32[]{:S(2)}, u32[]{:S(2)}) collective-permute-start(bf16[128,1024]{1,0:T(8,128)(2,1)S(1)} %get-tuple-element.31), channel_id=1, source_target_pairs={{0,2},{2,4},{4,6},{6,0},{1,3},{3,5},{5,7},{7,1},{8,10},{10,12},{12... | collective-permute-start | bytes 786440 | tf_op jit(solution)/shard_map/ppermute | solution.py:43
  78.8 3.7 %collective-permute-start.3 = (bf16[128,1024]{1,0:T(8,128)(2,1)S(1)}, bf16[128,1024]{1,0:T(8,128)(2,1)S(1)}, u32[]{:S(2)}, u32[]{:S(2)}) collective-permute-start(bf16[128,1024]{1,0:T(8,128)(2,1)S(1)} %get-tuple-element.32), channel_id=1, source_target_pairs={{0,4},{2,6},{4,0},{6,2},{1,5},{3,7},{5,1},{7,3},{8,12},{10,14},{12... | collective-permute-start | bytes 786440 | tf_op jit(solution)/shard_map/ppermute | solution.py:43
  82.5 2.9 %collective-permute-start.4 = (bf16[128,1024]{1,0:T(8,128)(2,1)S(1)}, bf16[128,1024]{1,0:T(8,128)(2,1)S(1)}, u32[]{:S(2)}, u32[]{:S(2)}) collective-permute-start(bf16[128,1024]{1,0:T(8,128)(2,1)S(1)} %get-tuple-element.33), channel_id=1, source_target_pairs={{0,6},{2,0},{4,2},{6,4},{1,7},{3,1},{5,3},{7,5},{8,14},{10,8},{12,... | collective-permute-start | bytes 786440 | tf_op jit(solution)/shard_map/ppermute | solution.py:43
  85.4 2.8 %all-to-all-done.2.refs_0_ = bf16[4,512,256]{2,1,0:T(8,128)(2,1)S(1)} async-done(((bf16[4,512,256]{2,1,0:T(8,128)(2,1)}), bf16[4,512,256]{2,1,0:T(8,128)(2,1)S(1)}, u32[]{:S(2)}, u32[]{:S(2)}) %all-to-all-start.2) | async-done | bytes 1048608 | tf_op jit(solution)/shard_map/all_to_all | solution.py:32
  88.2 0.7 shard_map.127.refs_1_.refs_0_
  88.8 1.3 collective-permute-start.5
  90.1 0.0 collective-permute-done.2.refs_2_.refs_1_
  90.2 0.5 collective-permute-done.3.refs_3_.refs_2_
  90.7 3.5 %collective-permute-done.4.refs_4_.refs_3_ = bf16[128,1024]{1,0:T(8,128)(2,1)S(1)} collective-permute-done((bf16[128,1024]{1,0:T(8,128)(2,1)S(1)}, bf16[128,1024]{1,0:T(8,128)(2,1)S(1)}, u32[]{:S(2)}, u32[]{:S(2)}) %collective-permute-start.4) | collective-permute-done | bytes 262176 | tf_op jit(solution)/shard_map/ppermute | solution.py:43
  94.1 4.5 %reduce-scatter.2.cloned.1.call-done.refs_0_.refs_1_ = bf16[128,512]{1,0:T(8,128)(2,1)} async-done(((bf16[512,512]{1,0:T(8,128)(2,1)}), bf16[128,512]{1,0:T(8,128)(2,1)}) %reduce-scatter.2.cloned.1.call-update) | async-done | bytes 131088 | tf_op jit(solution)/shard_map/reduce_scatter | solution.py:329
  98.6 0.9 copy-done.2
  99.5 1.4 shard_map.128
  100.9 5.3 %all-to-all-start.3 = ((f32[16,8,128]{2,1,0:T(8,128)}), f32[16,8,128]{2,1,0:T(8,128)S(1)}, u32[]{:S(2)}, u32[]{:S(2)}) async-start(f32[16,8,128]{2,1,0:T(8,128)} %shard_map.128), calls=%async_computation.4 | async-start | bytes 131072 | tf_op jit(solution)/shard_map/all_to_all | solution.py:32
  106.2 0.0 collective-permute-done.5.refs_1_
  106.2 1.3 shard_map.130
  107.5 1.4 collective-permute-start.6
  108.9 8.9 %all-to-all-done.3.refs_0_ = f32[16,8,128]{2,1,0:T(8,128)S(1)} async-done(((f32[16,8,128]{2,1,0:T(8,128)}), f32[16,8,128]{2,1,0:T(8,128)S(1)}, u32[]{:S(2)}, u32[]{:S(2)}) %all-to-all-start.3) | async-done | bytes 65568 | tf_op jit(solution)/shard_map/all_to_all | solution.py:32
  117.8 1.2 shard_map.129
  119.1 11.1 %all-to-all-start.4 = ((f32[32,8,128]{2,1,0:T(8,128)}), f32[32,8,128]{2,1,0:T(8,128)S(1)}, u32[]{:S(2)}, u32[]{:S(2)}) async-start(f32[32,8,128]{2,1,0:T(8,128)} %shard_map.129), calls=%async_computation.5 | async-start | bytes 262144 | tf_op jit(solution)/shard_map/all_to_all | solution.py:32
  130.2 0.0 collective-permute-done.6.refs_2_
  130.2 2.2 %shard_map.131.refs_5_ = bf16[16,128,256]{2,1,0:T(8,128)(2,1)} custom-call(s32[5]{0:T(128)S(1)} %copy-done.6, bf16[4,512,256]{2,1,0:T(8,128)(2,1)S(1)} %all-to-all-done.2.refs_0_, bf16[512,256]{1,0:T(8,128)(2,1)S(1)} %collective-permute-done.5.refs_1_, bf16[512,256]{1,0:T(8,128)(2,1)} %collective-permute-done.6.refs_2_), custom_call_target="tpu_custom_call" | custom-call | tf_op jit(solution)/shard_map/pallas_call | solution.py:68
  132.3 5.5 %all-to-all-done.4.refs_0_ = f32[32,8,128]{2,1,0:T(8,128)S(1)} async-done(((f32[32,8,128]{2,1,0:T(8,128)}), f32[32,8,128]{2,1,0:T(8,128)S(1)}, u32[]{:S(2)}, u32[]{:S(2)}) %all-to-all-start.4) | async-done | bytes 131104 | tf_op jit(solution)/shard_map/all_to_all | solution.py:32
  137.8 0.0 copy-done.1
  137.8 0.0 copy-done.3
  137.8 1.5 shard_map.132
  139.3 3.7 %all-to-all-start.5 = ((bf16[16,128,256]{2,1,0:T(8,128)(2,1)}), bf16[16,128,256]{2,1,0:T(8,128)(2,1)S(1)}, u32[]{:S(2)}, u32[]{:S(2)}) async-start(bf16[16,128,256]{2,1,0:T(8,128)(2,1)} %shard_map.131.refs_5_), calls=%async_computation.6 | async-start | bytes 2097152 | tf_op jit(solution)/shard_map/all_to_all | solution.py:32
  143.0 20.7 %all_gather.7.refs_4_ = bf16[512,512]{1,0:T(8,128)(2,1)S(1)} all-gather(bf16[128,512]{1,0:T(8,128)(2,1)S(1)} %get-tuple-element.36), channel_id=1, replica_groups=mesh['zlo'=4,'y'=4,'zhi'=4,'x'=4,'core'=2] {'zhi'}, dimensions={0}, use_global_device_ids=true | all-gather | bytes 655360 | tf_op jit(solution)/shard_map/all_gather | solution.py:401
  163.6 3.1 %collective-permute-start.7 = (bf16[512,512]{1,0:T(8,128)(2,1)S(1)}, bf16[512,512]{1,0:T(8,128)(2,1)S(1)}, u32[]{:S(2)}, u32[]{:S(2)}) collective-permute-start(bf16[512,512]{1,0:T(8,128)(2,1)S(1)} %all_gather.7.refs_4_), channel_id=1, source_target_pairs={{0,1},{1,0},{2,3},{3,2},{4,5},{5,4},{6,7},{7,6},{8,9},{9,8},{10,11... | collective-permute-start | bytes 1572872 | tf_op jit(solution)/shard_map/ppermute | solution.py:48
  166.7 1.0 shard_map.133.refs_5_
  167.7 0.5 collective-permute-done.7.refs_4_
  168.2 1.8 shard_map.134
  170.0 0.0 all-to-all-done.5.refs_0_
  170.1 5.1 %all-to-all-start.6 = ((bf16[4,128,512]{2,1,0:T(8,128)(2,1)}), bf16[4,128,512]{2,1,0:T(8,128)(2,1)S(1)}, u32[]{:S(2)}, u32[]{:S(2)}) async-start(bf16[4,128,512]{2,1,0:T(8,128)(2,1)} %shard_map.134), calls=%async_computation.7 | async-start | bytes 1048576 | tf_op jit(solution)/shard_map/all_to_all | solution.py:32
  175.2 1.8 shard_map.135
  177.0 7.1 %all-to-all-done.6 = bf16[4,128,512]{2,1,0:T(8,128)(2,1)S(1)} async-done(((bf16[4,128,512]{2,1,0:T(8,128)(2,1)}), bf16[4,128,512]{2,1,0:T(8,128)(2,1)S(1)}, u32[]{:S(2)}, u32[]{:S(2)}) %all-to-all-start.6) | async-done | bytes 524320 | tf_op jit(solution)/shard_map/all_to_all | solution.py:32
  184.1 0.7 reduce_sum.12
  (14 shorter events, 0.0 us)
Async XLA Ops:
  11.6 5.0 %copy-start.8 = (f32[1,4096]{1,0:T(1,128)S(1)}, f32[1,4096]{1,0:T(1,128)}, u32[]{:S(2)}) copy-start(f32[1,4096]{1,0:T(1,128)} %refs_2_.1) | copy-start | bytes 49156
  11.6 5.2 %copy-start.10 = (bf16[128,512]{1,0:T(8,128)(2,1)S(1)}, bf16[128,512]{1,0:T(8,128)(2,1)}, u32[]{:S(2)}) copy-start(bf16[128,512]{1,0:T(8,128)(2,1)} %get-tuple-element.24) | copy-start | bytes 393220
  11.6 36.0 %copy-start.6 = (s32[5]{0:T(128)S(1)}, s32[5]{0:T(128)}, u32[]{:S(2)}) copy-start(s32[5]{0:T(128)} %stack.23.spots) | copy-start | bytes 64
  11.6 36.0 %all-to-all-start = ((bf16[4,128,1536]{2,1,0:T(8,128)(2,1)}), bf16[4,128,1536]{2,1,0:T(8,128)(2,1)S(1)}, u32[]{:S(2)}, u32[]{:S(2)}) async-start(bf16[4,128,1536]{2,1,0:T(8,128)(2,1)} %get-tuple-element.23), calls=%async_computation | async-start | bytes 3145728 | tf_op jit(solution)/shard_map/all_to_all | solution.py:32
  16.6 82.0 %reduce-scatter.2.cloned.1.call-start = ((), (), s32[]{:S(2)}) async-start(), calls=%async_computation.8 | async-start | bytes 655360 | tf_op jit(solution)/shard_map/reduce_scatter | solution.py:329
  48.7 9.6 %collective-permute-start.1 = (bf16[512,512]{1,0:T(8,128)(2,1)S(1)}, bf16[512,512]{1,0:T(8,128)(2,1)S(1)}, u32[]{:S(2)}, u32[]{:S(2)}) collective-permute-start(bf16[512,512]{1,0:T(8,128)(2,1)S(1)} %shard_map.121.refs_2_), channel_id=1, source_target_pairs={{0,1},{1,0},{2,3},{3,2},{4,5},{5,4},{6,7},{7,6},{8,9},{9,8},{10,11... | collective-permute-start | bytes 1572872 | tf_op jit(solution)/shard_map/ppermute | solution.py:48
  55.2 4.6 %collective-permute-start = (bf16[512,512]{1,0:T(8,128)(2,1)S(1)}, bf16[512,512]{1,0:T(8,128)(2,1)}, u32[]{:S(2)}, u32[]{:S(2)}) collective-permute-start(bf16[512,512]{1,0:T(8,128)(2,1)S(1)} %all_gather.6.refs_1_), channel_id=1, source_target_pairs={{0,1},{1,0},{2,3},{3,2},{4,5},{5,4},{6,7},{7,6},{8,9},{9,8},{10,11... | collective-permute-start | bytes 1572872 | tf_op jit(solution)/shard_map/ppermute | solution.py:48
  70.6 4.3 %copy-start = (bf16[2,1,64,4096]{3,2,1,0:T(8,128)(2,1)S(1)}, bf16[2,1,64,4096]{3,2,1,0:T(8,128)(2,1)}, u32[]{:S(2)}) copy-start(bf16[2,1,64,4096]{3,2,1,0:T(8,128)(2,1)} %param.15) | copy-start | bytes 3145732
  70.6 4.3 %copy-start.7 = (bf16[5,4096]{1,0:T(8,128)(2,1)S(1)}, bf16[5,4096]{1,0:T(8,128)(2,1)}, u32[]{:S(2)}) copy-start(bf16[5,4096]{1,0:T(8,128)(2,1)} %refs_3_.1) | copy-start | bytes 122884
  70.6 4.3 %copy-start.9 = (s32[2,32]{1,0:T(2,128)S(1)}, s32[2,32]{1,0:T(2,128)}, u32[]{:S(2)}) copy-start(s32[2,32]{1,0:T(2,128)} %refs_0_.1) | copy-start | bytes 772
  70.6 17.5 %all-to-all-start.2 = ((bf16[4,512,256]{2,1,0:T(8,128)(2,1)}), bf16[4,512,256]{2,1,0:T(8,128)(2,1)S(1)}, u32[]{:S(2)}, u32[]{:S(2)}) async-start(bf16[4,512,256]{2,1,0:T(8,128)(2,1)} %shard_map.125), calls=%async_computation.3 | async-start | bytes 2097152 | tf_op jit(solution)/shard_map/all_to_all | solution.py:32
  76.6 13.6 %collective-permute-start.2 = (bf16[128,1024]{1,0:T(8,128)(2,1)S(1)}, bf16[128,1024]{1,0:T(8,128)(2,1)S(1)}, u32[]{:S(2)}, u32[]{:S(2)}) collective-permute-start(bf16[128,1024]{1,0:T(8,128)(2,1)S(1)} %get-tuple-element.31), channel_id=1, source_target_pairs={{0,2},{2,4},{4,6},{6,0},{1,3},{3,5},{5,7},{7,1},{8,10},{10,12},{12... | collective-permute-start | bytes 786440 | tf_op jit(solution)/shard_map/ppermute | solution.py:43
  78.8 11.9 %collective-permute-start.3 = (bf16[128,1024]{1,0:T(8,128)(2,1)S(1)}, bf16[128,1024]{1,0:T(8,128)(2,1)S(1)}, u32[]{:S(2)}, u32[]{:S(2)}) collective-permute-start(bf16[128,1024]{1,0:T(8,128)(2,1)S(1)} %get-tuple-element.32), channel_id=1, source_target_pairs={{0,4},{2,6},{4,0},{6,2},{1,5},{3,7},{5,1},{7,3},{8,12},{10,14},{12... | collective-permute-start | bytes 786440 | tf_op jit(solution)/shard_map/ppermute | solution.py:43
  82.5 11.7 %collective-permute-start.4 = (bf16[128,1024]{1,0:T(8,128)(2,1)S(1)}, bf16[128,1024]{1,0:T(8,128)(2,1)S(1)}, u32[]{:S(2)}, u32[]{:S(2)}) collective-permute-start(bf16[128,1024]{1,0:T(8,128)(2,1)S(1)} %get-tuple-element.33), channel_id=1, source_target_pairs={{0,6},{2,0},{4,2},{6,4},{1,7},{3,1},{5,3},{7,5},{8,14},{10,8},{12,... | collective-permute-start | bytes 786440 | tf_op jit(solution)/shard_map/ppermute | solution.py:43
  88.8 17.3 %collective-permute-start.5 = (bf16[512,256]{1,0:T(8,128)(2,1)S(1)}, bf16[512,256]{1,0:T(8,128)(2,1)S(1)}, u32[]{:S(2)}, u32[]{:S(2)}) collective-permute-start(bf16[512,256]{1,0:T(8,128)(2,1)S(1)} %shard_map.127.refs_1_.refs_0_), channel_id=1, source_target_pairs={{128,0},{256,128},{384,256},{129,1},{257,129},{385,257},{130,2},{2... | collective-permute-start | bytes 786440 | tf_op jit(solution)/shard_map/ppermute | solution.py:53
  98.6 0.9 copy-start.2
  100.9 17.0 %all-to-all-start.3 = ((f32[16,8,128]{2,1,0:T(8,128)}), f32[16,8,128]{2,1,0:T(8,128)S(1)}, u32[]{:S(2)}, u32[]{:S(2)}) async-start(f32[16,8,128]{2,1,0:T(8,128)} %shard_map.128), calls=%async_computation.4 | async-start | bytes 131072 | tf_op jit(solution)/shard_map/all_to_all | solution.py:32
  107.5 30.3 %copy-start.1 = (f32[1,128,512]{2,1,0:T(8,128)S(1)}, f32[1,128,512]{2,1,0:T(8,128)}, u32[]{:S(2)}) copy-start(f32[1,128,512]{2,1,0:T(8,128)} %param.12) | copy-start | bytes 786436
  107.5 30.3 %copy-start.3 = (bf16[128,512]{1,0:T(8,128)(2,1)S(1)}, bf16[128,512]{1,0:T(8,128)(2,1)}, u32[]{:S(2)}) copy-start(bf16[128,512]{1,0:T(8,128)(2,1)} %reduce-scatter.2.cloned.1.call-done.refs_0_.refs_1_) | copy-start | bytes 393220
  107.5 30.3 %copy-start.4 = (f32[1,128,512]{2,1,0:T(8,128)S(1)}, f32[1,128,512]{2,1,0:T(8,128)}, u32[]{:S(2)}) copy-start(f32[1,128,512]{2,1,0:T(8,128)} %param.13) | copy-start | bytes 786436
  107.5 30.3 %copy-start.5 = (f32[1,128,512]{2,1,0:T(8,128)S(1)}, f32[1,128,512]{2,1,0:T(8,128)}, u32[]{:S(2)}) copy-start(f32[1,128,512]{2,1,0:T(8,128)} %param.14) | copy-start | bytes 786436
  107.5 22.7 %collective-permute-start.6 = (bf16[512,256]{1,0:T(8,128)(2,1)}, bf16[512,256]{1,0:T(8,128)(2,1)}, u32[]{:S(2)}, u32[]{:S(2)}) collective-permute-start(bf16[512,256]{1,0:T(8,128)(2,1)} %shard_map.130), channel_id=1, source_target_pairs={{256,0},{384,128},{257,1},{385,129},{258,2},{386,130},{259,3},{387... | collective-permute-start | bytes 786440 | tf_op jit(solution)/shard_map/ppermute | solution.py:53
  119.1 18.7 %all-to-all-start.4 = ((f32[32,8,128]{2,1,0:T(8,128)}), f32[32,8,128]{2,1,0:T(8,128)S(1)}, u32[]{:S(2)}, u32[]{:S(2)}) async-start(f32[32,8,128]{2,1,0:T(8,128)} %shard_map.129), calls=%async_computation.5 | async-start | bytes 262144 | tf_op jit(solution)/shard_map/all_to_all | solution.py:32
  139.3 30.8 %all-to-all-start.5 = ((bf16[16,128,256]{2,1,0:T(8,128)(2,1)}), bf16[16,128,256]{2,1,0:T(8,128)(2,1)S(1)}, u32[]{:S(2)}, u32[]{:S(2)}) async-start(bf16[16,128,256]{2,1,0:T(8,128)(2,1)} %shard_map.131.refs_5_), calls=%async_computation.6 | async-start | bytes 2097152 | tf_op jit(solution)/shard_map/all_to_all | solution.py:32
  163.6 4.6 %collective-permute-start.7 = (bf16[512,512]{1,0:T(8,128)(2,1)S(1)}, bf16[512,512]{1,0:T(8,128)(2,1)S(1)}, u32[]{:S(2)}, u32[]{:S(2)}) collective-permute-start(bf16[512,512]{1,0:T(8,128)(2,1)S(1)} %all_gather.7.refs_4_), channel_id=1, source_target_pairs={{0,1},{1,0},{2,3},{3,2},{4,5},{5,4},{6,7},{7,6},{8,9},{9,8},{10,11... | collective-permute-start | bytes 1572872 | tf_op jit(solution)/shard_map/ppermute | solution.py:48
  170.1 14.1 %all-to-all-start.6 = ((bf16[4,128,512]{2,1,0:T(8,128)(2,1)}), bf16[4,128,512]{2,1,0:T(8,128)(2,1)S(1)}, u32[]{:S(2)}, u32[]{:S(2)}) async-start(bf16[4,128,512]{2,1,0:T(8,128)(2,1)} %shard_map.134), calls=%async_computation.7 | async-start | bytes 1048576 | tf_op jit(solution)/shard_map/all_to_all | solution.py:32
Sparse Core Ops, SparseCore 0:
  59.9 38.6 reduce-scatter.1

commit v10 on v9

--- a/solution.py
+++ b/solution.py
@@ -61,15 +61,14 @@
     return lax.rsqrt(jnp.mean(floats * floats, axis=-1, keepdims=True) + rms_epsilon)
 
 
-def local(kernel, out_shapes, spots, *arrays, weight=0, scratch=(), after=()):
-    def body(spots, *refs):
-        kernel(spots, *refs[: len(arrays)], *refs[len(arrays) + len(after) :])
+def local(kernel, out_shapes, *arrays, weight=0, scratch=(), after=()):
+    def body(*refs):
+        kernel(*refs[: len(arrays)], *refs[len(arrays) + len(after) :])
 
     return pl.pallas_call(
         body,
         out_shape=out_shapes,
-        in_specs=[pl.BlockSpec(memory_space=pltpu.SMEM)]
-        + [
+        in_specs=[
             pl.BlockSpec(memory_space=pltpu.SMEM if a.dtype == jnp.int32 else pltpu.VMEM)
             for a in arrays
         ]
@@ -78,16 +77,16 @@
         scratch_shapes=scratch,
         compiler_params=pltpu.CompilerParams(vmem_limit_bytes=48 * 1024 * 1024),
         cost_estimate=pl.CostEstimate(flops=weight, bytes_accessed=0, transcendentals=0),
-    )(spots, *arrays, *after)
+    )(*arrays, *after)
 
 
 def strip_at(start, rows):
     return pl.ds(pl.multiple_of(start, rows), rows)
 
 
-def split_kernel(sizes, spots, acts, values, master, out, weights):
+def split_kernel(sizes, acts, values, master, out, weights):
     far, group, cores, rows = sizes
-    core = spots[0]
+    core = lax.axis_index("core")
     half = far * rows
     weights[...] = master[...].astype(bf16)
     floats = acts[...].astype(f32)
@@ -102,7 +101,7 @@
         out[x, :, cores * half :] = scaled
 
 
-def split(sizes, spots, acts, values, master):
+def split(sizes, acts, values, master):
     far, group, cores, rows = sizes
     toks, width = acts.shape
     kvw = values.shape[1]
@@ -117,7 +116,6 @@
             jax.ShapeDtypeStruct((rows, kvw), bf16),
         ],
         in_specs=[
-            pl.BlockSpec(memory_space=pltpu.SMEM),
             pl.BlockSpec((cut, width), lambda i: (i, 0)),
             pl.BlockSpec((cut, kvw), lambda i: (i, 0)),
             pl.BlockSpec((rows // steps, kvw), lambda i: (i, 0)),
@@ -128,10 +126,10 @@
         ],
         compiler_params=pltpu.CompilerParams(vmem_limit_bytes=63 * 1024 * 1024),
         cost_estimate=pl.CostEstimate(flops=0, bytes_accessed=0, transcendentals=0),
-    )(spots, acts, values, master)
-
-
-def other_kernel(half, spots, mine, gain, out):
+    )(acts, values, master)
+
+
+def other_kernel(half, mine, gain, out):
     left = mine[:, half : 2 * half]
     part = lax.dot_general(
         left, mine[:, 2 * half :], (((0,), (0,)), ((), ())), preferred_element_type=f32
@@ -139,18 +137,18 @@
     out[...] = (part * gain[...]).astype(bf16)
 
 
-def own_kernel(half, spots, mine, gain, out):
+def own_kernel(half, mine, gain, out):
     part = lax.dot_general(
         mine[:, :half], mine[:, 2 * half :], (((0,), (0,)), ((), ())), preferred_element_type=f32
     )
     out[...] = part * gain[...]
 
 
-def add_kernel(spots, own, came, out):
+def add_kernel(own, came, out):
     out[...] = (own[...] + came[...].astype(f32)).astype(bf16)
 
 
-def upstream_kernel(half, spots, mine, own, other, gain, mixed, sums):
+def upstream_kernel(half, mine, own, other, gain, mixed, sums):
     values = mine[:, 2 * half :]
     squares, products = 0.0, 0.0
     for c, weights in enumerate((own, other)):
@@ -169,7 +167,7 @@
         sums[x] = both.T[:8]
 
 
-def branch_kernel(sizes, spots, mine, mixed, sums, out):
+def branch_kernel(sizes, mine, mixed, sums, out):
     far, rows, width = sizes
     half = far * rows
     both = jnp.concatenate([jnp.sum(sums[...], axis=0)] * 16, axis=0).T
@@ -182,7 +180,7 @@
             out[z, :, c * rows : (c + 1) * rows] = block.astype(bf16)
 
 
-def fresh_kernel(sizes, spots, ids, acts, gain, table, *refs):
+def fresh_kernel(sizes, ids, acts, gain, table, *refs):
     *outs, normed = refs
     far, group, cores, rows = sizes
     micro = ids.shape[0]
@@ -191,47 +189,47 @@
     toks = floats.shape[0]
     row = lax.broadcasted_iota(jnp.int32, (toks, 1), 0)
     for m in range(micro):
-        bin_id = ids[m, spots[3]]
+        bin_id = ids[m, lax.axis_index(dp)]
         embed = jnp.zeros((1, floats.shape[1]), f32)
         for b in range(table.shape[0]):
             embed = jnp.where(bin_id == b, table[b : b + 1, :].astype(f32), embed)
-        first = jnp.logical_and(row == m * (toks // micro), spots[2] == 0)
+        first = jnp.logical_and(row == m * (toks // micro), lax.axis_index(section) == 0)
         floats = jnp.where(first, embed, floats)
     normed[...] = (floats * inverse_rms(floats) * gain[...]).astype(bf16)
     for k, out in enumerate(outs):
-        x = (spots[4] + k) & (group - 1)
+        x = (lax.axis_index("x") + k) & (group - 1)
         for z in range(far):
             for c in range(cores):
-                start = ((z * group + x) * cores + ((spots[0] + c) & (cores - 1))) * rows
+                start = ((z * group + x) * cores + ((lax.axis_index("core") + c) & (cores - 1))) * rows
                 out[:, c * half + z * rows : c * half + (z + 1) * rows] = normed[
                     :, strip_at(start, rows)
                 ]
 
 
-def first_kernel(half, spots, *refs):
+def first_kernel(half, *refs):
     *blocks, weights, out = refs
     for k, block in enumerate(blocks):
         part = jnp.dot(block[:, :half], weights[...], preferred_element_type=f32)
-        out[(spots[4] - k) & (len(blocks) - 1)] = part
-
-
-def second_kernel(half, spots, *refs):
+        out[(lax.axis_index("x") - k) & (len(blocks) - 1)] = part
+
+
+def second_kernel(half, *refs):
     *blocks, weights, first, out = refs
     for k, block in enumerate(blocks):
-        x = (spots[4] - k) & (len(blocks) - 1)
+        x = (lax.axis_index("x") - k) & (len(blocks) - 1)
         part = jnp.dot(block[:, half:], weights[...], preferred_element_type=f32)
         out[x] = (first[x] + part).astype(bf16)
 
 
-def top_kernel(spots, came, out):
+def top_kernel(came, out):
     out[...] = jnp.sum(came[...].astype(f32), axis=0).astype(bf16)
 
 
-def pair_kernel(spots, top, behind, out):
+def pair_kernel(top, behind, out):
     out[...] = (top[...].astype(f32) + behind[...].astype(f32)).astype(bf16)
 
 
-def suffix_kernel(group, spots, came, *refs):
+def suffix_kernel(group, came, *refs):
     *parts, out = refs
     block = sum(part[...].astype(f32) for part in parts)
     toks = out.shape[1]
@@ -241,16 +239,16 @@
             out[layer * group + x] = block[x * toks : (x + 1) * toks].astype(bf16)
 
 
-def squares_kernel(spots, grad, out):
+def squares_kernel(grad, out):
     floats = grad[...].astype(f32)
     out[...] = jnp.broadcast_to(jnp.sum(floats * floats), out.shape)
 
 
-def relay_kernel(spots, sums, out):
+def relay_kernel(sums, out):
     out[...] = jnp.broadcast_to(jnp.sum(sums[...], axis=0, keepdims=True), out.shape)
 
 
-def adam_kernel(entries, spots, sums, grad, master, first, second, first_new, second_new, weights):
+def adam_kernel(entries, sums, grad, master, first, second, first_new, second_new, weights):
     squares = jnp.sum(sums[...], axis=0)
     clip = jnp.minimum(1.0, clip_level / jnp.sqrt(squares / entries + 1e-12))[0:1, 0:1]
     clipped = grad[...].astype(f32) * clip
@@ -265,11 +263,11 @@
     weights[...] = (master[...] - learn_rate * update).astype(bf16)
 
 
-def join_kernel(rows, spots, back, out):
+def join_kernel(rows, back, out):
     cores = back.shape[2] // rows
     for j in range(back.shape[0]):
         for c in range(cores):
-            start = (j * cores + ((spots[0] + c) & (cores - 1))) * rows
+            start = (j * cores + ((lax.axis_index("core") + c) & (cores - 1))) * rows
             out[:, strip_at(start, rows)] = back[j, :, c * rows : (c + 1) * rows]
 
 
@@ -286,8 +284,7 @@
     rows = width // (far * group * cores)
     half = far * rows
     all_toks = group * toks
-    core, spot_y, spot_x = (lax.axis_index(name) for name in ("core", "y", "x"))
-    spots = jnp.stack([core, spot_y, lax.axis_index(section), lax.axis_index(dp), spot_x])
+    core, spot_x = lax.axis_index("core"), lax.axis_index("x")
     shape = jax.ShapeDtypeStruct
     gain = norm_gain[0]
 
@@ -303,7 +300,7 @@
 
     flat = acts[:, 0].reshape(toks, width)
     blocks, weights_old = split(
-        (far, group, cores, rows), spots, flat, value_grads[:, 0].reshape(toks, kvw), master[0]
+        (far, group, cores, rows), flat, value_grads[:, 0].reshape(toks, kvw), master[0]
     )
     mine = exchange(blocks, "x").reshape(all_toks, cores * half + kvw)
     weights_old = lax.all_gather(weights_old, "zhi", axis=0, tiled=True)
@@ -312,7 +309,6 @@
     other = local(
         functools.partial(other_kernel, half),
         [shape((half, kvw), bf16)],
-        spots,
         mine,
         own_gain[half:, None],
     )[0]
@@ -320,19 +316,17 @@
     own = local(
         functools.partial(own_kernel, half),
         [shape((half, kvw), f32)],
-        spots,
         mine,
         own_gain[:half, None],
         after=[other],
     )[0]
-    partial = local(add_kernel, [shape((half, kvw), bf16)], spots, own, came)[0]
+    partial = local(add_kernel, [shape((half, kvw), bf16)], own, came)[0]
     grad = lax.psum_scatter(partial, "zhi", scatter_dimension=0, tiled=True)
     weights_other = swap_cores(weights_old)
 
     mixed, sums = local(
         functools.partial(upstream_kernel, half),
         [shape((all_toks, cores * half), f32), shape((group, 8, all_toks), f32)],
-        spots,
         mine,
         weights_old,
         weights_other,
@@ -343,7 +337,6 @@
     parts = local(
         functools.partial(branch_kernel, (far, rows, width)),
         [shape((layers_y, all_toks, cores * rows), bf16)],
-        spots,
         mine,
         mixed,
         sums,
@@ -354,7 +347,6 @@
     fresh_blocks = local(
         functools.partial(fresh_kernel, (far, group, cores, rows)),
         [shape((toks, cores * half), bf16)] * group,
-        spots,
         reward_ids,
         next_flat,
         norm_gain,
@@ -364,24 +356,23 @@
     fresh_normed = shift(fresh_blocks, "x")
 
     top_shape = shape((all_toks, cores * rows), bf16)
-    top = local(top_kernel, [top_shape], spots, came, after=fresh_blocks[:1])[0]
+    top = local(top_kernel, [top_shape], came, after=fresh_blocks[:1])[0]
     behind = [from_behind(top, "zlo", 1)]
-    pair = local(pair_kernel, [top_shape], spots, top, behind[0])[0]
+    pair = local(pair_kernel, [top_shape], top, behind[0])[0]
     behind.append(from_behind(pair, "zlo", 2))
 
     first_axes = ("zlo", "zhi")
     last_axes = ("y", "x", "core")
     tile = (8, 128)
     squares = local(
-        squares_kernel, [shape((lax.axis_size(first_axes),) + tile, f32)], spots, grad, after=[top] + fresh_normed[1:]
+        squares_kernel, [shape((lax.axis_size(first_axes),) + tile, f32)], grad, after=[top] + fresh_normed[1:]
     )[0]
     squares = exchange(squares, first_axes)
-    squares = local(relay_kernel, [shape((lax.axis_size(last_axes),) + tile, f32)], spots, squares)[0]
+    squares = local(relay_kernel, [shape((lax.axis_size(last_axes),) + tile, f32)], squares)[0]
     squares = exchange(squares, last_axes)
     suffix = local(
         functools.partial(suffix_kernel, group),
         [shape((layers_y * group, toks, cores * rows), bf16)],
-        spots,
         came,
         *behind,
     )[0]
@@ -389,7 +380,6 @@
     moment1_new, moment2_new, weights_new = local(
         functools.partial(adam_kernel, lax.axis_size(section) * width * kvw),
         [shard, shard, shape((rows, kvw), bf16)],
-        spots,
         squares,
         grad,
         master[0],
@@ -405,14 +395,12 @@
     first = local(
         functools.partial(first_kernel, half),
         [shape((group, toks, kvw), f32)],
-        spots,
         *fresh_normed,
         weights_new,
     )[0]
     fresh = local(
         functools.partial(second_kernel, half),
         [shape((group, toks, kvw), bf16)],
-        spots,
         *fresh_normed,
         weights_other,
         first,
@@ -422,7 +410,7 @@
     fresh_values = fresh.reshape(micro, 1, tok_dev, kvw)
 
     input_grads = local(
-        functools.partial(join_kernel, rows), [shape((toks, width), bf16)], spots, back
+        functools.partial(join_kernel, rows), [shape((toks, width), bf16)], back
     )[0].reshape(micro, 1, tok_dev, width)
     return (input_grads, moment1_new[None], moment2_new[None], fresh_values)
 

time: 195 us -> 200 us (1.026)
  the two profiles are of different devices: /device:TPU:1 before, /device:TPU:96 now
where the time goes in v10:
time: 200 us; the launch traced here: 199 us
  blocking collectives  69.2 us (35%)
  starting transfers between devices  61 us (30%)
  waiting for transfers between devices  33.2 us (17%)
  Pallas kernels  18.3 us (9%)
  between operations  14.3 us (7%)
  local copies, waits for them, and re-layouts  2.18 us (1%)
    all_to_all x6, starting transfers between devices, exchange(): return lax.all_to_all(blocks, axis, 0, 0)  38.6 us
    all_gather x1, blocking collectives, per_device(): weights_old = lax.all_gather(weights_old, 'zhi', axis=0, tiled=True)  30.6 us
    all_gather x1, blocking collectives, per_device(): weights_new = lax.all_gather(weights_new, 'zhi', axis=0, tiled=True)  29.6 us
    all_to_all x6, waiting for transfers between devices, exchange(): return lax.all_to_all(blocks, axis, 0, 0)  25.1 us
    pallas_call x15, Pallas kernels, local(): pl.pallas_call(body, out_shape=out_shapes, in_specs=[pl.BlockSpec(memory_...  14.4 us
    ppermute x3, starting transfers between devices, shift(): lax.ppermute(parts[k], axis, [(i, (i + k) % size) for i in range(size)])  9.34 us
    all_to_all x1, blocking collectives, exchange(): return lax.all_to_all(blocks, axis, 0, 0)  8.99 us
    ppermute x2, starting transfers between devices, from_behind(): lax.ppermute(block, axis, [(i + distance, i) for i in range(size - distan...  6.89 us
  transfers between devices with their start and end apart: 15, of which 7 were waited for; matrix products, arithmetic and copies ran while one was open for 0% of the time, Pallas kernels for 7%

profile of v10, /device:TPU:96, one launch (start us, length us, event | category | flops | bytes accessed | tf_op | source)
XLA Modules:
  0.0 198.9 jit_solution(1766887155934654275)
XLA Ops:
  7.2 3.8 %shard_map.120 = (bf16[4,128,1536]{2,1,0:T(8,128)(2,1)}, bf16[128,512]{1,0:T(8,128)(2,1)}) custom-call(bf16[128,4096]{1,0:T(8,128)(2,1)} %bitcast.36, bf16[128,512]{1,0:T(8,128)(2,1)} %bitcast.39, f32[128,512]{1,0:T(8,128)} %bitcast.30), custom_call_target="tpu_custom_call" | custom-call | tf_op jit(solution)/shard_map/pallas_call | solution.py:111
  11.0 4.4 %all-to-all-start = ((bf16[4,128,1536]{2,1,0:T(8,128)(2,1)}), bf16[4,128,1536]{2,1,0:T(8,128)(2,1)S(1)}, u32[]{:S(2)}, u32[]{:S(2)}) async-start(bf16[4,128,1536]{2,1,0:T(8,128)(2,1)} %get-tuple-element.23), calls=%async_computation | async-start | bytes 3145728 | tf_op jit(solution)/shard_map/all_to_all | solution.py:32
  15.5 0.0 reduce-scatter.2.cloned.1.call-start
  15.5 0.0 copy-done.7
  15.5 0.1 copy.18.refs_1_
  15.6 0.0 copy-done.9
  15.6 30.6 %all_gather.6.refs_1_ = bf16[512,512]{1,0:T(8,128)(2,1)S(1)} all-gather(bf16[128,512]{1,0:T(8,128)(2,1)S(1)} %copy-done.9), channel_id=1, replica_groups=mesh['zlo'=4,'y'=4,'zhi'=4,'x'=4,'core'=2] {'zhi'}, dimensions={0}, use_global_device_ids=true | all-gather | bytes 655360 | tf_op jit(solution)/shard_map/all_gather | solution.py:306
  46.2 0.0 all-to-all-done
  46.2 0.5 shard_map.121.refs_2_
  46.7 1.9 collective-permute-start.1
  48.6 2.4 %collective-permute-start = (bf16[512,512]{1,0:T(8,128)(2,1)S(1)}, bf16[512,512]{1,0:T(8,128)(2,1)S(1)}, u32[]{:S(2)}, u32[]{:S(2)}) collective-permute-start(bf16[512,512]{1,0:T(8,128)(2,1)S(1)} %all_gather.6.refs_1_), channel_id=1, source_target_pairs={{0,1},{1,0},{2,3},{3,2},{4,5},{5,4},{6,7},{7,6},{8,9},{9,8},{10,11... | collective-permute-start | bytes 1572872 | tf_op jit(solution)/shard_map/ppermute | solution.py:48
  51.1 0.1 copy.19.refs_1_
  51.2 0.5 shard_map.122.refs_0_
  51.7 0.0 collective-permute-done.1.refs_1_
  51.7 1.9 shard_map.123.refs_4_
  53.6 0.0 reduce-scatter.2.cloned.1.call-update
  53.7 0.0 collective-permute-done.refs_2_
  53.7 0.9 shard_map.124
  54.6 9.0 %all_to_all.35.refs_2_ = f32[4,8,512]{2,1,0:T(8,128)S(1)} all-to-all(f32[4,8,512]{2,1,0:T(8,128)S(1)} %get-tuple-element.28), channel_id=1, replica_groups=mesh['zlo'=4,'y'=4,'zhi'=4,'x'=4,'core'=2] {'x'}, dimensions={0} | all-to-all | bytes 131072 | tf_op jit(solution)/shard_map/all_to_all | solution.py:32
  63.6 1.5 shard_map.125
  65.1 4.6 %all-to-all-start.2 = ((bf16[4,512,256]{2,1,0:T(8,128)(2,1)}), bf16[4,512,256]{2,1,0:T(8,128)(2,1)S(1)}, u32[]{:S(2)}, u32[]{:S(2)}) async-start(bf16[4,512,256]{2,1,0:T(8,128)(2,1)} %shard_map.125), calls=%async_computation.3 | async-start | bytes 2097152 | tf_op jit(solution)/shard_map/all_to_all | solution.py:32
  69.7 0.0 copy-done
  69.7 0.0 copy-done.6
  69.7 0.0 copy-done.8
  69.7 2.4 %shard_map.126 = (bf16[128,1024]{1,0:T(8,128)(2,1)S(1)}, bf16[128,1024]{1,0:T(8,128)(2,1)}, bf16[128,1024]{1,0:T(8,128)(2,1)}, bf16[128,1024]{1,0:T(8,128)(2,1)}) custom-call(s32[2,32]{1,0:T(2,128)S(1)} %copy-done.8, bf16[128,4096]{1,0:T(8,128)(2,1)S(1)} %bitcast.29, f32[1,4096]{1,0:T(1,128)S(1)} %copy-done.7, bf16[5,4096]{1,0:T(8,128)(2,1)S(1)} %copy-done.6), custom_call_target="tpu_custom_call" | custom-call | tf_op jit(solution)/shard_map/pallas_call | solution.py:68
  72.1 2.5 %collective-permute-start.2 = (bf16[128,1024]{1,0:T(8,128)(2,1)}, bf16[128,1024]{1,0:T(8,128)(2,1)S(1)}, u32[]{:S(2)}, u32[]{:S(2)}) collective-permute-start(bf16[128,1024]{1,0:T(8,128)(2,1)} %get-tuple-element.31), channel_id=1, source_target_pairs={{0,2},{2,4},{4,6},{6,0},{1,3},{3,5},{5,7},{7,1},{8,10},{10,12},{12... | collective-permute-start | bytes 786440 | tf_op jit(solution)/shard_map/ppermute | solution.py:43
  74.5 4.0 %collective-permute-start.3 = (bf16[128,1024]{1,0:T(8,128)(2,1)}, bf16[128,1024]{1,0:T(8,128)(2,1)S(1)}, u32[]{:S(2)}, u32[]{:S(2)}) collective-permute-start(bf16[128,1024]{1,0:T(8,128)(2,1)} %get-tuple-element.32), channel_id=1, source_target_pairs={{0,4},{2,6},{4,0},{6,2},{1,5},{3,7},{5,1},{7,3},{8,12},{10,14},{12... | collective-permute-start | bytes 786440 | tf_op jit(solution)/shard_map/ppermute | solution.py:43
  78.5 2.9 %collective-permute-start.4 = (bf16[128,1024]{1,0:T(8,128)(2,1)}, bf16[128,1024]{1,0:T(8,128)(2,1)S(1)}, u32[]{:S(2)}, u32[]{:S(2)}) collective-permute-start(bf16[128,1024]{1,0:T(8,128)(2,1)} %get-tuple-element.33), channel_id=1, source_target_pairs={{0,6},{2,0},{4,2},{6,4},{1,7},{3,1},{5,3},{7,5},{8,14},{10,8},{12,... | collective-permute-start | bytes 786440 | tf_op jit(solution)/shard_map/ppermute | solution.py:43
  81.4 2.1 %all-to-all-done.2.refs_0_ = bf16[4,512,256]{2,1,0:T(8,128)(2,1)S(1)} async-done(((bf16[4,512,256]{2,1,0:T(8,128)(2,1)}), bf16[4,512,256]{2,1,0:T(8,128)(2,1)S(1)}, u32[]{:S(2)}, u32[]{:S(2)}) %all-to-all-start.2) | async-done | bytes 1048608 | tf_op jit(solution)/shard_map/all_to_all | solution.py:32
  83.5 0.1 shard_map.127.refs_1_.refs_0_
  83.7 4.3 %collective-permute-start.5 = (bf16[512,256]{1,0:T(8,128)(2,1)S(1)}, bf16[512,256]{1,0:T(8,128)(2,1)S(1)}, u32[]{:S(2)}, u32[]{:S(2)}) collective-permute-start(bf16[512,256]{1,0:T(8,128)(2,1)S(1)} %shard_map.127.refs_1_.refs_0_), channel_id=1, source_target_pairs={{128,0},{256,128},{384,256},{129,1},{257,129},{385,257},{130,2},{2... | collective-permute-start | bytes 786440 | tf_op jit(solution)/shard_map/ppermute | solution.py:53
  87.9 0.0 collective-permute-done.2.refs_2_.refs_1_
  87.9 0.0 collective-permute-done.3.refs_3_.refs_2_
  88.0 2.0 %collective-permute-done.4.refs_4_.refs_3_ = bf16[128,1024]{1,0:T(8,128)(2,1)S(1)} collective-permute-done((bf16[128,1024]{1,0:T(8,128)(2,1)}, bf16[128,1024]{1,0:T(8,128)(2,1)S(1)}, u32[]{:S(2)}, u32[]{:S(2)}) %collective-permute-start.4) | collective-permute-done | bytes 262176 | tf_op jit(solution)/shard_map/ppermute | solution.py:43
  90.0 4.7 %reduce-scatter.2.cloned.1.call-done.refs_0_.refs_1_ = bf16[128,512]{1,0:T(8,128)(2,1)} async-done(((bf16[512,512]{1,0:T(8,128)(2,1)}), bf16[128,512]{1,0:T(8,128)(2,1)}) %reduce-scatter.2.cloned.1.call-update) | async-done | bytes 131088 | tf_op jit(solution)/shard_map/reduce_scatter | solution.py:324
  94.7 0.9 copy-done.2
  95.6 0.8 shard_map.128
  96.4 7.0 %all-to-all-start.3 = ((f32[16,8,128]{2,1,0:T(8,128)}), f32[16,8,128]{2,1,0:T(8,128)S(1)}, u32[]{:S(2)}, u32[]{:S(2)}) async-start(f32[16,8,128]{2,1,0:T(8,128)} %shard_map.128), calls=%async_computation.4 | async-start | bytes 131072 | tf_op jit(solution)/shard_map/all_to_all | solution.py:32
  103.4 0.0 collective-permute-done.5.refs_1_
  103.4 0.1 shard_map.130
  103.5 0.0 copy-start.1
  103.5 2.6 %collective-permute-start.6 = (bf16[512,256]{1,0:T(8,128)(2,1)S(1)}, bf16[512,256]{1,0:T(8,128)(2,1)S(1)}, u32[]{:S(2)}, u32[]{:S(2)}) collective-permute-start(bf16[512,256]{1,0:T(8,128)(2,1)S(1)} %shard_map.130), channel_id=1, source_target_pairs={{256,0},{384,128},{257,1},{385,129},{258,2},{386,130},{259,3},{387... | collective-permute-start | bytes 786440 | tf_op jit(solution)/shard_map/ppermute | solution.py:53
  106.1 7.9 %all-to-all-done.3.refs_0_ = f32[16,8,128]{2,1,0:T(8,128)S(1)} async-done(((f32[16,8,128]{2,1,0:T(8,128)}), f32[16,8,128]{2,1,0:T(8,128)S(1)}, u32[]{:S(2)}, u32[]{:S(2)}) %all-to-all-start.3) | async-done | bytes 65568 | tf_op jit(solution)/shard_map/all_to_all | solution.py:32
  114.0 0.7 shard_map.129
  114.7 14.3 %all-to-all-start.4 = ((f32[32,8,128]{2,1,0:T(8,128)}), f32[32,8,128]{2,1,0:T(8,128)S(1)}, u32[]{:S(2)}, u32[]{:S(2)}) async-start(f32[32,8,128]{2,1,0:T(8,128)} %shard_map.129), calls=%async_computation.5 | async-start | bytes 262144 | tf_op jit(solution)/shard_map/all_to_all | solution.py:32
  128.9 0.0 collective-permute-done.6.refs_2_
  129.0 0.0 copy-start.4
  129.0 1.2 shard_map.131.refs_5_
  130.2 6.6 %all-to-all-done.4.refs_0_ = f32[32,8,128]{2,1,0:T(8,128)S(1)} async-done(((f32[32,8,128]{2,1,0:T(8,128)}), f32[32,8,128]{2,1,0:T(8,128)S(1)}, u32[]{:S(2)}, u32[]{:S(2)}) %all-to-all-start.4) | async-done | bytes 131104 | tf_op jit(solution)/shard_map/all_to_all | solution.py:32
  136.7 0.0 copy-done.1
  136.8 0.0 copy-start.5
  136.8 0.9 copy-done.5
  137.7 0.9 shard_map.132
  138.7 3.7 %all-to-all-start.5 = ((bf16[16,128,256]{2,1,0:T(8,128)(2,1)}), bf16[16,128,256]{2,1,0:T(8,128)(2,1)S(1)}, u32[]{:S(2)}, u32[]{:S(2)}) async-start(bf16[16,128,256]{2,1,0:T(8,128)(2,1)} %shard_map.131.refs_5_), calls=%async_computation.6 | async-start | bytes 2097152 | tf_op jit(solution)/shard_map/all_to_all | solution.py:32
  142.3 29.6 %all_gather.7.refs_4_ = bf16[512,512]{1,0:T(8,128)(2,1)S(1)} all-gather(bf16[128,512]{1,0:T(8,128)(2,1)S(1)} %get-tuple-element.36), channel_id=1, replica_groups=mesh['zlo'=4,'y'=4,'zhi'=4,'x'=4,'core'=2] {'zhi'}, dimensions={0}, use_global_device_ids=true | all-gather | bytes 655360 | tf_op jit(solution)/shard_map/all_gather | solution.py:391
  171.9 1.9 collective-permute-start.7
  173.8 0.4 shard_map.133.refs_5_
  174.3 1.4 collective-permute-done.7.refs_4_
  175.7 1.3 shard_map.134
  176.9 0.0 all-to-all-done.5.refs_0_
  176.9 4.6 %all-to-all-start.6 = ((bf16[4,128,512]{2,1,0:T(8,128)(2,1)}), bf16[4,128,512]{2,1,0:T(8,128)(2,1)S(1)}, u32[]{:S(2)}, u32[]{:S(2)}) async-start(bf16[4,128,512]{2,1,0:T(8,128)(2,1)} %shard_map.134), calls=%async_computation.7 | async-start | bytes 1048576 | tf_op jit(solution)/shard_map/all_to_all | solution.py:32
  181.5 1.2 shard_map.135
  182.8 8.5 %all-to-all-done.6 = bf16[4,128,512]{2,1,0:T(8,128)(2,1)S(1)} async-done(((bf16[4,128,512]{2,1,0:T(8,128)(2,1)}), bf16[4,128,512]{2,1,0:T(8,128)(2,1)S(1)}, u32[]{:S(2)}, u32[]{:S(2)}) %all-to-all-start.6) | async-done | bytes 524320 | tf_op jit(solution)/shard_map/all_to_all | solution.py:32
  191.3 0.7 reduce_sum.12
  (11 shorter events, 0.0 us)
Async XLA Ops:
  11.0 4.4 %copy-start.7 = (f32[1,4096]{1,0:T(1,128)S(1)}, f32[1,4096]{1,0:T(1,128)}, u32[]{:S(2)}) copy-start(f32[1,4096]{1,0:T(1,128)} %refs_2_.1) | copy-start | bytes 49156
  11.0 4.6 %copy-start.9 = (bf16[128,512]{1,0:T(8,128)(2,1)S(1)}, bf16[128,512]{1,0:T(8,128)(2,1)}, u32[]{:S(2)}) copy-start(bf16[128,512]{1,0:T(8,128)(2,1)} %get-tuple-element.24) | copy-start | bytes 393220
  11.0 35.2 %all-to-all-start = ((bf16[4,128,1536]{2,1,0:T(8,128)(2,1)}), bf16[4,128,1536]{2,1,0:T(8,128)(2,1)S(1)}, u32[]{:S(2)}, u32[]{:S(2)}) async-start(bf16[4,128,1536]{2,1,0:T(8,128)(2,1)} %get-tuple-element.23), calls=%async_computation | async-start | bytes 3145728 | tf_op jit(solution)/shard_map/all_to_all | solution.py:32
  15.5 79.2 %reduce-scatter.2.cloned.1.call-start = ((), (), s32[]{:S(2)}) async-start(), calls=%async_computation.8 | async-start | bytes 655360 | tf_op jit(solution)/shard_map/reduce_scatter | solution.py:324
  46.7 5.0 %collective-permute-start.1 = (bf16[512,512]{1,0:T(8,128)(2,1)S(1)}, bf16[512,512]{1,0:T(8,128)(2,1)}, u32[]{:S(2)}, u32[]{:S(2)}) collective-permute-start(bf16[512,512]{1,0:T(8,128)(2,1)S(1)} %shard_map.121.refs_2_), channel_id=1, source_target_pairs={{0,1},{1,0},{2,3},{3,2},{4,5},{5,4},{6,7},{7,6},{8,9},{9,8},{10,11... | collective-permute-start | bytes 1572872 | tf_op jit(solution)/shard_map/ppermute | solution.py:48
  48.6 5.0 %collective-permute-start = (bf16[512,512]{1,0:T(8,128)(2,1)S(1)}, bf16[512,512]{1,0:T(8,128)(2,1)S(1)}, u32[]{:S(2)}, u32[]{:S(2)}) collective-permute-start(bf16[512,512]{1,0:T(8,128)(2,1)S(1)} %all_gather.6.refs_1_), channel_id=1, source_target_pairs={{0,1},{1,0},{2,3},{3,2},{4,5},{5,4},{6,7},{7,6},{8,9},{9,8},{10,11... | collective-permute-start | bytes 1572872 | tf_op jit(solution)/shard_map/ppermute | solution.py:48
  65.1 4.6 %copy-start = (bf16[2,1,64,4096]{3,2,1,0:T(8,128)(2,1)S(1)}, bf16[2,1,64,4096]{3,2,1,0:T(8,128)(2,1)}, u32[]{:S(2)}) copy-start(bf16[2,1,64,4096]{3,2,1,0:T(8,128)(2,1)} %param.15) | copy-start | bytes 3145732
  65.1 4.6 %copy-start.6 = (bf16[5,4096]{1,0:T(8,128)(2,1)S(1)}, bf16[5,4096]{1,0:T(8,128)(2,1)}, u32[]{:S(2)}) copy-start(bf16[5,4096]{1,0:T(8,128)(2,1)} %refs_3_.1) | copy-start | bytes 122884
  65.1 4.6 %copy-start.8 = (s32[2,32]{1,0:T(2,128)S(1)}, s32[2,32]{1,0:T(2,128)}, u32[]{:S(2)}) copy-start(s32[2,32]{1,0:T(2,128)} %refs_0_.1) | copy-start | bytes 772
  65.1 18.4 %all-to-all-start.2 = ((bf16[4,512,256]{2,1,0:T(8,128)(2,1)}), bf16[4,512,256]{2,1,0:T(8,128)(2,1)S(1)}, u32[]{:S(2)}, u32[]{:S(2)}) async-start(bf16[4,512,256]{2,1,0:T(8,128)(2,1)} %shard_map.125), calls=%async_computation.3 | async-start | bytes 2097152 | tf_op jit(solution)/shard_map/all_to_all | solution.py:32
  72.1 15.9 %collective-permute-start.2 = (bf16[128,1024]{1,0:T(8,128)(2,1)}, bf16[128,1024]{1,0:T(8,128)(2,1)S(1)}, u32[]{:S(2)}, u32[]{:S(2)}) collective-permute-start(bf16[128,1024]{1,0:T(8,128)(2,1)} %get-tuple-element.31), channel_id=1, source_target_pairs={{0,2},{2,4},{4,6},{6,0},{1,3},{3,5},{5,7},{7,1},{8,10},{10,12},{12... | collective-permute-start | bytes 786440 | tf_op jit(solution)/shard_map/ppermute | solution.py:43
  74.5 13.4 %collective-permute-start.3 = (bf16[128,1024]{1,0:T(8,128)(2,1)}, bf16[128,1024]{1,0:T(8,128)(2,1)S(1)}, u32[]{:S(2)}, u32[]{:S(2)}) collective-permute-start(bf16[128,1024]{1,0:T(8,128)(2,1)} %get-tuple-element.32), channel_id=1, source_target_pairs={{0,4},{2,6},{4,0},{6,2},{1,5},{3,7},{5,1},{7,3},{8,12},{10,14},{12... | collective-permute-start | bytes 786440 | tf_op jit(solution)/shard_map/ppermute | solution.py:43
  78.5 11.5 %collective-permute-start.4 = (bf16[128,1024]{1,0:T(8,128)(2,1)}, bf16[128,1024]{1,0:T(8,128)(2,1)S(1)}, u32[]{:S(2)}, u32[]{:S(2)}) collective-permute-start(bf16[128,1024]{1,0:T(8,128)(2,1)} %get-tuple-element.33), channel_id=1, source_target_pairs={{0,6},{2,0},{4,2},{6,4},{1,7},{3,1},{5,3},{7,5},{8,14},{10,8},{12,... | collective-permute-start | bytes 786440 | tf_op jit(solution)/shard_map/ppermute | solution.py:43
  83.7 19.8 %collective-permute-start.5 = (bf16[512,256]{1,0:T(8,128)(2,1)S(1)}, bf16[512,256]{1,0:T(8,128)(2,1)S(1)}, u32[]{:S(2)}, u32[]{:S(2)}) collective-permute-start(bf16[512,256]{1,0:T(8,128)(2,1)S(1)} %shard_map.127.refs_1_.refs_0_), channel_id=1, source_target_pairs={{128,0},{256,128},{384,256},{129,1},{257,129},{385,257},{130,2},{2... | collective-permute-start | bytes 786440 | tf_op jit(solution)/shard_map/ppermute | solution.py:53
  94.7 0.9 copy-start.2
  96.4 17.6 %all-to-all-start.3 = ((f32[16,8,128]{2,1,0:T(8,128)}), f32[16,8,128]{2,1,0:T(8,128)S(1)}, u32[]{:S(2)}, u32[]{:S(2)}) async-start(f32[16,8,128]{2,1,0:T(8,128)} %shard_map.128), calls=%async_computation.4 | async-start | bytes 131072 | tf_op jit(solution)/shard_map/all_to_all | solution.py:32
  103.5 33.3 %copy-start.1 = (f32[1,128,512]{2,1,0:T(8,128)S(1)}, f32[1,128,512]{2,1,0:T(8,128)}, u32[]{:S(2)}) copy-start(f32[1,128,512]{2,1,0:T(8,128)} %param.12) | copy-start | bytes 786436
  103.5 33.2 %copy-start.3 = (bf16[128,512]{1,0:T(8,128)(2,1)S(1)}, bf16[128,512]{1,0:T(8,128)(2,1)}, u32[]{:S(2)}) copy-start(bf16[128,512]{1,0:T(8,128)(2,1)} %reduce-scatter.2.cloned.1.call-done.refs_0_.refs_1_) | copy-start | bytes 393220
  103.5 25.4 %collective-permute-start.6 = (bf16[512,256]{1,0:T(8,128)(2,1)S(1)}, bf16[512,256]{1,0:T(8,128)(2,1)S(1)}, u32[]{:S(2)}, u32[]{:S(2)}) collective-permute-start(bf16[512,256]{1,0:T(8,128)(2,1)S(1)} %shard_map.130), channel_id=1, source_target_pairs={{256,0},{384,128},{257,1},{385,129},{258,2},{386,130},{259,3},{387... | collective-permute-start | bytes 786440 | tf_op jit(solution)/shard_map/ppermute | solution.py:53
  114.7 22.1 %all-to-all-start.4 = ((f32[32,8,128]{2,1,0:T(8,128)}), f32[32,8,128]{2,1,0:T(8,128)S(1)}, u32[]{:S(2)}, u32[]{:S(2)}) async-start(f32[32,8,128]{2,1,0:T(8,128)} %shard_map.129), calls=%async_computation.5 | async-start | bytes 262144 | tf_op jit(solution)/shard_map/all_to_all | solution.py:32
  129.0 7.8 %copy-start.4 = (f32[1,128,512]{2,1,0:T(8,128)S(1)}, f32[1,128,512]{2,1,0:T(8,128)}, u32[]{:S(2)}) copy-start(f32[1,128,512]{2,1,0:T(8,128)} %param.13) | copy-start | bytes 786436
  136.8 1.0 copy-start.5
  138.7 38.3 %all-to-all-start.5 = ((bf16[16,128,256]{2,1,0:T(8,128)(2,1)}), bf16[16,128,256]{2,1,0:T(8,128)(2,1)S(1)}, u32[]{:S(2)}, u32[]{:S(2)}) async-start(bf16[16,128,256]{2,1,0:T(8,128)(2,1)} %shard_map.131.refs_5_), calls=%async_computation.6 | async-start | bytes 2097152 | tf_op jit(solution)/shard_map/all_to_all | solution.py:32
  171.9 3.8 %collective-permute-start.7 = (bf16[512,512]{1,0:T(8,128)(2,1)S(1)}, bf16[512,512]{1,0:T(8,128)(2,1)S(1)}, u32[]{:S(2)}, u32[]{:S(2)}) collective-permute-start(bf16[512,512]{1,0:T(8,128)(2,1)S(1)} %all_gather.7.refs_4_), channel_id=1, source_target_pairs={{0,1},{1,0},{2,3},{3,2},{4,5},{5,4},{6,7},{7,6},{8,9},{9,8},{10,11... | collective-permute-start | bytes 1572872 | tf_op jit(solution)/shard_map/ppermute | solution.py:48
  176.9 14.3 %all-to-all-start.6 = ((bf16[4,128,512]{2,1,0:T(8,128)(2,1)}), bf16[4,128,512]{2,1,0:T(8,128)(2,1)S(1)}, u32[]{:S(2)}, u32[]{:S(2)}) async-start(bf16[4,128,512]{2,1,0:T(8,128)(2,1)} %shard_map.134), calls=%async_computation.7 | async-start | bytes 1048576 | tf_op jit(solution)/shard_map/all_to_all | solution.py:32
Sparse Core Ops, SparseCore 0:
  53.8 40.8 reduce-scatter.1

commit v11 on v10

--- a/solution.py
+++ b/solution.py
@@ -358,8 +358,6 @@
     top_shape = shape((all_toks, cores * rows), bf16)
     top = local(top_kernel, [top_shape], came, after=fresh_blocks[:1])[0]
     behind = [from_behind(top, "zlo", 1)]
-    pair = local(pair_kernel, [top_shape], top, behind[0])[0]
-    behind.append(from_behind(pair, "zlo", 2))
 
     first_axes = ("zlo", "zhi")
     last_axes = ("y", "x", "core")
@@ -368,6 +366,8 @@
         squares_kernel, [shape((lax.axis_size(first_axes),) + tile, f32)], grad, after=[top] + fresh_normed[1:]
     )[0]
     squares = exchange(squares, first_axes)
+    pair = local(pair_kernel, [top_shape], top, behind[0], after=[squares])[0]
+    behind.append(from_behind(pair, "zlo", 2))
     squares = local(relay_kernel, [shape((lax.axis_size(last_axes),) + tile, f32)], squares)[0]
     squares = exchange(squares, last_axes)
     suffix = local(

time: 200 us -> 198 us (0.990)
  the two profiles are of different devices: /device:TPU:96 before, /device:TPU:1 now
where the time goes in v11:
time: 198 us; the launch traced here: 197 us
  starting transfers between devices  63.6 us (32%)
  blocking collectives  58.5 us (30%)
  waiting for transfers between devices  39.8 us (20%)
  Pallas kernels  18.3 us (9%)
  between operations  14.3 us (7%)
  local copies, waits for them, and re-layouts  2.18 us (1%)
    all_to_all x6, starting transfers between devices, exchange(): return lax.all_to_all(blocks, axis, 0, 0)  32.7 us
    all_gather x1, blocking collectives, per_device(): weights_old = lax.all_gather(weights_old, 'zhi', axis=0, tiled=True)  30.9 us
    all_to_all x6, waiting for transfers between devices, exchange(): return lax.all_to_all(blocks, axis, 0, 0)  25.7 us
    all_gather x1, blocking collectives, per_device(): weights_new = lax.all_gather(weights_new, 'zhi', axis=0, tiled=True)  20.8 us
    ppermute x3, starting transfers between devices, swap_cores(): return lax.ppermute(block, 'core', [(0, 1), (1, 0)])  19.3 us
    pallas_call x15, Pallas kernels, local(): pl.pallas_call(body, out_shape=out_shapes, in_specs=[pl.BlockSpec(memory_...  14.4 us
    ppermute x3, starting transfers between devices, shift(): lax.ppermute(parts[k], axis, [(i, (i + k) % size) for i in range(size)])  8.77 us
    all_to_all x1, blocking collectives, exchange(): return lax.all_to_all(blocks, axis, 0, 0)  6.84 us
  transfers between devices with their start and end apart: 15, of which 9 were waited for; matrix products, arithmetic and copies ran while one was open for 0% of the time, Pallas kernels for 7%

profile of v11, /device:TPU:1, one launch (start us, length us, event | category | flops | bytes accessed | tf_op | source)
XLA Modules:
  0.0 197.3 jit_solution(13294978300798977415)
XLA Ops:
  7.2 3.8 %shard_map.120 = (bf16[4,128,1536]{2,1,0:T(8,128)(2,1)}, bf16[128,512]{1,0:T(8,128)(2,1)}) custom-call(bf16[128,4096]{1,0:T(8,128)(2,1)} %bitcast.36, bf16[128,512]{1,0:T(8,128)(2,1)} %bitcast.39, f32[128,512]{1,0:T(8,128)} %bitcast.30), custom_call_target="tpu_custom_call" | custom-call | tf_op jit(solution)/shard_map/pallas_call | solution.py:111
  11.0 5.0 %all-to-all-start = ((bf16[4,128,1536]{2,1,0:T(8,128)(2,1)}), bf16[4,128,1536]{2,1,0:T(8,128)(2,1)S(1)}, u32[]{:S(2)}, u32[]{:S(2)}) async-start(bf16[4,128,1536]{2,1,0:T(8,128)(2,1)} %get-tuple-element.23), calls=%async_computation | async-start | bytes 3145728 | tf_op jit(solution)/shard_map/all_to_all | solution.py:32
  16.0 0.0 reduce-scatter.2.cloned.1.call-start
  16.0 0.0 copy-done.7
  16.0 0.1 copy.18.refs_1_
  16.2 0.0 copy-done.9
  16.2 30.9 %all_gather.6.refs_1_ = bf16[512,512]{1,0:T(8,128)(2,1)S(1)} all-gather(bf16[128,512]{1,0:T(8,128)(2,1)S(1)} %copy-done.9), channel_id=1, replica_groups=mesh['zlo'=4,'y'=4,'zhi'=4,'x'=4,'core'=2] {'zhi'}, dimensions={0}, use_global_device_ids=true | all-gather | bytes 655360 | tf_op jit(solution)/shard_map/all_gather | solution.py:306
  47.0 0.0 all-to-all-done
  47.0 0.5 shard_map.121.refs_2_
  47.5 6.5 %collective-permute-start.1 = (bf16[512,512]{1,0:T(8,128)(2,1)S(1)}, bf16[512,512]{1,0:T(8,128)(2,1)}, u32[]{:S(2)}, u32[]{:S(2)}) collective-permute-start(bf16[512,512]{1,0:T(8,128)(2,1)S(1)} %shard_map.121.refs_2_), channel_id=1, source_target_pairs={{0,1},{1,0},{2,3},{3,2},{4,5},{5,4},{6,7},{7,6},{8,9},{9,8},{10,11... | collective-permute-start | bytes 1572872 | tf_op jit(solution)/shard_map/ppermute | solution.py:48
  54.0 1.9 collective-permute-start
  55.9 0.1 copy.19.refs_1_
  56.1 0.5 shard_map.122.refs_0_
  56.6 0.0 collective-permute-done.1.refs_1_
  56.6 1.9 shard_map.123.refs_4_
  58.5 0.0 reduce-scatter.2.cloned.1.call-update
  58.5 0.0 collective-permute-done.refs_2_
  58.6 0.9 shard_map.124
  59.5 6.8 %all_to_all.35.refs_2_ = f32[4,8,512]{2,1,0:T(8,128)S(1)} all-to-all(f32[4,8,512]{2,1,0:T(8,128)S(1)} %get-tuple-element.28), channel_id=1, replica_groups=mesh['zlo'=4,'y'=4,'zhi'=4,'x'=4,'core'=2] {'x'}, dimensions={0} | all-to-all | bytes 131072 | tf_op jit(solution)/shard_map/all_to_all | solution.py:32
  66.3 1.5 shard_map.125
  67.8 4.3 %all-to-all-start.2 = ((bf16[4,512,256]{2,1,0:T(8,128)(2,1)}), bf16[4,512,256]{2,1,0:T(8,128)(2,1)S(1)}, u32[]{:S(2)}, u32[]{:S(2)}) async-start(bf16[4,512,256]{2,1,0:T(8,128)(2,1)} %shard_map.125), calls=%async_computation.3 | async-start | bytes 2097152 | tf_op jit(solution)/shard_map/all_to_all | solution.py:32
  72.1 0.0 copy-done
  72.1 0.0 copy-done.6
  72.1 0.0 copy-done.8
  72.1 2.4 %shard_map.126 = (bf16[128,1024]{1,0:T(8,128)(2,1)S(1)}, bf16[128,1024]{1,0:T(8,128)(2,1)}, bf16[128,1024]{1,0:T(8,128)(2,1)}, bf16[128,1024]{1,0:T(8,128)(2,1)}) custom-call(s32[2,32]{1,0:T(2,128)S(1)} %copy-done.8, bf16[128,4096]{1,0:T(8,128)(2,1)S(1)} %bitcast.29, f32[1,4096]{1,0:T(1,128)S(1)} %copy-done.7, bf16[5,4096]{1,0:T(8,128)(2,1)S(1)} %copy-done.6), custom_call_target="tpu_custom_call" | custom-call | tf_op jit(solution)/shard_map/pallas_call | solution.py:68
  74.5 2.2 %collective-permute-start.2 = (bf16[128,1024]{1,0:T(8,128)(2,1)}, bf16[128,1024]{1,0:T(8,128)(2,1)S(1)}, u32[]{:S(2)}, u32[]{:S(2)}) collective-permute-start(bf16[128,1024]{1,0:T(8,128)(2,1)} %get-tuple-element.31), channel_id=1, source_target_pairs={{0,2},{2,4},{4,6},{6,0},{1,3},{3,5},{5,7},{7,1},{8,10},{10,12},{12... | collective-permute-start | bytes 786440 | tf_op jit(solution)/shard_map/ppermute | solution.py:43
  76.7 3.7 %collective-permute-start.3 = (bf16[128,1024]{1,0:T(8,128)(2,1)}, bf16[128,1024]{1,0:T(8,128)(2,1)S(1)}, u32[]{:S(2)}, u32[]{:S(2)}) collective-permute-start(bf16[128,1024]{1,0:T(8,128)(2,1)} %get-tuple-element.32), channel_id=1, source_target_pairs={{0,4},{2,6},{4,0},{6,2},{1,5},{3,7},{5,1},{7,3},{8,12},{10,14},{12... | collective-permute-start | bytes 786440 | tf_op jit(solution)/shard_map/ppermute | solution.py:43
  80.4 2.9 %collective-permute-start.4 = (bf16[128,1024]{1,0:T(8,128)(2,1)}, bf16[128,1024]{1,0:T(8,128)(2,1)S(1)}, u32[]{:S(2)}, u32[]{:S(2)}) collective-permute-start(bf16[128,1024]{1,0:T(8,128)(2,1)} %get-tuple-element.33), channel_id=1, source_target_pairs={{0,6},{2,0},{4,2},{6,4},{1,7},{3,1},{5,3},{7,5},{8,14},{10,8},{12,... | collective-permute-start | bytes 786440 | tf_op jit(solution)/shard_map/ppermute | solution.py:43
  83.3 2.0 %all-to-all-done.2.refs_0_ = bf16[4,512,256]{2,1,0:T(8,128)(2,1)S(1)} async-done(((bf16[4,512,256]{2,1,0:T(8,128)(2,1)}), bf16[4,512,256]{2,1,0:T(8,128)(2,1)S(1)}, u32[]{:S(2)}, u32[]{:S(2)}) %all-to-all-start.2) | async-done | bytes 1048608 | tf_op jit(solution)/shard_map/all_to_all | solution.py:32
  85.4 0.1 shard_map.127.refs_1_.refs_0_
  85.5 1.3 collective-permute-start.5
  86.8 0.0 collective-permute-done.2.refs_2_.refs_1_
  86.8 2.0 %collective-permute-done.3.refs_3_.refs_2_ = bf16[128,1024]{1,0:T(8,128)(2,1)S(1)} collective-permute-done((bf16[128,1024]{1,0:T(8,128)(2,1)}, bf16[128,1024]{1,0:T(8,128)(2,1)S(1)}, u32[]{:S(2)}, u32[]{:S(2)}) %collective-permute-start.3) | collective-permute-done | bytes 262176 | tf_op jit(solution)/shard_map/ppermute | solution.py:43
  88.8 3.6 %collective-permute-done.4.refs_4_.refs_3_ = bf16[128,1024]{1,0:T(8,128)(2,1)S(1)} collective-permute-done((bf16[128,1024]{1,0:T(8,128)(2,1)}, bf16[128,1024]{1,0:T(8,128)(2,1)S(1)}, u32[]{:S(2)}, u32[]{:S(2)}) %collective-permute-start.4) | collective-permute-done | bytes 262176 | tf_op jit(solution)/shard_map/ppermute | solution.py:43
  92.4 5.0 %reduce-scatter.2.cloned.1.call-done.refs_0_.refs_1_ = bf16[128,512]{1,0:T(8,128)(2,1)} async-done(((bf16[512,512]{1,0:T(8,128)(2,1)}), bf16[128,512]{1,0:T(8,128)(2,1)}) %reduce-scatter.2.cloned.1.call-update) | async-done | bytes 131088 | tf_op jit(solution)/shard_map/reduce_scatter | solution.py:324
  97.4 0.9 copy-done.2
  98.3 0.8 shard_map.128
  99.1 4.9 %all-to-all-start.3 = ((f32[16,8,128]{2,1,0:T(8,128)}), f32[16,8,128]{2,1,0:T(8,128)S(1)}, u32[]{:S(2)}, u32[]{:S(2)}) async-start(f32[16,8,128]{2,1,0:T(8,128)} %shard_map.128), calls=%async_computation.4 | async-start | bytes 131072 | tf_op jit(solution)/shard_map/all_to_all | solution.py:32
  104.0 0.0 collective-permute-done.5.refs_1_
  104.0 11.7 %all-to-all-done.3.refs_0_.refs_2_ = f32[16,8,128]{2,1,0:T(8,128)S(1)} async-done(((f32[16,8,128]{2,1,0:T(8,128)}), f32[16,8,128]{2,1,0:T(8,128)S(1)}, u32[]{:S(2)}, u32[]{:S(2)}) %all-to-all-start.3) | async-done | bytes 65568 | tf_op jit(solution)/shard_map/all_to_all | solution.py:32
  115.6 0.1 shard_map.130
  115.7 0.0 copy-start.1
  115.7 0.0 copy-start.3
  115.7 1.4 collective-permute-start.6
  117.2 0.7 shard_map.129
  117.8 11.5 %all-to-all-start.4 = ((f32[32,8,128]{2,1,0:T(8,128)}), f32[32,8,128]{2,1,0:T(8,128)S(1)}, u32[]{:S(2)}, u32[]{:S(2)}) async-start(f32[32,8,128]{2,1,0:T(8,128)} %shard_map.129), calls=%async_computation.5 | async-start | bytes 262144 | tf_op jit(solution)/shard_map/all_to_all | solution.py:32
  129.3 2.4 %collective-permute-done.6.refs_2_ = bf16[512,256]{1,0:T(8,128)(2,1)S(1)} collective-permute-done((bf16[512,256]{1,0:T(8,128)(2,1)S(1)}, bf16[512,256]{1,0:T(8,128)(2,1)S(1)}, u32[]{:S(2)}, u32[]{:S(2)}) %collective-permute-start.6) | collective-permute-done | bytes 262176 | tf_op jit(solution)/shard_map/ppermute | solution.py:53
  131.7 1.2 shard_map.131.refs_5_
  132.9 4.0 %all-to-all-done.4.refs_0_ = f32[32,8,128]{2,1,0:T(8,128)S(1)} async-done(((f32[32,8,128]{2,1,0:T(8,128)}), f32[32,8,128]{2,1,0:T(8,128)S(1)}, u32[]{:S(2)}, u32[]{:S(2)}) %all-to-all-start.4) | async-done | bytes 131104 | tf_op jit(solution)/shard_map/all_to_all | solution.py:32
  136.9 0.0 copy-done.1
  137.0 0.0 copy-start.5
  137.0 0.9 copy-done.5
  137.9 0.9 shard_map.132
  138.8 3.7 %all-to-all-start.5 = ((bf16[16,128,256]{2,1,0:T(8,128)(2,1)}), bf16[16,128,256]{2,1,0:T(8,128)(2,1)S(1)}, u32[]{:S(2)}, u32[]{:S(2)}) async-start(bf16[16,128,256]{2,1,0:T(8,128)(2,1)} %shard_map.131.refs_5_), calls=%async_computation.6 | async-start | bytes 2097152 | tf_op jit(solution)/shard_map/all_to_all | solution.py:32
  142.5 20.8 %all_gather.7.refs_4_ = bf16[512,512]{1,0:T(8,128)(2,1)S(1)} all-gather(bf16[128,512]{1,0:T(8,128)(2,1)S(1)} %get-tuple-element.36), channel_id=1, replica_groups=mesh['zlo'=4,'y'=4,'zhi'=4,'x'=4,'core'=2] {'zhi'}, dimensions={0}, use_global_device_ids=true | all-gather | bytes 655360 | tf_op jit(solution)/shard_map/all_gather | solution.py:391
  163.3 10.9 %collective-permute-start.7 = (bf16[512,512]{1,0:T(8,128)(2,1)S(1)}, bf16[512,512]{1,0:T(8,128)(2,1)S(1)}, u32[]{:S(2)}, u32[]{:S(2)}) collective-permute-start(bf16[512,512]{1,0:T(8,128)(2,1)S(1)} %all_gather.7.refs_4_), channel_id=1, source_target_pairs={{0,1},{1,0},{2,3},{3,2},{4,5},{5,4},{6,7},{7,6},{8,9},{9,8},{10,11... | collective-permute-start | bytes 1572872 | tf_op jit(solution)/shard_map/ppermute | solution.py:48
  174.2 0.4 shard_map.133.refs_5_
  174.7 1.1 collective-permute-done.7.refs_4_
  175.8 1.3 shard_map.134
  177.0 0.0 all-to-all-done.5.refs_0_
  177.0 3.5 %all-to-all-start.6 = ((bf16[4,128,512]{2,1,0:T(8,128)(2,1)}), bf16[4,128,512]{2,1,0:T(8,128)(2,1)S(1)}, u32[]{:S(2)}, u32[]{:S(2)}) async-start(bf16[4,128,512]{2,1,0:T(8,128)(2,1)} %shard_map.134), calls=%async_computation.7 | async-start | bytes 1048576 | tf_op jit(solution)/shard_map/all_to_all | solution.py:32
  180.5 1.2 shard_map.135
  181.7 8.0 %all-to-all-done.6 = bf16[4,128,512]{2,1,0:T(8,128)(2,1)S(1)} async-done(((bf16[4,128,512]{2,1,0:T(8,128)(2,1)}), bf16[4,128,512]{2,1,0:T(8,128)(2,1)S(1)}, u32[]{:S(2)}, u32[]{:S(2)}) %all-to-all-start.6) | async-done | bytes 524320 | tf_op jit(solution)/shard_map/all_to_all | solution.py:32
  189.7 0.7 reduce_sum.12
  (11 shorter events, 0.0 us)
Async XLA Ops:
  11.0 5.0 %copy-start.7 = (f32[1,4096]{1,0:T(1,128)S(1)}, f32[1,4096]{1,0:T(1,128)}, u32[]{:S(2)}) copy-start(f32[1,4096]{1,0:T(1,128)} %refs_2_.1) | copy-start | bytes 49156
  11.0 5.2 %copy-start.9 = (bf16[128,512]{1,0:T(8,128)(2,1)S(1)}, bf16[128,512]{1,0:T(8,128)(2,1)}, u32[]{:S(2)}) copy-start(bf16[128,512]{1,0:T(8,128)(2,1)} %get-tuple-element.24) | copy-start | bytes 393220
  11.0 36.0 %all-to-all-start = ((bf16[4,128,1536]{2,1,0:T(8,128)(2,1)}), bf16[4,128,1536]{2,1,0:T(8,128)(2,1)S(1)}, u32[]{:S(2)}, u32[]{:S(2)}) async-start(bf16[4,128,1536]{2,1,0:T(8,128)(2,1)} %get-tuple-element.23), calls=%async_computation | async-start | bytes 3145728 | tf_op jit(solution)/shard_map/all_to_all | solution.py:32
  16.0 81.4 %reduce-scatter.2.cloned.1.call-start = ((), (), s32[]{:S(2)}) async-start(), calls=%async_computation.8 | async-start | bytes 655360 | tf_op jit(solution)/shard_map/reduce_scatter | solution.py:324
  47.5 9.0 %collective-permute-start.1 = (bf16[512,512]{1,0:T(8,128)(2,1)S(1)}, bf16[512,512]{1,0:T(8,128)(2,1)}, u32[]{:S(2)}, u32[]{:S(2)}) collective-permute-start(bf16[512,512]{1,0:T(8,128)(2,1)S(1)} %shard_map.121.refs_2_), channel_id=1, source_target_pairs={{0,1},{1,0},{2,3},{3,2},{4,5},{5,4},{6,7},{7,6},{8,9},{9,8},{10,11... | collective-permute-start | bytes 1572872 | tf_op jit(solution)/shard_map/ppermute | solution.py:48
  54.0 4.5 %collective-permute-start = (bf16[512,512]{1,0:T(8,128)(2,1)S(1)}, bf16[512,512]{1,0:T(8,128)(2,1)S(1)}, u32[]{:S(2)}, u32[]{:S(2)}) collective-permute-start(bf16[512,512]{1,0:T(8,128)(2,1)S(1)} %all_gather.6.refs_1_), channel_id=1, source_target_pairs={{0,1},{1,0},{2,3},{3,2},{4,5},{5,4},{6,7},{7,6},{8,9},{9,8},{10,11... | collective-permute-start | bytes 1572872 | tf_op jit(solution)/shard_map/ppermute | solution.py:48
  67.8 4.3 %copy-start = (bf16[2,1,64,4096]{3,2,1,0:T(8,128)(2,1)S(1)}, bf16[2,1,64,4096]{3,2,1,0:T(8,128)(2,1)}, u32[]{:S(2)}) copy-start(bf16[2,1,64,4096]{3,2,1,0:T(8,128)(2,1)} %param.15) | copy-start | bytes 3145732
  67.8 4.3 %copy-start.6 = (bf16[5,4096]{1,0:T(8,128)(2,1)S(1)}, bf16[5,4096]{1,0:T(8,128)(2,1)}, u32[]{:S(2)}) copy-start(bf16[5,4096]{1,0:T(8,128)(2,1)} %refs_3_.1) | copy-start | bytes 122884
  67.8 4.3 %copy-start.8 = (s32[2,32]{1,0:T(2,128)S(1)}, s32[2,32]{1,0:T(2,128)}, u32[]{:S(2)}) copy-start(s32[2,32]{1,0:T(2,128)} %refs_0_.1) | copy-start | bytes 772
  67.8 17.5 %all-to-all-start.2 = ((bf16[4,512,256]{2,1,0:T(8,128)(2,1)}), bf16[4,512,256]{2,1,0:T(8,128)(2,1)S(1)}, u32[]{:S(2)}, u32[]{:S(2)}) async-start(bf16[4,512,256]{2,1,0:T(8,128)(2,1)} %shard_map.125), calls=%async_computation.3 | async-start | bytes 2097152 | tf_op jit(solution)/shard_map/all_to_all | solution.py:32
  74.5 12.3 %collective-permute-start.2 = (bf16[128,1024]{1,0:T(8,128)(2,1)}, bf16[128,1024]{1,0:T(8,128)(2,1)S(1)}, u32[]{:S(2)}, u32[]{:S(2)}) collective-permute-start(bf16[128,1024]{1,0:T(8,128)(2,1)} %get-tuple-element.31), channel_id=1, source_target_pairs={{0,2},{2,4},{4,6},{6,0},{1,3},{3,5},{5,7},{7,1},{8,10},{10,12},{12... | collective-permute-start | bytes 786440 | tf_op jit(solution)/shard_map/ppermute | solution.py:43
  76.7 12.1 %collective-permute-start.3 = (bf16[128,1024]{1,0:T(8,128)(2,1)}, bf16[128,1024]{1,0:T(8,128)(2,1)S(1)}, u32[]{:S(2)}, u32[]{:S(2)}) collective-permute-start(bf16[128,1024]{1,0:T(8,128)(2,1)} %get-tuple-element.32), channel_id=1, source_target_pairs={{0,4},{2,6},{4,0},{6,2},{1,5},{3,7},{5,1},{7,3},{8,12},{10,14},{12... | collective-permute-start | bytes 786440 | tf_op jit(solution)/shard_map/ppermute | solution.py:43
  80.4 12.0 %collective-permute-start.4 = (bf16[128,1024]{1,0:T(8,128)(2,1)}, bf16[128,1024]{1,0:T(8,128)(2,1)S(1)}, u32[]{:S(2)}, u32[]{:S(2)}) collective-permute-start(bf16[128,1024]{1,0:T(8,128)(2,1)} %get-tuple-element.33), channel_id=1, source_target_pairs={{0,6},{2,0},{4,2},{6,4},{1,7},{3,1},{5,3},{7,5},{8,14},{10,8},{12,... | collective-permute-start | bytes 786440 | tf_op jit(solution)/shard_map/ppermute | solution.py:43
  85.5 18.5 %collective-permute-start.5 = (bf16[512,256]{1,0:T(8,128)(2,1)S(1)}, bf16[512,256]{1,0:T(8,128)(2,1)S(1)}, u32[]{:S(2)}, u32[]{:S(2)}) collective-permute-start(bf16[512,256]{1,0:T(8,128)(2,1)S(1)} %shard_map.127.refs_1_.refs_0_), channel_id=1, source_target_pairs={{128,0},{256,128},{384,256},{129,1},{257,129},{385,257},{130,2},{2... | collective-permute-start | bytes 786440 | tf_op jit(solution)/shard_map/ppermute | solution.py:53
  97.4 0.9 copy-start.2
  99.1 16.5 %all-to-all-start.3 = ((f32[16,8,128]{2,1,0:T(8,128)}), f32[16,8,128]{2,1,0:T(8,128)S(1)}, u32[]{:S(2)}, u32[]{:S(2)}) async-start(f32[16,8,128]{2,1,0:T(8,128)} %shard_map.128), calls=%async_computation.4 | async-start | bytes 131072 | tf_op jit(solution)/shard_map/all_to_all | solution.py:32
  115.7 21.2 %copy-start.1 = (f32[1,128,512]{2,1,0:T(8,128)S(1)}, f32[1,128,512]{2,1,0:T(8,128)}, u32[]{:S(2)}) copy-start(f32[1,128,512]{2,1,0:T(8,128)} %param.12) | copy-start | bytes 786436
  115.7 21.2 %copy-start.3 = (bf16[128,512]{1,0:T(8,128)(2,1)S(1)}, bf16[128,512]{1,0:T(8,128)(2,1)}, u32[]{:S(2)}) copy-start(bf16[128,512]{1,0:T(8,128)(2,1)} %reduce-scatter.2.cloned.1.call-done.refs_0_.refs_1_) | copy-start | bytes 393220
  115.7 16.0 %collective-permute-start.6 = (bf16[512,256]{1,0:T(8,128)(2,1)S(1)}, bf16[512,256]{1,0:T(8,128)(2,1)S(1)}, u32[]{:S(2)}, u32[]{:S(2)}) collective-permute-start(bf16[512,256]{1,0:T(8,128)(2,1)S(1)} %shard_map.130), channel_id=1, source_target_pairs={{256,0},{384,128},{257,1},{385,129},{258,2},{386,130},{259,3},{387... | collective-permute-start | bytes 786440 | tf_op jit(solution)/shard_map/ppermute | solution.py:53
  117.8 19.1 %all-to-all-start.4 = ((f32[32,8,128]{2,1,0:T(8,128)}), f32[32,8,128]{2,1,0:T(8,128)S(1)}, u32[]{:S(2)}, u32[]{:S(2)}) async-start(f32[32,8,128]{2,1,0:T(8,128)} %shard_map.129), calls=%async_computation.5 | async-start | bytes 262144 | tf_op jit(solution)/shard_map/all_to_all | solution.py:32
  131.7 5.3 %copy-start.4 = (f32[1,128,512]{2,1,0:T(8,128)S(1)}, f32[1,128,512]{2,1,0:T(8,128)}, u32[]{:S(2)}) copy-start(f32[1,128,512]{2,1,0:T(8,128)} %param.13) | copy-start | bytes 786436
  137.0 1.0 copy-start.5
  138.8 38.2 %all-to-all-start.5 = ((bf16[16,128,256]{2,1,0:T(8,128)(2,1)}), bf16[16,128,256]{2,1,0:T(8,128)(2,1)S(1)}, u32[]{:S(2)}, u32[]{:S(2)}) async-start(bf16[16,128,256]{2,1,0:T(8,128)(2,1)} %shard_map.131.refs_5_), calls=%async_computation.6 | async-start | bytes 2097152 | tf_op jit(solution)/shard_map/all_to_all | solution.py:32
  163.3 12.4 %collective-permute-start.7 = (bf16[512,512]{1,0:T(8,128)(2,1)S(1)}, bf16[512,512]{1,0:T(8,128)(2,1)S(1)}, u32[]{:S(2)}, u32[]{:S(2)}) collective-permute-start(bf16[512,512]{1,0:T(8,128)(2,1)S(1)} %all_gather.7.refs_4_), channel_id=1, source_target_pairs={{0,1},{1,0},{2,3},{3,2},{4,5},{5,4},{6,7},{7,6},{8,9},{9,8},{10,11... | collective-permute-start | bytes 1572872 | tf_op jit(solution)/shard_map/ppermute | solution.py:48
  177.0 12.7 %all-to-all-start.6 = ((bf16[4,128,512]{2,1,0:T(8,128)(2,1)}), bf16[4,128,512]{2,1,0:T(8,128)(2,1)S(1)}, u32[]{:S(2)}, u32[]{:S(2)}) async-start(bf16[4,128,512]{2,1,0:T(8,128)(2,1)} %shard_map.134), calls=%async_computation.7 | async-start | bytes 1048576 | tf_op jit(solution)/shard_map/all_to_all | solution.py:32
Sparse Core Ops, SparseCore 0:
  58.7 38.6 reduce-scatter.1

commit v12 on v11

--- a/solution.py
+++ b/solution.py
@@ -366,9 +366,9 @@
         squares_kernel, [shape((lax.axis_size(first_axes),) + tile, f32)], grad, after=[top] + fresh_normed[1:]
     )[0]
     squares = exchange(squares, first_axes)
+    squares = local(relay_kernel, [shape((lax.axis_size(last_axes),) + tile, f32)], squares)[0]
     pair = local(pair_kernel, [top_shape], top, behind[0], after=[squares])[0]
     behind.append(from_behind(pair, "zlo", 2))
-    squares = local(relay_kernel, [shape((lax.axis_size(last_axes),) + tile, f32)], squares)[0]
     squares = exchange(squares, last_axes)
     suffix = local(
         functools.partial(suffix_kernel, group),

time: 198 us -> 194 us (0.980)
  blocking collectives: 58.5 us -> 73.3 us
  waiting for transfers between devices: 39.8 us -> 27.8 us
  starting transfers between devices: 63.6 us -> 56 us
    all_to_all x1 -> x2, blocking collectives: 6.84 us -> 23.2 us  [exchange(): return lax.all_to_all(blocks, axis, 0, 0)]
    all_to_all x6 -> x5, waiting for transfers between devices: 25.7 us -> 12.9 us  [exchange(): return lax.all_to_all(blocks, axis, 0, 0)]
    all_to_all x6 -> x5, starting transfers between devices: 32.7 us -> 28.9 us  [exchange(): return lax.all_to_all(blocks, axis, 0, 0)]
    ppermute x3, starting transfers between devices: 19.3 us -> 15.6 us  [swap_cores(): return lax.ppermute(block, 'core', [(0, 1), (1, 0)])]
  transfers between devices with their start and end apart: 15 -> 14, of which waited for: 9 -> 8; matrix products, arithmetic and copies ran while one was open for 0% -> 0% of each run, Pallas kernels for 7% -> 6%
where the time goes in v12:
time: 194 us; the launch traced here: 192 us
  blocking collectives  73.3 us (38%)
  starting transfers between devices  56 us (29%)
  waiting for transfers between devices  27.8 us (14%)
  Pallas kernels  17.7 us (9%)
  between operations  14.2 us (7%)
  local copies, waits for them, and re-layouts  2.18 us (1%)
    all_gather x1, blocking collectives, per_device(): weights_old = lax.all_gather(weights_old, 'zhi', axis=0, tiled=True)  30.9 us
    all_to_all x5, starting transfers between devices, exchange(): return lax.all_to_all(blocks, axis, 0, 0)  28.9 us
    all_to_all x2, blocking collectives, exchange(): return lax.all_to_all(blocks, axis, 0, 0)  23.2 us
    all_gather x1, blocking collectives, per_device(): weights_new = lax.all_gather(weights_new, 'zhi', axis=0, tiled=True)  19.2 us
    ppermute x3, starting transfers between devices, swap_cores(): return lax.ppermute(block, 'core', [(0, 1), (1, 0)])  15.6 us
    pallas_call x15, Pallas kernels, local(): pl.pallas_call(body, out_shape=out_shapes, in_specs=[pl.BlockSpec(memory_...  13.8 us
    all_to_all x5, waiting for transfers between devices, exchange(): return lax.all_to_all(blocks, axis, 0, 0)  12.9 us
    ppermute x3, starting transfers between devices, shift(): lax.ppermute(parts[k], axis, [(i, (i + k) % size) for i in range(size)])  8.78 us
  transfers between devices with their start and end apart: 14, of which 8 were waited for; matrix products, arithmetic and copies ran while one was open for 0% of the time, Pallas kernels for 6%

profile of v12, /device:TPU:1, one launch (start us, length us, event | category | flops | bytes accessed | tf_op | source)
XLA Modules:
  0.0 191.9 jit_solution(8607194487627650311)
XLA Ops:
  7.2 3.8 %shard_map.120 = (bf16[4,128,1536]{2,1,0:T(8,128)(2,1)}, bf16[128,512]{1,0:T(8,128)(2,1)}) custom-call(bf16[128,4096]{1,0:T(8,128)(2,1)} %bitcast.36, bf16[128,512]{1,0:T(8,128)(2,1)} %bitcast.39, f32[128,512]{1,0:T(8,128)} %bitcast.30), custom_call_target="tpu_custom_call" | custom-call | tf_op jit(solution)/shard_map/pallas_call | solution.py:111
  11.0 5.0 %all-to-all-start = ((bf16[4,128,1536]{2,1,0:T(8,128)(2,1)}), bf16[4,128,1536]{2,1,0:T(8,128)(2,1)S(1)}, u32[]{:S(2)}, u32[]{:S(2)}) async-start(bf16[4,128,1536]{2,1,0:T(8,128)(2,1)} %get-tuple-element.23), calls=%async_computation | async-start | bytes 3145728 | tf_op jit(solution)/shard_map/all_to_all | solution.py:32
  16.0 0.0 reduce-scatter.2.cloned.1.call-start
  16.0 0.0 copy-done.7
  16.0 0.1 copy.18.refs_1_
  16.2 0.0 copy-done.9
  16.2 30.9 %all_gather.6.refs_1_ = bf16[512,512]{1,0:T(8,128)(2,1)S(1)} all-gather(bf16[128,512]{1,0:T(8,128)(2,1)S(1)} %copy-done.9), channel_id=1, replica_groups=mesh['zlo'=4,'y'=4,'zhi'=4,'x'=4,'core'=2] {'zhi'}, dimensions={0}, use_global_device_ids=true | all-gather | bytes 655360 | tf_op jit(solution)/shard_map/all_gather | solution.py:306
  47.0 0.0 all-to-all-done
  47.0 0.5 shard_map.121.refs_2_
  47.5 6.5 %collective-permute-start.1 = (bf16[512,512]{1,0:T(8,128)(2,1)S(1)}, bf16[512,512]{1,0:T(8,128)(2,1)}, u32[]{:S(2)}, u32[]{:S(2)}) collective-permute-start(bf16[512,512]{1,0:T(8,128)(2,1)S(1)} %shard_map.121.refs_2_), channel_id=1, source_target_pairs={{0,1},{1,0},{2,3},{3,2},{4,5},{5,4},{6,7},{7,6},{8,9},{9,8},{10,11... | collective-permute-start | bytes 1572872 | tf_op jit(solution)/shard_map/ppermute | solution.py:48
  54.0 1.9 %collective-permute-start = (bf16[512,512]{1,0:T(8,128)(2,1)S(1)}, bf16[512,512]{1,0:T(8,128)(2,1)S(1)}, u32[]{:S(2)}, u32[]{:S(2)}) collective-permute-start(bf16[512,512]{1,0:T(8,128)(2,1)S(1)} %all_gather.6.refs_1_), channel_id=1, source_target_pairs={{0,1},{1,0},{2,3},{3,2},{4,5},{5,4},{6,7},{7,6},{8,9},{9,8},{10,11... | collective-permute-start | bytes 1572872 | tf_op jit(solution)/shard_map/ppermute | solution.py:48
  55.9 0.1 copy.19.refs_1_
  56.1 0.5 shard_map.122.refs_0_
  56.5 0.0 collective-permute-done.1.refs_1_
  56.6 2.0 %shard_map.123.refs_4_ = bf16[512,512]{1,0:T(8,128)(2,1)} custom-call(f32[512,512]{1,0:T(8,128)S(1)} %shard_map.122.refs_0_, bf16[512,512]{1,0:T(8,128)(2,1)} %collective-permute-done.1.refs_1_), custom_call_target="tpu_custom_call" | custom-call | tf_op jit(solution)/shard_map/pallas_call | solution.py:68
  58.5 0.0 reduce-scatter.2.cloned.1.call-update
  58.5 0.0 collective-permute-done.refs_2_
  58.6 0.9 shard_map.124
  59.5 6.8 %all_to_all.35.refs_2_ = f32[4,8,512]{2,1,0:T(8,128)S(1)} all-to-all(f32[4,8,512]{2,1,0:T(8,128)S(1)} %get-tuple-element.28), channel_id=1, replica_groups=mesh['zlo'=4,'y'=4,'zhi'=4,'x'=4,'core'=2] {'x'}, dimensions={0} | all-to-all | bytes 131072 | tf_op jit(solution)/shard_map/all_to_all | solution.py:32
  66.3 1.5 shard_map.125
  67.8 4.3 %all-to-all-start.2 = ((bf16[4,512,256]{2,1,0:T(8,128)(2,1)}), bf16[4,512,256]{2,1,0:T(8,128)(2,1)S(1)}, u32[]{:S(2)}, u32[]{:S(2)}) async-start(bf16[4,512,256]{2,1,0:T(8,128)(2,1)} %shard_map.125), calls=%async_computation.3 | async-start | bytes 2097152 | tf_op jit(solution)/shard_map/all_to_all | solution.py:32
  72.1 0.0 copy-done
  72.1 0.0 copy-done.6
  72.1 0.0 copy-done.8
  72.1 2.4 %shard_map.126 = (bf16[128,1024]{1,0:T(8,128)(2,1)S(1)}, bf16[128,1024]{1,0:T(8,128)(2,1)}, bf16[128,1024]{1,0:T(8,128)(2,1)}, bf16[128,1024]{1,0:T(8,128)(2,1)}) custom-call(s32[2,32]{1,0:T(2,128)S(1)} %copy-done.8, bf16[128,4096]{1,0:T(8,128)(2,1)S(1)} %bitcast.29, f32[1,4096]{1,0:T(1,128)S(1)} %copy-done.7, bf16[5,4096]{1,0:T(8,128)(2,1)S(1)} %copy-done.6), custom_call_target="tpu_custom_call" | custom-call | tf_op jit(solution)/shard_map/pallas_call | solution.py:68
  74.5 2.2 %collective-permute-start.2 = (bf16[128,1024]{1,0:T(8,128)(2,1)}, bf16[128,1024]{1,0:T(8,128)(2,1)S(1)}, u32[]{:S(2)}, u32[]{:S(2)}) collective-permute-start(bf16[128,1024]{1,0:T(8,128)(2,1)} %get-tuple-element.31), channel_id=1, source_target_pairs={{0,2},{2,4},{4,6},{6,0},{1,3},{3,5},{5,7},{7,1},{8,10},{10,12},{12... | collective-permute-start | bytes 786440 | tf_op jit(solution)/shard_map/ppermute | solution.py:43
  76.7 3.7 %collective-permute-start.3 = (bf16[128,1024]{1,0:T(8,128)(2,1)}, bf16[128,1024]{1,0:T(8,128)(2,1)S(1)}, u32[]{:S(2)}, u32[]{:S(2)}) collective-permute-start(bf16[128,1024]{1,0:T(8,128)(2,1)} %get-tuple-element.32), channel_id=1, source_target_pairs={{0,4},{2,6},{4,0},{6,2},{1,5},{3,7},{5,1},{7,3},{8,12},{10,14},{12... | collective-permute-start | bytes 786440 | tf_op jit(solution)/shard_map/ppermute | solution.py:43
  80.4 2.9 %collective-permute-start.4 = (bf16[128,1024]{1,0:T(8,128)(2,1)}, bf16[128,1024]{1,0:T(8,128)(2,1)S(1)}, u32[]{:S(2)}, u32[]{:S(2)}) collective-permute-start(bf16[128,1024]{1,0:T(8,128)(2,1)} %get-tuple-element.33), channel_id=1, source_target_pairs={{0,6},{2,0},{4,2},{6,4},{1,7},{3,1},{5,3},{7,5},{8,14},{10,8},{12,... | collective-permute-start | bytes 786440 | tf_op jit(solution)/shard_map/ppermute | solution.py:43
  83.3 2.0 %all-to-all-done.2.refs_0_ = bf16[4,512,256]{2,1,0:T(8,128)(2,1)S(1)} async-done(((bf16[4,512,256]{2,1,0:T(8,128)(2,1)}), bf16[4,512,256]{2,1,0:T(8,128)(2,1)S(1)}, u32[]{:S(2)}, u32[]{:S(2)}) %all-to-all-start.2) | async-done | bytes 1048608 | tf_op jit(solution)/shard_map/all_to_all | solution.py:32
  85.4 0.1 shard_map.127.refs_1_.refs_0_
  85.5 1.3 collective-permute-start.5
  86.8 0.0 collective-permute-done.2.refs_2_.refs_1_
  86.8 2.0 %collective-permute-done.3.refs_3_.refs_2_ = bf16[128,1024]{1,0:T(8,128)(2,1)S(1)} collective-permute-done((bf16[128,1024]{1,0:T(8,128)(2,1)}, bf16[128,1024]{1,0:T(8,128)(2,1)S(1)}, u32[]{:S(2)}, u32[]{:S(2)}) %collective-permute-start.3) | collective-permute-done | bytes 262176 | tf_op jit(solution)/shard_map/ppermute | solution.py:43
  88.8 3.6 %collective-permute-done.4.refs_4_.refs_3_ = bf16[128,1024]{1,0:T(8,128)(2,1)S(1)} collective-permute-done((bf16[128,1024]{1,0:T(8,128)(2,1)}, bf16[128,1024]{1,0:T(8,128)(2,1)S(1)}, u32[]{:S(2)}, u32[]{:S(2)}) %collective-permute-start.4) | collective-permute-done | bytes 262176 | tf_op jit(solution)/shard_map/ppermute | solution.py:43
  92.4 5.0 %reduce-scatter.2.cloned.1.call-done.refs_0_.refs_1_ = bf16[128,512]{1,0:T(8,128)(2,1)} async-done(((bf16[512,512]{1,0:T(8,128)(2,1)}), bf16[128,512]{1,0:T(8,128)(2,1)}) %reduce-scatter.2.cloned.1.call-update) | async-done | bytes 131088 | tf_op jit(solution)/shard_map/reduce_scatter | solution.py:324
  97.4 0.9 copy-done.2
  98.3 0.2 shard_map.128
  98.5 16.4 %all_to_all.36.refs_0_ = f32[16,8,128]{2,1,0:T(8,128)S(1)} all-to-all(f32[16,8,128]{2,1,0:T(8,128)S(1)} %shard_map.128), channel_id=1, replica_groups=mesh['zlo'=4,'y'=4,'zhi'=4,'x'=4,'core'=2] {'zlo','zhi'}, dimensions={0} | all-to-all | bytes 131072 | tf_op jit(solution)/shard_map/all_to_all | solution.py:32
  114.9 0.7 shard_map.129.refs_2_
  115.5 0.0 collective-permute-done.5.refs_1_
  115.5 0.1 shard_map.130
  115.6 0.0 copy-start.1
  115.6 0.0 copy-start.3
  115.6 1.4 collective-permute-start.6
  117.1 11.3 %all-to-all-start.4 = ((f32[32,8,128]{2,1,0:T(8,128)}), f32[32,8,128]{2,1,0:T(8,128)S(1)}, u32[]{:S(2)}, u32[]{:S(2)}) async-start(f32[32,8,128]{2,1,0:T(8,128)} %shard_map.129.refs_2_), calls=%async_computation.5 | async-start | bytes 262144 | tf_op jit(solution)/shard_map/all_to_all | solution.py:32
  128.4 3.2 %collective-permute-done.6.refs_2_ = bf16[512,256]{1,0:T(8,128)(2,1)S(1)} collective-permute-done((bf16[512,256]{1,0:T(8,128)(2,1)S(1)}, bf16[512,256]{1,0:T(8,128)(2,1)S(1)}, u32[]{:S(2)}, u32[]{:S(2)}) %collective-permute-start.6) | collective-permute-done | bytes 262176 | tf_op jit(solution)/shard_map/ppermute | solution.py:53
  131.6 1.2 shard_map.131.refs_5_
  132.8 3.2 %all-to-all-done.4.refs_0_ = f32[32,8,128]{2,1,0:T(8,128)S(1)} async-done(((f32[32,8,128]{2,1,0:T(8,128)}), f32[32,8,128]{2,1,0:T(8,128)S(1)}, u32[]{:S(2)}, u32[]{:S(2)}) %all-to-all-start.4) | async-done | bytes 131104 | tf_op jit(solution)/shard_map/all_to_all | solution.py:32
  136.0 0.0 copy-done.1
  136.0 0.0 copy-done.3
  136.0 0.0 copy-start.5
  136.0 0.9 copy-done.5
  137.0 0.9 shard_map.132
  137.9 3.7 %all-to-all-start.5 = ((bf16[16,128,256]{2,1,0:T(8,128)(2,1)}), bf16[16,128,256]{2,1,0:T(8,128)(2,1)S(1)}, u32[]{:S(2)}, u32[]{:S(2)}) async-start(bf16[16,128,256]{2,1,0:T(8,128)(2,1)} %shard_map.131.refs_5_), calls=%async_computation.6 | async-start | bytes 2097152 | tf_op jit(solution)/shard_map/all_to_all | solution.py:32
  141.6 19.2 %all_gather.7.refs_4_ = bf16[512,512]{1,0:T(8,128)(2,1)S(1)} all-gather(bf16[128,512]{1,0:T(8,128)(2,1)S(1)} %get-tuple-element.36), channel_id=1, replica_groups=mesh['zlo'=4,'y'=4,'zhi'=4,'x'=4,'core'=2] {'zhi'}, dimensions={0}, use_global_device_ids=true | all-gather | bytes 655360 | tf_op jit(solution)/shard_map/all_gather | solution.py:391
  160.7 7.1 %collective-permute-start.7 = (bf16[512,512]{1,0:T(8,128)(2,1)S(1)}, bf16[512,512]{1,0:T(8,128)(2,1)S(1)}, u32[]{:S(2)}, u32[]{:S(2)}) collective-permute-start(bf16[512,512]{1,0:T(8,128)(2,1)S(1)} %all_gather.7.refs_4_), channel_id=1, source_target_pairs={{0,1},{1,0},{2,3},{3,2},{4,5},{5,4},{6,7},{7,6},{8,9},{9,8},{10,11... | collective-permute-start | bytes 1572872 | tf_op jit(solution)/shard_map/ppermute | solution.py:48
  167.9 0.4 shard_map.133.refs_5_
  168.3 1.1 collective-permute-done.7.refs_4_
  169.4 1.3 shard_map.134
  170.7 0.0 all-to-all-done.5.refs_0_
  170.7 4.7 %all-to-all-start.6 = ((bf16[4,128,512]{2,1,0:T(8,128)(2,1)}), bf16[4,128,512]{2,1,0:T(8,128)(2,1)S(1)}, u32[]{:S(2)}, u32[]{:S(2)}) async-start(bf16[4,128,512]{2,1,0:T(8,128)(2,1)} %shard_map.134), calls=%async_computation.7 | async-start | bytes 1048576 | tf_op jit(solution)/shard_map/all_to_all | solution.py:32
  175.4 1.2 shard_map.135
  176.6 7.7 %all-to-all-done.6 = bf16[4,128,512]{2,1,0:T(8,128)(2,1)S(1)} async-done(((bf16[4,128,512]{2,1,0:T(8,128)(2,1)}), bf16[4,128,512]{2,1,0:T(8,128)(2,1)S(1)}, u32[]{:S(2)}, u32[]{:S(2)}) %all-to-all-start.6) | async-done | bytes 524320 | tf_op jit(solution)/shard_map/all_to_all | solution.py:32
  184.3 0.7 reduce_sum.12
  (10 shorter events, 0.0 us)
Async XLA Ops:
  11.0 5.0 %copy-start.7 = (f32[1,4096]{1,0:T(1,128)S(1)}, f32[1,4096]{1,0:T(1,128)}, u32[]{:S(2)}) copy-start(f32[1,4096]{1,0:T(1,128)} %refs_2_.1) | copy-start | bytes 49156
  11.0 5.2 %copy-start.9 = (bf16[128,512]{1,0:T(8,128)(2,1)S(1)}, bf16[128,512]{1,0:T(8,128)(2,1)}, u32[]{:S(2)}) copy-start(bf16[128,512]{1,0:T(8,128)(2,1)} %get-tuple-element.24) | copy-start | bytes 393220
  11.0 36.0 %all-to-all-start = ((bf16[4,128,1536]{2,1,0:T(8,128)(2,1)}), bf16[4,128,1536]{2,1,0:T(8,128)(2,1)S(1)}, u32[]{:S(2)}, u32[]{:S(2)}) async-start(bf16[4,128,1536]{2,1,0:T(8,128)(2,1)} %get-tuple-element.23), calls=%async_computation | async-start | bytes 3145728 | tf_op jit(solution)/shard_map/all_to_all | solution.py:32
  16.0 81.4 %reduce-scatter.2.cloned.1.call-start = ((), (), s32[]{:S(2)}) async-start(), calls=%async_computation.8 | async-start | bytes 655360 | tf_op jit(solution)/shard_map/reduce_scatter | solution.py:324
  47.5 9.1 %collective-permute-start.1 = (bf16[512,512]{1,0:T(8,128)(2,1)S(1)}, bf16[512,512]{1,0:T(8,128)(2,1)}, u32[]{:S(2)}, u32[]{:S(2)}) collective-permute-start(bf16[512,512]{1,0:T(8,128)(2,1)S(1)} %shard_map.121.refs_2_), channel_id=1, source_target_pairs={{0,1},{1,0},{2,3},{3,2},{4,5},{5,4},{6,7},{7,6},{8,9},{9,8},{10,11... | collective-permute-start | bytes 1572872 | tf_op jit(solution)/shard_map/ppermute | solution.py:48
  54.0 4.6 %collective-permute-start = (bf16[512,512]{1,0:T(8,128)(2,1)S(1)}, bf16[512,512]{1,0:T(8,128)(2,1)S(1)}, u32[]{:S(2)}, u32[]{:S(2)}) collective-permute-start(bf16[512,512]{1,0:T(8,128)(2,1)S(1)} %all_gather.6.refs_1_), channel_id=1, source_target_pairs={{0,1},{1,0},{2,3},{3,2},{4,5},{5,4},{6,7},{7,6},{8,9},{9,8},{10,11... | collective-permute-start | bytes 1572872 | tf_op jit(solution)/shard_map/ppermute | solution.py:48
  67.8 4.3 %copy-start = (bf16[2,1,64,4096]{3,2,1,0:T(8,128)(2,1)S(1)}, bf16[2,1,64,4096]{3,2,1,0:T(8,128)(2,1)}, u32[]{:S(2)}) copy-start(bf16[2,1,64,4096]{3,2,1,0:T(8,128)(2,1)} %param.15) | copy-start | bytes 3145732
  67.8 4.3 %copy-start.6 = (bf16[5,4096]{1,0:T(8,128)(2,1)S(1)}, bf16[5,4096]{1,0:T(8,128)(2,1)}, u32[]{:S(2)}) copy-start(bf16[5,4096]{1,0:T(8,128)(2,1)} %refs_3_.1) | copy-start | bytes 122884
  67.8 4.3 %copy-start.8 = (s32[2,32]{1,0:T(2,128)S(1)}, s32[2,32]{1,0:T(2,128)}, u32[]{:S(2)}) copy-start(s32[2,32]{1,0:T(2,128)} %refs_0_.1) | copy-start | bytes 772
  67.8 17.5 %all-to-all-start.2 = ((bf16[4,512,256]{2,1,0:T(8,128)(2,1)}), bf16[4,512,256]{2,1,0:T(8,128)(2,1)S(1)}, u32[]{:S(2)}, u32[]{:S(2)}) async-start(bf16[4,512,256]{2,1,0:T(8,128)(2,1)} %shard_map.125), calls=%async_computation.3 | async-start | bytes 2097152 | tf_op jit(solution)/shard_map/all_to_all | solution.py:32
  74.5 12.3 %collective-permute-start.2 = (bf16[128,1024]{1,0:T(8,128)(2,1)}, bf16[128,1024]{1,0:T(8,128)(2,1)S(1)}, u32[]{:S(2)}, u32[]{:S(2)}) collective-permute-start(bf16[128,1024]{1,0:T(8,128)(2,1)} %get-tuple-element.31), channel_id=1, source_target_pairs={{0,2},{2,4},{4,6},{6,0},{1,3},{3,5},{5,7},{7,1},{8,10},{10,12},{12... | collective-permute-start | bytes 786440 | tf_op jit(solution)/shard_map/ppermute | solution.py:43
  76.7 12.1 %collective-permute-start.3 = (bf16[128,1024]{1,0:T(8,128)(2,1)}, bf16[128,1024]{1,0:T(8,128)(2,1)S(1)}, u32[]{:S(2)}, u32[]{:S(2)}) collective-permute-start(bf16[128,1024]{1,0:T(8,128)(2,1)} %get-tuple-element.32), channel_id=1, source_target_pairs={{0,4},{2,6},{4,0},{6,2},{1,5},{3,7},{5,1},{7,3},{8,12},{10,14},{12... | collective-permute-start | bytes 786440 | tf_op jit(solution)/shard_map/ppermute | solution.py:43
  80.4 12.0 %collective-permute-start.4 = (bf16[128,1024]{1,0:T(8,128)(2,1)}, bf16[128,1024]{1,0:T(8,128)(2,1)S(1)}, u32[]{:S(2)}, u32[]{:S(2)}) collective-permute-start(bf16[128,1024]{1,0:T(8,128)(2,1)} %get-tuple-element.33), channel_id=1, source_target_pairs={{0,6},{2,0},{4,2},{6,4},{1,7},{3,1},{5,3},{7,5},{8,14},{10,8},{12,... | collective-permute-start | bytes 786440 | tf_op jit(solution)/shard_map/ppermute | solution.py:43
  85.5 30.1 %collective-permute-start.5 = (bf16[512,256]{1,0:T(8,128)(2,1)S(1)}, bf16[512,256]{1,0:T(8,128)(2,1)S(1)}, u32[]{:S(2)}, u32[]{:S(2)}) collective-permute-start(bf16[512,256]{1,0:T(8,128)(2,1)S(1)} %shard_map.127.refs_1_.refs_0_), channel_id=1, source_target_pairs={{128,0},{256,128},{384,256},{129,1},{257,129},{385,257},{130,2},{2... | collective-permute-start | bytes 786440 | tf_op jit(solution)/shard_map/ppermute | solution.py:53
  97.4 0.9 copy-start.2
  115.6 20.4 %copy-start.1 = (f32[1,128,512]{2,1,0:T(8,128)S(1)}, f32[1,128,512]{2,1,0:T(8,128)}, u32[]{:S(2)}) copy-start(f32[1,128,512]{2,1,0:T(8,128)} %param.12) | copy-start | bytes 786436
  115.6 20.4 %copy-start.3 = (bf16[128,512]{1,0:T(8,128)(2,1)S(1)}, bf16[128,512]{1,0:T(8,128)(2,1)}, u32[]{:S(2)}) copy-start(bf16[128,512]{1,0:T(8,128)(2,1)} %reduce-scatter.2.cloned.1.call-done.refs_0_.refs_1_) | copy-start | bytes 393220
  115.6 16.0 %collective-permute-start.6 = (bf16[512,256]{1,0:T(8,128)(2,1)S(1)}, bf16[512,256]{1,0:T(8,128)(2,1)S(1)}, u32[]{:S(2)}, u32[]{:S(2)}) collective-permute-start(bf16[512,256]{1,0:T(8,128)(2,1)S(1)} %shard_map.130), channel_id=1, source_target_pairs={{256,0},{384,128},{257,1},{385,129},{258,2},{386,130},{259,3},{387... | collective-permute-start | bytes 786440 | tf_op jit(solution)/shard_map/ppermute | solution.py:53
  117.1 18.9 %all-to-all-start.4 = ((f32[32,8,128]{2,1,0:T(8,128)}), f32[32,8,128]{2,1,0:T(8,128)S(1)}, u32[]{:S(2)}, u32[]{:S(2)}) async-start(f32[32,8,128]{2,1,0:T(8,128)} %shard_map.129.refs_2_), calls=%async_computation.5 | async-start | bytes 262144 | tf_op jit(solution)/shard_map/all_to_all | solution.py:32
  131.6 4.4 %copy-start.4 = (f32[1,128,512]{2,1,0:T(8,128)S(1)}, f32[1,128,512]{2,1,0:T(8,128)}, u32[]{:S(2)}) copy-start(f32[1,128,512]{2,1,0:T(8,128)} %param.13) | copy-start | bytes 786436
  136.0 1.0 copy-start.5
  137.9 32.8 %all-to-all-start.5 = ((bf16[16,128,256]{2,1,0:T(8,128)(2,1)}), bf16[16,128,256]{2,1,0:T(8,128)(2,1)S(1)}, u32[]{:S(2)}, u32[]{:S(2)}) async-start(bf16[16,128,256]{2,1,0:T(8,128)(2,1)} %shard_map.131.refs_5_), calls=%async_computation.6 | async-start | bytes 2097152 | tf_op jit(solution)/shard_map/all_to_all | solution.py:32
  160.7 8.7 %collective-permute-start.7 = (bf16[512,512]{1,0:T(8,128)(2,1)S(1)}, bf16[512,512]{1,0:T(8,128)(2,1)S(1)}, u32[]{:S(2)}, u32[]{:S(2)}) collective-permute-start(bf16[512,512]{1,0:T(8,128)(2,1)S(1)} %all_gather.7.refs_4_), channel_id=1, source_target_pairs={{0,1},{1,0},{2,3},{3,2},{4,5},{5,4},{6,7},{7,6},{8,9},{9,8},{10,11... | collective-permute-start | bytes 1572872 | tf_op jit(solution)/shard_map/ppermute | solution.py:48
  170.7 13.6 %all-to-all-start.6 = ((bf16[4,128,512]{2,1,0:T(8,128)(2,1)}), bf16[4,128,512]{2,1,0:T(8,128)(2,1)S(1)}, u32[]{:S(2)}, u32[]{:S(2)}) async-start(bf16[4,128,512]{2,1,0:T(8,128)(2,1)} %shard_map.134), calls=%async_computation.7 | async-start | bytes 1048576 | tf_op jit(solution)/shard_map/all_to_all | solution.py:32
Sparse Core Ops, SparseCore 0:
  58.7 38.6 reduce-scatter.1

commit v13 on v12

--- a/solution.py
+++ b/solution.py
@@ -361,7 +361,7 @@
 
     first_axes = ("zlo", "zhi")
     last_axes = ("y", "x", "core")
-    tile = (8, 128)
+    tile = (1, 128)
     squares = local(
         squares_kernel, [shape((lax.axis_size(first_axes),) + tile, f32)], grad, after=[top] + fresh_normed[1:]
     )[0]

time: 194 us -> 207 us (1.067)
  waiting for transfers between devices: 27.8 us -> 40.7 us
    reduce_scatter x1, waiting for transfers between devices: 4.97 us -> 13.8 us  [per_device(): grad = lax.psum_scatter(partial, 'zhi', scatter_dimension=0, tiled=True)]
    all_to_all x2 -> x1, blocking collectives: 23.2 us -> 17.8 us  [exchange(): return lax.all_to_all(blocks, axis, 0, 0)]
    all_gather x1, blocking collectives: 19.2 us -> 24.5 us  [per_device(): weights_new = lax.all_gather(weights_new, 'zhi', axis=0, tiled=True)]
    ppermute x3, starting transfers between devices: 15.6 us -> 11.3 us  [swap_cores(): return lax.ppermute(block, 'core', [(0, 1), (1, 0)])]
    all_to_all x5 -> x6, starting transfers between devices: 28.9 us -> 32.2 us  [exchange(): return lax.all_to_all(blocks, axis, 0, 0)]
    ppermute x2, waiting for transfers between devices: 3.23 us -> 6.47 us  [from_behind(): lax.ppermute(block, axis, [(i + distance, i) for i in range(size - distan...]
    all_to_all x5 -> x6, waiting for transfers between devices: 12.9 us -> 14.3 us  [exchange(): return lax.all_to_all(blocks, axis, 0, 0)]
  transfers between devices with their start and end apart: 14 -> 15, of which waited for: 8 -> 8; matrix products, arithmetic and copies ran while one was open for 0% -> 0% of each run, Pallas kernels for 6% -> 5%
where the time goes in v13:
time: 207 us; the launch traced here: 206 us
  blocking collectives  73.2 us (35%)
  starting transfers between devices  54.9 us (27%)
  waiting for transfers between devices  40.7 us (20%)
  Pallas kernels  18.1 us (9%)
  between operations  14.3 us (7%)
  local copies, waits for them, and re-layouts  4.18 us (2%)
    all_to_all x6, starting transfers between devices, exchange(): return lax.all_to_all(blocks, axis, 0, 0)  32.2 us
    all_gather x1, blocking collectives, per_device(): weights_old = lax.all_gather(weights_old, 'zhi', axis=0, tiled=True)  30.9 us
    all_gather x1, blocking collectives, per_device(): weights_new = lax.all_gather(weights_new, 'zhi', axis=0, tiled=True)  24.5 us
    all_to_all x1, blocking collectives, exchange(): return lax.all_to_all(blocks, axis, 0, 0)  17.8 us
    pallas_call x15, Pallas kernels, local(): pl.pallas_call(body, out_shape=out_shapes, in_specs=[pl.BlockSpec(memory_...  14.3 us
    all_to_all x6, waiting for transfers between devices, exchange(): return lax.all_to_all(blocks, axis, 0, 0)  14.3 us
    reduce_scatter x1, waiting for transfers between devices, per_device(): grad = lax.psum_scatter(partial, 'zhi', scatter_dimension=0, tiled=True)  13.8 us
    ppermute x3, starting transfers between devices, swap_cores(): return lax.ppermute(block, 'core', [(0, 1), (1, 0)])  11.3 us
  transfers between devices with their start and end apart: 15, of which 8 were waited for; matrix products, arithmetic and copies ran while one was open for 0% of the time, Pallas kernels for 5%

profile of v13, /device:TPU:1, one launch (start us, length us, event | category | flops | bytes accessed | tf_op | source)
XLA Modules:
  0.0 206.1 jit_solution(5359701020470631663)
XLA Ops:
  7.2 3.9 %shard_map.120 = (bf16[4,128,1536]{2,1,0:T(8,128)(2,1)}, bf16[128,512]{1,0:T(8,128)(2,1)}) custom-call(bf16[128,4096]{1,0:T(8,128)(2,1)} %bitcast.36, bf16[128,512]{1,0:T(8,128)(2,1)} %bitcast.39, f32[128,512]{1,0:T(8,128)} %bitcast.30), custom_call_target="tpu_custom_call" | custom-call | tf_op jit(solution)/shard_map/pallas_call | solution.py:111
  11.0 5.0 %all-to-all-start = ((bf16[4,128,1536]{2,1,0:T(8,128)(2,1)}), bf16[4,128,1536]{2,1,0:T(8,128)(2,1)S(1)}, u32[]{:S(2)}, u32[]{:S(2)}) async-start(bf16[4,128,1536]{2,1,0:T(8,128)(2,1)} %get-tuple-element.23), calls=%async_computation | async-start | bytes 3145728 | tf_op jit(solution)/shard_map/all_to_all | solution.py:32
  16.0 0.0 copy-done.9
  16.0 0.1 copy.18.refs_1_
  16.2 0.0 copy-done.11
  16.2 30.9 %all_gather.6.refs_1_ = bf16[512,512]{1,0:T(8,128)(2,1)S(1)} all-gather(bf16[128,512]{1,0:T(8,128)(2,1)S(1)} %copy-done.11), channel_id=1, replica_groups=mesh['zlo'=4,'y'=4,'zhi'=4,'x'=4,'core'=2] {'zhi'}, dimensions={0}, use_global_device_ids=true | all-gather | bytes 655360 | tf_op jit(solution)/shard_map/all_gather | solution.py:306
  47.0 0.0 all-to-all-done
  47.0 0.5 shard_map.121.refs_2_
  47.5 6.5 %collective-permute-start.1 = (bf16[512,512]{1,0:T(8,128)(2,1)S(1)}, bf16[512,512]{1,0:T(8,128)(2,1)}, u32[]{:S(2)}, u32[]{:S(2)}) collective-permute-start(bf16[512,512]{1,0:T(8,128)(2,1)S(1)} %shard_map.121.refs_2_), channel_id=1, source_target_pairs={{0,1},{1,0},{2,3},{3,2},{4,5},{5,4},{6,7},{7,6},{8,9},{9,8},{10,11... | collective-permute-start | bytes 1572872 | tf_op jit(solution)/shard_map/ppermute | solution.py:48
  54.0 1.9 collective-permute-start
  55.9 0.1 copy.19.refs_1_
  56.1 0.5 shard_map.122.refs_0_
  56.6 0.0 collective-permute-done.1.refs_1_
  56.6 1.9 shard_map.123.refs_4_
  58.5 0.0 collective-permute-done.refs_2_
  58.5 1.6 shard_map.124
  60.1 1.3 copy-done
  61.4 3.3 %all-to-all-start.1 = ((f32[4,8,512]{2,1,0:T(8,128)}), f32[4,8,512]{2,1,0:T(8,128)S(1)}, u32[]{:S(2)}, u32[]{:S(2)}) async-start(f32[4,8,512]{2,1,0:T(8,128)} %get-tuple-element.28), calls=%async_computation.1 | async-start | bytes 131072 | tf_op jit(solution)/shard_map/all_to_all | solution.py:32
  64.7 0.0 reduce-scatter.2.cloned.1.call-start
  64.8 0.7 reduce-scatter.2.cloned.1.call-update
  65.5 3.7 %all-to-all-done.1.refs_2_ = f32[4,8,512]{2,1,0:T(8,128)S(1)} async-done(((f32[4,8,512]{2,1,0:T(8,128)}), f32[4,8,512]{2,1,0:T(8,128)S(1)}, u32[]{:S(2)}, u32[]{:S(2)}) %all-to-all-start.1) | async-done | bytes 65568 | tf_op jit(solution)/shard_map/all_to_all | solution.py:32
  69.2 1.6 copy-done.1
  70.8 1.5 shard_map.125
  72.2 4.3 %all-to-all-start.2 = ((bf16[4,512,256]{2,1,0:T(8,128)(2,1)}), bf16[4,512,256]{2,1,0:T(8,128)(2,1)S(1)}, u32[]{:S(2)}, u32[]{:S(2)}) async-start(bf16[4,512,256]{2,1,0:T(8,128)(2,1)} %shard_map.125), calls=%async_computation.3 | async-start | bytes 2097152 | tf_op jit(solution)/shard_map/all_to_all | solution.py:32
  76.6 0.0 copy-done.2
  76.6 0.0 copy-done.8
  76.6 0.0 copy-done.10
  76.6 1.6 shard_map.126
  78.2 2.2 %collective-permute-start.2 = (bf16[128,1024]{1,0:T(8,128)(2,1)S(1)}, bf16[128,1024]{1,0:T(8,128)(2,1)S(1)}, u32[]{:S(2)}, u32[]{:S(2)}) collective-permute-start(bf16[128,1024]{1,0:T(8,128)(2,1)S(1)} %get-tuple-element.31), channel_id=1, source_target_pairs={{0,2},{2,4},{4,6},{6,0},{1,3},{3,5},{5,7},{7,1},{8,10},{10,12},{12... | collective-permute-start | bytes 786440 | tf_op jit(solution)/shard_map/ppermute | solution.py:43
  80.4 3.7 %collective-permute-start.3 = (bf16[128,1024]{1,0:T(8,128)(2,1)S(1)}, bf16[128,1024]{1,0:T(8,128)(2,1)S(1)}, u32[]{:S(2)}, u32[]{:S(2)}) collective-permute-start(bf16[128,1024]{1,0:T(8,128)(2,1)S(1)} %get-tuple-element.32), channel_id=1, source_target_pairs={{0,4},{2,6},{4,0},{6,2},{1,5},{3,7},{5,1},{7,3},{8,12},{10,14},{12... | collective-permute-start | bytes 786440 | tf_op jit(solution)/shard_map/ppermute | solution.py:43
  84.0 2.9 %collective-permute-start.4 = (bf16[128,1024]{1,0:T(8,128)(2,1)S(1)}, bf16[128,1024]{1,0:T(8,128)(2,1)S(1)}, u32[]{:S(2)}, u32[]{:S(2)}) collective-permute-start(bf16[128,1024]{1,0:T(8,128)(2,1)S(1)} %get-tuple-element.33), channel_id=1, source_target_pairs={{0,6},{2,0},{4,2},{6,4},{1,7},{3,1},{5,3},{7,5},{8,14},{10,8},{12,... | collective-permute-start | bytes 786440 | tf_op jit(solution)/shard_map/ppermute | solution.py:43
  87.0 2.9 %all-to-all-done.2.refs_0_ = bf16[4,512,256]{2,1,0:T(8,128)(2,1)S(1)} async-done(((bf16[4,512,256]{2,1,0:T(8,128)(2,1)}), bf16[4,512,256]{2,1,0:T(8,128)(2,1)S(1)}, u32[]{:S(2)}, u32[]{:S(2)}) %all-to-all-start.2) | async-done | bytes 1048608 | tf_op jit(solution)/shard_map/all_to_all | solution.py:32
  89.9 0.1 shard_map.127.refs_1_.refs_0_
  90.0 1.3 collective-permute-start.5
  91.3 0.0 collective-permute-done.2.refs_2_.refs_1_
  91.3 0.9 collective-permute-done.3.refs_3_.refs_2_
  92.2 3.5 %collective-permute-done.4.refs_4_.refs_3_ = bf16[128,1024]{1,0:T(8,128)(2,1)S(1)} collective-permute-done((bf16[128,1024]{1,0:T(8,128)(2,1)S(1)}, bf16[128,1024]{1,0:T(8,128)(2,1)S(1)}, u32[]{:S(2)}, u32[]{:S(2)}) %collective-permute-start.4) | collective-permute-done | bytes 262176 | tf_op jit(solution)/shard_map/ppermute | solution.py:43
  95.7 13.8 %reduce-scatter.2.cloned.1.call-done.refs_0_.refs_1_ = bf16[128,512]{1,0:T(8,128)(2,1)} async-done(((bf16[512,512]{1,0:T(8,128)(2,1)}), bf16[128,512]{1,0:T(8,128)(2,1)}) %reduce-scatter.2.cloned.1.call-update) | async-done | bytes 131088 | tf_op jit(solution)/shard_map/reduce_scatter | solution.py:324
  109.5 0.9 copy-done.4
  110.4 0.2 shard_map.128
  110.6 17.8 %all_to_all.35.refs_0_ = f32[16,1,128]{2,1,0:T(1,128)S(1)} all-to-all(f32[16,1,128]{2,1,0:T(1,128)S(1)} %shard_map.128), channel_id=1, replica_groups=mesh['zlo'=4,'y'=4,'zhi'=4,'x'=4,'core'=2] {'zlo','zhi'}, dimensions={0} | all-to-all | bytes 16384 | tf_op jit(solution)/shard_map/all_to_all | solution.py:32
  128.4 0.6 shard_map.129.refs_2_
  129.0 0.0 collective-permute-done.5.refs_1_
  129.1 0.8 shard_map.130
  129.8 1.3 collective-permute-start.6
  131.1 9.0 %all-to-all-start.4 = ((f32[32,1,128]{2,1,0:T(1,128)}), f32[32,1,128]{2,1,0:T(1,128)S(1)}, u32[]{:S(2)}, u32[]{:S(2)}) async-start(f32[32,1,128]{2,1,0:T(1,128)} %shard_map.129.refs_2_), calls=%async_computation.5 | async-start | bytes 32768 | tf_op jit(solution)/shard_map/all_to_all | solution.py:32
  140.1 6.5 %collective-permute-done.6.refs_2_ = bf16[512,256]{1,0:T(8,128)(2,1)S(1)} collective-permute-done((bf16[512,256]{1,0:T(8,128)(2,1)}, bf16[512,256]{1,0:T(8,128)(2,1)S(1)}, u32[]{:S(2)}, u32[]{:S(2)}) %collective-permute-start.6) | collective-permute-done | bytes 262176 | tf_op jit(solution)/shard_map/ppermute | solution.py:53
  146.6 1.2 shard_map.131.refs_5_
  147.8 0.0 all-to-all-done.4.refs_0_
  147.8 0.0 copy-done.3
  147.8 0.0 copy-done.5
  147.8 0.0 copy-done.6
  147.8 0.9 shard_map.132
  148.8 6.7 %all-to-all-start.5 = ((bf16[16,128,256]{2,1,0:T(8,128)(2,1)}), bf16[16,128,256]{2,1,0:T(8,128)(2,1)S(1)}, u32[]{:S(2)}, u32[]{:S(2)}) async-start(bf16[16,128,256]{2,1,0:T(8,128)(2,1)} %shard_map.131.refs_5_), calls=%async_computation.6 | async-start | bytes 2097152 | tf_op jit(solution)/shard_map/all_to_all | solution.py:32
  155.5 24.5 %all_gather.7.refs_4_ = bf16[512,512]{1,0:T(8,128)(2,1)S(1)} all-gather(bf16[128,512]{1,0:T(8,128)(2,1)S(1)} %get-tuple-element.36), channel_id=1, replica_groups=mesh['zlo'=4,'y'=4,'zhi'=4,'x'=4,'core'=2] {'zhi'}, dimensions={0}, use_global_device_ids=true | all-gather | bytes 655360 | tf_op jit(solution)/shard_map/all_gather | solution.py:391
  180.0 3.0 %collective-permute-start.7 = (bf16[512,512]{1,0:T(8,128)(2,1)S(1)}, bf16[512,512]{1,0:T(8,128)(2,1)S(1)}, u32[]{:S(2)}, u32[]{:S(2)}) collective-permute-start(bf16[512,512]{1,0:T(8,128)(2,1)S(1)} %all_gather.7.refs_4_), channel_id=1, source_target_pairs={{0,1},{1,0},{2,3},{3,2},{4,5},{5,4},{6,7},{7,6},{8,9},{9,8},{10,11... | collective-permute-start | bytes 1572872 | tf_op jit(solution)/shard_map/ppermute | solution.py:48
  183.0 0.4 shard_map.133.refs_5_
  183.4 1.1 collective-permute-done.7.refs_4_
  184.5 1.2 shard_map.134
  185.7 0.0 all-to-all-done.5.refs_0_
  185.7 3.9 %all-to-all-start.6 = ((bf16[4,128,512]{2,1,0:T(8,128)(2,1)}), bf16[4,128,512]{2,1,0:T(8,128)(2,1)S(1)}, u32[]{:S(2)}, u32[]{:S(2)}) async-start(bf16[4,128,512]{2,1,0:T(8,128)(2,1)} %shard_map.134), calls=%async_computation.7 | async-start | bytes 1048576 | tf_op jit(solution)/shard_map/all_to_all | solution.py:32
  189.6 1.2 shard_map.135
  190.9 7.7 %all-to-all-done.6 = bf16[4,128,512]{2,1,0:T(8,128)(2,1)S(1)} async-done(((bf16[4,128,512]{2,1,0:T(8,128)(2,1)}), bf16[4,128,512]{2,1,0:T(8,128)(2,1)S(1)}, u32[]{:S(2)}, u32[]{:S(2)}) %all-to-all-start.6) | async-done | bytes 524320 | tf_op jit(solution)/shard_map/all_to_all | solution.py:32
  198.5 0.7 reduce_sum.12
  (15 shorter events, 0.0 us)
Async XLA Ops:
  11.0 5.0 %copy-start.9 = (f32[1,4096]{1,0:T(1,128)S(1)}, f32[1,4096]{1,0:T(1,128)}, u32[]{:S(2)}) copy-start(f32[1,4096]{1,0:T(1,128)} %refs_2_.1) | copy-start | bytes 49156
  11.0 5.2 %copy-start.11 = (bf16[128,512]{1,0:T(8,128)(2,1)S(1)}, bf16[128,512]{1,0:T(8,128)(2,1)}, u32[]{:S(2)}) copy-start(bf16[128,512]{1,0:T(8,128)(2,1)} %get-tuple-element.24) | copy-start | bytes 393220
  11.0 36.0 %all-to-all-start = ((bf16[4,128,1536]{2,1,0:T(8,128)(2,1)}), bf16[4,128,1536]{2,1,0:T(8,128)(2,1)S(1)}, u32[]{:S(2)}, u32[]{:S(2)}) async-start(bf16[4,128,1536]{2,1,0:T(8,128)(2,1)} %get-tuple-element.23), calls=%async_computation | async-start | bytes 3145728 | tf_op jit(solution)/shard_map/all_to_all | solution.py:32
  47.5 9.1 %collective-permute-start.1 = (bf16[512,512]{1,0:T(8,128)(2,1)S(1)}, bf16[512,512]{1,0:T(8,128)(2,1)}, u32[]{:S(2)}, u32[]{:S(2)}) collective-permute-start(bf16[512,512]{1,0:T(8,128)(2,1)S(1)} %shard_map.121.refs_2_), channel_id=1, source_target_pairs={{0,1},{1,0},{2,3},{3,2},{4,5},{5,4},{6,7},{7,6},{8,9},{9,8},{10,11... | collective-permute-start | bytes 1572872 | tf_op jit(solution)/shard_map/ppermute | solution.py:48
  54.0 4.5 %collective-permute-start = (bf16[512,512]{1,0:T(8,128)(2,1)S(1)}, bf16[512,512]{1,0:T(8,128)(2,1)S(1)}, u32[]{:S(2)}, u32[]{:S(2)}) collective-permute-start(bf16[512,512]{1,0:T(8,128)(2,1)S(1)} %all_gather.6.refs_1_), channel_id=1, source_target_pairs={{0,1},{1,0},{2,3},{3,2},{4,5},{5,4},{6,7},{7,6},{8,9},{9,8},{10,11... | collective-permute-start | bytes 1572872 | tf_op jit(solution)/shard_map/ppermute | solution.py:48
  60.1 1.4 copy-start
  61.4 7.7 %all-to-all-start.1 = ((f32[4,8,512]{2,1,0:T(8,128)}), f32[4,8,512]{2,1,0:T(8,128)S(1)}, u32[]{:S(2)}, u32[]{:S(2)}) async-start(f32[4,8,512]{2,1,0:T(8,128)} %get-tuple-element.28), calls=%async_computation.1 | async-start | bytes 131072 | tf_op jit(solution)/shard_map/all_to_all | solution.py:32
  64.7 44.7 %reduce-scatter.2.cloned.1.call-start = ((), (), s32[]{:S(2)}) async-start(), calls=%async_computation.8 | async-start | bytes 655360 | tf_op jit(solution)/shard_map/reduce_scatter | solution.py:324
  69.2 1.6 copy-start.1
  72.2 4.3 %copy-start.2 = (bf16[2,1,64,4096]{3,2,1,0:T(8,128)(2,1)S(1)}, bf16[2,1,64,4096]{3,2,1,0:T(8,128)(2,1)}, u32[]{:S(2)}) copy-start(bf16[2,1,64,4096]{3,2,1,0:T(8,128)(2,1)} %param.15) | copy-start | bytes 3145732
  72.2 4.3 %copy-start.8 = (bf16[5,4096]{1,0:T(8,128)(2,1)S(1)}, bf16[5,4096]{1,0:T(8,128)(2,1)}, u32[]{:S(2)}) copy-start(bf16[5,4096]{1,0:T(8,128)(2,1)} %refs_3_.1) | copy-start | bytes 122884
  72.2 4.3 %copy-start.10 = (s32[2,32]{1,0:T(2,128)S(1)}, s32[2,32]{1,0:T(2,128)}, u32[]{:S(2)}) copy-start(s32[2,32]{1,0:T(2,128)} %refs_0_.1) | copy-start | bytes 772
  72.2 17.6 %all-to-all-start.2 = ((bf16[4,512,256]{2,1,0:T(8,128)(2,1)}), bf16[4,512,256]{2,1,0:T(8,128)(2,1)S(1)}, u32[]{:S(2)}, u32[]{:S(2)}) async-start(bf16[4,512,256]{2,1,0:T(8,128)(2,1)} %shard_map.125), calls=%async_computation.3 | async-start | bytes 2097152 | tf_op jit(solution)/shard_map/all_to_all | solution.py:32
  78.2 13.1 %collective-permute-start.2 = (bf16[128,1024]{1,0:T(8,128)(2,1)S(1)}, bf16[128,1024]{1,0:T(8,128)(2,1)S(1)}, u32[]{:S(2)}, u32[]{:S(2)}) collective-permute-start(bf16[128,1024]{1,0:T(8,128)(2,1)S(1)} %get-tuple-element.31), channel_id=1, source_target_pairs={{0,2},{2,4},{4,6},{6,0},{1,3},{3,5},{5,7},{7,1},{8,10},{10,12},{12... | collective-permute-start | bytes 786440 | tf_op jit(solution)/shard_map/ppermute | solution.py:43
  80.4 11.9 %collective-permute-start.3 = (bf16[128,1024]{1,0:T(8,128)(2,1)S(1)}, bf16[128,1024]{1,0:T(8,128)(2,1)S(1)}, u32[]{:S(2)}, u32[]{:S(2)}) collective-permute-start(bf16[128,1024]{1,0:T(8,128)(2,1)S(1)} %get-tuple-element.32), channel_id=1, source_target_pairs={{0,4},{2,6},{4,0},{6,2},{1,5},{3,7},{5,1},{7,3},{8,12},{10,14},{12... | collective-permute-start | bytes 786440 | tf_op jit(solution)/shard_map/ppermute | solution.py:43
  84.0 11.7 %collective-permute-start.4 = (bf16[128,1024]{1,0:T(8,128)(2,1)S(1)}, bf16[128,1024]{1,0:T(8,128)(2,1)S(1)}, u32[]{:S(2)}, u32[]{:S(2)}) collective-permute-start(bf16[128,1024]{1,0:T(8,128)(2,1)S(1)} %get-tuple-element.33), channel_id=1, source_target_pairs={{0,6},{2,0},{4,2},{6,4},{1,7},{3,1},{5,3},{7,5},{8,14},{10,8},{12,... | collective-permute-start | bytes 786440 | tf_op jit(solution)/shard_map/ppermute | solution.py:43
  90.0 39.1 %collective-permute-start.5 = (bf16[512,256]{1,0:T(8,128)(2,1)S(1)}, bf16[512,256]{1,0:T(8,128)(2,1)S(1)}, u32[]{:S(2)}, u32[]{:S(2)}) collective-permute-start(bf16[512,256]{1,0:T(8,128)(2,1)S(1)} %shard_map.127.refs_1_.refs_0_), channel_id=1, source_target_pairs={{128,0},{256,128},{384,256},{129,1},{257,129},{385,257},{130,2},{2... | collective-permute-start | bytes 786440 | tf_op jit(solution)/shard_map/ppermute | solution.py:53
  109.5 0.9 copy-start.4
  129.0 18.8 %copy-start.3 = (f32[1,128,512]{2,1,0:T(8,128)S(1)}, f32[1,128,512]{2,1,0:T(8,128)}, u32[]{:S(2)}) copy-start(f32[1,128,512]{2,1,0:T(8,128)} %param.12) | copy-start | bytes 786436
  129.0 18.8 %copy-start.5 = (bf16[128,512]{1,0:T(8,128)(2,1)S(1)}, bf16[128,512]{1,0:T(8,128)(2,1)}, u32[]{:S(2)}) copy-start(bf16[128,512]{1,0:T(8,128)(2,1)} %reduce-scatter.2.cloned.1.call-done.refs_0_.refs_1_) | copy-start | bytes 393220
  129.0 18.8 %copy-start.6 = (f32[1,128,512]{2,1,0:T(8,128)S(1)}, f32[1,128,512]{2,1,0:T(8,128)}, u32[]{:S(2)}) copy-start(f32[1,128,512]{2,1,0:T(8,128)} %param.13) | copy-start | bytes 786436
  129.0 18.8 %copy-start.7 = (f32[1,128,512]{2,1,0:T(8,128)S(1)}, f32[1,128,512]{2,1,0:T(8,128)}, u32[]{:S(2)}) copy-start(f32[1,128,512]{2,1,0:T(8,128)} %param.14) | copy-start | bytes 786436
  129.8 16.8 %collective-permute-start.6 = (bf16[512,256]{1,0:T(8,128)(2,1)}, bf16[512,256]{1,0:T(8,128)(2,1)S(1)}, u32[]{:S(2)}, u32[]{:S(2)}) collective-permute-start(bf16[512,256]{1,0:T(8,128)(2,1)} %shard_map.130), channel_id=1, source_target_pairs={{256,0},{384,128},{257,1},{385,129},{258,2},{386,130},{259,3},{387... | collective-permute-start | bytes 786440 | tf_op jit(solution)/shard_map/ppermute | solution.py:53
  131.1 16.7 %all-to-all-start.4 = ((f32[32,1,128]{2,1,0:T(1,128)}), f32[32,1,128]{2,1,0:T(1,128)S(1)}, u32[]{:S(2)}, u32[]{:S(2)}) async-start(f32[32,1,128]{2,1,0:T(1,128)} %shard_map.129.refs_2_), calls=%async_computation.5 | async-start | bytes 32768 | tf_op jit(solution)/shard_map/all_to_all | solution.py:32
  148.8 37.0 %all-to-all-start.5 = ((bf16[16,128,256]{2,1,0:T(8,128)(2,1)}), bf16[16,128,256]{2,1,0:T(8,128)(2,1)S(1)}, u32[]{:S(2)}, u32[]{:S(2)}) async-start(bf16[16,128,256]{2,1,0:T(8,128)(2,1)} %shard_map.131.refs_5_), calls=%async_computation.6 | async-start | bytes 2097152 | tf_op jit(solution)/shard_map/all_to_all | solution.py:32
  180.0 4.5 %collective-permute-start.7 = (bf16[512,512]{1,0:T(8,128)(2,1)S(1)}, bf16[512,512]{1,0:T(8,128)(2,1)S(1)}, u32[]{:S(2)}, u32[]{:S(2)}) collective-permute-start(bf16[512,512]{1,0:T(8,128)(2,1)S(1)} %all_gather.7.refs_4_), channel_id=1, source_target_pairs={{0,1},{1,0},{2,3},{3,2},{4,5},{5,4},{6,7},{7,6},{8,9},{9,8},{10,11... | collective-permute-start | bytes 1572872 | tf_op jit(solution)/shard_map/ppermute | solution.py:48
  185.7 12.8 %all-to-all-start.6 = ((bf16[4,128,512]{2,1,0:T(8,128)(2,1)}), bf16[4,128,512]{2,1,0:T(8,128)(2,1)S(1)}, u32[]{:S(2)}, u32[]{:S(2)}) async-start(bf16[4,128,512]{2,1,0:T(8,128)(2,1)} %shard_map.134), calls=%async_computation.7 | async-start | bytes 1048576 | tf_op jit(solution)/shard_map/all_to_all | solution.py:32
Sparse Core Ops, SparseCore 0:
  68.4 41.0 reduce-scatter.1
